TPU v7x, 512 devices: a whole 4x4x16 slice. The times are simulated.
512 devices in a mesh: dp: 8 (over y, z_hi), ctx: 64 (over z_lo, x, core).
Axes of the slice: x: 4, y: 4, z: 16 (z_hi: 2, z_lo: 8; z = z_hi * 8 + z_lo), core: 2. Of those that a mesh axis runs over, the one named last changes fastest.
Arguments:
- values: bfloat16 [8, 4096, 8192], P('dp', None, 'ctx'), may hold values from -6 to 6
- grads: bfloat16 [8, 4096, 8192], P('dp', None, 'ctx'), may hold values from -6 to 6
- filter_taps: bfloat16 [4096, 8192], P('ctx', 'dp'), may hold values from -6 to 6
Outputs:
- conv_out: bfloat16 [8, 4096, 8192], P('dp', None, 'ctx')
- value_grads: bfloat16 [8, 4096, 8192], P('dp', None, 'ctx')
- filter_grads: float32 [4096, 8192], P('ctx', 'dp')
All inputs are finite; a program needn't handle non-finite values.
Results may differ from a plain program's by a relative error of at most 0.022.
Values may be sent and summed in bfloat16 or wider, within the bound.
No kernel may reach another device: no remote copies, remote signals or barrier semaphores. Data moves between devices by JAX's collectives and lax.ppermute only.
A program may use at most 128 MiB of HBM per device.

v0:
```python
import math

import jax
import jax.numpy as jnp
from jax import lax
from jax.sharding import PartitionSpec as P


def build_tables(slow, fast):
    total = slow * fast
    first = jnp.arange(slow // 2, dtype=jnp.int32)
    second = jnp.arange(slow, dtype=jnp.int32)
    inner = jnp.arange(fast, dtype=jnp.int32)
    coarse = (second[:, None] * first[None, :] % slow).astype(jnp.float32) * (2.0 * math.pi / slow)
    twist = (second[:, None] * inner[None, :] % total).astype(jnp.float32) * (2.0 * math.pi / total)
    fine = (inner[:, None] * inner[None, :] % fast).astype(jnp.float32) * (2.0 * math.pi / fast)
    slow_cos = jnp.cos(coarse).astype(jnp.bfloat16)
    slow_sin = jnp.sin(coarse).astype(jnp.bfloat16)
    slow_table = jnp.stack([slow_cos, -slow_sin], axis=0)
    twid_cos = jnp.cos(twist).astype(jnp.bfloat16)
    twid_sin = jnp.sin(twist).astype(jnp.bfloat16)
    fast_cos = jnp.cos(fine).astype(jnp.bfloat16)
    fast_sin = jnp.sin(fine).astype(jnp.bfloat16)
    fwd_real = jnp.stack([fast_cos, fast_sin], axis=0)
    fwd_imag = jnp.stack([-fast_sin, fast_cos], axis=0)
    fwd_table = jnp.stack([fwd_real, fwd_imag], axis=2)
    inv_real = jnp.stack([fast_cos, -fast_sin], axis=0)
    inv_imag = jnp.stack([fast_sin, fast_cos], axis=0)
    inv_table = jnp.stack([inv_real, inv_imag], axis=2)
    return (slow_table, twid_cos, twid_sin, fwd_table, inv_table)


def mix(form, left, right):
    return jnp.einsum(form, left, right, preferred_element_type=jnp.float32)


def forward_transform(signal, tables):
    slow_table, twid_cos, twid_sin, fwd_table, inv_table = tables
    rows = signal.shape[0]
    blocks = signal.reshape(rows, slow_table.shape[2], twid_cos.shape[1])
    section = mix("pca,hab->hcpb", slow_table, blocks)
    wr, wi = (twid_cos.astype(jnp.float32), twid_sin.astype(jnp.float32))
    part_real, part_imag = (section[:, :, 0], section[:, :, 1])
    twisted = jnp.stack(
        [part_real * wr + part_imag * wi, part_imag * wr - part_real * wi], axis=2
    ).astype(jnp.bfloat16)
    return mix("hcpb,pbqd->hcqd", twisted, fwd_table).astype(jnp.bfloat16)


def inverse_transform(spectrum, tables):
    slow_table, twid_cos, twid_sin, fwd_table, inv_table = tables
    rows = spectrum.shape[0]
    section = mix("hcqd,qdpb->hcpb", spectrum, inv_table)
    wr, wi = (twid_cos.astype(jnp.float32), twid_sin.astype(jnp.float32))
    part_real, part_imag = (section[:, :, 0], section[:, :, 1])
    twisted = jnp.stack(
        [part_real * wr - part_imag * wi, part_imag * wr + part_real * wi], axis=2
    ).astype(jnp.bfloat16)
    result = mix("pca,hcpb->hab", slow_table, twisted)
    return result.reshape(rows, -1)


def spectral_products(u_spec, g_spec, k_spec):
    ur, ui = (u_spec[:, :, 0].astype(jnp.float32), u_spec[:, :, 1].astype(jnp.float32))
    gr, gi = (g_spec[:, :, 0].astype(jnp.float32), g_spec[:, :, 1].astype(jnp.float32))
    kr, ki = (k_spec[:, :, 0].astype(jnp.float32), k_spec[:, :, 1].astype(jnp.float32))
    out_spec = jnp.stack([ur * kr - ui * ki, ur * ki + ui * kr], axis=2).astype(jnp.bfloat16)
    back_spec = jnp.stack([kr * gr + ki * gi, kr * gi - ki * gr], axis=2).astype(jnp.bfloat16)
    taps_spec = jnp.stack([ur * gr + ui * gi, ur * gi - ui * gr], axis=2).astype(jnp.bfloat16)
    return (out_spec, back_spec, taps_spec)


def in_blocks(func, arrays):
    rows = arrays[0].shape[0]
    width = math.gcd(rows, 8)
    count = rows // width
    stacked = tuple((item.reshape((count, width) + item.shape[1:]) for item in arrays))
    results = lax.map(func, stacked)
    return tuple((item.reshape((rows,) + item.shape[2:]) for item in results))


def local(values, grads, filter_taps):
    groups = lax.axis_size("ctx")
    chans = values.shape[1] // groups
    tok_local = values.shape[2]
    length = tok_local * groups
    fast = min(128, length)
    slow = 2 * length // fast
    tables = build_tables(slow, fast)
    factor = 1.0 / (2 * length * math.sqrt(length))

    def forward_both(pair):
        return (forward_transform(pair[0], tables), forward_transform(pair[1], tables))

    u_spec, g_spec = in_blocks(
        forward_both,
        (
            lax.all_to_all(
                values.reshape(groups, chans, tok_local),
                "ctx",
                split_axis=0,
                concat_axis=2,
                tiled=True,
            )[0],
            lax.all_to_all(
                grads.reshape(groups, chans, tok_local),
                "ctx",
                split_axis=0,
                concat_axis=2,
                tiled=True,
            )[0],
        ),
    )
    mine = lax.all_to_all(filter_taps, "dp", split_axis=0, concat_axis=1, tiled=True)
    own_spec = forward_transform(mine, tables)
    k_spec = lax.all_gather(own_spec, "dp", axis=0, tiled=True)

    def convolve_block(group):
        out_spec, back_spec, taps_spec = spectral_products(group[0], group[1], group[2])
        width = out_spec.shape[0]
        joined = (
            inverse_transform(jnp.concatenate([out_spec, back_spec, taps_spec], axis=0), tables)
            * factor
        )
        return (
            joined[:width].astype(jnp.bfloat16),
            joined[width : 2 * width].astype(jnp.bfloat16),
            joined[2 * width :],
        )

    conv_local, back_local, taps_local = in_blocks(convolve_block, (u_spec, g_spec, k_spec))
    conv_out, value_grads = (
        lax.all_to_all(
            conv_local.reshape(1, chans, length), "ctx", split_axis=2, concat_axis=1, tiled=True
        ),
        lax.all_to_all(
            back_local.reshape(1, chans, length), "ctx", split_axis=2, concat_axis=1, tiled=True
        ),
    )
    filter_grads = lax.psum_scatter(taps_local, "dp", scatter_dimension=1, tiled=True)
    return (conv_out, value_grads, filter_grads)


def solution(mesh):
    placed = (P("dp", None, "ctx"), P("dp", None, "ctx"), P("ctx", "dp"))
    return jax.shard_map(
        local,
        mesh=mesh,
        in_specs=placed,
        out_specs=(P("dp", None, "ctx"), P("dp", None, "ctx"), P("ctx", "dp")),
        check_vma=False,
    )
```

profile of v0, /device:TPU:1, one launch (start us, length us, event | category | flops | bytes accessed | tf_op | source)
XLA Modules:
  0.0 652.0 jit_solution(8818892959441516694)
XLA Ops:
  7.2 32.5 %all_to_all.82 = bf16[8,8,1024]{2,1,0:T(8,128)(2,1)S(1)} all-to-all(bf16[8,8,1024]{2,1,0:T(8,128)(2,1)} %bitcast.236), channel_id=1, replica_groups=mesh['dp'=8,'ctx'=64] {'dp'}, dimensions={0} | all-to-all | bytes 262144 | tf_op jit(solution)/shard_map/all_to_all | solution.py:114
  39.7 62.6 %all_to_all.83 = bf16[64,64,128]{2,1,0:T(8,128)(2,1)S(1)} all-to-all(bf16[64,64,128]{2,1,0:T(8,128)(2,1)} %bitcast.231), channel_id=1, replica_groups=mesh['dp'=8,'ctx'=64] {'ctx'}, dimensions={0} | all-to-all | bytes 2097152 | tf_op jit(solution)/shard_map/all_to_all | solution.py:98
  102.3 7.8 %all-to-all-start.1 = ((bf16[64,64,128]{2,1,0:T(8,128)(2,1)}), bf16[64,64,128]{2,1,0:T(8,128)(2,1)S(1)}, u32[]{:S(2)}, u32[]{:S(2)}) async-start(bf16[64,64,128]{2,1,0:T(8,128)(2,1)} %bitcast.232), calls=%async_computation.1 | async-start | bytes 2097152 | tf_op jit(solution)/shard_map/all_to_all | solution.py:105
  112.3 1.1 fusion.81
  113.4 1.7 copy.38
  115.1 2.3 reshape_squeeze.6
  117.4 66.7 %all-to-all-done.1 = bf16[64,64,128]{2,1,0:T(8,128)(2,1)S(1)} async-done(((bf16[64,64,128]{2,1,0:T(8,128)(2,1)}), bf16[64,64,128]{2,1,0:T(8,128)(2,1)S(1)}, u32[]{:S(2)}, u32[]{:S(2)}) %all-to-all-start.1) | async-done | bytes 1048608 | tf_op jit(solution)/shard_map/all_to_all | solution.py:105
  185.2 36.4 %while.30 = (s32[]{:T(128)}, bf16[8,8,128,2,128]{4,2,3,1,0:T(8,128)(2,1)}, bf16[8,8,128,2,128]{4,2,3,1,0:T(8,128)(2,1)}, bf16[8,8,8192]{2,1,0:T(8,128)(2,1)}, bf...) while((s32[]{:T(128)}, ...), condition=%wide.region_1.2_spmd.clone.clone, body=%wide.region_0.1_spmd.clone.clone.sunk | while | flops 340557824 | bytes 8717401 | solution.py:78
  185.3 1.0 dynamic-slice_bitcast_fusion.8
  187.5 1.2 fusion.133
  188.8 1.2 fusion.132
  189.9 0.9 dynamic-slice_bitcast_fusion.8
  192.1 1.2 fusion.133
  193.3 1.2 fusion.132
  194.4 0.9 dynamic-slice_bitcast_fusion.8
  196.6 1.2 fusion.133
  197.8 1.2 fusion.132
  199.0 0.9 dynamic-slice_bitcast_fusion.8
  201.2 1.2 fusion.133
  202.4 1.2 fusion.132
  203.5 0.9 dynamic-slice_bitcast_fusion.8
  205.7 1.2 fusion.133
  206.9 1.2 fusion.132
  208.0 0.9 dynamic-slice_bitcast_fusion.8
  210.2 1.2 fusion.133
  211.4 1.2 fusion.132
  214.7 1.2 fusion.133
  215.9 1.2 fusion.132
  219.2 1.2 fusion.133
  220.4 1.2 fusion.132
  221.6 85.0 %all-gather.2.cloned.1.call-done = bf16[64,128,2,128]{3,1,2,0:T(8,128)(2,1)} async-done(((bf16[8,128,2,128]{3,1,2,0:T(8,128)(2,1)}), bf16[64,128,2,128]{3,1,2,0:T(8,128)(2,1)}) %all-gather.2.cloned.1.call-update) | async-done | bytes 4194320 | tf_op jit(solution)/shard_map/all_gather | solution.py:116
  306.6 50.9 %while.31 = (s32[]{:T(128)}, bf16[8,8,8192]{2,1,0:T(8,128)(2,1)S(1)}, bf16[8,8,8192]{2,1,0:T(8,128)(2,1)}, f32[8,8,8192]{2,1,0:T(8,128)}, bf16[8,8,128,2,128]{4,...) while((s32[]{:T(128)}, ...), condition=%wide.region_3.4_spmd.clone.clone, body=%wide.region_2.3_spmd.clone.clone.sunk | while | flops 524189696 | bytes 23102576 | solution.py:78
  306.6 1.3 dynamic-slice_bitcast_fusion.9
  307.9 1.1 dynamic-slice_bitcast_fusion.10
  313.0 1.3 dynamic-slice_bitcast_fusion.9
  314.3 1.1 dynamic-slice_bitcast_fusion.10
  319.4 1.3 dynamic-slice_bitcast_fusion.9
  320.6 1.1 dynamic-slice_bitcast_fusion.10
  325.7 1.3 dynamic-slice_bitcast_fusion.9
  327.0 1.1 dynamic-slice_bitcast_fusion.10
  332.1 1.3 dynamic-slice_bitcast_fusion.9
  333.4 1.1 dynamic-slice_bitcast_fusion.10
  338.4 1.3 dynamic-slice_bitcast_fusion.9
  339.7 1.1 dynamic-slice_bitcast_fusion.10
  344.8 1.3 dynamic-slice_bitcast_fusion.9
  346.1 1.1 dynamic-slice_bitcast_fusion.10
  351.1 1.3 dynamic-slice_bitcast_fusion.9
  352.4 1.1 dynamic-slice_bitcast_fusion.10
  357.5 6.8 %copy.42 = bf16[1,64,8192]{1,0,2:T(2,128)(2,1)} copy(bf16[1,64,8192]{2,1,0:T(8,128)(2,1)S(1)} %bitcast.229) | data formatting | bytes 2097152 | tf_op jit(solution)/shard_map/reshape;reshape | solution.py:134
  364.8 45.2 %reduce = bf16[8192,64]{1,0:T(8,128)(2,1)S(1)} reduce(bf16[8192,1,64]{2,1,0:T(2,128)(2,1)} %bitcast.217, bf16[]{:T(256)} %broadcast.325), dimensions={1}, to_apply=%bitcast.160.reduce_sub_computation | reduce | bytes 2097154
  410.1 2.5 reshape.286
  412.6 6.8 %all-to-all-start.3 = ((bf16[64,2,4096]{2,1,0:T(2,128)(2,1)}), bf16[64,2,4096]{2,1,0:T(2,128)(2,1)S(1)}, u32[]{:S(2)}, u32[]{:S(2)}) async-start(bf16[64,2,4096]{2,1,0:T(2,128)(2,1)} %reshape.286), calls=%async_computation.3 | async-start | bytes 2097152 | tf_op jit(solution)/shard_map/all_to_all | solution.py:133
  419.4 9.2 %copy.45 = bf16[1,64,8192]{1,0,2:T(2,128)(2,1)} copy(bf16[1,64,8192]{2,1,0:T(8,128)(2,1)} %bitcast.230) | data formatting | bytes 2097152 | tf_op jit(solution)/shard_map/reshape;reshape | solution.py:137
  428.6 45.2 %reduce.1 = bf16[8192,64]{1,0:T(8,128)(2,1)S(1)} reduce(bf16[8192,1,64]{2,1,0:T(2,128)(2,1)} %bitcast.218, bf16[]{:T(256)} %broadcast.325), dimensions={1}, to_apply=%bitcast.162.reduce_sub_computation | reduce | bytes 2097154
  473.8 2.3 reshape.288
  476.1 13.2 %all-to-all-start.4 = ((bf16[64,2,4096]{2,1,0:T(2,128)(2,1)}), bf16[64,2,4096]{2,1,0:T(2,128)(2,1)S(1)}, u32[]{:S(2)}, u32[]{:S(2)}) async-start(bf16[64,2,4096]{2,1,0:T(2,128)(2,1)} %reshape.288), calls=%async_computation.4 | async-start | bytes 2097152 | tf_op jit(solution)/shard_map/all_to_all | solution.py:136
  490.0 7.0 %reshape.287 = bf16[8192,1,64]{2,1,0:T(2,128)(2,1)} reshape(bf16[64,2,4096]{2,1,0:T(2,128)(2,1)S(1)} %all-to-all-done.3) | data formatting | bytes 2097152
  497.0 8.2 %copy.43 = bf16[1,64,8192]{2,1,0:T(8,128)(2,1)S(1)} copy(bf16[1,64,8192]{1,0,2:T(2,128)(2,1)} %bitcast.219) | data formatting | bytes 2097152 | tf_op jit(solution)/shard_map/all_to_all | solution.py:133
  505.5 1.6 copy.44
  507.2 67.3 %all-to-all-done.4 = bf16[64,2,4096]{2,1,0:T(2,128)(2,1)S(1)} async-done(((bf16[64,2,4096]{2,1,0:T(2,128)(2,1)}), bf16[64,2,4096]{2,1,0:T(2,128)(2,1)S(1)}, u32[]{:S(2)}, u32[]{:S(2)}) %all-to-all-start.4) | async-done | bytes 1048608 | tf_op jit(solution)/shard_map/all_to_all | solution.py:136
  574.5 7.0 %reshape.289 = bf16[8192,1,64]{2,1,0:T(2,128)(2,1)} reshape(bf16[64,2,4096]{2,1,0:T(2,128)(2,1)S(1)} %all-to-all-done.4) | data formatting | bytes 2097152
  581.5 8.2 %copy.46 = bf16[1,64,8192]{2,1,0:T(8,128)(2,1)S(1)} copy(bf16[1,64,8192]{1,0,2:T(2,128)(2,1)} %bitcast.220) | data formatting | bytes 2097152 | tf_op jit(solution)/shard_map/all_to_all | solution.py:136
  590.0 1.6 copy.47
  591.7 53.5 %reduce-scatter.2.cloned.1.call-done = f32[64,1024]{1,0:T(8,128)} async-done(((f32[64,8192]{1,0:T(8,128)}), f32[64,1024]{1,0:T(8,128)}) %reduce-scatter.2.cloned.1.call-update) | async-done | bytes 262160 | tf_op jit(solution)/shard_map/reduce_scatter | solution.py:140
  (178 shorter events, 48.2 us)
Async XLA Ops:
  102.3 81.8 %all-to-all-start.1 = ((bf16[64,64,128]{2,1,0:T(8,128)(2,1)}), bf16[64,64,128]{2,1,0:T(8,128)(2,1)S(1)}, u32[]{:S(2)}, u32[]{:S(2)}) async-start(bf16[64,64,128]{2,1,0:T(8,128)(2,1)} %bitcast.232), calls=%async_computation.1 | async-start | bytes 2097152 | tf_op jit(solution)/shard_map/all_to_all | solution.py:105
  110.1 196.5 %all-gather.2.cloned.1.call-start = ((), (), s32[]{:S(2)}) async-start(), calls=%async_computation.6 | async-start | bytes 4718592 | tf_op jit(solution)/shard_map/all_gather | solution.py:116
  185.2 121.4 %copy-start = (bf16[8,8,8192]{2,1,0:T(8,128)(2,1)S(1)}, bf16[8,8,8192]{2,1,0:T(8,128)(2,1)}, u32[]{:S(2)}) copy-start(bf16[8,8,8192]{2,1,0:T(8,128)(2,1)} %custom-call.2) | copy-start | bytes 3145732
  412.6 63.5 %all-to-all-start.3 = ((bf16[64,2,4096]{2,1,0:T(2,128)(2,1)}), bf16[64,2,4096]{2,1,0:T(2,128)(2,1)S(1)}, u32[]{:S(2)}, u32[]{:S(2)}) async-start(bf16[64,2,4096]{2,1,0:T(2,128)(2,1)} %reshape.286), calls=%async_computation.3 | async-start | bytes 2097152 | tf_op jit(solution)/shard_map/all_to_all | solution.py:133
  476.1 98.4 %all-to-all-start.4 = ((bf16[64,2,4096]{2,1,0:T(2,128)(2,1)}), bf16[64,2,4096]{2,1,0:T(2,128)(2,1)S(1)}, u32[]{:S(2)}, u32[]{:S(2)}) async-start(bf16[64,2,4096]{2,1,0:T(2,128)(2,1)} %reshape.288), calls=%async_computation.4 | async-start | bytes 2097152 | tf_op jit(solution)/shard_map/all_to_all | solution.py:136
  489.3 155.9 %reduce-scatter.2.cloned.1.call-start = ((), (), s32[]{:S(2)}) async-start(), calls=%async_computation.7 | async-start | bytes 2359296 | tf_op jit(solution)/shard_map/reduce_scatter | solution.py:140
Sparse Core Ops, SparseCore 0:
  114.2 192.4 all-gather.1
  495.3 149.7 reduce-scatter.1
where the time goes:
time: 655 us; the launch traced here: 652 us
  waiting for transfers between devices  273 us (42%)
  other arithmetic  107 us (16%)
  local copies, waits for them, and re-layouts  100 us (15%)
  blocking collectives  95.1 us (15%)
  matrix products  33.1 us (5%)
  starting transfers between devices  27.9 us (4%)
  between operations  14.3 us (2%)
    unnamed x2, other arithmetic  90.4 us
    all_gather x1, waiting for transfers between devices, local(): k_spec = lax.all_gather(own_spec, 'dp', axis=0, tiled=True)  85 us
    all_to_all x1, waiting for transfers between devices, local(): lax.all_to_all(back_local.reshape(1, chans, length), 'ctx', split_axis=2,...  67.3 us
    all_to_all x1, waiting for transfers between devices, local(): lax.all_to_all(grads.reshape(groups, chans, tok_local), 'ctx', split_axis...  66.7 us
    all_to_all x1, blocking collectives, local(): lax.all_to_all(values.reshape(groups, chans, tok_local), 'ctx', split_axi...  62.6 us
    reduce_scatter x1, waiting for transfers between devices, local(): lax.psum_scatter(taps_local, 'dp', scatter_dimension=1, tiled=True)  53.5 us
    dot_general x50, matrix products, mix(): return jnp.einsum(form, left, right, preferred_element_type=jnp.float32)  33.1 us
    all_to_all x1, blocking collectives, local(): lax.all_to_all(filter_taps, 'dp', split_axis=0, concat_axis=1, tiled=True)  32.5 us
  transfers between devices with their start and end apart: 5, of which 4 were waited for; matrix products, arithmetic and copies ran while one was open for 21% of the time, Pallas kernels for 0%

commit v1 on v0

v1 whole, which is shorter than its diff:
```python
import functools
import math

import jax
import jax.numpy as jnp
import numpy as np
from jax import lax
from jax.experimental import pallas as pl
from jax.experimental.pallas import tpu as pltpu
from jax.sharding import Mesh, PartitionSpec as P

SLOW = 128
FAST = 128
TOTAL = SLOW * FAST
HALF = SLOW // 2
ROWS = 80
FACTOR = 1.0 / (TOTAL * math.sqrt(TOTAL // 2))
BLOCK = 8


def tables():
    bf16 = jnp.bfloat16

    def angles(left, right, period):
        steps = (left[:, None] * right[None, :]) % period
        return steps.astype(np.float32) * np.float32(2.0 * math.pi / period)

    rows, first, inner = np.arange(ROWS), np.arange(HALF), np.arange(FAST)
    coarse = angles(rows, first, SLOW)
    twist = angles(rows, inner, TOTAL)
    fine = angles(inner, inner, FAST)
    cast = lambda item: item.astype(bf16)
    slow_cos, slow_sin = cast(np.cos(coarse)), cast(np.sin(coarse))
    twid_cos, twid_sin = cast(np.cos(twist)), cast(np.sin(twist))
    fast_cos, fast_sin = cast(np.cos(fine)), cast(np.sin(fine))
    weight = np.where(rows > HALF, 0.0, np.where(rows % HALF == 0, 1.0, 2.0))
    weight = weight.astype(np.float32)[:, None]
    slow_fwd = np.concatenate([slow_cos, -slow_sin], axis=0)
    slow_inv = np.concatenate(
        [cast(slow_cos.astype(np.float32) * weight), cast(-slow_sin.astype(np.float32) * weight)], axis=0
    ).T
    fast_fwd = np.block([[fast_cos, -fast_sin], [fast_sin, fast_cos]])
    fast_inv = np.block([[fast_cos, fast_sin], [-fast_sin, fast_cos]])
    twid = np.stack([twid_cos, twid_sin]).astype(np.float32)
    return tuple(map(np.ascontiguousarray, (slow_fwd, slow_inv, fast_fwd, fast_inv, twid)))


def dot(left, right):
    return jnp.dot(left, right, preferred_element_type=jnp.float32)


def forward(signal, slow_fwd, twid, fast_fwd):
    lanes = jnp.concatenate([signal[j] for j in range(BLOCK)], axis=1)
    section = dot(slow_fwd[...], lanes)
    wr, wi = twid[0], twid[1]
    parts = []
    for j in range(BLOCK):
        sr = section[:ROWS, j * FAST : (j + 1) * FAST]
        si = section[ROWS:, j * FAST : (j + 1) * FAST]
        parts.append(jnp.concatenate([sr * wr + si * wi, si * wr - sr * wi], axis=1).astype(jnp.bfloat16))
    return dot(jnp.concatenate(parts, axis=0), fast_fwd[...]).astype(jnp.bfloat16)


def inverse(spectrum, out, slow_inv, twid, fast_inv):
    section = dot(spectrum, fast_inv[...])
    wr, wi = twid[0], twid[1]
    parts = []
    for j in range(BLOCK):
        br = section[j * ROWS : (j + 1) * ROWS, :FAST]
        bi = section[j * ROWS : (j + 1) * ROWS, FAST:]
        parts.append(jnp.concatenate([br * wr - bi * wi, bi * wr + br * wi], axis=0).astype(jnp.bfloat16))
    result = dot(slow_inv[...], jnp.concatenate(parts, axis=1)) * FACTOR
    for j in range(BLOCK):
        out[j] = result[:, j * FAST : (j + 1) * FAST].astype(out.dtype)


def halves(spectrum):
    return spectrum[:, :FAST].astype(jnp.float32), spectrum[:, FAST:].astype(jnp.float32)


def joined(real, imag):
    return jnp.concatenate([real, imag], axis=1).astype(jnp.bfloat16)


def conv_kernel(values, taps, slow_fwd, slow_inv, fast_fwd, fast_inv, twid, u_out, k_out, conv):
    u_spec = forward(values, slow_fwd, twid, fast_fwd)
    k_spec = forward(taps, slow_fwd, twid, fast_fwd)
    u_out[...] = u_spec
    k_out[...] = k_spec
    (ur, ui), (kr, ki) = halves(u_spec), halves(k_spec)
    inverse(joined(ur * kr - ui * ki, ur * ki + ui * kr), conv, slow_inv, twid, fast_inv)


def taps_kernel(grads, u_in, slow_fwd, slow_inv, fast_fwd, fast_inv, twid, z_out, taps):
    z_spec = forward(grads, slow_fwd, twid, fast_fwd)
    z_out[...] = z_spec
    (ur, ui), (zr, zi) = halves(u_in[...]), halves(z_spec)
    inverse(joined(ur * zr + ui * zi, ur * zi - ui * zr), taps, slow_inv, twid, fast_inv)


def back_kernel(z_in, k_in, slow_fwd, slow_inv, fast_fwd, fast_inv, twid, back):
    (zr, zi), (kr, ki) = halves(z_in[...]), halves(k_in[...])
    inverse(joined(kr * zr + ki * zi, kr * zi - ki * zr), back, slow_inv, twid, fast_inv)


def call(kernel, signals, outs, consts, flops):
    chans = max(item.shape[0] for item, kind in signals if kind == "x") if any(
        kind == "x" for _, kind in signals
    ) else signals[0][0].shape[0] // ROWS
    specs = {
        "x": pl.BlockSpec((BLOCK, HALF, FAST), lambda i: (i, 0, 0)),
        "s": pl.BlockSpec((BLOCK * ROWS, 2 * FAST), lambda i: (i, 0)),
    }
    shapes = {
        "x": jax.ShapeDtypeStruct((chans, HALF, FAST), jnp.bfloat16),
        "s": jax.ShapeDtypeStruct((chans * ROWS, 2 * FAST), jnp.bfloat16),
    }
    whole = [pl.BlockSpec(item.shape, functools.partial(lambda n, i: (0,) * n, item.ndim)) for item in consts]
    moved = sum(item.size * 2 for item, _ in signals) + sum(shapes[kind].size * 2 for kind in outs)
    return pl.pallas_call(
        kernel,
        grid=(chans // BLOCK,),
        in_specs=[specs[kind] for _, kind in signals] + whole,
        out_specs=[specs[kind] for kind in outs],
        out_shape=[shapes[kind] for kind in outs],
        compiler_params=pltpu.CompilerParams(vmem_limit_bytes=40 * 1024 * 1024),
        cost_estimate=pl.CostEstimate(flops=flops * chans, bytes_accessed=moved, transcendentals=0),
    )(*[item for item, _ in signals], *consts)


def exchange(item, axis):
    return lax.ppermute(item, axis, [(0, 1), (1, 0)])


def local(values, grads, filter_taps):
    ctx = ("zl", "x", "c")
    groups = lax.axis_size(ctx)
    chans = values.shape[1] // groups
    consts = tuple(jnp.asarray(item) for item in tables())
    high = lax.axis_index("zh")
    row = lax.axis_index("y")
    n_row = lax.axis_size("y")
    wide = filter_taps.shape[1]

    def inward(item):
        moved = lax.all_to_all(item.reshape(groups, chans, FAST), ctx, split_axis=0, concat_axis=0, tiled=True)
        return moved.transpose(1, 0, 2)

    def outward(item):
        moved = lax.all_to_all(item.transpose(1, 0, 2), ctx, split_axis=0, concat_axis=0, tiled=True)
        return moved.reshape(1, groups * chans, FAST)

    other = exchange(filter_taps, "zh")
    pair = jnp.stack([jnp.where(high == 0, filter_taps, other), jnp.where(high == 0, other, filter_taps)])
    gathered = lax.all_gather(pair, "y", axis=0, tiled=True)
    taps = gathered.transpose(1, 0, 2).reshape(chans, HALF, FAST)

    v_mine = inward(values)
    g_mine = inward(grads)
    fft = 2 * 2 * ROWS * FAST * (HALF + 2 * FAST)
    u_spec, k_spec, conv = call(conv_kernel, [(v_mine, "x"), (taps, "x")], "ssx", consts, 3 * fft)
    conv_out = outward(conv)
    z_spec, terms = call(taps_kernel, [(g_mine, "x"), (u_spec, "s")], "sx", consts, 2 * fft)
    (back,) = call(back_kernel, [(z_spec, "s"), (k_spec, "s")], "x", consts, fft)
    value_grads = outward(back)

    parts = terms.reshape(chans, n_row, 2, wide).transpose(1, 2, 0, 3)
    total = lax.dynamic_index_in_dim(parts, row, 0, keepdims=False).astype(jnp.float32)
    for step in range(1, n_row):
        block = lax.dynamic_index_in_dim(parts, (row + step) % n_row, 0, keepdims=False)
        arrived = lax.ppermute(block, "y", [(i, (i + step) % n_row) for i in range(n_row)])
        total = total + arrived.astype(jnp.float32)
    mine = jnp.where(high == 0, total[0], total[1])
    sent = jnp.where(high == 0, total[1], total[0]).astype(jnp.bfloat16)
    filter_grads = mine + exchange(sent, "zh").astype(jnp.float32)
    return conv_out, value_grads, filter_grads


def solution(mesh):
    fine = Mesh(mesh.devices.reshape(4, 2, 8, 4, 2), ("y", "zh", "zl", "x", "c"))
    dp, ctx = ("y", "zh"), ("zl", "x", "c")
    tokens = P(dp, None, ctx)
    return jax.shard_map(
        local,
        mesh=fine,
        in_specs=(tokens, tokens, P(ctx, dp)),
        out_specs=(tokens, tokens, P(ctx, dp)),
        check_vma=False,
    )
```

time: 655 us -> 336 us (0.51)
  waiting for transfers between devices: 273 us -> 163 us
  other arithmetic: 107 us -> 1.69 us
  local copies, waits for them, and re-layouts: 100 us -> 18.2 us
  matrix products: 33.1 us -> 0 us
  blocking collectives: 95.1 us -> 68.6 us
  starting transfers between devices: 27.9 us -> 51.9 us
  Pallas kernels: 0 us -> 17.3 us
    unnamed x2 -> x0, other arithmetic: 90.4 us -> none
    all_to_all x3, waiting for transfers between devices: 134 us -> 60.6 us  [the longest x2 60.6 us: outward(): lax.all_to_all(item.transpose(1, 0, 2), ctx, split_axis=0, concat_axis=0,...]
    reduce_scatter x1 -> x0, waiting for transfers between devices: 53.5 us -> none  [local(): lax.psum_scatter(taps_local, 'dp', scatter_dimension=1, tiled=True)]
    ppermute x0 -> x5, waiting for transfers between devices: none -> 46.1 us  [the longest x2 33.9 us: exchange(): return lax.ppermute(item, axis, [(0, 1), (1, 0)])]
    dot_general x50 -> x0, matrix products: 33.1 us -> none  [mix(): return jnp.einsum(form, left, right, preferred_element_type=jnp.float32)]
    all_gather x1, waiting for transfers between devices: 85 us -> 56.4 us  [local(): gathered = lax.all_gather(pair, 'y', axis=0, tiled=True)]
    all_to_all x2 -> x1, blocking collectives: 95.1 us -> 68.6 us  [inward(): lax.all_to_all(item.reshape(groups, chans, FAST), ctx, split_axis=0, conc...]
    ppermute x0 -> x5, starting transfers between devices: none -> 21.3 us  [the longest x2 13 us: exchange(): return lax.ppermute(item, axis, [(0, 1), (1, 0)])]
  transfers between devices with their start and end apart: 5 -> 9, of which waited for: 4 -> 8; matrix products, arithmetic and copies ran while one was open for 21% -> 4% of each run, Pallas kernels for 0% -> 5%
where the time goes in v1:
time: 336 us; the launch traced here: 335 us
  waiting for transfers between devices  163 us (49%)
  blocking collectives  68.6 us (20%)
  starting transfers between devices  51.9 us (15%)
  local copies, waits for them, and re-layouts  18.2 us (5%)
  Pallas kernels  17.3 us (5%)
  between operations  14.4 us (4%)
    all_to_all x1, blocking collectives, inward(): lax.all_to_all(item.reshape(groups, chans, FAST), ctx, split_axis=0, conc...  68.6 us
    all_to_all x2, waiting for transfers between devices, outward(): lax.all_to_all(item.transpose(1, 0, 2), ctx, split_axis=0, concat_axis=0,...  60.6 us
    all_gather x1, waiting for transfers between devices, local(): gathered = lax.all_gather(pair, 'y', axis=0, tiled=True)  56.4 us
    ppermute x2, waiting for transfers between devices, exchange(): return lax.ppermute(item, axis, [(0, 1), (1, 0)])  33.9 us
    all_to_all x2, starting transfers between devices, outward(): lax.all_to_all(item.transpose(1, 0, 2), ctx, split_axis=0, concat_axis=0,...  22.5 us
    pallas_call x3, Pallas kernels, call(): pl.pallas_call(kernel, grid=(chans // BLOCK,), in_specs=[specs[kind] for...  17.3 us
    ppermute x2, starting transfers between devices, exchange(): return lax.ppermute(item, axis, [(0, 1), (1, 0)])  13 us
    ppermute x3, waiting for transfers between devices, local(): lax.ppermute(block, 'y', [(i, (i + step) % n_row) for i in range(n_row)])  12.2 us
  transfers between devices with their start and end apart: 9, of which 8 were waited for; matrix products, arithmetic and copies ran while one was open for 4% of the time, Pallas kernels for 5%

profile of v1, /device:TPU:1, one launch (start us, length us, event | category | flops | bytes accessed | tf_op | source)
XLA Modules:
  0.0 335.3 jit_solution(15833778543754453251)
XLA Ops:
  7.2 0.0 copy-start.10
  7.2 68.6 %all_to_all.20 = bf16[64,64,128]{2,1,0:T(8,128)(2,1)S(1)} all-to-all(bf16[64,64,128]{2,1,0:T(8,128)(2,1)} %bitcast.49), channel_id=1, replica_groups=mesh['y'=4,'zh'=2,'zl'=8,'x'=4,'c'=2] {'zl','x','c'}, dimensions={0} | all-to-all | bytes 2097152 | tf_op jit(solution)/shard_map/all_to_all | solution.py:146
  75.8 8.0 %all-to-all-start.2 = ((bf16[64,64,128]{2,1,0:T(8,128)(2,1)}), bf16[64,64,128]{2,1,0:T(8,128)(2,1)}, u32[]{:S(2)}, u32[]{:S(2)}) async-start(bf16[64,64,128]{2,1,0:T(8,128)(2,1)} %bitcast.50), calls=%async_computation.2 | async-start | bytes 2097152 | tf_op jit(solution)/shard_map/all_to_all | solution.py:146
  83.8 0.0 all-gather.2.cloned.1.call-start
  83.9 0.0 copy-done.10
  83.9 7.9 %collective-permute-start = (bf16[64,1024]{1,0:T(8,128)(2,1)S(1)}, bf16[64,1024]{1,0:T(8,128)(2,1)S(1)}, u32[]{:S(2)}, u32[]{:S(2)}) collective-permute-start(bf16[64,1024]{1,0:T(8,128)(2,1)S(1)} %copy-done.10), channel_id=1, source_target_pairs={{0,64},{64,0},{1,65},{65,1},{2,66},{66,2},{3,67},{67,3},{4,68},{68... | collective-permute-start | bytes 393224 | tf_op jit(solution)/shard_map/ppermute | solution.py:132
  91.9 23.7 %collective-permute-done = bf16[64,1024]{1,0:T(8,128)(2,1)S(1)} collective-permute-done((bf16[64,1024]{1,0:T(8,128)(2,1)S(1)}, bf16[64,1024]{1,0:T(8,128)(2,1)S(1)}, u32[]{:S(2)}, u32[]{:S(2)}) %collective-permute-start) | collective-permute-done | bytes 131104 | tf_op jit(solution)/shard_map/ppermute | solution.py:132
  115.6 0.7 pad_maximum_fusion
  116.4 0.0 all-gather.2.cloned.1.call-update
  116.4 56.4 %all-gather.2.cloned.1.call-done = bf16[8,64,1024]{2,1,0:T(8,128)(2,1)} async-done(((bf16[2,64,1024]{2,1,0:T(8,128)(2,1)}), bf16[8,64,1024]{2,1,0:T(8,128)(2,1)}) %all-gather.2.cloned.1.call-update) | async-done | bytes 1048592 | tf_op jit(solution)/shard_map/all_gather | solution.py:155
  172.8 1.8 copy.26
  174.6 0.0 copy-start.3
  174.6 0.0 copy-start.4
  174.6 0.0 copy-start.5
  174.7 0.0 copy-start.6
  174.7 0.0 copy-start.7
  174.7 1.3 reshape.32.taps
  176.0 0.7 copy.45
  176.6 0.0 copy-done.3
  176.6 0.0 copy-done.4
  176.7 0.0 copy-done.5
  176.7 0.0 copy-done.6
  176.7 0.0 copy-done.7
  176.7 0.0 copy-start.2
  176.7 1.2 copy-done.2
  177.9 7.5 %shard_map.103 = (bf16[5120,256]{1,0:T(8,128)(2,1)S(1)}, bf16[5120,256]{1,0:T(8,128)(2,1)S(1)}, bf16[64,64,128]{2,1,0:T(8,128)(2,1)S(1)}) custom-call(bf16[64,64,128]{2,1,0:T(8,128)(2,1)S(1)} %bitcast.45, bf16[64,64,128]{2,1,0:T(8,128)(2,1)S(1)} %copy-done.2, bf16[160,64]{1,0:T(8,128)(2,1)S(1)} %copy-done.6, bf16[64,160]{1,0:T(8,128)(2,1)S(1)} %copy-done.7, ...), custom_call_target="tpu_custom_call" | custom-call | flops 2516582400 | bytes 8388608 | tf_op jit(solution)/shard_map/pallas_call | solution.py:120
  185.4 0.0 copy-start.8
  185.4 1.5 copy-done.8
  186.9 1.6 copy.27
  188.6 0.0 all-to-all-done.2
  188.6 14.7 %all-to-all-start.1 = ((bf16[64,64,128]{2,1,0:T(8,128)(2,1)}), bf16[64,64,128]{2,1,0:T(8,128)(2,1)}, u32[]{:S(2)}, u32[]{:S(2)}) async-start(bf16[64,64,128]{2,1,0:T(8,128)(2,1)} %copy.27), calls=%async_computation.1 | async-start | bytes 2097152 | tf_op jit(solution)/shard_map/all_to_all | solution.py:150
  203.3 1.9 copy.44
  205.2 0.0 copy-start.9
  205.2 1.7 copy-done.9
  206.9 6.0 %shard_map.104 = (bf16[5120,256]{1,0:T(8,128)(2,1)S(1)}, bf16[64,64,128]{2,1,0:T(8,128)(2,1)S(1)}) custom-call(bf16[64,64,128]{2,1,0:T(8,128)(2,1)S(1)} %bitcast.47, bf16[5120,256]{1,0:T(8,128)(2,1)S(1)} %copy-done.9, bf16[160,64]{1,0:T(8,128)(2,1)S(1)} %copy-done.6, bf16[64,160]{1,0:T(8,128)(2,1)S(1)} %copy-done.7, bf16[256,256]{1,0:T(8,128)(2,1)S(1)} %copy-done.3, ...), custom_call_target="tpu_custom_call" | custom-call | flops 1677721600 | bytes 7340032 | tf_op jit(solution)/shard_map/pallas_call | solution.py:120
  213.0 0.0 copy-start
  213.0 3.7 %shard_map.105 = bf16[64,64,128]{2,1,0:T(8,128)(2,1)S(1)} custom-call(bf16[5120,256]{1,0:T(8,128)(2,1)S(1)} %get-tuple-element.10.z_in, bf16[5120,256]{1,0:T(8,128)(2,1)S(1)} %get-tuple-element.11.k_in, bf16[160,64]{1,0:T(8,128)(2,1)S(1)} %copy-done.6, bf16[64,160]{1,0:T(8,128)(2,1)S(1)} %copy-done.7, bf16[256,256]{1,0:T(8,128)(2,1)S(1)} %copy-done.3, ...), custom_call_target="tpu_custom_call" | custom-call | flops 838860800 | bytes 6291456 | tf_op jit(solution)/shard_map/pallas_call | solution.py:120
  216.7 0.0 copy-done
  216.8 0.0 copy-start.1
  216.8 1.6 copy.29
  218.4 36.3 %all-to-all-done.1 = bf16[64,64,128]{2,1,0:T(8,128)(2,1)} async-done(((bf16[64,64,128]{2,1,0:T(8,128)(2,1)}), bf16[64,64,128]{2,1,0:T(8,128)(2,1)}, u32[]{:S(2)}, u32[]{:S(2)}) %all-to-all-start.1) | async-done | bytes 1048608 | tf_op jit(solution)/shard_map/all_to_all | solution.py:150
  254.7 7.8 %all-to-all-start.3 = ((bf16[64,64,128]{2,1,0:T(8,128)(2,1)}), bf16[64,64,128]{2,1,0:T(8,128)(2,1)S(1)}, u32[]{:S(2)}, u32[]{:S(2)}) async-start(bf16[64,64,128]{2,1,0:T(8,128)(2,1)} %copy.29), calls=%async_computation.3 | async-start | bytes 2097152 | tf_op jit(solution)/shard_map/all_to_all | solution.py:150
  262.6 0.0 copy-done.1
  262.6 0.3 reshape.36
  262.9 1.0 constant_dynamic-slice_fusion.3
  263.9 3.4 %collective-permute-start.3 = (bf16[2,64,1024]{2,1,0:T(8,128)(2,1)S(1)}, bf16[2,64,1024]{2,1,0:T(8,128)(2,1)S(1)}, u32[]{:S(2)}, u32[]{:S(2)}) collective-permute-start(bf16[2,64,1024]{2,1,0:T(8,128)(2,1)S(1)} %bitcast.52), channel_id=1, source_target_pairs={{0,384},{128,0},{256,128},{384,256},{1,385},{129,1},{257,129},{385... | collective-permute-start | bytes 786440 | tf_op jit(solution)/shard_map/ppermute | solution.py:171
  267.4 2.5 collective-permute-start.2
  270.0 2.5 collective-permute-start.1
  272.4 0.8 collective-permute-done.3
  273.3 4.7 %collective-permute-done.2 = bf16[2,64,1024]{2,1,0:T(8,128)(2,1)S(1)} collective-permute-done((bf16[2,64,1024]{2,1,0:T(8,128)(2,1)S(1)}, bf16[2,64,1024]{2,1,0:T(8,128)(2,1)S(1)}, u32[]{:S(2)}, u32[]{:S(2)}) %collective-permute-start.2) | collective-permute-done | bytes 262176 | tf_op jit(solution)/shard_map/ppermute | solution.py:171
  277.9 6.7 %collective-permute-done.1 = bf16[2,64,1024]{2,1,0:T(8,128)(2,1)S(1)} collective-permute-done((bf16[2,64,1024]{2,1,0:T(8,128)(2,1)S(1)}, bf16[2,64,1024]{2,1,0:T(8,128)(2,1)S(1)}, u32[]{:S(2)}, u32[]{:S(2)}) %collective-permute-start.1) | collective-permute-done | bytes 262176 | tf_op jit(solution)/shard_map/ppermute | solution.py:171
  284.6 0.2 fusion.1
  284.9 5.0 %collective-permute-start.4 = (bf16[64,1024]{1,0:T(8,128)(2,1)S(1)}, bf16[64,1024]{1,0:T(8,128)(2,1)S(1)}, u32[]{:S(2)}, u32[]{:S(2)}) collective-permute-start(bf16[64,1024]{1,0:T(8,128)(2,1)S(1)} %fusion.2), channel_id=1, source_target_pairs={{0,64},{64,0},{1,65},{65,1},{2,66},{66,2},{3,67},{67,3},{4,68},{68... | collective-permute-start | bytes 393224 | tf_op jit(solution)/shard_map/ppermute | solution.py:132
  289.9 10.2 %collective-permute-done.4 = bf16[64,1024]{1,0:T(8,128)(2,1)S(1)} collective-permute-done((bf16[64,1024]{1,0:T(8,128)(2,1)S(1)}, bf16[64,1024]{1,0:T(8,128)(2,1)S(1)}, u32[]{:S(2)}, u32[]{:S(2)}) %collective-permute-start.4) | collective-permute-done | bytes 131104 | tf_op jit(solution)/shard_map/ppermute | solution.py:132
  300.1 0.7 bitcast_add_fusion.1
  300.8 24.4 %all-to-all-done.3 = bf16[64,64,128]{2,1,0:T(8,128)(2,1)S(1)} async-done(((bf16[64,64,128]{2,1,0:T(8,128)(2,1)}), bf16[64,64,128]{2,1,0:T(8,128)(2,1)S(1)}, u32[]{:S(2)}, u32[]{:S(2)}) %all-to-all-start.3) | async-done | bytes 1048608 | tf_op jit(solution)/shard_map/all_to_all | solution.py:150
  325.2 2.3 copy.51
  327.5 1.0 copy.52
  (5 shorter events, 0.2 us)
Async XLA Ops:
  7.2 76.7 %copy-start.10 = (bf16[64,1024]{1,0:T(8,128)(2,1)S(1)}, bf16[64,1024]{1,0:T(8,128)(2,1)}, u32[]{:S(2)}) copy-start(bf16[64,1024]{1,0:T(8,128)(2,1)} %param.10) | copy-start | bytes 393220
  75.8 112.7 %all-to-all-start.2 = ((bf16[64,64,128]{2,1,0:T(8,128)(2,1)}), bf16[64,64,128]{2,1,0:T(8,128)(2,1)}, u32[]{:S(2)}, u32[]{:S(2)}) async-start(bf16[64,64,128]{2,1,0:T(8,128)(2,1)} %bitcast.50), calls=%async_computation.2 | async-start | bytes 2097152 | tf_op jit(solution)/shard_map/all_to_all | solution.py:146
  83.8 89.0 %all-gather.2.cloned.1.call-start = ((), (), s32[]{:S(2)}) async-start(), calls=%async_computation.4 | async-start | bytes 1310720 | tf_op jit(solution)/shard_map/all_gather | solution.py:155
  83.9 31.7 %collective-permute-start = (bf16[64,1024]{1,0:T(8,128)(2,1)S(1)}, bf16[64,1024]{1,0:T(8,128)(2,1)S(1)}, u32[]{:S(2)}, u32[]{:S(2)}) collective-permute-start(bf16[64,1024]{1,0:T(8,128)(2,1)S(1)} %copy-done.10), channel_id=1, source_target_pairs={{0,64},{64,0},{1,65},{65,1},{2,66},{66,2},{3,67},{67,3},{4,68},{68... | collective-permute-start | bytes 393224 | tf_op jit(solution)/shard_map/ppermute | solution.py:132
  174.6 2.0 copy-start.3
  174.6 2.0 copy-start.4
  174.6 2.0 copy-start.5
  174.7 2.0 copy-start.6
  174.7 2.0 copy-start.7
  176.7 1.2 copy-start.2
  185.4 1.5 copy-start.8
  188.6 66.1 %all-to-all-start.1 = ((bf16[64,64,128]{2,1,0:T(8,128)(2,1)}), bf16[64,64,128]{2,1,0:T(8,128)(2,1)}, u32[]{:S(2)}, u32[]{:S(2)}) async-start(bf16[64,64,128]{2,1,0:T(8,128)(2,1)} %copy.27), calls=%async_computation.1 | async-start | bytes 2097152 | tf_op jit(solution)/shard_map/all_to_all | solution.py:150
  205.2 1.7 copy-start.9
  213.0 3.7 %copy-start = (bf16[64,64,128]{2,1,0:T(8,128)(2,1)}, bf16[64,64,128]{2,1,0:T(8,128)(2,1)S(1)}, u32[]{:S(2)}) copy-start(bf16[64,64,128]{2,1,0:T(8,128)(2,1)S(1)} %get-tuple-element.12) | copy-start | bytes 3145732
  216.8 45.8 %copy-start.1 = (bf16[64,64,128]{2,1,0:T(8,128)(2,1)S(1)}, bf16[64,64,128]{2,1,0:T(8,128)(2,1)}, u32[]{:S(2)}) copy-start(bf16[64,64,128]{2,1,0:T(8,128)(2,1)} %copy-done) | copy-start | bytes 3145732
  254.7 70.5 %all-to-all-start.3 = ((bf16[64,64,128]{2,1,0:T(8,128)(2,1)}), bf16[64,64,128]{2,1,0:T(8,128)(2,1)S(1)}, u32[]{:S(2)}, u32[]{:S(2)}) async-start(bf16[64,64,128]{2,1,0:T(8,128)(2,1)} %copy.29), calls=%async_computation.3 | async-start | bytes 2097152 | tf_op jit(solution)/shard_map/all_to_all | solution.py:150
  263.9 9.3 %collective-permute-start.3 = (bf16[2,64,1024]{2,1,0:T(8,128)(2,1)S(1)}, bf16[2,64,1024]{2,1,0:T(8,128)(2,1)S(1)}, u32[]{:S(2)}, u32[]{:S(2)}) collective-permute-start(bf16[2,64,1024]{2,1,0:T(8,128)(2,1)S(1)} %bitcast.52), channel_id=1, source_target_pairs={{0,384},{128,0},{256,128},{384,256},{1,385},{129,1},{257,129},{385... | collective-permute-start | bytes 786440 | tf_op jit(solution)/shard_map/ppermute | solution.py:171
  267.4 10.5 %collective-permute-start.2 = (bf16[2,64,1024]{2,1,0:T(8,128)(2,1)S(1)}, bf16[2,64,1024]{2,1,0:T(8,128)(2,1)S(1)}, u32[]{:S(2)}, u32[]{:S(2)}) collective-permute-start(bf16[2,64,1024]{2,1,0:T(8,128)(2,1)S(1)} %bitcast.53), channel_id=1, source_target_pairs={{0,256},{128,384},{256,0},{384,128},{1,257},{129,385},{257,1},{385... | collective-permute-start | bytes 786440 | tf_op jit(solution)/shard_map/ppermute | solution.py:171
  270.0 14.7 %collective-permute-start.1 = (bf16[2,64,1024]{2,1,0:T(8,128)(2,1)S(1)}, bf16[2,64,1024]{2,1,0:T(8,128)(2,1)S(1)}, u32[]{:S(2)}, u32[]{:S(2)}) collective-permute-start(bf16[2,64,1024]{2,1,0:T(8,128)(2,1)S(1)} %bitcast.54), channel_id=1, source_target_pairs={{0,128},{128,256},{256,384},{384,0},{1,129},{129,257},{257,385},{3... | collective-permute-start | bytes 786440 | tf_op jit(solution)/shard_map/ppermute | solution.py:171
  284.9 15.2 %collective-permute-start.4 = (bf16[64,1024]{1,0:T(8,128)(2,1)S(1)}, bf16[64,1024]{1,0:T(8,128)(2,1)S(1)}, u32[]{:S(2)}, u32[]{:S(2)}) collective-permute-start(bf16[64,1024]{1,0:T(8,128)(2,1)S(1)} %fusion.2), channel_id=1, source_target_pairs={{0,64},{64,0},{1,65},{65,1},{2,66},{66,2},{3,67},{67,3},{4,68},{68... | collective-permute-start | bytes 393224 | tf_op jit(solution)/shard_map/ppermute | solution.py:132
Sparse Core Ops, SparseCore 0:
  116.5 56.2 all-gather.1

commit v2 on v1

v2 whole, which is shorter than its diff:
```python
import functools
import math

import jax
import jax.numpy as jnp
import numpy as np
from jax import lax
from jax.experimental import pallas as pl
from jax.experimental.pallas import tpu as pltpu
from jax.sharding import Mesh, PartitionSpec as P

SLOW = 128
FAST = 128
TOTAL = SLOW * FAST
HALF = SLOW // 2
ROWS = 80
FACTOR = 1.0 / (TOTAL * math.sqrt(TOTAL // 2))
NEAR = HALF // 2
RING = 4
QUARTER = HALF // RING
BLOCK = 8


def tables():
    bf16 = jnp.bfloat16

    def angles(left, right, period):
        steps = (left[:, None] * right[None, :]) % period
        return steps.astype(np.float32) * np.float32(2.0 * math.pi / period)

    rows, first, inner = np.arange(ROWS), np.arange(HALF), np.arange(FAST)
    coarse = angles(rows, first, SLOW)
    twist = angles(rows, inner, TOTAL)
    fine = angles(inner, inner, FAST)
    cast = lambda item: item.astype(bf16)
    slow_cos, slow_sin = cast(np.cos(coarse)), cast(np.sin(coarse))
    twid_cos, twid_sin = cast(np.cos(twist)), cast(np.sin(twist))
    fast_cos, fast_sin = cast(np.cos(fine)), cast(np.sin(fine))
    weight = np.where(rows > HALF, 0.0, np.where(rows % HALF == 0, 1.0, 2.0))
    weight = weight.astype(np.float32)[:, None]
    slow_fwd = np.concatenate([slow_cos, -slow_sin], axis=0)
    slow_inv = np.concatenate(
        [cast(slow_cos.astype(np.float32) * weight), cast(-slow_sin.astype(np.float32) * weight)], axis=0
    ).T
    fast_fwd = np.block([[fast_cos, -fast_sin], [fast_sin, fast_cos]])
    fast_inv = np.block([[fast_cos, fast_sin], [-fast_sin, fast_cos]])
    twid = np.stack([twid_cos, twid_sin]).astype(np.float32)
    near = HALF // 2
    slow_half = np.stack([slow_fwd[:, :near], slow_fwd[:, near:]])
    slow_taps = np.stack([np.concatenate(
        [slow_fwd[:, (y - k) % RING * QUARTER : ((y - k) % RING + 1) * QUARTER] for k in range(RING)], axis=1
    ) for y in range(RING)])
    out_half = np.stack([slow_inv[:near], slow_inv[near:]])
    named = dict(slow_half=slow_half, slow_taps=slow_taps, out_half=out_half, out_full=slow_inv,
                 fast_fwd=fast_fwd, fast_inv=fast_inv, twid=twid)
    return {name: np.ascontiguousarray(item) for name, item in named.items()}


def dot(left, right):
    return jnp.dot(left, right, preferred_element_type=jnp.float32)


def lanes(signal):
    return jnp.concatenate([signal[j] for j in range(BLOCK)], axis=1)


def spectrum(section, twid, fast_fwd):
    wr, wi = twid[0], twid[1]
    parts = []
    for j in range(BLOCK):
        sr = section[:ROWS, j * FAST : (j + 1) * FAST]
        si = section[ROWS:, j * FAST : (j + 1) * FAST]
        parts.append(jnp.concatenate([sr * wr + si * wi, si * wr - sr * wi], axis=1).astype(jnp.bfloat16))
    return dot(jnp.concatenate(parts, axis=0), fast_fwd[...])


def inverse(product, out, slow_out, twid, fast_inv):
    section = dot(product, fast_inv[...])
    wr, wi = twid[0], twid[1]
    parts = []
    for j in range(BLOCK):
        br = section[j * ROWS : (j + 1) * ROWS, :FAST]
        bi = section[j * ROWS : (j + 1) * ROWS, FAST:]
        parts.append(jnp.concatenate([br * wr - bi * wi, bi * wr + br * wi], axis=0).astype(jnp.bfloat16))
    result = dot(slow_out, jnp.concatenate(parts, axis=1)) * FACTOR
    for j in range(BLOCK):
        out[j] = result[:, j * FAST : (j + 1) * FAST].astype(out.dtype)


def halves(spec):
    return spec[:, :FAST].astype(jnp.float32), spec[:, FAST:].astype(jnp.float32)


def joined(real, imag):
    return jnp.concatenate([real, imag], axis=1).astype(jnp.bfloat16)


def sign_of(place):
    return jnp.where(place[0] == 0, 1.0, -1.0).astype(jnp.float32)


def first_kernel(place, first, near, fast_fwd, twid, h_out):
    h_out[...] = spectrum(dot(near[0], lanes(first)), twid, fast_fwd).astype(jnp.bfloat16)


def local_kernel(place, h_in, taps, taps_table, slow_out, fast_fwd, fast_inv, twid, k_out, out):
    kr, ki = halves(spectrum(dot(taps_table[0], lanes(taps)), twid, fast_fwd).astype(jnp.bfloat16))
    ki = ki * sign_of(place)
    k_out[...] = joined(kr, ki)
    hr, hi = halves(h_in[...])
    inverse(joined(hr * kr - hi * ki, hr * ki + hi * kr), out, slow_out[0], twid, fast_inv)


def other_kernel(place, second, h_in, near, slow_out, fast_fwd, fast_inv, twid, terms):
    s_spec = spectrum(dot(near[0], lanes(second)), twid, fast_fwd).astype(jnp.bfloat16)
    (hr, hi), (sr, si) = halves(h_in[...]), halves(s_spec)
    inverse(joined(hr * sr + hi * si, (hr * si - hi * sr) * sign_of(place)), terms, slow_out[0], twid, fast_inv)


def full_spectrum(second, crossed, near, far, fast_fwd, twid):
    section = dot(near[0], lanes(second)) + dot(far[0], lanes(crossed))
    return halves(spectrum(section, twid, fast_fwd).astype(jnp.bfloat16))


def own_kernel(
    place, second, crossed, h_in, k_in, near, far, slow_out, out_full, fast_fwd, fast_inv, twid, terms, out
):
    fr, fi = full_spectrum(second, crossed, near, far, fast_fwd, twid)
    hr, hi = halves(h_in[...])
    product = joined(hr * fr + hi * fi, (hr * fi - hi * fr) * sign_of(place))
    inverse(product, terms, out_full[...], twid, fast_inv)
    kr, ki = halves(k_in[...])
    inverse(joined(kr * fr + ki * fi, kr * fi - ki * fr), out, slow_out[0], twid, fast_inv)


def cross_kernel(place, second, crossed, k_in, near, far, slow_out, fast_fwd, fast_inv, twid, out):
    fr, fi = full_spectrum(second, crossed, near, far, fast_fwd, twid)
    kr, ki = halves(k_in[...])
    inverse(joined(kr * fr + ki * fi, kr * fi - ki * fr), out, slow_out[0], twid, fast_inv)


def call(kernel, place, chans, items, outs):
    in_specs, arrays = [], []
    for item, kind, pick in items:
        if kind == "x":
            spec = pl.BlockSpec((BLOCK,) + item.shape[1:], lambda i, p, pick=pick: (pick(p) + i, 0, 0))
        elif kind == "s":
            spec = pl.BlockSpec((BLOCK * ROWS, 2 * FAST), lambda i, p, pick=pick: (pick(p) + i, 0))
        elif kind == "t":
            spec = pl.BlockSpec((1,) + item.shape[1:], lambda i, p, pick=pick: (pick(p), 0, 0))
        else:
            spec = pl.BlockSpec(item.shape, lambda i, p, n=item.ndim: (0,) * n)
        in_specs.append(spec)
        arrays.append(item)
    out_specs, shapes = [], []
    for rows in outs:
        if rows:
            out_specs.append(pl.BlockSpec((BLOCK, rows, FAST), lambda i, p: (i, 0, 0)))
            shapes.append(jax.ShapeDtypeStruct((chans, rows, FAST), jnp.bfloat16))
        else:
            out_specs.append(pl.BlockSpec((BLOCK * ROWS, 2 * FAST), lambda i, p: (i, 0)))
            shapes.append(jax.ShapeDtypeStruct((chans * ROWS, 2 * FAST), jnp.bfloat16))
    return pl.pallas_call(
        kernel,
        grid_spec=pltpu.PrefetchScalarGridSpec(
            num_scalar_prefetch=1, grid=(chans // BLOCK,), in_specs=in_specs, out_specs=out_specs
        ),
        out_shape=shapes,
        compiler_params=pltpu.CompilerParams(vmem_limit_bytes=40 * 1024 * 1024),
        cost_estimate=pl.CostEstimate(flops=1, bytes_accessed=1, transcendentals=0),
    )(place, *arrays)


def swap(item, axis):
    return lax.ppermute(item, axis, [(0, 1), (1, 0)])


def diagonal(item):
    return lax.ppermute(item, ("zh", "zb"), [(0, 3), (1, 2), (2, 1), (3, 0)])


def pick_half(item, index, axis=0):
    size = item.shape[axis] // 2
    return lax.dynamic_slice_in_dim(item, index * size, size, axis)


def ordered(low, near, far, axis=0):
    return jnp.concatenate([jnp.where(low, near, far), jnp.where(low, far, near)], axis=axis)


def local(values, grads, filter_taps):
    span = ("za", "x", "c")
    n_span = lax.axis_size(span)
    chans = values.shape[1] // n_span
    own = chans // 2
    consts = {name: jnp.asarray(item) for name, item in tables().items()}
    zh, zb, y = lax.axis_index("zh"), lax.axis_index("zb"), lax.axis_index("y")
    low, left = zb == 0, zh == 0
    place = jnp.stack([zb, y]).astype(jnp.int32)

    def ring(item, step, reach=RING):
        pairs = [(i, (i + step) % RING) for i in range(RING) if (i + step) % RING < reach]
        return lax.ppermute(item, "y", pairs)

    def spread(item):
        return item.reshape(2, n_span, own, FAST).transpose(1, 0, 2, 3).reshape(n_span, chans, FAST)

    def move(item):
        return lax.all_to_all(item, span, split_axis=0, concat_axis=0, tiled=True)

    taps = filter_taps.reshape(own, HALF // 8, FAST)
    across = diagonal(taps)

    v_parts, g_parts = spread(values), spread(grads)
    first_raw = move(jnp.where(low, v_parts, g_parts))
    second_in = jnp.where(low, g_parts, v_parts)
    swapped = swap(jnp.stack([taps, across]), "zb")
    first_raw, second_in, swapped = lax.optimization_barrier((first_raw, second_in, swapped))

    first = first_raw.transpose(1, 0, 2)
    crossed_own = swap(pick_half(first, 1 - zb), "zb")
    second = move(second_in).transpose(1, 0, 2)
    near_taps = ordered(left, taps, swapped[1], axis=1)
    far_taps = ordered(left, swapped[0], across, axis=1)
    taps = ordered(low, near_taps, far_taps)
    taps = jnp.concatenate([taps] + [ring(taps, step) for step in range(1, RING)], axis=1)

    n_own = own // BLOCK
    at_start, at_own, at_far = (lambda p: 0), (lambda p: p[0] * n_own), (lambda p: (1 - p[0]) * n_own)
    here, there, row = (lambda p: p[0]), (lambda p: 1 - p[0]), (lambda p: p[1])
    near = (consts["slow_half"], "t", here)
    far = (consts["slow_half"], "t", there)
    out_near = (consts["out_half"], "t", here)
    out_start = (consts["out_half"], "t", at_start)
    out_full = (consts["out_full"], None, None)
    fast_fwd, fast_inv, twid = [(consts[name], None, None) for name in ("fast_fwd", "fast_inv", "twid")]

    (h_spec,) = call(first_kernel, place, chans, [(first, "x", at_start), near, fast_fwd, twid], [0])
    k_spec, local_out = call(
        local_kernel, place, chans,
        [(h_spec, "s", at_start), (taps, "x", at_start), (consts["slow_taps"], "t", row), out_near,
         fast_fwd, fast_inv, twid], [0, NEAR],
    )
    local_in = local_out.transpose(1, 0, 2)
    local_in, crossed_own, second, first = lax.optimization_barrier((local_in, crossed_own, second, first))

    local_back = move(local_in)
    mine = pick_half(first, zb)
    crossed_a = swap(mine[: own // 2], "zb")
    mine_b, crossed_a = lax.optimization_barrier((mine[own // 2 :], crossed_a))
    crossed_far = jnp.concatenate([crossed_a, swap(mine_b, "zb")])
    own_terms, out_own = call(
        own_kernel, place, own,
        [(second, "x", at_own), (crossed_own, "x", at_start), (h_spec, "s", at_own), (k_spec, "s", at_own),
         near, far, out_near, out_full, fast_fwd, fast_inv, twid], [HALF, NEAR],
    )
    (far_terms,) = call(
        other_kernel, place, own,
        [(second, "x", at_far), (h_spec, "s", at_far), near, out_start, fast_fwd, fast_inv, twid], [NEAR],
    )

    def along(item, reach):
        total = None
        for step in range(RING):
            index = jnp.minimum((y + step) % RING, reach - 1)
            block = lax.dynamic_slice_in_dim(item, index * QUARTER, QUARTER, 1)
            block = (ring(block, step, reach) if step else block).astype(jnp.float32)
            total = block if total is None else total + block
        return total

    own_sum = along(own_terms, RING)
    far_sum = jnp.where(y < RING // 2, along(far_terms, RING // 2), 0.0)
    crossed_far, local_back, own_sum, far_sum = lax.optimization_barrier(
        (crossed_far, local_back, own_sum, far_sum)
    )

    (out_far,) = call(
        cross_kernel, place, own,
        [(second, "x", at_far), (crossed_far, "x", at_start), (k_spec, "s", at_far), near, far, out_near,
         fast_fwd, fast_inv, twid], [NEAR],
    )
    cross_back = move(ordered(low, out_own, out_far).transpose(1, 0, 2))

    def gathered(item):
        return item.reshape(n_span, 2, own, FAST).transpose(1, 0, 2, 3).reshape(values.shape)

    conv_out = gathered(jnp.where(low, local_back, cross_back))
    value_grads = gathered(jnp.where(low, cross_back, local_back))

    far_here, far_there = pick_half(far_sum, zh, 1), pick_half(far_sum, 1 - zh, 1)
    own_here, own_there = pick_half(own_sum, zh, 1), pick_half(own_sum, 1 - zh, 1)
    arrived = swap(jnp.stack([far_here, own_there]).astype(jnp.bfloat16), "zb").astype(jnp.float32)
    passed = diagonal((far_there + arrived[1]).astype(jnp.bfloat16)).astype(jnp.float32)
    filter_grads = own_here + arrived[0] + passed
    return conv_out, value_grads, filter_grads.reshape(filter_taps.shape)


def solution(mesh):
    fine = Mesh(mesh.devices.reshape(RING, 2, 2, 4, 4, 2), ("y", "zh", "zb", "za", "x", "c"))
    dp, ctx = ("y", "zh"), ("zb", "za", "x", "c")
    tokens = P(dp, None, ctx)
    return jax.shard_map(
        local,
        mesh=fine,
        in_specs=(tokens, tokens, P(ctx, dp)),
        out_specs=(tokens, tokens, P(ctx, dp)),
        check_vma=False,
    )
```

time: 336 us -> 309 us (0.920)
  the two profiles are of different devices: /device:TPU:1 before, /device:TPU:90 now
where the time goes in v2:
time: 309 us; the launch traced here: 308 us
  starting transfers between devices  126 us (41%)
  waiting for transfers between devices  92 us (30%)
  Pallas kernels  42.9 us (14%)
  local copies, waits for them, and re-layouts  33.3 us (11%)
  other arithmetic  12.1 us (4%)
    ppermute x5, waiting for transfers between devices, swap(): return lax.ppermute(item, axis, [(0, 1), (1, 0)])  55.7 us
    all_to_all x4, starting transfers between devices, move(): return lax.all_to_all(item, span, split_axis=0, concat_axis=0, tiled=True)  49.6 us
    pallas_call x5, Pallas kernels, call(): pl.pallas_call(kernel, grid_spec=pltpu.PrefetchScalarGridSpec(num_scalar_...  42.9 us
    ppermute x5, starting transfers between devices, swap(): return lax.ppermute(item, axis, [(0, 1), (1, 0)])  36.3 us
    ppermute x9, starting transfers between devices, ring(): return lax.ppermute(item, 'y', pairs)  28.2 us
    ppermute x2, waiting for transfers between devices, diagonal(): return lax.ppermute(item, ('zh', 'zb'), [(0, 3), (1, 2), (2, 1), (3, 0)])  27.5 us
    unnamed x44, local copies, waits for them, and re-layouts  17.5 us
    ppermute x2, starting transfers between devices, diagonal(): return lax.ppermute(item, ('zh', 'zb'), [(0, 3), (1, 2), (2, 1), (3, 0)])  12 us
  transfers between devices with their start and end apart: 20, of which 8 were waited for; matrix products, arithmetic and copies ran while one was open for 6% of the time, Pallas kernels for 12%

profile of v2, /device:TPU:90, one launch (start us, length us, event | category | flops | bytes accessed | tf_op | source)
XLA Modules:
  0.0 307.5 jit_solution(14828418028488865242)
XLA Ops:
  0.6 1.7 broadcast_select_fusion
  2.4 1.0 copy.17
  3.4 8.1 %all-to-all-start = ((bf16[32,128,128]{2,1,0:T(8,128)(2,1)}), bf16[32,128,128]{2,1,0:T(8,128)(2,1)S(1)}, u32[]{:S(2)}, u32[]{:S(2)}) async-start(bf16[32,128,128]{2,1,0:T(8,128)(2,1)} %bitcast.72), calls=%async_computation | async-start | bytes 2097152 | tf_op jit(solution)/shard_map/all_to_all | solution.py:209
  11.6 10.0 %collective-permute-start = (bf16[64,8,128]{2,1,0:T(8,128)(2,1)S(1)}, bf16[64,8,128]{2,1,0:T(8,128)(2,1)S(1)}, u32[]{:S(2)}, u32[]{:S(2)}) collective-permute-start(bf16[64,8,128]{2,1,0:T(8,128)(2,1)S(1)} %bitcast.73), channel_id=1, source_target_pairs={{0,96},{32,64},{64,32},{96,0},{1,97},{33,65},{65,33},{97,1},{2,98}... | collective-permute-start | bytes 393224 | tf_op jit(solution)/shard_map/ppermute | solution.py:179
  21.6 18.7 %collective-permute-done = bf16[64,8,128]{2,1,0:T(8,128)(2,1)S(1)} collective-permute-done((bf16[64,8,128]{2,1,0:T(8,128)(2,1)S(1)}, bf16[64,8,128]{2,1,0:T(8,128)(2,1)S(1)}, u32[]{:S(2)}, u32[]{:S(2)}) %collective-permute-start) | collective-permute-done | bytes 131104 | tf_op jit(solution)/shard_map/ppermute | solution.py:179
  40.4 15.5 %collective-permute-start.1 = (bf16[2,64,8,128]{3,2,1,0:T(8,128)(2,1)S(1)}, bf16[2,64,8,128]{3,2,1,0:T(8,128)(2,1)S(1)}, u32[]{:S(2)}, u32[]{:S(2)}) collective-permute-start(bf16[2,64,8,128]{3,2,1,0:T(8,128)(2,1)S(1)} %pad_maximum_fusion.3), channel_id=1, source_target_pairs={{0,32},{32,0},{1,33},{33,1},{2,34},{34,2},{3,35},{35,3},{4,36},{36... | collective-permute-start | bytes 786440 | tf_op jit(solution)/shard_map/ppermute | solution.py:175
  55.8 1.1 copy.18
  56.9 9.9 %collective-permute-done.1 = bf16[2,64,8,128]{3,2,1,0:T(8,128)(2,1)S(1)} collective-permute-done((bf16[2,64,8,128]{3,2,1,0:T(8,128)(2,1)S(1)}, bf16[2,64,8,128]{3,2,1,0:T(8,128)(2,1)S(1)}, u32[]{:S(2)}, u32[]{:S(2)}) %collective-permute-start.1) | collective-permute-done | bytes 262176 | tf_op jit(solution)/shard_map/ppermute | solution.py:175
  66.8 9.4 %all-to-all-start.1 = ((bf16[32,128,128]{2,1,0:T(8,128)(2,1)}), bf16[32,128,128]{2,1,0:T(8,128)(2,1)}, u32[]{:S(2)}, u32[]{:S(2)}) async-start(bf16[32,128,128]{2,1,0:T(8,128)(2,1)} %bitcast.7), calls=%async_computation.1 | async-start | bytes 2097152 | tf_op jit(solution)/shard_map/all_to_all | solution.py:209
  76.3 0.1 broadcast_select_fusion.7
  76.4 0.8 pad_maximum_fusion.1
  77.3 2.6 collective-permute-start.4
  79.9 2.9 collective-permute-start.3
  82.8 4.1 %collective-permute-start.2 = (bf16[128,16,128]{2,1,0:T(8,128)(2,1)}, bf16[128,16,128]{2,1,0:T(8,128)(2,1)}, u32[]{:S(2)}, u32[]{:S(2)}) collective-permute-start(bf16[128,16,128]{2,1,0:T(8,128)(2,1)} %pad_maximum_fusion.1), channel_id=1, source_target_pairs={{0,128},{128,256},{256,384},{384,0},{1,129},{129,257},{257,385},{3... | collective-permute-start | bytes 1572872 | tf_op jit(solution)/shard_map/ppermute | solution.py:203
  86.9 1.9 copy.35
  88.8 0.9 dynamic-slice_bitcast_fusion
  89.7 5.8 %collective-permute-start.5 = (bf16[64,32,128]{2,1,0:T(8,128)(2,1)}, bf16[64,32,128]{2,1,0:T(8,128)(2,1)S(1)}, u32[]{:S(2)}, u32[]{:S(2)}) collective-permute-start(bf16[64,32,128]{2,1,0:T(8,128)(2,1)} %dynamic-slice_bitcast_fusion), channel_id=1, source_target_pairs={{0,32},{32,0},{1,33},{33,1},{2,34},{34,2},{3,35},{35,3},{4,36},{36... | collective-permute-start | bytes 1572872 | tf_op jit(solution)/shard_map/ppermute | solution.py:175
  95.5 0.1 pad_add_fusion.place
  95.6 7.3 %shard_map.121.h_in = bf16[10240,256]{1,0:T(8,128)(2,1)S(1)} custom-call(s32[2]{0:T(128)S(1)} %pad_add_fusion.place, bf16[128,32,128]{2,1,0:T(8,128)(2,1)S(1)} %bitcast.65, bf16[2,160,32]{2,1,0:T(8,128)(2,1)S(1)} %copy-done.7, bf16[256,256]{1,0:T(8,128)(2,1)S(1)} %copy-done.6, f32[2,80,128]{2,1,0:T(8,128)S(1)} %copy-done.9), custom_call_target="tpu_custom_call" | custom-call | flops 1 | bytes 1 | tf_op jit(solution)/shard_map/pallas_call | solution.py:163
  102.9 3.0 collective-permute-done.4
  105.9 2.5 collective-permute-done.2
  108.4 3.2 %pad_maximum_fusion.taps = bf16[128,64,128]{2,1,0:T(8,128)(2,1)S(1)} fusion(bf16[128,16,128]{2,1,0:T(8,128)(2,1)} %collective-permute-done.4, bf16[128,16,128]{2,1,0:T(8,128)(2,1)} %collective-permute-done.3, bf16[128,16,128]{2,1,0:T(8,128)(2,1)} %collective-permute-done.2, bf16[64,16,128]{2,1,0:T(8,128)(2,1)S(1)} %get-tuple-element.54, ...), kind=kLoop, calls=%fused_computation | loop fusion | flops 10485760 | bytes 4194304 | tf_op jit(solution)/shard_map/concatenate | solution.py:226
  111.7 12.5 %shard_map.122 = (bf16[10240,256]{1,0:T(8,128)(2,1)S(1)}, bf16[128,32,128]{2,1,0:T(8,128)(2,1)S(1)}) custom-call(s32[2]{0:T(128)S(1)} %pad_add_fusion.place, bf16[10240,256]{1,0:T(8,128)(2,1)S(1)} %shard_map.121.h_in, bf16[128,64,128]{2,1,0:T(8,128)(2,1)S(1)} %pad_maximum_fusion.taps, bf16[4,160,64]{2,1,0:T(8,128)(2,1)S(1)} %copy-done.16, ...), custom_call_target="tpu_custom_call" | custom-call | flops 1 | bytes 1 | tf_op jit(solution)/shard_map/pallas_call | solution.py:163
  124.2 2.4 copy-done
  126.6 2.3 copy-done.3
  128.9 1.0 copy-done.10
  129.9 1.9 copy.33
  131.8 2.8 copy.22
  134.6 16.1 %all-to-all-start.2 = ((bf16[32,128,128]{2,1,0:T(8,128)(2,1)}), bf16[32,128,128]{2,1,0:T(8,128)(2,1)}, u32[]{:S(2)}, u32[]{:S(2)}) async-start(bf16[32,128,128]{2,1,0:T(8,128)(2,1)} %copy.22), calls=%async_computation.2 | async-start | bytes 2097152 | tf_op jit(solution)/shard_map/all_to_all | solution.py:209
  150.7 0.7 constant_dynamic-slice_fusion.7
  151.5 8.2 %collective-permute-start.6 = (bf16[32,32,128]{2,1,0:T(8,128)(2,1)}, bf16[32,32,128]{2,1,0:T(8,128)(2,1)}, u32[]{:S(2)}, u32[]{:S(2)}) collective-permute-start(bf16[32,32,128]{2,1,0:T(8,128)(2,1)} %get-tuple-element.46), channel_id=1, source_target_pairs={{0,32},{32,0},{1,33},{33,1},{2,34},{34,2},{3,35},{35,3},{4,36},{36... | collective-permute-start | bytes 786440 | tf_op jit(solution)/shard_map/ppermute | solution.py:175
  159.7 2.5 copy-done.1
  162.2 2.5 copy-done.4
  164.7 1.0 copy-done.15
  165.7 9.6 %shard_map.123 = (bf16[64,64,128]{2,1,0:T(8,128)(2,1)S(1)}, bf16[64,32,128]{2,1,0:T(8,128)(2,1)S(1)}) custom-call(s32[2]{0:T(128)S(1)} %pad_add_fusion.place, bf16[128,32,128]{2,1,0:T(8,128)(2,1)S(1)} %bitcast.62, bf16[64,32,128]{2,1,0:T(8,128)(2,1)S(1)} %copy-done.15, bf16[10240,256]{1,0:T(8,128)(2,1)S(1)} %copy-done.1, bf16[10240,256]{1,0:T(8,128)(2,1)S(1)} %copy-done.4, ...), custom_call_target="tpu_custom_call" | custom-call | flops 1 | bytes 1 | tf_op jit(solution)/shard_map/pallas_call | solution.py:163
  175.3 1.0 constant_dynamic-slice_fusion.6
  176.3 2.4 collective-permute-start.10
  178.8 3.8 %collective-permute-start.9 = (bf16[64,16,128]{2,1,0:T(8,128)(2,1)}, bf16[64,16,128]{2,1,0:T(8,128)(2,1)}, u32[]{:S(2)}, u32[]{:S(2)}) collective-permute-start(bf16[64,16,128]{2,1,0:T(8,128)(2,1)} %get-tuple-element.45), channel_id=1, source_target_pairs={{0,256},{128,384},{256,0},{384,128},{1,257},{129,385},{257,1},{385... | collective-permute-start | bytes 786440 | tf_op jit(solution)/shard_map/ppermute | solution.py:203
  182.6 4.4 %collective-permute-start.8 = (bf16[64,16,128]{2,1,0:T(8,128)(2,1)}, bf16[64,16,128]{2,1,0:T(8,128)(2,1)}, u32[]{:S(2)}, u32[]{:S(2)}) collective-permute-start(bf16[64,16,128]{2,1,0:T(8,128)(2,1)} %get-tuple-element.43), channel_id=1, source_target_pairs={{0,128},{128,256},{256,384},{384,0},{1,129},{129,257},{257,385},{3... | collective-permute-start | bytes 786440 | tf_op jit(solution)/shard_map/ppermute | solution.py:203
  187.1 2.5 copy-done.2
  189.5 6.4 %shard_map.124 = bf16[64,32,128]{2,1,0:T(8,128)(2,1)S(1)} custom-call(s32[2]{0:T(128)S(1)} %pad_add_fusion.place, bf16[128,32,128]{2,1,0:T(8,128)(2,1)S(1)} %bitcast.63, bf16[10240,256]{1,0:T(8,128)(2,1)S(1)} %copy-done.2, bf16[2,160,32]{2,1,0:T(8,128)(2,1)S(1)} %copy-done.7, bf16[2,32,160]{2,1,0:T(8,128)(2,1)S(1)} %copy-done.11, ...), custom_call_target="tpu_custom_call" | custom-call | flops 1 | bytes 1 | tf_op jit(solution)/shard_map/pallas_call | solution.py:163
  196.0 0.9 constant_dynamic-slice_fusion.3
  196.9 1.3 collective-permute-start.13
  198.3 4.6 %collective-permute-start.12 = (bf16[64,16,128]{2,1,0:T(8,128)(2,1)}, bf16[64,16,128]{2,1,0:T(8,128)(2,1)}, u32[]{:S(2)}, u32[]{:S(2)}) collective-permute-start(bf16[64,16,128]{2,1,0:T(8,128)(2,1)} %get-tuple-element.52), channel_id=1, source_target_pairs={{256,0},{384,128},{257,1},{385,129},{258,2},{386,130},{259,3},{387... | collective-permute-start | bytes 786440 | tf_op jit(solution)/shard_map/ppermute | solution.py:203
  202.9 2.0 collective-permute-start.11
  204.9 1.9 collective-permute-start.7
  206.8 2.1 convert_add_fusion
  208.9 3.2 %collective-permute-done.11 = bf16[64,16,128]{2,1,0:T(8,128)(2,1)} collective-permute-done((bf16[64,16,128]{2,1,0:T(8,128)(2,1)}, bf16[64,16,128]{2,1,0:T(8,128)(2,1)}, u32[]{:S(2)}, u32[]{:S(2)}) %collective-permute-start.11) | collective-permute-done | bytes 262176 | tf_op jit(solution)/shard_map/ppermute | solution.py:203
  212.1 1.2 add_select_fusion
  213.3 10.1 %collective-permute-done.7 = bf16[32,32,128]{2,1,0:T(8,128)(2,1)S(1)} collective-permute-done((bf16[32,32,128]{2,1,0:T(8,128)(2,1)S(1)}, bf16[32,32,128]{2,1,0:T(8,128)(2,1)S(1)}, u32[]{:S(2)}, u32[]{:S(2)}) %collective-permute-start.7) | collective-permute-done | bytes 262176 | tf_op jit(solution)/shard_map/ppermute | solution.py:175
  223.5 1.0 pad_maximum_fusion.2.crossed
  224.5 2.5 copy-done.5
  227.0 7.1 %shard_map.125 = bf16[64,32,128]{2,1,0:T(8,128)(2,1)S(1)} custom-call(s32[2]{0:T(128)S(1)} %pad_add_fusion.place, bf16[128,32,128]{2,1,0:T(8,128)(2,1)S(1)} %bitcast.64, bf16[64,32,128]{2,1,0:T(8,128)(2,1)S(1)} %pad_maximum_fusion.2.crossed, bf16[10240,256]{1,0:T(8,128)(2,1)S(1)} %copy-done.5, bf16[2,160,32]{2,1,0:T(8,128)(2,1)S(1)} %copy-done.7, ...), custom_call_target="tpu_custom_call" | custom-call | flops 1 | bytes 1 | tf_op jit(solution)/shard_map/pallas_call | solution.py:163
  234.2 0.1 maximum_bitcast_fusion
  234.3 1.4 copy.23
  235.7 16.0 %all-to-all-start.3 = ((bf16[32,128,128]{2,1,0:T(8,128)(2,1)}), bf16[32,128,128]{2,1,0:T(8,128)(2,1)S(1)}, u32[]{:S(2)}, u32[]{:S(2)}) async-start(bf16[32,128,128]{2,1,0:T(8,128)(2,1)} %copy.23), calls=%async_computation.3 | async-start | bytes 2097152 | tf_op jit(solution)/shard_map/all_to_all | solution.py:209
  251.8 4.9 %collective-permute-start.14 = (bf16[2,64,8,128]{3,2,1,0:T(8,128)(2,1)S(1)}, bf16[2,64,8,128]{3,2,1,0:T(8,128)(2,1)S(1)}, u32[]{:S(2)}, u32[]{:S(2)}) collective-permute-start(bf16[2,64,8,128]{3,2,1,0:T(8,128)(2,1)S(1)} %pad_maximum_fusion.6), channel_id=1, source_target_pairs={{0,32},{32,0},{1,33},{33,1},{2,34},{34,2},{3,35},{35,3},{4,36},{36... | collective-permute-start | bytes 786440 | tf_op jit(solution)/shard_map/ppermute | solution.py:175
  256.7 35.7 %collective-permute-done.14 = bf16[2,64,8,128]{3,2,1,0:T(8,128)(2,1)S(1)} collective-permute-done((bf16[2,64,8,128]{3,2,1,0:T(8,128)(2,1)S(1)}, bf16[2,64,8,128]{3,2,1,0:T(8,128)(2,1)S(1)}, u32[]{:S(2)}, u32[]{:S(2)}) %collective-permute-start.14) | collective-permute-done | bytes 262176 | tf_op jit(solution)/shard_map/ppermute | solution.py:175
  292.5 1.9 collective-permute-start.15
  294.4 8.8 %collective-permute-done.15 = bf16[64,8,128]{2,1,0:T(8,128)(2,1)S(1)} collective-permute-done((bf16[64,8,128]{2,1,0:T(8,128)(2,1)S(1)}, bf16[64,8,128]{2,1,0:T(8,128)(2,1)S(1)}, u32[]{:S(2)}, u32[]{:S(2)}) %collective-permute-start.15) | collective-permute-done | bytes 131104 | tf_op jit(solution)/shard_map/ppermute | solution.py:179
  303.3 0.8 copy.34
  304.1 1.4 broadcast_select_fusion.2
  305.4 1.0 copy.24
  306.5 1.0 copy.25
  (55 shorter events, 0.5 us)
Async XLA Ops:
  0.6 10.9 %copy-start.20 = (bf16[64,1024]{1,0:T(8,128)(2,1)S(1)}, bf16[64,1024]{1,0:T(8,128)(2,1)}, u32[]{:S(2)}) copy-start(bf16[64,1024]{1,0:T(8,128)(2,1)} %param.12) | copy-start | bytes 393220
  3.4 63.4 %all-to-all-start = ((bf16[32,128,128]{2,1,0:T(8,128)(2,1)}), bf16[32,128,128]{2,1,0:T(8,128)(2,1)S(1)}, u32[]{:S(2)}, u32[]{:S(2)}) async-start(bf16[32,128,128]{2,1,0:T(8,128)(2,1)} %bitcast.72), calls=%async_computation | async-start | bytes 2097152 | tf_op jit(solution)/shard_map/all_to_all | solution.py:209
  11.6 28.7 %collective-permute-start = (bf16[64,8,128]{2,1,0:T(8,128)(2,1)S(1)}, bf16[64,8,128]{2,1,0:T(8,128)(2,1)S(1)}, u32[]{:S(2)}, u32[]{:S(2)}) collective-permute-start(bf16[64,8,128]{2,1,0:T(8,128)(2,1)S(1)} %bitcast.73), channel_id=1, source_target_pairs={{0,96},{32,64},{64,32},{96,0},{1,97},{33,65},{65,33},{97,1},{2,98}... | collective-permute-start | bytes 393224 | tf_op jit(solution)/shard_map/ppermute | solution.py:179
  40.4 26.4 %collective-permute-start.1 = (bf16[2,64,8,128]{3,2,1,0:T(8,128)(2,1)S(1)}, bf16[2,64,8,128]{3,2,1,0:T(8,128)(2,1)S(1)}, u32[]{:S(2)}, u32[]{:S(2)}) collective-permute-start(bf16[2,64,8,128]{3,2,1,0:T(8,128)(2,1)S(1)} %pad_maximum_fusion.3), channel_id=1, source_target_pairs={{0,32},{32,0},{1,33},{33,1},{2,34},{34,2},{3,35},{35,3},{4,36},{36... | collective-permute-start | bytes 786440 | tf_op jit(solution)/shard_map/ppermute | solution.py:175
  66.8 20.1 %copy-start.18 = (bf16[32,128,128]{2,1,0:T(8,128)(2,1)}, bf16[32,128,128]{2,1,0:T(8,128)(2,1)S(1)}, u32[]{:S(2)}) copy-start(bf16[32,128,128]{2,1,0:T(8,128)(2,1)S(1)} %all-to-all-done) | copy-start | bytes 3145732
  66.8 28.8 %copy-start.6 = (bf16[256,256]{1,0:T(8,128)(2,1)S(1)}, bf16[256,256]{1,0:T(8,128)(2,1)}, u32[]{:S(2)}) copy-start(bf16[256,256]{1,0:T(8,128)(2,1)} %constant.85.clone.fast_fwd) | copy-start | bytes 393220
  66.8 28.8 %copy-start.7 = (bf16[2,160,32]{2,1,0:T(8,128)(2,1)S(1)}, bf16[2,160,32]{2,1,0:T(8,128)(2,1)}, u32[]{:S(2)}) copy-start(bf16[2,160,32]{2,1,0:T(8,128)(2,1)} %constant.81.clone.near.far) | copy-start | bytes 61444
  66.8 28.8 %copy-start.9 = (f32[2,80,128]{2,1,0:T(8,128)S(1)}, f32[2,80,128]{2,1,0:T(8,128)}, u32[]{:S(2)}) copy-start(f32[2,80,128]{2,1,0:T(8,128)} %constant.87.clone.twid) | copy-start | bytes 245764
  66.8 63.1 %all-to-all-start.1 = ((bf16[32,128,128]{2,1,0:T(8,128)(2,1)}), bf16[32,128,128]{2,1,0:T(8,128)(2,1)}, u32[]{:S(2)}, u32[]{:S(2)}) async-start(bf16[32,128,128]{2,1,0:T(8,128)(2,1)} %bitcast.7), calls=%async_computation.1 | async-start | bytes 2097152 | tf_op jit(solution)/shard_map/all_to_all | solution.py:209
  77.3 28.6 %collective-permute-start.4 = (bf16[128,16,128]{2,1,0:T(8,128)(2,1)}, bf16[128,16,128]{2,1,0:T(8,128)(2,1)}, u32[]{:S(2)}, u32[]{:S(2)}) collective-permute-start(bf16[128,16,128]{2,1,0:T(8,128)(2,1)} %pad_maximum_fusion.1), channel_id=1, source_target_pairs={{0,384},{128,0},{256,128},{384,256},{1,385},{129,1},{257,129},{385... | collective-permute-start | bytes 1572872 | tf_op jit(solution)/shard_map/ppermute | solution.py:203
  79.9 26.0 %collective-permute-start.3 = (bf16[128,16,128]{2,1,0:T(8,128)(2,1)}, bf16[128,16,128]{2,1,0:T(8,128)(2,1)}, u32[]{:S(2)}, u32[]{:S(2)}) collective-permute-start(bf16[128,16,128]{2,1,0:T(8,128)(2,1)} %pad_maximum_fusion.1), channel_id=1, source_target_pairs={{0,256},{128,384},{256,0},{384,128},{1,257},{129,385},{257,1},{385... | collective-permute-start | bytes 1572872 | tf_op jit(solution)/shard_map/ppermute | solution.py:203
  82.8 25.7 %collective-permute-start.2 = (bf16[128,16,128]{2,1,0:T(8,128)(2,1)}, bf16[128,16,128]{2,1,0:T(8,128)(2,1)}, u32[]{:S(2)}, u32[]{:S(2)}) collective-permute-start(bf16[128,16,128]{2,1,0:T(8,128)(2,1)} %pad_maximum_fusion.1), channel_id=1, source_target_pairs={{0,128},{128,256},{256,384},{384,0},{1,129},{129,257},{257,385},{3... | collective-permute-start | bytes 1572872 | tf_op jit(solution)/shard_map/ppermute | solution.py:203
  89.7 42.2 %collective-permute-start.5 = (bf16[64,32,128]{2,1,0:T(8,128)(2,1)}, bf16[64,32,128]{2,1,0:T(8,128)(2,1)S(1)}, u32[]{:S(2)}, u32[]{:S(2)}) collective-permute-start(bf16[64,32,128]{2,1,0:T(8,128)(2,1)} %dynamic-slice_bitcast_fusion), channel_id=1, source_target_pairs={{0,32},{32,0},{1,33},{33,1},{2,34},{34,2},{3,35},{35,3},{4,36},{36... | collective-permute-start | bytes 1572872 | tf_op jit(solution)/shard_map/ppermute | solution.py:175
  95.6 16.1 %copy-start.8 = (bf16[256,256]{1,0:T(8,128)(2,1)S(1)}, bf16[256,256]{1,0:T(8,128)(2,1)}, u32[]{:S(2)}) copy-start(bf16[256,256]{1,0:T(8,128)(2,1)} %constant.86.clone.fast_inv) | copy-start | bytes 393220
  95.6 16.1 %copy-start.11 = (bf16[2,32,160]{2,1,0:T(8,128)(2,1)S(1)}, bf16[2,32,160]{2,1,0:T(8,128)(2,1)}, u32[]{:S(2)}) copy-start(bf16[2,32,160]{2,1,0:T(8,128)(2,1)} %constant.83.clone.slow_out) | copy-start | bytes 61444
  95.6 16.1 %copy-start.16 = (bf16[4,160,64]{2,1,0:T(8,128)(2,1)S(1)}, bf16[4,160,64]{2,1,0:T(8,128)(2,1)}, u32[]{:S(2)}) copy-start(bf16[4,160,64]{2,1,0:T(8,128)(2,1)} %constant.82.clone.taps_table) | copy-start | bytes 245764
  124.2 2.4 copy-start
  126.6 2.3 copy-start.3
  128.9 1.0 copy-start.10
  129.9 29.8 %copy-start.17 = (bf16[64,160]{1,0:T(8,128)(2,1)S(1)}, bf16[64,160]{1,0:T(8,128)(2,1)}, u32[]{:S(2)}) copy-start(bf16[64,160]{1,0:T(8,128)(2,1)} %constant.84.clone.out_full) | copy-start | bytes 61444
  131.8 27.9 %copy-start.14 = (bf16[64,32,128]{2,1,0:T(8,128)(2,1)}, bf16[64,32,128]{2,1,0:T(8,128)(2,1)S(1)}, u32[]{:S(2)}) copy-start(bf16[64,32,128]{2,1,0:T(8,128)(2,1)S(1)} %collective-permute-done.5.crossed) | copy-start | bytes 1572868
  134.6 89.9 %all-to-all-start.2 = ((bf16[32,128,128]{2,1,0:T(8,128)(2,1)}), bf16[32,128,128]{2,1,0:T(8,128)(2,1)}, u32[]{:S(2)}, u32[]{:S(2)}) async-start(bf16[32,128,128]{2,1,0:T(8,128)(2,1)} %copy.22), calls=%async_computation.2 | async-start | bytes 2097152 | tf_op jit(solution)/shard_map/all_to_all | solution.py:209
  151.5 46.8 %collective-permute-start.6 = (bf16[32,32,128]{2,1,0:T(8,128)(2,1)}, bf16[32,32,128]{2,1,0:T(8,128)(2,1)}, u32[]{:S(2)}, u32[]{:S(2)}) collective-permute-start(bf16[32,32,128]{2,1,0:T(8,128)(2,1)} %get-tuple-element.46), channel_id=1, source_target_pairs={{0,32},{32,0},{1,33},{33,1},{2,34},{34,2},{3,35},{35,3},{4,36},{36... | collective-permute-start | bytes 786440 | tf_op jit(solution)/shard_map/ppermute | solution.py:175
  159.7 2.5 copy-start.1
  162.2 2.5 copy-start.4
  164.7 1.0 copy-start.15
  175.3 11.8 %copy-start.12 = (bf16[64,32,128]{2,1,0:T(8,128)(2,1)}, bf16[64,32,128]{2,1,0:T(8,128)(2,1)S(1)}, u32[]{:S(2)}) copy-start(bf16[64,32,128]{2,1,0:T(8,128)(2,1)S(1)} %get-tuple-element.33) | copy-start | bytes 1572868
  176.3 26.6 %collective-permute-start.10 = (bf16[64,16,128]{2,1,0:T(8,128)(2,1)}, bf16[64,16,128]{2,1,0:T(8,128)(2,1)}, u32[]{:S(2)}, u32[]{:S(2)}) collective-permute-start(bf16[64,16,128]{2,1,0:T(8,128)(2,1)} %get-tuple-element.44), channel_id=1, source_target_pairs={{0,384},{128,0},{256,128},{384,256},{1,385},{129,1},{257,129},{385... | collective-permute-start | bytes 786440 | tf_op jit(solution)/shard_map/ppermute | solution.py:203
  178.8 26.1 %collective-permute-start.9 = (bf16[64,16,128]{2,1,0:T(8,128)(2,1)}, bf16[64,16,128]{2,1,0:T(8,128)(2,1)}, u32[]{:S(2)}, u32[]{:S(2)}) collective-permute-start(bf16[64,16,128]{2,1,0:T(8,128)(2,1)} %get-tuple-element.45), channel_id=1, source_target_pairs={{0,256},{128,384},{256,0},{384,128},{1,257},{129,385},{257,1},{385... | collective-permute-start | bytes 786440 | tf_op jit(solution)/shard_map/ppermute | solution.py:203
  182.6 24.2 %collective-permute-start.8 = (bf16[64,16,128]{2,1,0:T(8,128)(2,1)}, bf16[64,16,128]{2,1,0:T(8,128)(2,1)}, u32[]{:S(2)}, u32[]{:S(2)}) collective-permute-start(bf16[64,16,128]{2,1,0:T(8,128)(2,1)} %get-tuple-element.43), channel_id=1, source_target_pairs={{0,128},{128,256},{256,384},{384,0},{1,129},{129,257},{257,385},{3... | collective-permute-start | bytes 786440 | tf_op jit(solution)/shard_map/ppermute | solution.py:203
  187.0 2.5 copy-start.2
  196.9 12.0 %collective-permute-start.13 = (bf16[64,16,128]{2,1,0:T(8,128)(2,1)}, bf16[64,16,128]{2,1,0:T(8,128)(2,1)}, u32[]{:S(2)}, u32[]{:S(2)}) collective-permute-start(bf16[64,16,128]{2,1,0:T(8,128)(2,1)} %get-tuple-element.51), channel_id=1, source_target_pairs={{128,0},{256,128},{129,1},{257,129},{130,2},{258,130},{131,3},{259... | collective-permute-start | bytes 786440 | tf_op jit(solution)/shard_map/ppermute | solution.py:203
  198.3 10.6 %collective-permute-start.12 = (bf16[64,16,128]{2,1,0:T(8,128)(2,1)}, bf16[64,16,128]{2,1,0:T(8,128)(2,1)}, u32[]{:S(2)}, u32[]{:S(2)}) collective-permute-start(bf16[64,16,128]{2,1,0:T(8,128)(2,1)} %get-tuple-element.52), channel_id=1, source_target_pairs={{256,0},{384,128},{257,1},{385,129},{258,2},{386,130},{259,3},{387... | collective-permute-start | bytes 786440 | tf_op jit(solution)/shard_map/ppermute | solution.py:203
  202.9 9.2 %collective-permute-start.11 = (bf16[64,16,128]{2,1,0:T(8,128)(2,1)}, bf16[64,16,128]{2,1,0:T(8,128)(2,1)}, u32[]{:S(2)}, u32[]{:S(2)}) collective-permute-start(bf16[64,16,128]{2,1,0:T(8,128)(2,1)} %get-tuple-element.50), channel_id=1, source_target_pairs={{0,128},{384,0},{1,129},{385,1},{2,130},{386,2},{3,131},{387,3},{4... | collective-permute-start | bytes 786440 | tf_op jit(solution)/shard_map/ppermute | solution.py:203
  204.9 18.6 %collective-permute-start.7 = (bf16[32,32,128]{2,1,0:T(8,128)(2,1)S(1)}, bf16[32,32,128]{2,1,0:T(8,128)(2,1)S(1)}, u32[]{:S(2)}, u32[]{:S(2)}) collective-permute-start(bf16[32,32,128]{2,1,0:T(8,128)(2,1)S(1)} %get-tuple-element.26), channel_id=1, source_target_pairs={{0,32},{32,0},{1,33},{33,1},{2,34},{34,2},{3,35},{35,3},{4,36},{36... | collective-permute-start | bytes 786440 | tf_op jit(solution)/shard_map/ppermute | solution.py:175
  224.5 2.5 copy-start.5
  227.0 7.2 %copy-start.13 = (bf16[64,32,128]{2,1,0:T(8,128)(2,1)S(1)}, bf16[64,32,128]{2,1,0:T(8,128)(2,1)}, u32[]{:S(2)}) copy-start(bf16[64,32,128]{2,1,0:T(8,128)(2,1)} %copy-done.12) | copy-start | bytes 1572868
  234.1 17.6 %copy-start.19 = (f32[64,16,128]{2,1,0:T(8,128)S(1)}, f32[64,16,128]{2,1,0:T(8,128)}, u32[]{:S(2)}) copy-start(f32[64,16,128]{2,1,0:T(8,128)} %convert_add_fusion) | copy-start | bytes 1572868
  235.7 68.4 %all-to-all-start.3 = ((bf16[32,128,128]{2,1,0:T(8,128)(2,1)}), bf16[32,128,128]{2,1,0:T(8,128)(2,1)S(1)}, u32[]{:S(2)}, u32[]{:S(2)}) async-start(bf16[32,128,128]{2,1,0:T(8,128)(2,1)} %copy.23), calls=%async_computation.3 | async-start | bytes 2097152 | tf_op jit(solution)/shard_map/all_to_all | solution.py:209
  251.8 40.6 %collective-permute-start.14 = (bf16[2,64,8,128]{3,2,1,0:T(8,128)(2,1)S(1)}, bf16[2,64,8,128]{3,2,1,0:T(8,128)(2,1)S(1)}, u32[]{:S(2)}, u32[]{:S(2)}) collective-permute-start(bf16[2,64,8,128]{3,2,1,0:T(8,128)(2,1)S(1)} %pad_maximum_fusion.6), channel_id=1, source_target_pairs={{0,32},{32,0},{1,33},{33,1},{2,34},{34,2},{3,35},{35,3},{4,36},{36... | collective-permute-start | bytes 786440 | tf_op jit(solution)/shard_map/ppermute | solution.py:175
  292.5 10.8 %collective-permute-start.15 = (bf16[64,8,128]{2,1,0:T(8,128)(2,1)S(1)}, bf16[64,8,128]{2,1,0:T(8,128)(2,1)S(1)}, u32[]{:S(2)}, u32[]{:S(2)}) collective-permute-start(bf16[64,8,128]{2,1,0:T(8,128)(2,1)S(1)} %fusion.1), channel_id=1, source_target_pairs={{0,96},{32,64},{64,32},{96,0},{1,97},{33,65},{65,33},{97,1},{2,98}... | collective-permute-start | bytes 393224 | tf_op jit(solution)/shard_map/ppermute | solution.py:179

commit v3 on v2

--- a/solution.py
+++ b/solution.py
@@ -166,7 +166,7 @@
             num_scalar_prefetch=1, grid=(chans // BLOCK,), in_specs=in_specs, out_specs=out_specs
         ),
         out_shape=shapes,
-        compiler_params=pltpu.CompilerParams(vmem_limit_bytes=40 * 1024 * 1024),
+        compiler_params=pltpu.CompilerParams(vmem_limit_bytes=56 * 1024 * 1024),
         cost_estimate=pl.CostEstimate(flops=1, bytes_accessed=1, transcendentals=0),
     )(place, *arrays)
 
@@ -198,9 +198,8 @@
     low, left = zb == 0, zh == 0
     place = jnp.stack([zb, y]).astype(jnp.int32)
 
-    def ring(item, step, reach=RING):
-        pairs = [(i, (i + step) % RING) for i in range(RING) if (i + step) % RING < reach]
-        return lax.ppermute(item, "y", pairs)
+    def ring(item, step):
+        return lax.ppermute(item, "y", [(i, (i + step) % RING) for i in range(RING)])
 
     def spread(item):
         return item.reshape(2, n_span, own, FAST).transpose(1, 0, 2, 3).reshape(n_span, chans, FAST)
@@ -218,7 +217,19 @@
     first_raw, second_in, swapped = lax.optimization_barrier((first_raw, second_in, swapped))
 
     first = first_raw.transpose(1, 0, 2)
-    crossed_own = swap(pick_half(first, 1 - zb), "zb")
+
+    def crossing(item, gate=None):
+        if gate is None:
+            return swap(item, "zb")
+        item, gate = lax.optimization_barrier((item, gate))
+        return swap(item, "zb"), gate
+
+    quarter = own // 2
+    to_own, to_far = pick_half(first, 1 - zb), pick_half(first, zb)
+    cross_1 = crossing(to_own[:quarter])
+    cross_2, cross_1 = crossing(to_own[quarter:], cross_1)
+    crossed_own = jnp.concatenate([cross_1, cross_2])
+
     second = move(second_in).transpose(1, 0, 2)
     near_taps = ordered(left, taps, swapped[1], axis=1)
     far_taps = ordered(left, swapped[0], across, axis=1)
@@ -241,57 +252,51 @@
         [(h_spec, "s", at_start), (taps, "x", at_start), (consts["slow_taps"], "t", row), out_near,
          fast_fwd, fast_inv, twid], [0, NEAR],
     )
-    local_in = local_out.transpose(1, 0, 2)
-    local_in, crossed_own, second, first = lax.optimization_barrier((local_in, crossed_own, second, first))
-
+    local_in, crossed_own = lax.optimization_barrier((local_out.transpose(1, 0, 2), crossed_own))
     local_back = move(local_in)
-    mine = pick_half(first, zb)
-    crossed_a = swap(mine[: own // 2], "zb")
-    mine_b, crossed_a = lax.optimization_barrier((mine[own // 2 :], crossed_a))
-    crossed_far = jnp.concatenate([crossed_a, swap(mine_b, "zb")])
+    cross_3, crossed_own = crossing(to_far[:quarter], crossed_own)
     own_terms, out_own = call(
         own_kernel, place, own,
         [(second, "x", at_own), (crossed_own, "x", at_start), (h_spec, "s", at_own), (k_spec, "s", at_own),
          near, far, out_near, out_full, fast_fwd, fast_inv, twid], [HALF, NEAR],
     )
+    cross_4, cross_3 = crossing(to_far[quarter:], cross_3)
+    crossed_far = jnp.concatenate([cross_3, cross_4])
     (far_terms,) = call(
         other_kernel, place, own,
         [(second, "x", at_far), (h_spec, "s", at_far), near, out_start, fast_fwd, fast_inv, twid], [NEAR],
     )
 
-    def along(item, reach):
-        total = None
-        for step in range(RING):
-            index = jnp.minimum((y + step) % RING, reach - 1)
-            block = lax.dynamic_slice_in_dim(item, index * QUARTER, QUARTER, 1)
-            block = (ring(block, step, reach) if step else block).astype(jnp.float32)
-            total = block if total is None else total + block
-        return total
-
-    own_sum = along(own_terms, RING)
-    far_sum = jnp.where(y < RING // 2, along(far_terms, RING // 2), 0.0)
-    crossed_far, local_back, own_sum, far_sum = lax.optimization_barrier(
-        (crossed_far, local_back, own_sum, far_sum)
-    )
-
-    (out_far,) = call(
-        cross_kernel, place, own,
-        [(second, "x", at_far), (crossed_far, "x", at_start), (k_spec, "s", at_far), near, far, out_near,
-         fast_fwd, fast_inv, twid], [NEAR],
-    )
-    cross_back = move(ordered(low, out_own, out_far).transpose(1, 0, 2))
-
-    def gathered(item):
-        return item.reshape(n_span, 2, own, FAST).transpose(1, 0, 2, 3).reshape(values.shape)
-
-    conv_out = gathered(jnp.where(low, local_back, cross_back))
-    value_grads = gathered(jnp.where(low, cross_back, local_back))
-
+    sums = None
+    for step in range(RING):
+        to = (y + step) % RING
+        block = jnp.stack([
+            lax.dynamic_slice_in_dim(own_terms, to * QUARTER, QUARTER, 1),
+            lax.dynamic_slice_in_dim(far_terms, jnp.minimum(to, 1) * QUARTER, QUARTER, 1),
+        ])
+        block = (ring(block, step) if step else block).astype(jnp.float32)
+        sums = block if sums is None else sums + block
+    crossed_far, local_back, sums = lax.optimization_barrier((crossed_far, local_back, sums))
+
+    own_sum, far_sum = sums[0], jnp.where(y < RING // 2, sums[1], 0.0)
     far_here, far_there = pick_half(far_sum, zh, 1), pick_half(far_sum, 1 - zh, 1)
     own_here, own_there = pick_half(own_sum, zh, 1), pick_half(own_sum, 1 - zh, 1)
     arrived = swap(jnp.stack([far_here, own_there]).astype(jnp.bfloat16), "zb").astype(jnp.float32)
     passed = diagonal((far_there + arrived[1]).astype(jnp.bfloat16)).astype(jnp.float32)
     filter_grads = own_here + arrived[0] + passed
+
+    (out_far,) = call(
+        cross_kernel, place, own,
+        [(second, "x", at_far), (crossed_far, "x", at_start), (k_spec, "s", at_far), near, far, out_near,
+         fast_fwd, fast_inv, twid], [NEAR],
+    )
+    cross_back = move(ordered(low, out_own, out_far).transpose(1, 0, 2))
+
+    def gathered(item):
+        return item.reshape(n_span, 2, own, FAST).transpose(1, 0, 2, 3).reshape(values.shape)
+
+    conv_out = gathered(jnp.where(low, local_back, cross_back))
+    value_grads = gathered(jnp.where(low, cross_back, local_back))
     return conv_out, value_grads, filter_grads.reshape(filter_taps.shape)
 
 

time: 309 us -> 338 us (1.094)
  the two profiles are of different devices: /device:TPU:90 before, /device:TPU:66 now
where the time goes in v3:
time: 338 us; the launch traced here: 336 us
  starting transfers between devices  142 us (42%)
  waiting for transfers between devices  105 us (31%)
  Pallas kernels  61.8 us (18%)
  local copies, waits for them, and re-layouts  14.8 us (4%)
  other arithmetic  11.3 us (3%)
    ppermute x6, waiting for transfers between devices, swap(): return lax.ppermute(item, axis, [(0, 1), (1, 0)])  77 us
    pallas_call x5, Pallas kernels, call(): pl.pallas_call(kernel, grid_spec=pltpu.PrefetchScalarGridSpec(num_scalar_...  61.8 us
    ppermute x6, starting transfers between devices, swap(): return lax.ppermute(item, axis, [(0, 1), (1, 0)])  47 us
    all_to_all x4, starting transfers between devices, move(): return lax.all_to_all(item, span, split_axis=0, concat_axis=0, tiled=True)  45.7 us
    ppermute x6, starting transfers between devices, ring(): lax.ppermute(item, 'y', [(i, (i + step) % RING) for i in range(RING)])  37.4 us
    ppermute x2, waiting for transfers between devices, diagonal(): return lax.ppermute(item, ('zh', 'zb'), [(0, 3), (1, 2), (2, 1), (3, 0)])  28.1 us
    ppermute x2, starting transfers between devices, diagonal(): return lax.ppermute(item, ('zh', 'zb'), [(0, 3), (1, 2), (2, 1), (3, 0)])  11.4 us
  transfers between devices with their start and end apart: 18, of which 6 were waited for; matrix products, arithmetic and copies ran while one was open for 6% of the time, Pallas kernels for 15%

profile of v3, /device:TPU:66, one launch (start us, length us, event | category | flops | bytes accessed | tf_op | source)
XLA Modules:
  0.0 335.8 jit_solution(12990391884500044610)
XLA Ops:
  0.6 1.7 broadcast_select_fusion
  2.4 1.1 copy.17
  3.4 8.7 %all-to-all-start = ((bf16[32,128,128]{2,1,0:T(8,128)(2,1)}), bf16[32,128,128]{2,1,0:T(8,128)(2,1)S(1)}, u32[]{:S(2)}, u32[]{:S(2)}) async-start(bf16[32,128,128]{2,1,0:T(8,128)(2,1)} %bitcast.2), calls=%async_computation | async-start | bytes 2097152 | tf_op jit(solution)/shard_map/all_to_all | solution.py:208
  12.2 9.5 %collective-permute-start = (bf16[64,8,128]{2,1,0:T(8,128)(2,1)S(1)}, bf16[64,8,128]{2,1,0:T(8,128)(2,1)S(1)}, u32[]{:S(2)}, u32[]{:S(2)}) collective-permute-start(bf16[64,8,128]{2,1,0:T(8,128)(2,1)S(1)} %bitcast.79), channel_id=1, source_target_pairs={{0,96},{32,64},{64,32},{96,0},{1,97},{33,65},{65,33},{97,1},{2,98}... | collective-permute-start | bytes 393224 | tf_op jit(solution)/shard_map/ppermute | solution.py:179
  21.7 19.2 %collective-permute-done = bf16[64,8,128]{2,1,0:T(8,128)(2,1)S(1)} collective-permute-done((bf16[64,8,128]{2,1,0:T(8,128)(2,1)S(1)}, bf16[64,8,128]{2,1,0:T(8,128)(2,1)S(1)}, u32[]{:S(2)}, u32[]{:S(2)}) %collective-permute-start) | collective-permute-done | bytes 131104 | tf_op jit(solution)/shard_map/ppermute | solution.py:179
  40.9 14.9 %collective-permute-start.1 = (bf16[2,64,8,128]{3,2,1,0:T(8,128)(2,1)S(1)}, bf16[2,64,8,128]{3,2,1,0:T(8,128)(2,1)S(1)}, u32[]{:S(2)}, u32[]{:S(2)}) collective-permute-start(bf16[2,64,8,128]{3,2,1,0:T(8,128)(2,1)S(1)} %pad_maximum_fusion.7), channel_id=1, source_target_pairs={{0,32},{32,0},{1,33},{33,1},{2,34},{34,2},{3,35},{35,3},{4,36},{36... | collective-permute-start | bytes 786440 | tf_op jit(solution)/shard_map/ppermute | solution.py:175
  55.9 1.1 copy.18
  57.0 7.1 %collective-permute-done.1 = bf16[2,64,8,128]{3,2,1,0:T(8,128)(2,1)S(1)} collective-permute-done((bf16[2,64,8,128]{3,2,1,0:T(8,128)(2,1)S(1)}, bf16[2,64,8,128]{3,2,1,0:T(8,128)(2,1)S(1)}, u32[]{:S(2)}, u32[]{:S(2)}) %collective-permute-start.1) | collective-permute-done | bytes 262176 | tf_op jit(solution)/shard_map/ppermute | solution.py:175
  64.0 0.0 all-to-all-done
  64.1 12.0 %all-to-all-start.2 = ((bf16[32,128,128]{2,1,0:T(8,128)(2,1)}), bf16[32,128,128]{2,1,0:T(8,128)(2,1)S(1)}, u32[]{:S(2)}, u32[]{:S(2)}) async-start(bf16[32,128,128]{2,1,0:T(8,128)(2,1)} %bitcast.5), calls=%async_computation.2 | async-start | bytes 2097152 | tf_op jit(solution)/shard_map/all_to_all | solution.py:208
  76.1 0.1 broadcast_select_fusion.7
  76.3 0.9 pad_maximum_fusion.1
  77.1 3.5 %collective-permute-start.2 = (bf16[128,16,128]{2,1,0:T(8,128)(2,1)}, bf16[128,16,128]{2,1,0:T(8,128)(2,1)}, u32[]{:S(2)}, u32[]{:S(2)}) collective-permute-start(bf16[128,16,128]{2,1,0:T(8,128)(2,1)} %pad_maximum_fusion.1), channel_id=1, source_target_pairs={{0,128},{128,256},{256,384},{384,0},{1,129},{129,257},{257,385},{3... | collective-permute-start | bytes 1572872 | tf_op jit(solution)/shard_map/ppermute | solution.py:202
  80.6 4.8 %collective-permute-start.3 = (bf16[128,16,128]{2,1,0:T(8,128)(2,1)}, bf16[128,16,128]{2,1,0:T(8,128)(2,1)}, u32[]{:S(2)}, u32[]{:S(2)}) collective-permute-start(bf16[128,16,128]{2,1,0:T(8,128)(2,1)} %pad_maximum_fusion.1), channel_id=1, source_target_pairs={{0,256},{128,384},{256,0},{384,128},{1,257},{129,385},{257,1},{385... | collective-permute-start | bytes 1572872 | tf_op jit(solution)/shard_map/ppermute | solution.py:202
  85.4 3.3 collective-permute-start.4
  88.7 0.7 copy.36
  89.4 0.0 copy-start
  89.4 1.0 dynamic-slice_bitcast_fusion
  90.4 0.7 fusion.4
  91.2 5.8 %collective-permute-start.5 = (bf16[32,32,128]{2,1,0:T(8,128)(2,1)}, bf16[32,32,128]{2,1,0:T(8,128)(2,1)S(1)}, u32[]{:S(2)}, u32[]{:S(2)}) collective-permute-start(bf16[32,32,128]{2,1,0:T(8,128)(2,1)} %get-tuple-element.59), channel_id=1, source_target_pairs={{0,32},{32,0},{1,33},{33,1},{2,34},{34,2},{3,35},{35,3},{4,36},{36... | collective-permute-start | bytes 786440 | tf_op jit(solution)/shard_map/ppermute | solution.py:175
  97.0 18.1 %collective-permute-done.5 = bf16[32,32,128]{2,1,0:T(8,128)(2,1)S(1)} collective-permute-done((bf16[32,32,128]{2,1,0:T(8,128)(2,1)}, bf16[32,32,128]{2,1,0:T(8,128)(2,1)S(1)}, u32[]{:S(2)}, u32[]{:S(2)}) %collective-permute-start.5) | collective-permute-done | bytes 262176 | tf_op jit(solution)/shard_map/ppermute | solution.py:175
  115.1 8.2 %collective-permute-start.6 = (bf16[32,32,128]{2,1,0:T(8,128)(2,1)S(1)}, bf16[32,32,128]{2,1,0:T(8,128)(2,1)S(1)}, u32[]{:S(2)}, u32[]{:S(2)}) collective-permute-start(bf16[32,32,128]{2,1,0:T(8,128)(2,1)S(1)} %get-tuple-element.25), channel_id=1, source_target_pairs={{0,32},{32,0},{1,33},{33,1},{2,34},{34,2},{3,35},{35,3},{4,36},{36... | collective-permute-start | bytes 786440 | tf_op jit(solution)/shard_map/ppermute | solution.py:175
  123.3 0.6 pad_add_fusion.place
  123.9 13.1 %shard_map.121.h_in = bf16[10240,256]{1,0:T(8,128)(2,1)} custom-call(s32[2]{0:T(128)} %pad_add_fusion.place, bf16[128,32,128]{2,1,0:T(8,128)(2,1)} %bitcast.74, bf16[2,160,32]{2,1,0:T(8,128)(2,1)} %constant.77.clone.near.far, bf16[256,256]{1,0:T(8,128)(2,1)} %constant.81.clone.fast_fwd, f32[2,80,128]{2,1,0:T(8,128)} %constant.83.clone.twid), custom_call_target="tpu_custom_call" | custom-call | flops 1 | bytes 1 | tf_op jit(solution)/shard_map/pallas_call | solution.py:163
  136.9 0.0 collective-permute-done.2
  136.9 0.0 collective-permute-done.3
  136.9 0.0 collective-permute-done.4
  137.0 4.3 %pad_maximum_fusion.taps = bf16[128,64,128]{2,1,0:T(8,128)(2,1)} fusion(bf16[128,16,128]{2,1,0:T(8,128)(2,1)} %collective-permute-done.4, bf16[128,16,128]{2,1,0:T(8,128)(2,1)} %collective-permute-done.3, bf16[128,16,128]{2,1,0:T(8,128)(2,1)} %collective-permute-done.2, bf16[64,16,128]{2,1,0:T(8,128)(2,1)S(1)} %copy-done.3, ...), kind=kLoop, calls=%fused_computation | loop fusion | flops 10485760 | bytes 4194304 | tf_op jit(solution)/shard_map/concatenate | solution.py:237
  141.2 16.7 %shard_map.122 = (bf16[10240,256]{1,0:T(8,128)(2,1)}, bf16[128,32,128]{2,1,0:T(8,128)(2,1)}) custom-call(s32[2]{0:T(128)} %pad_add_fusion.place, bf16[10240,256]{1,0:T(8,128)(2,1)} %shard_map.121.h_in, bf16[128,64,128]{2,1,0:T(8,128)(2,1)} %pad_maximum_fusion.taps, bf16[4,160,64]{2,1,0:T(8,128)(2,1)} %constant.78.clone.taps_table, ...), custom_call_target="tpu_custom_call" | custom-call | flops 1 | bytes 1 | tf_op jit(solution)/shard_map/pallas_call | solution.py:163
  157.9 0.0 collective-permute-done.6
  157.9 0.9 pad_maximum_fusion.2.crossed
  158.8 2.6 copy.22
  161.4 0.0 all-to-all-done.2
  161.4 11.8 %all-to-all-start.1 = ((bf16[32,128,128]{2,1,0:T(8,128)(2,1)}), bf16[32,128,128]{2,1,0:T(8,128)(2,1)S(1)}, u32[]{:S(2)}, u32[]{:S(2)}) async-start(bf16[32,128,128]{2,1,0:T(8,128)(2,1)} %copy.22), calls=%async_computation.1 | async-start | bytes 2097152 | tf_op jit(solution)/shard_map/all_to_all | solution.py:208
  173.4 1.9 collective-permute-start.7
  175.3 1.6 copy.34
  177.0 9.4 %shard_map.124 = bf16[64,32,128]{2,1,0:T(8,128)(2,1)} custom-call(s32[2]{0:T(128)} %pad_add_fusion.place, bf16[128,32,128]{2,1,0:T(8,128)(2,1)} %bitcast.71, bf16[10240,256]{1,0:T(8,128)(2,1)} %shard_map.121.h_in, bf16[2,160,32]{2,1,0:T(8,128)(2,1)} %constant.77.clone.near.far, bf16[2,32,160]{2,1,0:T(8,128)(2,1)} %constant.79.clone.slow_out, ...), custom_call_target="tpu_custom_call" | custom-call | flops 1 | bytes 1 | tf_op jit(solution)/shard_map/pallas_call | solution.py:163
  186.4 12.4 %shard_map.123 = (bf16[64,64,128]{2,1,0:T(8,128)(2,1)}, bf16[64,32,128]{2,1,0:T(8,128)(2,1)}) custom-call(s32[2]{0:T(128)} %pad_add_fusion.place, bf16[128,32,128]{2,1,0:T(8,128)(2,1)} %bitcast.72, bf16[64,32,128]{2,1,0:T(8,128)(2,1)} %pad_maximum_fusion.2.crossed, bf16[10240,256]{1,0:T(8,128)(2,1)} %shard_map.121.h_in, ...), custom_call_target="tpu_custom_call" | custom-call | flops 1 | bytes 1 | tf_op jit(solution)/shard_map/pallas_call | solution.py:163
  198.7 1.6 dynamic-slice_bitcast_fusion.8
  200.4 0.1 pad_maximum_fusion.4
  200.4 19.4 %collective-permute-start.9 = (bf16[2,64,16,128]{3,2,1,0:T(8,128)(2,1)S(1)}, bf16[2,64,16,128]{3,2,1,0:T(8,128)(2,1)S(1)}, u32[]{:S(2)}, u32[]{:S(2)}) collective-permute-start(bf16[2,64,16,128]{3,2,1,0:T(8,128)(2,1)S(1)} %pad_maximum_fusion.4), channel_id=1, source_target_pairs={{0,128},{128,256},{256,384},{384,0},{1,129},{129,257},{257,385},{3... | collective-permute-start | bytes 1572872 | tf_op jit(solution)/shard_map/ppermute | solution.py:202
  219.8 0.1 pad_maximum_fusion.5
  219.9 3.0 collective-permute-start.10
  222.9 0.1 pad_maximum_fusion.6
  222.9 3.5 %collective-permute-start.11 = (bf16[2,64,16,128]{3,2,1,0:T(8,128)(2,1)S(1)}, bf16[2,64,16,128]{3,2,1,0:T(8,128)(2,1)S(1)}, u32[]{:S(2)}, u32[]{:S(2)}) collective-permute-start(bf16[2,64,16,128]{3,2,1,0:T(8,128)(2,1)S(1)} %pad_maximum_fusion.6), channel_id=1, source_target_pairs={{0,384},{128,0},{256,128},{384,256},{1,385},{129,1},{257,129},{385... | collective-permute-start | bytes 1572872 | tf_op jit(solution)/shard_map/ppermute | solution.py:202
  226.5 0.0 collective-permute-done.7
  226.5 7.8 %collective-permute-start.8 = (bf16[32,32,128]{2,1,0:T(8,128)(2,1)S(1)}, bf16[32,32,128]{2,1,0:T(8,128)(2,1)S(1)}, u32[]{:S(2)}, u32[]{:S(2)}) collective-permute-start(bf16[32,32,128]{2,1,0:T(8,128)(2,1)S(1)} %get-tuple-element.29), channel_id=1, source_target_pairs={{0,32},{32,0},{1,33},{33,1},{2,34},{34,2},{3,35},{35,3},{4,36},{36... | collective-permute-start | bytes 786440 | tf_op jit(solution)/shard_map/ppermute | solution.py:175
  234.3 16.3 %collective-permute-done.8 = bf16[32,32,128]{2,1,0:T(8,128)(2,1)S(1)} collective-permute-done((bf16[32,32,128]{2,1,0:T(8,128)(2,1)S(1)}, bf16[32,32,128]{2,1,0:T(8,128)(2,1)S(1)}, u32[]{:S(2)}, u32[]{:S(2)}) %collective-permute-start.8) | collective-permute-done | bytes 262176 | tf_op jit(solution)/shard_map/ppermute | solution.py:175
  250.6 0.8 pad_maximum_fusion.3.crossed
  251.5 0.2 convert_add_fusion
  251.7 10.2 %shard_map.125 = bf16[64,32,128]{2,1,0:T(8,128)(2,1)} custom-call(s32[2]{0:T(128)} %pad_add_fusion.place, bf16[128,32,128]{2,1,0:T(8,128)(2,1)} %bitcast.73, bf16[64,32,128]{2,1,0:T(8,128)(2,1)} %pad_maximum_fusion.3.crossed, bf16[10240,256]{1,0:T(8,128)(2,1)} %get-tuple-element.33.k_in, bf16[2,160,32]{2,1,0:T(8,128)(2,1)} %constant.77.clone.near.far, ...), custom_call_target="tpu_custom_call" | custom-call | flops 1 | bytes 1 | tf_op jit(solution)/shard_map/pallas_call | solution.py:163
  261.9 1.1 broadcast_select_fusion.5
  263.1 0.1 maximum_bitcast_fusion
  263.2 1.4 copy.24
  264.5 13.2 %all-to-all-start.3 = ((bf16[32,128,128]{2,1,0:T(8,128)(2,1)}), bf16[32,128,128]{2,1,0:T(8,128)(2,1)S(1)}, u32[]{:S(2)}, u32[]{:S(2)}) async-start(bf16[32,128,128]{2,1,0:T(8,128)(2,1)} %copy.24), calls=%async_computation.3 | async-start | bytes 2097152 | tf_op jit(solution)/shard_map/all_to_all | solution.py:208
  277.8 0.1 slice_select_fusion
  278.0 8.3 %collective-permute-start.12 = (bf16[2,64,8,128]{3,2,1,0:T(8,128)(2,1)S(1)}, bf16[2,64,8,128]{3,2,1,0:T(8,128)(2,1)S(1)}, u32[]{:S(2)}, u32[]{:S(2)}) collective-permute-start(bf16[2,64,8,128]{3,2,1,0:T(8,128)(2,1)S(1)} %pad_maximum_fusion.10), channel_id=1, source_target_pairs={{0,32},{32,0},{1,33},{33,1},{2,34},{34,2},{3,35},{35,3},{4,36},{36... | collective-permute-start | bytes 786440 | tf_op jit(solution)/shard_map/ppermute | solution.py:175
  286.3 35.6 %collective-permute-done.12 = bf16[2,64,8,128]{3,2,1,0:T(8,128)(2,1)S(1)} collective-permute-done((bf16[2,64,8,128]{3,2,1,0:T(8,128)(2,1)S(1)}, bf16[2,64,8,128]{3,2,1,0:T(8,128)(2,1)S(1)}, u32[]{:S(2)}, u32[]{:S(2)}) %collective-permute-start.12) | collective-permute-done | bytes 262176 | tf_op jit(solution)/shard_map/ppermute | solution.py:175
  322.0 1.9 collective-permute-start.13
  323.9 8.9 %collective-permute-done.13 = bf16[64,8,128]{2,1,0:T(8,128)(2,1)S(1)} collective-permute-done((bf16[64,8,128]{2,1,0:T(8,128)(2,1)S(1)}, bf16[64,8,128]{2,1,0:T(8,128)(2,1)S(1)}, u32[]{:S(2)}, u32[]{:S(2)}) %collective-permute-start.13) | collective-permute-done | bytes 131104 | tf_op jit(solution)/shard_map/ppermute | solution.py:179
  332.8 0.8 copy.35
  333.6 0.1 broadcast_select_fusion.2
  333.7 1.0 copy.25
  334.8 1.0 copy.26
  (28 shorter events, 0.4 us)
Async XLA Ops:
  0.6 11.5 %copy-start.6 = (bf16[64,1024]{1,0:T(8,128)(2,1)S(1)}, bf16[64,1024]{1,0:T(8,128)(2,1)}, u32[]{:S(2)}) copy-start(bf16[64,1024]{1,0:T(8,128)(2,1)} %param.12) | copy-start | bytes 393220
  3.4 60.6 %all-to-all-start = ((bf16[32,128,128]{2,1,0:T(8,128)(2,1)}), bf16[32,128,128]{2,1,0:T(8,128)(2,1)S(1)}, u32[]{:S(2)}, u32[]{:S(2)}) async-start(bf16[32,128,128]{2,1,0:T(8,128)(2,1)} %bitcast.2), calls=%async_computation | async-start | bytes 2097152 | tf_op jit(solution)/shard_map/all_to_all | solution.py:208
  12.2 28.7 %collective-permute-start = (bf16[64,8,128]{2,1,0:T(8,128)(2,1)S(1)}, bf16[64,8,128]{2,1,0:T(8,128)(2,1)S(1)}, u32[]{:S(2)}, u32[]{:S(2)}) collective-permute-start(bf16[64,8,128]{2,1,0:T(8,128)(2,1)S(1)} %bitcast.79), channel_id=1, source_target_pairs={{0,96},{32,64},{64,32},{96,0},{1,97},{33,65},{65,33},{97,1},{2,98}... | collective-permute-start | bytes 393224 | tf_op jit(solution)/shard_map/ppermute | solution.py:179
  40.9 23.1 %collective-permute-start.1 = (bf16[2,64,8,128]{3,2,1,0:T(8,128)(2,1)S(1)}, bf16[2,64,8,128]{3,2,1,0:T(8,128)(2,1)S(1)}, u32[]{:S(2)}, u32[]{:S(2)}) collective-permute-start(bf16[2,64,8,128]{3,2,1,0:T(8,128)(2,1)S(1)} %pad_maximum_fusion.7), channel_id=1, source_target_pairs={{0,32},{32,0},{1,33},{33,1},{2,34},{34,2},{3,35},{35,3},{4,36},{36... | collective-permute-start | bytes 786440 | tf_op jit(solution)/shard_map/ppermute | solution.py:175
  64.1 97.4 %all-to-all-start.2 = ((bf16[32,128,128]{2,1,0:T(8,128)(2,1)}), bf16[32,128,128]{2,1,0:T(8,128)(2,1)S(1)}, u32[]{:S(2)}, u32[]{:S(2)}) async-start(bf16[32,128,128]{2,1,0:T(8,128)(2,1)} %bitcast.5), calls=%async_computation.2 | async-start | bytes 2097152 | tf_op jit(solution)/shard_map/all_to_all | solution.py:208
  76.2 9.2 %copy-start.2 = (bf16[64,16,128]{2,1,0:T(8,128)(2,1)}, bf16[64,16,128]{2,1,0:T(8,128)(2,1)S(1)}, u32[]{:S(2)}) copy-start(bf16[64,16,128]{2,1,0:T(8,128)(2,1)S(1)} %get-tuple-element.62) | copy-start | bytes 786436
  77.1 59.8 %collective-permute-start.2 = (bf16[128,16,128]{2,1,0:T(8,128)(2,1)}, bf16[128,16,128]{2,1,0:T(8,128)(2,1)}, u32[]{:S(2)}, u32[]{:S(2)}) collective-permute-start(bf16[128,16,128]{2,1,0:T(8,128)(2,1)} %pad_maximum_fusion.1), channel_id=1, source_target_pairs={{0,128},{128,256},{256,384},{384,0},{1,129},{129,257},{257,385},{3... | collective-permute-start | bytes 1572872 | tf_op jit(solution)/shard_map/ppermute | solution.py:202
  80.6 56.3 %collective-permute-start.3 = (bf16[128,16,128]{2,1,0:T(8,128)(2,1)}, bf16[128,16,128]{2,1,0:T(8,128)(2,1)}, u32[]{:S(2)}, u32[]{:S(2)}) collective-permute-start(bf16[128,16,128]{2,1,0:T(8,128)(2,1)} %pad_maximum_fusion.1), channel_id=1, source_target_pairs={{0,256},{128,384},{256,0},{384,128},{1,257},{129,385},{257,1},{385... | collective-permute-start | bytes 1572872 | tf_op jit(solution)/shard_map/ppermute | solution.py:202
  85.4 51.5 %collective-permute-start.4 = (bf16[128,16,128]{2,1,0:T(8,128)(2,1)}, bf16[128,16,128]{2,1,0:T(8,128)(2,1)}, u32[]{:S(2)}, u32[]{:S(2)}) collective-permute-start(bf16[128,16,128]{2,1,0:T(8,128)(2,1)} %pad_maximum_fusion.1), channel_id=1, source_target_pairs={{0,384},{128,0},{256,128},{384,256},{1,385},{129,1},{257,129},{385... | collective-permute-start | bytes 1572872 | tf_op jit(solution)/shard_map/ppermute | solution.py:202
  89.4 34.5 %copy-start = (bf16[32,128,128]{2,0,1:T(8,128)(2,1)}, bf16[32,128,128]{2,0,1:T(8,128)(2,1)S(1)}, u32[]{:S(2)}) copy-start(bf16[32,128,128]{2,0,1:T(8,128)(2,1)S(1)} %copy.36) | copy-start | bytes 3145732
  90.4 46.5 %copy-start.3 = (bf16[64,16,128]{2,1,0:T(8,128)(2,1)S(1)}, bf16[64,16,128]{2,1,0:T(8,128)(2,1)}, u32[]{:S(2)}) copy-start(bf16[64,16,128]{2,1,0:T(8,128)(2,1)} %copy-done.2) | copy-start | bytes 786436
  91.2 23.9 %collective-permute-start.5 = (bf16[32,32,128]{2,1,0:T(8,128)(2,1)}, bf16[32,32,128]{2,1,0:T(8,128)(2,1)S(1)}, u32[]{:S(2)}, u32[]{:S(2)}) collective-permute-start(bf16[32,32,128]{2,1,0:T(8,128)(2,1)} %get-tuple-element.59), channel_id=1, source_target_pairs={{0,32},{32,0},{1,33},{33,1},{2,34},{34,2},{3,35},{35,3},{4,36},{36... | collective-permute-start | bytes 786440 | tf_op jit(solution)/shard_map/ppermute | solution.py:175
  115.1 42.9 %collective-permute-start.6 = (bf16[32,32,128]{2,1,0:T(8,128)(2,1)S(1)}, bf16[32,32,128]{2,1,0:T(8,128)(2,1)S(1)}, u32[]{:S(2)}, u32[]{:S(2)}) collective-permute-start(bf16[32,32,128]{2,1,0:T(8,128)(2,1)S(1)} %get-tuple-element.25), channel_id=1, source_target_pairs={{0,32},{32,0},{1,33},{33,1},{2,34},{34,2},{3,35},{35,3},{4,36},{36... | collective-permute-start | bytes 786440 | tf_op jit(solution)/shard_map/ppermute | solution.py:175
  157.9 15.4 %copy-start.4 = (bf16[64,32,128]{2,1,0:T(8,128)(2,1)S(1)}, bf16[64,32,128]{2,1,0:T(8,128)(2,1)}, u32[]{:S(2)}) copy-start(bf16[64,32,128]{2,1,0:T(8,128)(2,1)} %get-tuple-element.52) | copy-start | bytes 1572868
  161.4 90.3 %all-to-all-start.1 = ((bf16[32,128,128]{2,1,0:T(8,128)(2,1)}), bf16[32,128,128]{2,1,0:T(8,128)(2,1)S(1)}, u32[]{:S(2)}, u32[]{:S(2)}) async-start(bf16[32,128,128]{2,1,0:T(8,128)(2,1)} %copy.22), calls=%async_computation.1 | async-start | bytes 2097152 | tf_op jit(solution)/shard_map/all_to_all | solution.py:208
  173.4 53.1 %collective-permute-start.7 = (bf16[32,32,128]{2,1,0:T(8,128)(2,1)S(1)}, bf16[32,32,128]{2,1,0:T(8,128)(2,1)S(1)}, u32[]{:S(2)}, u32[]{:S(2)}) collective-permute-start(bf16[32,32,128]{2,1,0:T(8,128)(2,1)S(1)} %get-tuple-element.27), channel_id=1, source_target_pairs={{0,32},{32,0},{1,33},{33,1},{2,34},{34,2},{3,35},{35,3},{4,36},{36... | collective-permute-start | bytes 786440 | tf_op jit(solution)/shard_map/ppermute | solution.py:175
  186.4 12.4 %copy-start.1 = (bf16[64,32,128]{2,1,0:T(8,128)(2,1)S(1)}, bf16[64,32,128]{2,1,0:T(8,128)(2,1)}, u32[]{:S(2)}) copy-start(bf16[64,32,128]{2,1,0:T(8,128)(2,1)} %shard_map.124) | copy-start | bytes 1572868
  200.4 51.0 %collective-permute-start.9 = (bf16[2,64,16,128]{3,2,1,0:T(8,128)(2,1)S(1)}, bf16[2,64,16,128]{3,2,1,0:T(8,128)(2,1)S(1)}, u32[]{:S(2)}, u32[]{:S(2)}) collective-permute-start(bf16[2,64,16,128]{3,2,1,0:T(8,128)(2,1)S(1)} %pad_maximum_fusion.4), channel_id=1, source_target_pairs={{0,128},{128,256},{256,384},{384,0},{1,129},{129,257},{257,385},{3... | collective-permute-start | bytes 1572872 | tf_op jit(solution)/shard_map/ppermute | solution.py:202
  219.9 31.6 %collective-permute-start.10 = (bf16[2,64,16,128]{3,2,1,0:T(8,128)(2,1)S(1)}, bf16[2,64,16,128]{3,2,1,0:T(8,128)(2,1)S(1)}, u32[]{:S(2)}, u32[]{:S(2)}) collective-permute-start(bf16[2,64,16,128]{3,2,1,0:T(8,128)(2,1)S(1)} %pad_maximum_fusion.5), channel_id=1, source_target_pairs={{0,256},{128,384},{256,0},{384,128},{1,257},{129,385},{257,1},{385... | collective-permute-start | bytes 1572872 | tf_op jit(solution)/shard_map/ppermute | solution.py:202
  222.9 28.5 %collective-permute-start.11 = (bf16[2,64,16,128]{3,2,1,0:T(8,128)(2,1)S(1)}, bf16[2,64,16,128]{3,2,1,0:T(8,128)(2,1)S(1)}, u32[]{:S(2)}, u32[]{:S(2)}) collective-permute-start(bf16[2,64,16,128]{3,2,1,0:T(8,128)(2,1)S(1)} %pad_maximum_fusion.6), channel_id=1, source_target_pairs={{0,384},{128,0},{256,128},{384,256},{1,385},{129,1},{257,129},{385... | collective-permute-start | bytes 1572872 | tf_op jit(solution)/shard_map/ppermute | solution.py:202
  226.5 24.1 %collective-permute-start.8 = (bf16[32,32,128]{2,1,0:T(8,128)(2,1)S(1)}, bf16[32,32,128]{2,1,0:T(8,128)(2,1)S(1)}, u32[]{:S(2)}, u32[]{:S(2)}) collective-permute-start(bf16[32,32,128]{2,1,0:T(8,128)(2,1)S(1)} %get-tuple-element.29), channel_id=1, source_target_pairs={{0,32},{32,0},{1,33},{33,1},{2,34},{34,2},{3,35},{35,3},{4,36},{36... | collective-permute-start | bytes 786440 | tf_op jit(solution)/shard_map/ppermute | solution.py:175
  251.7 10.2 %copy-start.5 = (bf16[64,32,128]{2,1,0:T(8,128)(2,1)S(1)}, bf16[64,32,128]{2,1,0:T(8,128)(2,1)}, u32[]{:S(2)}) copy-start(bf16[64,32,128]{2,1,0:T(8,128)(2,1)} %get-tuple-element.36) | copy-start | bytes 1572868
  264.5 69.1 %all-to-all-start.3 = ((bf16[32,128,128]{2,1,0:T(8,128)(2,1)}), bf16[32,128,128]{2,1,0:T(8,128)(2,1)S(1)}, u32[]{:S(2)}, u32[]{:S(2)}) async-start(bf16[32,128,128]{2,1,0:T(8,128)(2,1)} %copy.24), calls=%async_computation.3 | async-start | bytes 2097152 | tf_op jit(solution)/shard_map/all_to_all | solution.py:208
  278.0 43.9 %collective-permute-start.12 = (bf16[2,64,8,128]{3,2,1,0:T(8,128)(2,1)S(1)}, bf16[2,64,8,128]{3,2,1,0:T(8,128)(2,1)S(1)}, u32[]{:S(2)}, u32[]{:S(2)}) collective-permute-start(bf16[2,64,8,128]{3,2,1,0:T(8,128)(2,1)S(1)} %pad_maximum_fusion.10), channel_id=1, source_target_pairs={{0,32},{32,0},{1,33},{33,1},{2,34},{34,2},{3,35},{35,3},{4,36},{36... | collective-permute-start | bytes 786440 | tf_op jit(solution)/shard_map/ppermute | solution.py:175
  322.0 10.8 %collective-permute-start.13 = (bf16[64,8,128]{2,1,0:T(8,128)(2,1)S(1)}, bf16[64,8,128]{2,1,0:T(8,128)(2,1)S(1)}, u32[]{:S(2)}, u32[]{:S(2)}) collective-permute-start(bf16[64,8,128]{2,1,0:T(8,128)(2,1)S(1)} %fusion.3), channel_id=1, source_target_pairs={{0,96},{32,64},{64,32},{96,0},{1,97},{33,65},{65,33},{97,1},{2,98}... | collective-permute-start | bytes 393224 | tf_op jit(solution)/shard_map/ppermute | solution.py:179

commit v4 on v3

--- a/solution.py
+++ b/solution.py
@@ -19,6 +19,7 @@
 RING = 4
 QUARTER = HALF // RING
 BLOCK = 8
+LONG = 30 * 10**9
 
 
 def tables():
@@ -139,7 +140,7 @@
     inverse(joined(kr * fr + ki * fi, kr * fi - ki * fr), out, slow_out[0], twid, fast_inv)
 
 
-def call(kernel, place, chans, items, outs):
+def call(kernel, place, chans, items, outs, flops=1):
     in_specs, arrays = [], []
     for item, kind, pick in items:
         if kind == "x":
@@ -166,8 +167,8 @@
             num_scalar_prefetch=1, grid=(chans // BLOCK,), in_specs=in_specs, out_specs=out_specs
         ),
         out_shape=shapes,
-        compiler_params=pltpu.CompilerParams(vmem_limit_bytes=56 * 1024 * 1024),
-        cost_estimate=pl.CostEstimate(flops=1, bytes_accessed=1, transcendentals=0),
+        compiler_params=pltpu.CompilerParams(vmem_limit_bytes=20 * 1024 * 1024),
+        cost_estimate=pl.CostEstimate(flops=flops, bytes_accessed=1, transcendentals=0),
     )(place, *arrays)
 
 
@@ -208,34 +209,16 @@
         return lax.all_to_all(item, span, split_axis=0, concat_axis=0, tiled=True)
 
     taps = filter_taps.reshape(own, HALF // 8, FAST)
-    across = diagonal(taps)
+    far_here, own_there, far_there = swap(taps, "zb"), swap(taps, "zh"), diagonal(taps)
 
     v_parts, g_parts = spread(values), spread(grads)
     first_raw = move(jnp.where(low, v_parts, g_parts))
     second_in = jnp.where(low, g_parts, v_parts)
-    swapped = swap(jnp.stack([taps, across]), "zb")
-    first_raw, second_in, swapped = lax.optimization_barrier((first_raw, second_in, swapped))
+    first_raw, second_in, far_here, own_there, far_there = lax.optimization_barrier(
+        (first_raw, second_in, far_here, own_there, far_there)
+    )
 
     first = first_raw.transpose(1, 0, 2)
-
-    def crossing(item, gate=None):
-        if gate is None:
-            return swap(item, "zb")
-        item, gate = lax.optimization_barrier((item, gate))
-        return swap(item, "zb"), gate
-
-    quarter = own // 2
-    to_own, to_far = pick_half(first, 1 - zb), pick_half(first, zb)
-    cross_1 = crossing(to_own[:quarter])
-    cross_2, cross_1 = crossing(to_own[quarter:], cross_1)
-    crossed_own = jnp.concatenate([cross_1, cross_2])
-
-    second = move(second_in).transpose(1, 0, 2)
-    near_taps = ordered(left, taps, swapped[1], axis=1)
-    far_taps = ordered(left, swapped[0], across, axis=1)
-    taps = ordered(low, near_taps, far_taps)
-    taps = jnp.concatenate([taps] + [ring(taps, step) for step in range(1, RING)], axis=1)
-
     n_own = own // BLOCK
     at_start, at_own, at_far = (lambda p: 0), (lambda p: p[0] * n_own), (lambda p: (1 - p[0]) * n_own)
     here, there, row = (lambda p: p[0]), (lambda p: 1 - p[0]), (lambda p: p[1])
@@ -247,24 +230,31 @@
     fast_fwd, fast_inv, twid = [(consts[name], None, None) for name in ("fast_fwd", "fast_inv", "twid")]
 
     (h_spec,) = call(first_kernel, place, chans, [(first, "x", at_start), near, fast_fwd, twid], [0])
+    quarter = own // 2
+    to_own, to_far = pick_half(first, 1 - zb), pick_half(first, zb)
+    cross_own, cross_far = swap(to_own, "zb"), swap(to_far, "zb")
+
+    second = move(second_in).transpose(1, 0, 2)
+    near_taps = ordered(left, taps, own_there, axis=1)
+    far_taps = ordered(left, far_here, far_there, axis=1)
+    taps = ordered(low, near_taps, far_taps)
+    taps = jnp.concatenate([taps] + [ring(taps, step) for step in range(1, RING)], axis=1)
+    (far_terms,) = call(
+        other_kernel, place, own,
+        [(second, "x", at_far), (h_spec, "s", at_far), near, out_start, fast_fwd, fast_inv, twid], [NEAR],
+    )
+    taps, cross_own, far_terms = lax.optimization_barrier((taps, cross_own, far_terms))
+
     k_spec, local_out = call(
         local_kernel, place, chans,
         [(h_spec, "s", at_start), (taps, "x", at_start), (consts["slow_taps"], "t", row), out_near,
          fast_fwd, fast_inv, twid], [0, NEAR],
     )
-    local_in, crossed_own = lax.optimization_barrier((local_out.transpose(1, 0, 2), crossed_own))
-    local_back = move(local_in)
-    cross_3, crossed_own = crossing(to_far[:quarter], crossed_own)
+    local_back = move(local_out.transpose(1, 0, 2))
     own_terms, out_own = call(
         own_kernel, place, own,
-        [(second, "x", at_own), (crossed_own, "x", at_start), (h_spec, "s", at_own), (k_spec, "s", at_own),
+        [(second, "x", at_own), (cross_own, "x", at_start), (h_spec, "s", at_own), (k_spec, "s", at_own),
          near, far, out_near, out_full, fast_fwd, fast_inv, twid], [HALF, NEAR],
-    )
-    cross_4, cross_3 = crossing(to_far[quarter:], cross_3)
-    crossed_far = jnp.concatenate([cross_3, cross_4])
-    (far_terms,) = call(
-        other_kernel, place, own,
-        [(second, "x", at_far), (h_spec, "s", at_far), near, out_start, fast_fwd, fast_inv, twid], [NEAR],
     )
 
     sums = None
@@ -276,7 +266,14 @@
         ])
         block = (ring(block, step) if step else block).astype(jnp.float32)
         sums = block if sums is None else sums + block
-    crossed_far, local_back, sums = lax.optimization_barrier((crossed_far, local_back, sums))
+    (out_far,) = call(
+        cross_kernel, place, own,
+        [(second, "x", at_far), (cross_far, "x", at_start), (k_spec, "s", at_far), near, far, out_near,
+         fast_fwd, fast_inv, twid], [NEAR], flops=LONG,
+    )
+    cross_in = ordered(low, out_own, out_far).transpose(1, 0, 2)
+    cross_in, local_back, sums = lax.optimization_barrier((cross_in, local_back, sums))
+    cross_back = move(cross_in)
 
     own_sum, far_sum = sums[0], jnp.where(y < RING // 2, sums[1], 0.0)
     far_here, far_there = pick_half(far_sum, zh, 1), pick_half(far_sum, 1 - zh, 1)
@@ -284,13 +281,6 @@
     arrived = swap(jnp.stack([far_here, own_there]).astype(jnp.bfloat16), "zb").astype(jnp.float32)
     passed = diagonal((far_there + arrived[1]).astype(jnp.bfloat16)).astype(jnp.float32)
     filter_grads = own_here + arrived[0] + passed
-
-    (out_far,) = call(
-        cross_kernel, place, own,
-        [(second, "x", at_far), (crossed_far, "x", at_start), (k_spec, "s", at_far), near, far, out_near,
-         fast_fwd, fast_inv, twid], [NEAR],
-    )
-    cross_back = move(ordered(low, out_own, out_far).transpose(1, 0, 2))
 
     def gathered(item):
         return item.reshape(n_span, 2, own, FAST).transpose(1, 0, 2, 3).reshape(values.shape)

time: 338 us -> 311 us (0.920)
  starting transfers between devices: 142 us -> 111 us
  Pallas kernels: 61.8 us -> 44.6 us
  waiting for transfers between devices: 105 us -> 119 us
  local copies, waits for them, and re-layouts: 14.8 us -> 28.4 us
  other arithmetic: 11.3 us -> 4.78 us
    ppermute x2, waiting for transfers between devices: 28.1 us -> 8.92 us  [diagonal(): return lax.ppermute(item, ('zh', 'zb'), [(0, 3), (1, 2), (2, 1), (3, 0)])]
    pallas_call x5, Pallas kernels: 61.8 us -> 44.6 us  [call(): pl.pallas_call(kernel, grid_spec=pltpu.PrefetchScalarGridSpec(num_scalar_...]
    ppermute x6, starting transfers between devices: 37.4 us -> 20.8 us  [ring(): lax.ppermute(item, 'y', [(i, (i + step) % RING) for i in range(RING)])]
    unnamed x16 -> x44, local copies, waits for them, and re-layouts: 0.8 us -> 17.3 us
    ppermute x6 -> x5, starting transfers between devices: 47 us -> 34.6 us  [swap(): return lax.ppermute(item, axis, [(0, 1), (1, 0)])]
    all_to_all x4, waiting for transfers between devices: 0.01 us -> 12.3 us  [move(): return lax.all_to_all(item, span, split_axis=0, concat_axis=0, tiled=True)]
    ppermute x6, waiting for transfers between devices: 0.02 us -> 10.8 us  [ring(): lax.ppermute(item, 'y', [(i, (i + step) % RING) for i in range(RING)])]
    ppermute x6 -> x5, waiting for transfers between devices: 77 us -> 87.5 us  [swap(): return lax.ppermute(item, axis, [(0, 1), (1, 0)])]
  transfers between devices with their start and end apart: 18 -> 17, of which waited for: 6 -> 7; matrix products, arithmetic and copies ran while one was open for 6% -> 3% of each run, Pallas kernels for 15% -> 14%
where the time goes in v4:
time: 311 us; the launch traced here: 309 us
  waiting for transfers between devices  119 us (38%)
  starting transfers between devices  111 us (36%)
  Pallas kernels  44.6 us (14%)
  local copies, waits for them, and re-layouts  28.4 us (9%)
  other arithmetic  4.78 us (2%)
    ppermute x5, waiting for transfers between devices, swap(): return lax.ppermute(item, axis, [(0, 1), (1, 0)])  87.5 us
    all_to_all x4, starting transfers between devices, move(): return lax.all_to_all(item, span, split_axis=0, concat_axis=0, tiled=True)  51.4 us
    pallas_call x5, Pallas kernels, call(): pl.pallas_call(kernel, grid_spec=pltpu.PrefetchScalarGridSpec(num_scalar_...  44.6 us
    ppermute x5, starting transfers between devices, swap(): return lax.ppermute(item, axis, [(0, 1), (1, 0)])  34.6 us
    ppermute x6, starting transfers between devices, ring(): lax.ppermute(item, 'y', [(i, (i + step) % RING) for i in range(RING)])  20.8 us
    unnamed x44, local copies, waits for them, and re-layouts  17.3 us
    all_to_all x4, waiting for transfers between devices, move(): return lax.all_to_all(item, span, split_axis=0, concat_axis=0, tiled=True)  12.3 us
    ppermute x6, waiting for transfers between devices, ring(): lax.ppermute(item, 'y', [(i, (i + step) % RING) for i in range(RING)])  10.8 us
  transfers between devices with their start and end apart: 17, of which 7 were waited for; matrix products, arithmetic and copies ran while one was open for 3% of the time, Pallas kernels for 14%

profile of v4, /device:TPU:66, one launch (start us, length us, event | category | flops | bytes accessed | tf_op | source)
XLA Modules:
  0.0 309.3 jit_solution(11726352327294113393)
XLA Ops:
  0.6 1.7 broadcast_select_fusion
  2.4 1.0 copy.17
  3.4 8.7 %all-to-all-start = ((bf16[32,128,128]{2,1,0:T(8,128)(2,1)}), bf16[32,128,128]{2,1,0:T(8,128)(2,1)S(1)}, u32[]{:S(2)}, u32[]{:S(2)}) async-start(bf16[32,128,128]{2,1,0:T(8,128)(2,1)} %bitcast.4), calls=%async_computation | async-start | bytes 2097152 | tf_op jit(solution)/shard_map/all_to_all | solution.py:209
  12.2 8.5 %collective-permute-start = (bf16[64,8,128]{2,1,0:T(8,128)(2,1)S(1)}, bf16[64,8,128]{2,1,0:T(8,128)(2,1)S(1)}, u32[]{:S(2)}, u32[]{:S(2)}) collective-permute-start(bf16[64,8,128]{2,1,0:T(8,128)(2,1)S(1)} %bitcast.73), channel_id=1, source_target_pairs={{0,32},{32,0},{1,33},{33,1},{2,34},{34,2},{3,35},{35,3},{4,36},{36... | collective-permute-start | bytes 393224 | tf_op jit(solution)/shard_map/ppermute | solution.py:176
  20.7 8.2 %collective-permute-start.1 = (bf16[64,8,128]{2,1,0:T(8,128)(2,1)S(1)}, bf16[64,8,128]{2,1,0:T(8,128)(2,1)S(1)}, u32[]{:S(2)}, u32[]{:S(2)}) collective-permute-start(bf16[64,8,128]{2,1,0:T(8,128)(2,1)S(1)} %bitcast.74), channel_id=1, source_target_pairs={{0,64},{64,0},{1,65},{65,1},{2,66},{66,2},{3,67},{67,3},{4,68},{68... | collective-permute-start | bytes 393224 | tf_op jit(solution)/shard_map/ppermute | solution.py:176
  28.9 1.9 collective-permute-start.2
  30.9 1.1 copy.18
  31.9 32.9 %collective-permute-done = bf16[64,8,128]{2,1,0:T(8,128)(2,1)S(1)} collective-permute-done((bf16[64,8,128]{2,1,0:T(8,128)(2,1)S(1)}, bf16[64,8,128]{2,1,0:T(8,128)(2,1)S(1)}, u32[]{:S(2)}, u32[]{:S(2)}) %collective-permute-start) | collective-permute-done | bytes 131104 | tf_op jit(solution)/shard_map/ppermute | solution.py:176
  64.8 6.8 %all-to-all-start.1 = ((bf16[32,128,128]{2,1,0:T(8,128)(2,1)}), bf16[32,128,128]{2,1,0:T(8,128)(2,1)}, u32[]{:S(2)}, u32[]{:S(2)}) async-start(bf16[32,128,128]{2,1,0:T(8,128)(2,1)} %bitcast.7), calls=%async_computation.1 | async-start | bytes 2097152 | tf_op jit(solution)/shard_map/all_to_all | solution.py:209
  71.7 0.0 copy-start.9
  71.8 0.1 broadcast_select_fusion.7
  72.0 3.5 %collective-permute-start.3 = (bf16[128,16,128]{2,1,0:T(8,128)(2,1)S(1)}, bf16[128,16,128]{2,1,0:T(8,128)(2,1)}, u32[]{:S(2)}, u32[]{:S(2)}) collective-permute-start(bf16[128,16,128]{2,1,0:T(8,128)(2,1)S(1)} %pad_maximum_fusion.1), channel_id=1, source_target_pairs={{0,128},{128,256},{256,384},{384,0},{1,129},{129,257},{257,385},{3... | collective-permute-start | bytes 1572872 | tf_op jit(solution)/shard_map/ppermute | solution.py:203
  75.5 4.8 %collective-permute-start.4 = (bf16[128,16,128]{2,1,0:T(8,128)(2,1)S(1)}, bf16[128,16,128]{2,1,0:T(8,128)(2,1)}, u32[]{:S(2)}, u32[]{:S(2)}) collective-permute-start(bf16[128,16,128]{2,1,0:T(8,128)(2,1)S(1)} %pad_maximum_fusion.1), channel_id=1, source_target_pairs={{0,256},{128,384},{256,0},{384,128},{1,257},{129,385},{257,1},{385... | collective-permute-start | bytes 1572872 | tf_op jit(solution)/shard_map/ppermute | solution.py:203
  80.3 3.3 %collective-permute-start.5 = (bf16[128,16,128]{2,1,0:T(8,128)(2,1)S(1)}, bf16[128,16,128]{2,1,0:T(8,128)(2,1)}, u32[]{:S(2)}, u32[]{:S(2)}) collective-permute-start(bf16[128,16,128]{2,1,0:T(8,128)(2,1)S(1)} %pad_maximum_fusion.1), channel_id=1, source_target_pairs={{0,384},{128,0},{256,128},{384,256},{1,385},{129,1},{257,129},{385... | collective-permute-start | bytes 1572872 | tf_op jit(solution)/shard_map/ppermute | solution.py:203
  83.6 0.7 copy.35
  84.3 1.0 dynamic-slice_bitcast_fusion.1
  85.3 6.3 %collective-permute-start.6 = (bf16[64,32,128]{2,1,0:T(8,128)(2,1)}, bf16[64,32,128]{2,1,0:T(8,128)(2,1)}, u32[]{:S(2)}, u32[]{:S(2)}) collective-permute-start(bf16[64,32,128]{2,1,0:T(8,128)(2,1)} %get-tuple-element.45), channel_id=1, source_target_pairs={{0,32},{32,0},{1,33},{33,1},{2,34},{34,2},{3,35},{35,3},{4,36},{36... | collective-permute-start | bytes 1572872 | tf_op jit(solution)/shard_map/ppermute | solution.py:176
  91.8 0.1 pad_add_fusion.place
  91.8 3.4 %collective-permute-start.7 = (bf16[64,32,128]{2,1,0:T(8,128)(2,1)}, bf16[64,32,128]{2,1,0:T(8,128)(2,1)}, u32[]{:S(2)}, u32[]{:S(2)}) collective-permute-start(bf16[64,32,128]{2,1,0:T(8,128)(2,1)} %get-tuple-element.46), channel_id=1, source_target_pairs={{0,32},{32,0},{1,33},{33,1},{2,34},{34,2},{3,35},{35,3},{4,36},{36... | collective-permute-start | bytes 1572872 | tf_op jit(solution)/shard_map/ppermute | solution.py:176
  95.3 7.3 %shard_map.121.h_in = bf16[10240,256]{1,0:T(8,128)(2,1)S(1)} custom-call(s32[2]{0:T(128)S(1)} %pad_add_fusion.place, bf16[128,32,128]{2,1,0:T(8,128)(2,1)S(1)} %bitcast.64, bf16[2,160,32]{2,1,0:T(8,128)(2,1)S(1)} %copy-done.10, bf16[256,256]{1,0:T(8,128)(2,1)S(1)} %copy-done.9, f32[2,80,128]{2,1,0:T(8,128)S(1)} %copy-done.11), custom_call_target="tpu_custom_call" | custom-call | flops 1 | bytes 1 | tf_op jit(solution)/shard_map/pallas_call | solution.py:164
  102.6 2.3 copy-done
  105.0 1.8 pad_maximum_fusion.taps
  106.8 12.3 %all-to-all-done.1 = bf16[32,128,128]{2,1,0:T(8,128)(2,1)} async-done(((bf16[32,128,128]{2,1,0:T(8,128)(2,1)}), bf16[32,128,128]{2,1,0:T(8,128)(2,1)}, u32[]{:S(2)}, u32[]{:S(2)}) %all-to-all-start.1) | async-done | bytes 1048608 | tf_op jit(solution)/shard_map/all_to_all | solution.py:209
  119.1 1.9 copy.33
  121.0 2.5 copy-done.1
  123.5 0.9 copy-done.12
  124.4 6.5 %shard_map.122 = bf16[64,32,128]{2,1,0:T(8,128)(2,1)S(1)} custom-call(s32[2]{0:T(128)S(1)} %pad_add_fusion.place, bf16[128,32,128]{2,1,0:T(8,128)(2,1)S(1)} %bitcast.61, bf16[10240,256]{1,0:T(8,128)(2,1)S(1)} %copy-done.1, bf16[2,160,32]{2,1,0:T(8,128)(2,1)S(1)} %copy-done.10, bf16[2,32,160]{2,1,0:T(8,128)(2,1)S(1)} %copy-done.15, ...), custom_call_target="tpu_custom_call" | custom-call | flops 1 | bytes 1 | tf_op jit(solution)/shard_map/pallas_call | solution.py:164
  130.9 0.0 copy-start.7
  130.9 19.0 %collective-permute-done.6.crossed = bf16[64,32,128]{2,1,0:T(8,128)(2,1)} collective-permute-done((bf16[64,32,128]{2,1,0:T(8,128)(2,1)}, bf16[64,32,128]{2,1,0:T(8,128)(2,1)}, u32[]{:S(2)}, u32[]{:S(2)}) %collective-permute-start.6) | collective-permute-done | bytes 524320 | tf_op jit(solution)/shard_map/ppermute | solution.py:176
  149.9 12.4 %shard_map.123 = (bf16[10240,256]{1,0:T(8,128)(2,1)S(1)}, bf16[128,32,128]{2,1,0:T(8,128)(2,1)S(1)}) custom-call(s32[2]{0:T(128)S(1)} %pad_add_fusion.place, bf16[10240,256]{1,0:T(8,128)(2,1)S(1)} %copy-done.2, bf16[128,64,128]{2,1,0:T(8,128)(2,1)S(1)} %pad_maximum_fusion.taps, bf16[4,160,64]{2,1,0:T(8,128)(2,1)S(1)} %copy-done.16, ...), custom_call_target="tpu_custom_call" | custom-call | flops 1 | bytes 1 | tf_op jit(solution)/shard_map/pallas_call | solution.py:164
  162.3 0.0 copy-done.7
  162.4 2.4 copy-done.4
  164.7 1.4 copy.23
  166.1 28.2 %all-to-all-start.2 = ((bf16[32,128,128]{2,1,0:T(8,128)(2,1)}), bf16[32,128,128]{2,1,0:T(8,128)(2,1)S(1)}, u32[]{:S(2)}, u32[]{:S(2)}) async-start(bf16[32,128,128]{2,1,0:T(8,128)(2,1)} %copy.23), calls=%async_computation.2 | async-start | bytes 2097152 | tf_op jit(solution)/shard_map/all_to_all | solution.py:209
  194.3 2.5 copy-done.3
  196.8 2.5 copy-done.5
  199.3 0.9 copy-done.13
  200.2 10.4 %shard_map.124 = (bf16[64,64,128]{2,1,0:T(8,128)(2,1)S(1)}, bf16[64,32,128]{2,1,0:T(8,128)(2,1)S(1)}) custom-call(s32[2]{0:T(128)S(1)} %pad_add_fusion.place, bf16[128,32,128]{2,1,0:T(8,128)(2,1)S(1)} %bitcast.62, bf16[64,32,128]{2,1,0:T(8,128)(2,1)} %collective-permute-done.6.crossed, bf16[10240,256]{1,0:T(8,128)(2,1)S(1)} %copy-done.3, ...), custom_call_target="tpu_custom_call" | custom-call | flops 1 | bytes 1 | tf_op jit(solution)/shard_map/pallas_call | solution.py:164
  210.6 0.3 dynamic-slice_bitcast_fusion.9
  210.9 0.2 dynamic-slice_bitcast_fusion.8
  211.1 0.1 pad_maximum_fusion.2
  211.1 2.8 collective-permute-start.8
  213.9 0.1 pad_maximum_fusion.3
  214.0 2.9 collective-permute-start.9
  216.9 0.1 pad_maximum_fusion.4
  217.0 3.6 %collective-permute-start.10 = (bf16[2,64,16,128]{3,2,1,0:T(8,128)(2,1)S(1)}, bf16[2,64,16,128]{3,2,1,0:T(8,128)(2,1)S(1)}, u32[]{:S(2)}, u32[]{:S(2)}) collective-permute-start(bf16[2,64,16,128]{3,2,1,0:T(8,128)(2,1)S(1)} %pad_maximum_fusion.4), channel_id=1, source_target_pairs={{0,384},{128,0},{256,128},{384,256},{1,385},{129,1},{257,129},{385... | collective-permute-start | bytes 1572872 | tf_op jit(solution)/shard_map/ppermute | solution.py:203
  220.6 2.5 copy-done.6
  223.1 8.0 %shard_map.125 = bf16[64,32,128]{2,1,0:T(8,128)(2,1)S(1)} custom-call(s32[2]{0:T(128)S(1)} %pad_add_fusion.place, bf16[128,32,128]{2,1,0:T(8,128)(2,1)S(1)} %bitcast.63, bf16[64,32,128]{2,1,0:T(8,128)(2,1)} %collective-permute-done.7.crossed, bf16[10240,256]{1,0:T(8,128)(2,1)S(1)} %copy-done.6, bf16[2,160,32]{2,1,0:T(8,128)(2,1)S(1)} %copy-done.10, ...), custom_call_target="tpu_custom_call" | custom-call | flops 30000001024 | bytes 1 | tf_op jit(solution)/shard_map/pallas_call | solution.py:164
  231.1 0.1 broadcast_select_fusion.5
  231.2 0.1 maximum_bitcast_fusion
  231.3 8.1 %collective-permute-done.8 = bf16[2,64,16,128]{3,2,1,0:T(8,128)(2,1)S(1)} collective-permute-done((bf16[2,64,16,128]{3,2,1,0:T(8,128)(2,1)S(1)}, bf16[2,64,16,128]{3,2,1,0:T(8,128)(2,1)S(1)}, u32[]{:S(2)}, u32[]{:S(2)}) %collective-permute-start.8) | collective-permute-done | bytes 524320 | tf_op jit(solution)/shard_map/ppermute | solution.py:203
  239.5 2.6 collective-permute-done.10
  242.0 0.3 convert_add_fusion
  242.3 1.4 copy.24
  243.7 7.7 %all-to-all-start.3 = ((bf16[32,128,128]{2,1,0:T(8,128)(2,1)}), bf16[32,128,128]{2,1,0:T(8,128)(2,1)S(1)}, u32[]{:S(2)}, u32[]{:S(2)}) async-start(bf16[32,128,128]{2,1,0:T(8,128)(2,1)} %copy.24), calls=%async_computation.3 | async-start | bytes 2097152 | tf_op jit(solution)/shard_map/all_to_all | solution.py:209
  251.5 0.1 slice_select_fusion
  251.6 8.1 %collective-permute-start.11 = (bf16[2,64,8,128]{3,2,1,0:T(8,128)(2,1)S(1)}, bf16[2,64,8,128]{3,2,1,0:T(8,128)(2,1)S(1)}, u32[]{:S(2)}, u32[]{:S(2)}) collective-permute-start(bf16[2,64,8,128]{3,2,1,0:T(8,128)(2,1)S(1)} %pad_maximum_fusion.7), channel_id=1, source_target_pairs={{0,32},{32,0},{1,33},{33,1},{2,34},{34,2},{3,35},{35,3},{4,36},{36... | collective-permute-start | bytes 786440 | tf_op jit(solution)/shard_map/ppermute | solution.py:176
  259.7 35.6 %collective-permute-done.11 = bf16[2,64,8,128]{3,2,1,0:T(8,128)(2,1)S(1)} collective-permute-done((bf16[2,64,8,128]{3,2,1,0:T(8,128)(2,1)S(1)}, bf16[2,64,8,128]{3,2,1,0:T(8,128)(2,1)S(1)}, u32[]{:S(2)}, u32[]{:S(2)}) %collective-permute-start.11) | collective-permute-done | bytes 262176 | tf_op jit(solution)/shard_map/ppermute | solution.py:176
  295.4 1.9 collective-permute-start.12
  297.3 8.9 %collective-permute-done.12 = bf16[64,8,128]{2,1,0:T(8,128)(2,1)S(1)} collective-permute-done((bf16[64,8,128]{2,1,0:T(8,128)(2,1)S(1)}, bf16[64,8,128]{2,1,0:T(8,128)(2,1)S(1)}, u32[]{:S(2)}, u32[]{:S(2)}) %collective-permute-start.12) | collective-permute-done | bytes 131104 | tf_op jit(solution)/shard_map/ppermute | solution.py:180
  306.3 0.8 copy.34
  307.0 0.1 broadcast_select_fusion.2
  307.2 1.0 copy.25
  308.2 1.0 copy.26
  (50 shorter events, 0.4 us)
Async XLA Ops:
  0.6 11.5 %copy-start.20 = (bf16[64,1024]{1,0:T(8,128)(2,1)S(1)}, bf16[64,1024]{1,0:T(8,128)(2,1)}, u32[]{:S(2)}) copy-start(bf16[64,1024]{1,0:T(8,128)(2,1)} %param.12) | copy-start | bytes 393220
  3.4 61.4 %all-to-all-start = ((bf16[32,128,128]{2,1,0:T(8,128)(2,1)}), bf16[32,128,128]{2,1,0:T(8,128)(2,1)S(1)}, u32[]{:S(2)}, u32[]{:S(2)}) async-start(bf16[32,128,128]{2,1,0:T(8,128)(2,1)} %bitcast.4), calls=%async_computation | async-start | bytes 2097152 | tf_op jit(solution)/shard_map/all_to_all | solution.py:209
  12.2 52.7 %collective-permute-start = (bf16[64,8,128]{2,1,0:T(8,128)(2,1)S(1)}, bf16[64,8,128]{2,1,0:T(8,128)(2,1)S(1)}, u32[]{:S(2)}, u32[]{:S(2)}) collective-permute-start(bf16[64,8,128]{2,1,0:T(8,128)(2,1)S(1)} %bitcast.73), channel_id=1, source_target_pairs={{0,32},{32,0},{1,33},{33,1},{2,34},{34,2},{3,35},{35,3},{4,36},{36... | collective-permute-start | bytes 393224 | tf_op jit(solution)/shard_map/ppermute | solution.py:176
  20.7 44.1 %collective-permute-start.1 = (bf16[64,8,128]{2,1,0:T(8,128)(2,1)S(1)}, bf16[64,8,128]{2,1,0:T(8,128)(2,1)S(1)}, u32[]{:S(2)}, u32[]{:S(2)}) collective-permute-start(bf16[64,8,128]{2,1,0:T(8,128)(2,1)S(1)} %bitcast.74), channel_id=1, source_target_pairs={{0,64},{64,0},{1,65},{65,1},{2,66},{66,2},{3,67},{67,3},{4,68},{68... | collective-permute-start | bytes 393224 | tf_op jit(solution)/shard_map/ppermute | solution.py:176
  28.9 35.9 %collective-permute-start.2 = (bf16[64,8,128]{2,1,0:T(8,128)(2,1)S(1)}, bf16[64,8,128]{2,1,0:T(8,128)(2,1)S(1)}, u32[]{:S(2)}, u32[]{:S(2)}) collective-permute-start(bf16[64,8,128]{2,1,0:T(8,128)(2,1)S(1)} %bitcast.75), channel_id=1, source_target_pairs={{0,96},{32,64},{64,32},{96,0},{1,97},{33,65},{65,33},{97,1},{2,98}... | collective-permute-start | bytes 393224 | tf_op jit(solution)/shard_map/ppermute | solution.py:180
  64.8 54.2 %all-to-all-start.1 = ((bf16[32,128,128]{2,1,0:T(8,128)(2,1)}), bf16[32,128,128]{2,1,0:T(8,128)(2,1)}, u32[]{:S(2)}, u32[]{:S(2)}) async-start(bf16[32,128,128]{2,1,0:T(8,128)(2,1)} %bitcast.7), calls=%async_computation.1 | async-start | bytes 2097152 | tf_op jit(solution)/shard_map/all_to_all | solution.py:209
  71.7 23.5 %copy-start.9 = (bf16[256,256]{1,0:T(8,128)(2,1)S(1)}, bf16[256,256]{1,0:T(8,128)(2,1)}, u32[]{:S(2)}) copy-start(bf16[256,256]{1,0:T(8,128)(2,1)} %constant.81.clone.fast_fwd) | copy-start | bytes 393220
  71.7 23.5 %copy-start.10 = (bf16[2,160,32]{2,1,0:T(8,128)(2,1)S(1)}, bf16[2,160,32]{2,1,0:T(8,128)(2,1)}, u32[]{:S(2)}) copy-start(bf16[2,160,32]{2,1,0:T(8,128)(2,1)} %constant.77.clone.near.far) | copy-start | bytes 61444
  71.7 23.5 %copy-start.11 = (f32[2,80,128]{2,1,0:T(8,128)S(1)}, f32[2,80,128]{2,1,0:T(8,128)}, u32[]{:S(2)}) copy-start(f32[2,80,128]{2,1,0:T(8,128)} %constant.83.clone.twid) | copy-start | bytes 245764
  71.9 33.0 %copy-start.18 = (bf16[64,16,128]{2,1,0:T(8,128)(2,1)}, bf16[64,16,128]{2,1,0:T(8,128)(2,1)S(1)}, u32[]{:S(2)}) copy-start(bf16[64,16,128]{2,1,0:T(8,128)(2,1)S(1)} %get-tuple-element.53) | copy-start | bytes 786436
  71.9 33.0 %copy-start.19 = (bf16[64,16,128]{2,1,0:T(8,128)(2,1)}, bf16[64,16,128]{2,1,0:T(8,128)(2,1)S(1)}, u32[]{:S(2)}) copy-start(bf16[64,16,128]{2,1,0:T(8,128)(2,1)S(1)} %get-tuple-element.54) | copy-start | bytes 786436
  72.0 32.9 %collective-permute-start.3 = (bf16[128,16,128]{2,1,0:T(8,128)(2,1)S(1)}, bf16[128,16,128]{2,1,0:T(8,128)(2,1)}, u32[]{:S(2)}, u32[]{:S(2)}) collective-permute-start(bf16[128,16,128]{2,1,0:T(8,128)(2,1)S(1)} %pad_maximum_fusion.1), channel_id=1, source_target_pairs={{0,128},{128,256},{256,384},{384,0},{1,129},{129,257},{257,385},{3... | collective-permute-start | bytes 1572872 | tf_op jit(solution)/shard_map/ppermute | solution.py:203
  75.5 29.4 %collective-permute-start.4 = (bf16[128,16,128]{2,1,0:T(8,128)(2,1)S(1)}, bf16[128,16,128]{2,1,0:T(8,128)(2,1)}, u32[]{:S(2)}, u32[]{:S(2)}) collective-permute-start(bf16[128,16,128]{2,1,0:T(8,128)(2,1)S(1)} %pad_maximum_fusion.1), channel_id=1, source_target_pairs={{0,256},{128,384},{256,0},{384,128},{1,257},{129,385},{257,1},{385... | collective-permute-start | bytes 1572872 | tf_op jit(solution)/shard_map/ppermute | solution.py:203
  80.3 24.6 %collective-permute-start.5 = (bf16[128,16,128]{2,1,0:T(8,128)(2,1)S(1)}, bf16[128,16,128]{2,1,0:T(8,128)(2,1)}, u32[]{:S(2)}, u32[]{:S(2)}) collective-permute-start(bf16[128,16,128]{2,1,0:T(8,128)(2,1)S(1)} %pad_maximum_fusion.1), channel_id=1, source_target_pairs={{0,384},{128,0},{256,128},{384,256},{1,385},{129,1},{257,129},{385... | collective-permute-start | bytes 1572872 | tf_op jit(solution)/shard_map/ppermute | solution.py:203
  85.3 64.6 %collective-permute-start.6 = (bf16[64,32,128]{2,1,0:T(8,128)(2,1)}, bf16[64,32,128]{2,1,0:T(8,128)(2,1)}, u32[]{:S(2)}, u32[]{:S(2)}) collective-permute-start(bf16[64,32,128]{2,1,0:T(8,128)(2,1)} %get-tuple-element.45), channel_id=1, source_target_pairs={{0,32},{32,0},{1,33},{33,1},{2,34},{34,2},{3,35},{35,3},{4,36},{36... | collective-permute-start | bytes 1572872 | tf_op jit(solution)/shard_map/ppermute | solution.py:176
  91.8 128.7 %collective-permute-start.7 = (bf16[64,32,128]{2,1,0:T(8,128)(2,1)}, bf16[64,32,128]{2,1,0:T(8,128)(2,1)}, u32[]{:S(2)}, u32[]{:S(2)}) collective-permute-start(bf16[64,32,128]{2,1,0:T(8,128)(2,1)} %get-tuple-element.46), channel_id=1, source_target_pairs={{0,32},{32,0},{1,33},{33,1},{2,34},{34,2},{3,35},{35,3},{4,36},{36... | collective-permute-start | bytes 1572872 | tf_op jit(solution)/shard_map/ppermute | solution.py:176
  102.6 2.3 copy-start
  104.9 16.1 %copy-start.15 = (bf16[2,32,160]{2,1,0:T(8,128)(2,1)S(1)}, bf16[2,32,160]{2,1,0:T(8,128)(2,1)}, u32[]{:S(2)}) copy-start(bf16[2,32,160]{2,1,0:T(8,128)(2,1)} %constant.79.clone.slow_out) | copy-start | bytes 61444
  119.1 30.8 %copy-start.16 = (bf16[4,160,64]{2,1,0:T(8,128)(2,1)S(1)}, bf16[4,160,64]{2,1,0:T(8,128)(2,1)}, u32[]{:S(2)}) copy-start(bf16[4,160,64]{2,1,0:T(8,128)(2,1)} %constant.78.clone.taps_table) | copy-start | bytes 245764
  121.0 2.5 copy-start.1
  123.5 0.9 copy-start.12
  124.4 25.5 %copy-start.2 = (bf16[10240,256]{1,0:T(8,128)(2,1)S(1)}, bf16[10240,256]{1,0:T(8,128)(2,1)}, u32[]{:S(2)}) copy-start(bf16[10240,256]{1,0:T(8,128)(2,1)} %copy-done) | copy-start | bytes 15728644
  130.9 31.4 %copy-start.7 = (bf16[64,32,128]{2,1,0:T(8,128)(2,1)}, bf16[64,32,128]{2,1,0:T(8,128)(2,1)S(1)}, u32[]{:S(2)}) copy-start(bf16[64,32,128]{2,1,0:T(8,128)(2,1)S(1)} %shard_map.122) | copy-start | bytes 1572868
  130.9 63.4 %copy-start.17 = (bf16[64,160]{1,0:T(8,128)(2,1)S(1)}, bf16[64,160]{1,0:T(8,128)(2,1)}, u32[]{:S(2)}) copy-start(bf16[64,160]{1,0:T(8,128)(2,1)} %constant.80.clone.out_full) | copy-start | bytes 61444
  162.3 2.4 copy-start.4
  166.1 76.2 %all-to-all-start.2 = ((bf16[32,128,128]{2,1,0:T(8,128)(2,1)}), bf16[32,128,128]{2,1,0:T(8,128)(2,1)S(1)}, u32[]{:S(2)}, u32[]{:S(2)}) async-start(bf16[32,128,128]{2,1,0:T(8,128)(2,1)} %copy.23), calls=%async_computation.2 | async-start | bytes 2097152 | tf_op jit(solution)/shard_map/all_to_all | solution.py:209
  194.3 2.5 copy-start.3
  196.8 2.5 copy-start.5
  199.3 0.9 copy-start.13
  200.2 10.7 %copy-start.8 = (bf16[64,32,128]{2,1,0:T(8,128)(2,1)S(1)}, bf16[64,32,128]{2,1,0:T(8,128)(2,1)}, u32[]{:S(2)}) copy-start(bf16[64,32,128]{2,1,0:T(8,128)(2,1)} %copy-done.7) | copy-start | bytes 1572868
  210.6 10.0 %copy-start.14 = (bf16[256,256]{1,0:T(8,128)(2,1)S(1)}, bf16[256,256]{1,0:T(8,128)(2,1)}, u32[]{:S(2)}) copy-start(bf16[256,256]{1,0:T(8,128)(2,1)} %constant.82.clone.fast_inv) | copy-start | bytes 393220
  211.1 28.3 %collective-permute-start.8 = (bf16[2,64,16,128]{3,2,1,0:T(8,128)(2,1)S(1)}, bf16[2,64,16,128]{3,2,1,0:T(8,128)(2,1)S(1)}, u32[]{:S(2)}, u32[]{:S(2)}) collective-permute-start(bf16[2,64,16,128]{3,2,1,0:T(8,128)(2,1)S(1)} %pad_maximum_fusion.2), channel_id=1, source_target_pairs={{0,128},{128,256},{256,384},{384,0},{1,129},{129,257},{257,385},{3... | collective-permute-start | bytes 1572872 | tf_op jit(solution)/shard_map/ppermute | solution.py:203
  214.0 25.5 %collective-permute-start.9 = (bf16[2,64,16,128]{3,2,1,0:T(8,128)(2,1)S(1)}, bf16[2,64,16,128]{3,2,1,0:T(8,128)(2,1)S(1)}, u32[]{:S(2)}, u32[]{:S(2)}) collective-permute-start(bf16[2,64,16,128]{3,2,1,0:T(8,128)(2,1)S(1)} %pad_maximum_fusion.3), channel_id=1, source_target_pairs={{0,256},{128,384},{256,0},{384,128},{1,257},{129,385},{257,1},{385... | collective-permute-start | bytes 1572872 | tf_op jit(solution)/shard_map/ppermute | solution.py:203
  217.0 25.0 %collective-permute-start.10 = (bf16[2,64,16,128]{3,2,1,0:T(8,128)(2,1)S(1)}, bf16[2,64,16,128]{3,2,1,0:T(8,128)(2,1)S(1)}, u32[]{:S(2)}, u32[]{:S(2)}) collective-permute-start(bf16[2,64,16,128]{3,2,1,0:T(8,128)(2,1)S(1)} %pad_maximum_fusion.4), channel_id=1, source_target_pairs={{0,384},{128,0},{256,128},{384,256},{1,385},{129,1},{257,129},{385... | collective-permute-start | bytes 1572872 | tf_op jit(solution)/shard_map/ppermute | solution.py:203
  220.6 2.5 copy-start.6
  243.7 63.3 %all-to-all-start.3 = ((bf16[32,128,128]{2,1,0:T(8,128)(2,1)}), bf16[32,128,128]{2,1,0:T(8,128)(2,1)S(1)}, u32[]{:S(2)}, u32[]{:S(2)}) async-start(bf16[32,128,128]{2,1,0:T(8,128)(2,1)} %copy.24), calls=%async_computation.3 | async-start | bytes 2097152 | tf_op jit(solution)/shard_map/all_to_all | solution.py:209
  251.6 43.7 %collective-permute-start.11 = (bf16[2,64,8,128]{3,2,1,0:T(8,128)(2,1)S(1)}, bf16[2,64,8,128]{3,2,1,0:T(8,128)(2,1)S(1)}, u32[]{:S(2)}, u32[]{:S(2)}) collective-permute-start(bf16[2,64,8,128]{3,2,1,0:T(8,128)(2,1)S(1)} %pad_maximum_fusion.7), channel_id=1, source_target_pairs={{0,32},{32,0},{1,33},{33,1},{2,34},{34,2},{3,35},{35,3},{4,36},{36... | collective-permute-start | bytes 786440 | tf_op jit(solution)/shard_map/ppermute | solution.py:176
  295.4 10.8 %collective-permute-start.12 = (bf16[64,8,128]{2,1,0:T(8,128)(2,1)S(1)}, bf16[64,8,128]{2,1,0:T(8,128)(2,1)S(1)}, u32[]{:S(2)}, u32[]{:S(2)}) collective-permute-start(bf16[64,8,128]{2,1,0:T(8,128)(2,1)S(1)} %fusion.3), channel_id=1, source_target_pairs={{0,96},{32,64},{64,32},{96,0},{1,97},{33,65},{65,33},{97,1},{2,98}... | collective-permute-start | bytes 393224 | tf_op jit(solution)/shard_map/ppermute | solution.py:180

commit v5 on v4

--- a/solution.py
+++ b/solution.py
@@ -19,7 +19,7 @@
 RING = 4
 QUARTER = HALF // RING
 BLOCK = 8
-LONG = 30 * 10**9
+LONG = 45 * 10**9
 
 
 def tables():
@@ -209,14 +209,15 @@
         return lax.all_to_all(item, span, split_axis=0, concat_axis=0, tiled=True)
 
     taps = filter_taps.reshape(own, HALF // 8, FAST)
-    far_here, own_there, far_there = swap(taps, "zb"), swap(taps, "zh"), diagonal(taps)
+    far_here, far_there = swap(taps, "zb"), diagonal(taps)
 
     v_parts, g_parts = spread(values), spread(grads)
     first_raw = move(jnp.where(low, v_parts, g_parts))
     second_in = jnp.where(low, g_parts, v_parts)
-    first_raw, second_in, far_here, own_there, far_there = lax.optimization_barrier(
-        (first_raw, second_in, far_here, own_there, far_there)
-    )
+    first_raw, second_in, far_here, far_there = lax.optimization_barrier(
+        (first_raw, second_in, far_here, far_there)
+    )
+    own_there = swap(far_there, "zb")
 
     first = first_raw.transpose(1, 0, 2)
     n_own = own // BLOCK
@@ -232,7 +233,9 @@
     (h_spec,) = call(first_kernel, place, chans, [(first, "x", at_start), near, fast_fwd, twid], [0])
     quarter = own // 2
     to_own, to_far = pick_half(first, 1 - zb), pick_half(first, zb)
-    cross_own, cross_far = swap(to_own, "zb"), swap(to_far, "zb")
+    cross_own = swap(to_own, "zb")
+    cross_own, to_far = lax.optimization_barrier((cross_own, to_far))
+    cross_far = swap(to_far, "zb")
 
     second = move(second_in).transpose(1, 0, 2)
     near_taps = ordered(left, taps, own_there, axis=1)
@@ -243,7 +246,6 @@
         other_kernel, place, own,
         [(second, "x", at_far), (h_spec, "s", at_far), near, out_start, fast_fwd, fast_inv, twid], [NEAR],
     )
-    taps, cross_own, far_terms = lax.optimization_barrier((taps, cross_own, far_terms))
 
     k_spec, local_out = call(
         local_kernel, place, chans,

time: 311 us -> 309 us (level)
  waiting for transfers between devices: 119 us -> 140 us
  starting transfers between devices: 111 us -> 96.8 us
  local copies, waits for them, and re-layouts: 28.4 us -> 17.8 us
  other arithmetic: 4.78 us -> 9.18 us
    ppermute x5, waiting for transfers between devices: 87.5 us -> 109 us  [swap(): return lax.ppermute(item, axis, [(0, 1), (1, 0)])]
    all_to_all x4, starting transfers between devices: 51.4 us -> 35.5 us  [move(): return lax.all_to_all(item, span, split_axis=0, concat_axis=0, tiled=True)]
    all_to_all x4, waiting for transfers between devices: 12.3 us -> 0.01 us  [move(): return lax.all_to_all(item, span, split_axis=0, concat_axis=0, tiled=True)]
    unnamed x44 -> x26, local copies, waits for them, and re-layouts: 17.3 us -> 5.7 us
    ppermute x6, waiting for transfers between devices: 10.8 us -> 21.7 us  [ring(): lax.ppermute(item, 'y', [(i, (i + step) % RING) for i in range(RING)])]
    ppermute x2, starting transfers between devices: 3.84 us -> 8.32 us  [diagonal(): return lax.ppermute(item, ('zh', 'zb'), [(0, 3), (1, 2), (2, 1), (3, 0)])]
  transfers between devices with their start and end apart: 17 -> 17, of which waited for: 7 -> 9; matrix products, arithmetic and copies ran while one was open for 3% -> 4% of each run, Pallas kernels for 14% -> 14%
where the time goes in v5:
time: 309 us; the launch traced here: 308 us
  waiting for transfers between devices  140 us (45%)
  starting transfers between devices  96.8 us (31%)
  Pallas kernels  42.9 us (14%)
  local copies, waits for them, and re-layouts  17.8 us (6%)
  other arithmetic  9.18 us (3%)
    ppermute x5, waiting for transfers between devices, swap(): return lax.ppermute(item, axis, [(0, 1), (1, 0)])  109 us
    pallas_call x5, Pallas kernels, call(): pl.pallas_call(kernel, grid_spec=pltpu.PrefetchScalarGridSpec(num_scalar_...  42.9 us
    all_to_all x4, starting transfers between devices, move(): return lax.all_to_all(item, span, split_axis=0, concat_axis=0, tiled=True)  35.5 us
    ppermute x5, starting transfers between devices, swap(): return lax.ppermute(item, axis, [(0, 1), (1, 0)])  34.9 us
    ppermute x6, waiting for transfers between devices, ring(): lax.ppermute(item, 'y', [(i, (i + step) % RING) for i in range(RING)])  21.7 us
    ppermute x6, starting transfers between devices, ring(): lax.ppermute(item, 'y', [(i, (i + step) % RING) for i in range(RING)])  18.1 us
    ppermute x2, waiting for transfers between devices, diagonal(): return lax.ppermute(item, ('zh', 'zb'), [(0, 3), (1, 2), (2, 1), (3, 0)])  8.92 us
    ppermute x2, starting transfers between devices, diagonal(): return lax.ppermute(item, ('zh', 'zb'), [(0, 3), (1, 2), (2, 1), (3, 0)])  8.32 us
  transfers between devices with their start and end apart: 17, of which 9 were waited for; matrix products, arithmetic and copies ran while one was open for 4% of the time, Pallas kernels for 14%

profile of v5, /device:TPU:66, one launch (start us, length us, event | category | flops | bytes accessed | tf_op | source)
XLA Modules:
  0.0 307.6 jit_solution(16274196637504257313)
XLA Ops:
  0.6 1.7 broadcast_select_fusion
  2.4 1.0 copy.17
  3.4 8.7 %all-to-all-start = ((bf16[32,128,128]{2,1,0:T(8,128)(2,1)}), bf16[32,128,128]{2,1,0:T(8,128)(2,1)S(1)}, u32[]{:S(2)}, u32[]{:S(2)}) async-start(bf16[32,128,128]{2,1,0:T(8,128)(2,1)} %bitcast.70), calls=%async_computation | async-start | bytes 2097152 | tf_op jit(solution)/shard_map/all_to_all | solution.py:209
  12.2 8.5 %collective-permute-start = (bf16[64,8,128]{2,1,0:T(8,128)(2,1)S(1)}, bf16[64,8,128]{2,1,0:T(8,128)(2,1)S(1)}, u32[]{:S(2)}, u32[]{:S(2)}) collective-permute-start(bf16[64,8,128]{2,1,0:T(8,128)(2,1)S(1)} %bitcast.74), channel_id=1, source_target_pairs={{0,32},{32,0},{1,33},{33,1},{2,34},{34,2},{3,35},{35,3},{4,36},{36... | collective-permute-start | bytes 393224 | tf_op jit(solution)/shard_map/ppermute | solution.py:176
  20.7 6.4 %collective-permute-start.1 = (bf16[64,8,128]{2,1,0:T(8,128)(2,1)S(1)}, bf16[64,8,128]{2,1,0:T(8,128)(2,1)S(1)}, u32[]{:S(2)}, u32[]{:S(2)}) collective-permute-start(bf16[64,8,128]{2,1,0:T(8,128)(2,1)S(1)} %bitcast.75), channel_id=1, source_target_pairs={{0,96},{32,64},{64,32},{96,0},{1,97},{33,65},{65,33},{97,1},{2,98}... | collective-permute-start | bytes 393224 | tf_op jit(solution)/shard_map/ppermute | solution.py:180
  27.1 1.1 copy.18
  28.2 25.4 %collective-permute-done = bf16[64,8,128]{2,1,0:T(8,128)(2,1)S(1)} collective-permute-done((bf16[64,8,128]{2,1,0:T(8,128)(2,1)S(1)}, bf16[64,8,128]{2,1,0:T(8,128)(2,1)S(1)}, u32[]{:S(2)}, u32[]{:S(2)}) %collective-permute-start) | collective-permute-done | bytes 131104 | tf_op jit(solution)/shard_map/ppermute | solution.py:176
  53.6 6.9 %all-to-all-start.1 = ((bf16[32,128,128]{2,1,0:T(8,128)(2,1)}), bf16[32,128,128]{2,1,0:T(8,128)(2,1)}, u32[]{:S(2)}, u32[]{:S(2)}) async-start(bf16[32,128,128]{2,1,0:T(8,128)(2,1)} %bitcast.7), calls=%async_computation.1 | async-start | bytes 2097152 | tf_op jit(solution)/shard_map/all_to_all | solution.py:209
  60.4 0.0 copy-start.4
  60.5 0.0 copy-start.5
  60.5 0.0 copy-start.6
  60.5 0.7 copy.35
  61.2 0.9 dynamic-slice_bitcast_fusion
  62.1 6.3 %collective-permute-start.2 = (bf16[64,32,128]{2,1,0:T(8,128)(2,1)S(1)}, bf16[64,32,128]{2,1,0:T(8,128)(2,1)S(1)}, u32[]{:S(2)}, u32[]{:S(2)}) collective-permute-start(bf16[64,32,128]{2,1,0:T(8,128)(2,1)S(1)} %get-tuple-element.44), channel_id=1, source_target_pairs={{0,32},{32,0},{1,33},{33,1},{2,34},{34,2},{3,35},{35,3},{4,36},{36... | collective-permute-start | bytes 1572872 | tf_op jit(solution)/shard_map/ppermute | solution.py:176
  68.4 3.4 %collective-permute-start.3 = (bf16[64,8,128]{2,1,0:T(8,128)(2,1)S(1)}, bf16[64,8,128]{2,1,0:T(8,128)(2,1)S(1)}, u32[]{:S(2)}, u32[]{:S(2)}) collective-permute-start(bf16[64,8,128]{2,1,0:T(8,128)(2,1)S(1)} %collective-permute-done.1), channel_id=1, source_target_pairs={{0,32},{32,0},{1,33},{33,1},{2,34},{34,2},{3,35},{35,3},{4,36},{36... | collective-permute-start | bytes 393224 | tf_op jit(solution)/shard_map/ppermute | solution.py:176
  71.9 48.2 %collective-permute-done.3 = bf16[64,8,128]{2,1,0:T(8,128)(2,1)S(1)} collective-permute-done((bf16[64,8,128]{2,1,0:T(8,128)(2,1)S(1)}, bf16[64,8,128]{2,1,0:T(8,128)(2,1)S(1)}, u32[]{:S(2)}, u32[]{:S(2)}) %collective-permute-start.3) | collective-permute-done | bytes 131104 | tf_op jit(solution)/shard_map/ppermute | solution.py:176
  120.0 0.1 broadcast_select_fusion.7
  120.2 0.8 pad_maximum_fusion.1
  121.0 4.9 %collective-permute-start.6 = (bf16[128,16,128]{2,1,0:T(8,128)(2,1)}, bf16[128,16,128]{2,1,0:T(8,128)(2,1)}, u32[]{:S(2)}, u32[]{:S(2)}) collective-permute-start(bf16[128,16,128]{2,1,0:T(8,128)(2,1)} %pad_maximum_fusion.1), channel_id=1, source_target_pairs={{0,384},{128,0},{256,128},{384,256},{1,385},{129,1},{257,129},{385... | collective-permute-start | bytes 1572872 | tf_op jit(solution)/shard_map/ppermute | solution.py:203
  126.0 2.5 collective-permute-start.5
  128.5 2.9 collective-permute-start.4
  131.5 0.1 pad_add_fusion.place
  131.6 0.0 copy-start.8
  131.6 0.0 copy-start.9
  131.6 7.3 %shard_map.121.h_in = bf16[10240,256]{1,0:T(8,128)(2,1)S(1)} custom-call(s32[2]{0:T(128)S(1)} %pad_add_fusion.place, bf16[128,32,128]{2,1,0:T(8,128)(2,1)S(1)} %bitcast.64, bf16[2,160,32]{2,1,0:T(8,128)(2,1)S(1)} %copy-done.5, bf16[256,256]{1,0:T(8,128)(2,1)S(1)} %copy-done.4, f32[2,80,128]{2,1,0:T(8,128)S(1)} %copy-done.6), custom_call_target="tpu_custom_call" | custom-call | flops 1 | bytes 1 | tf_op jit(solution)/shard_map/pallas_call | solution.py:164
  138.9 8.3 %collective-permute-start.7 = (bf16[64,32,128]{2,1,0:T(8,128)(2,1)}, bf16[64,32,128]{2,1,0:T(8,128)(2,1)S(1)}, u32[]{:S(2)}, u32[]{:S(2)}) collective-permute-start(bf16[64,32,128]{2,1,0:T(8,128)(2,1)} %get-tuple-element.23), channel_id=1, source_target_pairs={{0,32},{32,0},{1,33},{33,1},{2,34},{34,2},{3,35},{35,3},{4,36},{36... | collective-permute-start | bytes 1572872 | tf_op jit(solution)/shard_map/ppermute | solution.py:176
  147.2 1.3 collective-permute-done.6
  148.6 5.6 %collective-permute-done.4 = bf16[128,16,128]{2,1,0:T(8,128)(2,1)} collective-permute-done((bf16[128,16,128]{2,1,0:T(8,128)(2,1)}, bf16[128,16,128]{2,1,0:T(8,128)(2,1)}, u32[]{:S(2)}, u32[]{:S(2)}) %collective-permute-start.4) | collective-permute-done | bytes 524320 | tf_op jit(solution)/shard_map/ppermute | solution.py:203
  154.2 3.2 %pad_maximum_fusion.taps = bf16[128,64,128]{2,1,0:T(8,128)(2,1)S(1)} fusion(bf16[128,16,128]{2,1,0:T(8,128)(2,1)} %collective-permute-done.6, bf16[128,16,128]{2,1,0:T(8,128)(2,1)} %collective-permute-done.5, bf16[128,16,128]{2,1,0:T(8,128)(2,1)} %collective-permute-done.4, bf16[64,16,128]{2,1,0:T(8,128)(2,1)S(1)} %get-tuple-element.50, ...), kind=kLoop, calls=%fused_computation | loop fusion | flops 10485760 | bytes 4194304 | tf_op jit(solution)/shard_map/concatenate | solution.py:244
  157.5 12.4 %shard_map.122 = (bf16[10240,256]{1,0:T(8,128)(2,1)S(1)}, bf16[128,32,128]{2,1,0:T(8,128)(2,1)S(1)}) custom-call(s32[2]{0:T(128)S(1)} %pad_add_fusion.place, bf16[10240,256]{1,0:T(8,128)(2,1)S(1)} %shard_map.121.h_in, bf16[128,64,128]{2,1,0:T(8,128)(2,1)S(1)} %pad_maximum_fusion.taps, bf16[4,160,64]{2,1,0:T(8,128)(2,1)S(1)} %copy-done.9, ...), custom_call_target="tpu_custom_call" | custom-call | flops 1 | bytes 1 | tf_op jit(solution)/shard_map/pallas_call | solution.py:164
  169.9 0.0 copy-done
  169.9 2.4 copy-done.2
  172.3 1.4 copy.23
  173.6 12.2 %all-to-all-start.2 = ((bf16[32,128,128]{2,1,0:T(8,128)(2,1)}), bf16[32,128,128]{2,1,0:T(8,128)(2,1)S(1)}, u32[]{:S(2)}, u32[]{:S(2)}) async-start(bf16[32,128,128]{2,1,0:T(8,128)(2,1)} %copy.23), calls=%async_computation.2 | async-start | bytes 2097152 | tf_op jit(solution)/shard_map/all_to_all | solution.py:209
  185.9 1.9 copy.33
  187.8 2.5 copy-done.1
  190.3 6.5 %shard_map.125 = bf16[64,32,128]{2,1,0:T(8,128)(2,1)S(1)} custom-call(s32[2]{0:T(128)S(1)} %pad_add_fusion.place, bf16[128,32,128]{2,1,0:T(8,128)(2,1)S(1)} %bitcast.61, bf16[10240,256]{1,0:T(8,128)(2,1)S(1)} %copy-done.1, bf16[2,160,32]{2,1,0:T(8,128)(2,1)S(1)} %copy-done.5, bf16[2,32,160]{2,1,0:T(8,128)(2,1)S(1)} %copy-done.8, ...), custom_call_target="tpu_custom_call" | custom-call | flops 1 | bytes 1 | tf_op jit(solution)/shard_map/pallas_call | solution.py:164
  196.7 0.0 copy-done.10
  196.7 9.6 %shard_map.123 = (bf16[64,64,128]{2,1,0:T(8,128)(2,1)S(1)}, bf16[64,32,128]{2,1,0:T(8,128)(2,1)S(1)}) custom-call(s32[2]{0:T(128)S(1)} %pad_add_fusion.place, bf16[128,32,128]{2,1,0:T(8,128)(2,1)S(1)} %bitcast.62, bf16[64,32,128]{2,1,0:T(8,128)(2,1)S(1)} %collective-permute-done.2.crossed, bf16[10240,256]{1,0:T(8,128)(2,1)S(1)} %copy-done.1, ...), custom_call_target="tpu_custom_call" | custom-call | flops 1 | bytes 1 | tf_op jit(solution)/shard_map/pallas_call | solution.py:164
  206.3 0.4 dynamic-slice_bitcast_fusion.8
  206.8 0.1 pad_maximum_fusion.4
  206.8 2.6 collective-permute-start.10
  209.4 0.1 pad_maximum_fusion.3
  209.5 2.5 collective-permute-start.9
  212.0 0.1 pad_maximum_fusion.2
  212.1 2.7 collective-permute-start.8
  214.8 7.1 %shard_map.124 = bf16[64,32,128]{2,1,0:T(8,128)(2,1)S(1)} custom-call(s32[2]{0:T(128)S(1)} %pad_add_fusion.place, bf16[128,32,128]{2,1,0:T(8,128)(2,1)S(1)} %bitcast.63, bf16[64,32,128]{2,1,0:T(8,128)(2,1)S(1)} %collective-permute-done.7.crossed, bf16[10240,256]{1,0:T(8,128)(2,1)S(1)} %copy-done.3, bf16[2,160,32]{2,1,0:T(8,128)(2,1)S(1)} %copy-done.5, ...), custom_call_target="tpu_custom_call" | custom-call | flops 44999999488 | bytes 1 | tf_op jit(solution)/shard_map/pallas_call | solution.py:164
  221.9 0.1 broadcast_select_fusion.5
  222.0 1.1 maximum_bitcast_fusion
  223.1 0.4 collective-permute-done.10
  223.5 4.2 %collective-permute-done.9 = bf16[2,64,16,128]{3,2,1,0:T(8,128)(2,1)S(1)} collective-permute-done((bf16[2,64,16,128]{3,2,1,0:T(8,128)(2,1)S(1)}, bf16[2,64,16,128]{3,2,1,0:T(8,128)(2,1)S(1)}, u32[]{:S(2)}, u32[]{:S(2)}) %collective-permute-start.9) | collective-permute-done | bytes 524320 | tf_op jit(solution)/shard_map/ppermute | solution.py:203
  227.7 10.1 %collective-permute-done.8 = bf16[2,64,16,128]{3,2,1,0:T(8,128)(2,1)S(1)} collective-permute-done((bf16[2,64,16,128]{3,2,1,0:T(8,128)(2,1)S(1)}, bf16[2,64,16,128]{3,2,1,0:T(8,128)(2,1)S(1)}, u32[]{:S(2)}, u32[]{:S(2)}) %collective-permute-start.8) | collective-permute-done | bytes 524320 | tf_op jit(solution)/shard_map/ppermute | solution.py:203
  237.8 0.2 convert_add_fusion
  238.1 2.6 copy.24
  240.7 7.8 %all-to-all-start.3 = ((bf16[32,128,128]{2,1,0:T(8,128)(2,1)}), bf16[32,128,128]{2,1,0:T(8,128)(2,1)}, u32[]{:S(2)}, u32[]{:S(2)}) async-start(bf16[32,128,128]{2,1,0:T(8,128)(2,1)} %copy.24), calls=%async_computation.3 | async-start | bytes 2097152 | tf_op jit(solution)/shard_map/all_to_all | solution.py:209
  248.5 0.1 slice_select_fusion
  248.7 8.3 %collective-permute-start.11 = (bf16[2,64,8,128]{3,2,1,0:T(8,128)(2,1)S(1)}, bf16[2,64,8,128]{3,2,1,0:T(8,128)(2,1)S(1)}, u32[]{:S(2)}, u32[]{:S(2)}) collective-permute-start(bf16[2,64,8,128]{3,2,1,0:T(8,128)(2,1)S(1)} %pad_maximum_fusion.7), channel_id=1, source_target_pairs={{0,32},{32,0},{1,33},{33,1},{2,34},{34,2},{3,35},{35,3},{4,36},{36... | collective-permute-start | bytes 786440 | tf_op jit(solution)/shard_map/ppermute | solution.py:176
  256.9 35.5 %collective-permute-done.11 = bf16[2,64,8,128]{3,2,1,0:T(8,128)(2,1)S(1)} collective-permute-done((bf16[2,64,8,128]{3,2,1,0:T(8,128)(2,1)S(1)}, bf16[2,64,8,128]{3,2,1,0:T(8,128)(2,1)S(1)}, u32[]{:S(2)}, u32[]{:S(2)}) %collective-permute-start.11) | collective-permute-done | bytes 262176 | tf_op jit(solution)/shard_map/ppermute | solution.py:176
  292.5 1.9 collective-permute-start.12
  294.5 8.9 %collective-permute-done.12 = bf16[64,8,128]{2,1,0:T(8,128)(2,1)S(1)} collective-permute-done((bf16[64,8,128]{2,1,0:T(8,128)(2,1)S(1)}, bf16[64,8,128]{2,1,0:T(8,128)(2,1)S(1)}, u32[]{:S(2)}, u32[]{:S(2)}) %collective-permute-start.12) | collective-permute-done | bytes 131104 | tf_op jit(solution)/shard_map/ppermute | solution.py:180
  303.4 0.8 copy.34
  304.2 1.4 broadcast_select_fusion.2
  305.6 1.0 copy.25
  306.6 1.0 copy.26
  (32 shorter events, 0.3 us)
Async XLA Ops:
  0.6 11.5 %copy-start.11 = (bf16[64,1024]{1,0:T(8,128)(2,1)S(1)}, bf16[64,1024]{1,0:T(8,128)(2,1)}, u32[]{:S(2)}) copy-start(bf16[64,1024]{1,0:T(8,128)(2,1)} %param.12) | copy-start | bytes 393220
  3.4 50.2 %all-to-all-start = ((bf16[32,128,128]{2,1,0:T(8,128)(2,1)}), bf16[32,128,128]{2,1,0:T(8,128)(2,1)S(1)}, u32[]{:S(2)}, u32[]{:S(2)}) async-start(bf16[32,128,128]{2,1,0:T(8,128)(2,1)} %bitcast.70), calls=%async_computation | async-start | bytes 2097152 | tf_op jit(solution)/shard_map/all_to_all | solution.py:209
  12.2 41.4 %collective-permute-start = (bf16[64,8,128]{2,1,0:T(8,128)(2,1)S(1)}, bf16[64,8,128]{2,1,0:T(8,128)(2,1)S(1)}, u32[]{:S(2)}, u32[]{:S(2)}) collective-permute-start(bf16[64,8,128]{2,1,0:T(8,128)(2,1)S(1)} %bitcast.74), channel_id=1, source_target_pairs={{0,32},{32,0},{1,33},{33,1},{2,34},{34,2},{3,35},{35,3},{4,36},{36... | collective-permute-start | bytes 393224 | tf_op jit(solution)/shard_map/ppermute | solution.py:176
  20.7 32.8 %collective-permute-start.1 = (bf16[64,8,128]{2,1,0:T(8,128)(2,1)S(1)}, bf16[64,8,128]{2,1,0:T(8,128)(2,1)S(1)}, u32[]{:S(2)}, u32[]{:S(2)}) collective-permute-start(bf16[64,8,128]{2,1,0:T(8,128)(2,1)S(1)} %bitcast.75), channel_id=1, source_target_pairs={{0,96},{32,64},{64,32},{96,0},{1,97},{33,65},{65,33},{97,1},{2,98}... | collective-permute-start | bytes 393224 | tf_op jit(solution)/shard_map/ppermute | solution.py:180
  53.6 120.1 %all-to-all-start.1 = ((bf16[32,128,128]{2,1,0:T(8,128)(2,1)}), bf16[32,128,128]{2,1,0:T(8,128)(2,1)}, u32[]{:S(2)}, u32[]{:S(2)}) async-start(bf16[32,128,128]{2,1,0:T(8,128)(2,1)} %bitcast.7), calls=%async_computation.1 | async-start | bytes 2097152 | tf_op jit(solution)/shard_map/all_to_all | solution.py:209
  60.4 71.1 %copy-start.4 = (bf16[256,256]{1,0:T(8,128)(2,1)S(1)}, bf16[256,256]{1,0:T(8,128)(2,1)}, u32[]{:S(2)}) copy-start(bf16[256,256]{1,0:T(8,128)(2,1)} %constant.81.clone.fast_fwd) | copy-start | bytes 393220
  60.5 71.1 %copy-start.5 = (bf16[2,160,32]{2,1,0:T(8,128)(2,1)S(1)}, bf16[2,160,32]{2,1,0:T(8,128)(2,1)}, u32[]{:S(2)}) copy-start(bf16[2,160,32]{2,1,0:T(8,128)(2,1)} %constant.77.clone.near.far) | copy-start | bytes 61444
  60.5 71.1 %copy-start.6 = (f32[2,80,128]{2,1,0:T(8,128)S(1)}, f32[2,80,128]{2,1,0:T(8,128)}, u32[]{:S(2)}) copy-start(f32[2,80,128]{2,1,0:T(8,128)} %constant.83.clone.twid) | copy-start | bytes 245764
  62.1 76.8 %collective-permute-start.2 = (bf16[64,32,128]{2,1,0:T(8,128)(2,1)S(1)}, bf16[64,32,128]{2,1,0:T(8,128)(2,1)S(1)}, u32[]{:S(2)}, u32[]{:S(2)}) collective-permute-start(bf16[64,32,128]{2,1,0:T(8,128)(2,1)S(1)} %get-tuple-element.44), channel_id=1, source_target_pairs={{0,32},{32,0},{1,33},{33,1},{2,34},{34,2},{3,35},{35,3},{4,36},{36... | collective-permute-start | bytes 1572872 | tf_op jit(solution)/shard_map/ppermute | solution.py:176
  68.4 51.6 %collective-permute-start.3 = (bf16[64,8,128]{2,1,0:T(8,128)(2,1)S(1)}, bf16[64,8,128]{2,1,0:T(8,128)(2,1)S(1)}, u32[]{:S(2)}, u32[]{:S(2)}) collective-permute-start(bf16[64,8,128]{2,1,0:T(8,128)(2,1)S(1)} %collective-permute-done.1), channel_id=1, source_target_pairs={{0,32},{32,0},{1,33},{33,1},{2,34},{34,2},{3,35},{35,3},{4,36},{36... | collective-permute-start | bytes 393224 | tf_op jit(solution)/shard_map/ppermute | solution.py:176
  121.0 27.5 %collective-permute-start.6 = (bf16[128,16,128]{2,1,0:T(8,128)(2,1)}, bf16[128,16,128]{2,1,0:T(8,128)(2,1)}, u32[]{:S(2)}, u32[]{:S(2)}) collective-permute-start(bf16[128,16,128]{2,1,0:T(8,128)(2,1)} %pad_maximum_fusion.1), channel_id=1, source_target_pairs={{0,384},{128,0},{256,128},{384,256},{1,385},{129,1},{257,129},{385... | collective-permute-start | bytes 1572872 | tf_op jit(solution)/shard_map/ppermute | solution.py:203
  126.0 22.6 %collective-permute-start.5 = (bf16[128,16,128]{2,1,0:T(8,128)(2,1)}, bf16[128,16,128]{2,1,0:T(8,128)(2,1)}, u32[]{:S(2)}, u32[]{:S(2)}) collective-permute-start(bf16[128,16,128]{2,1,0:T(8,128)(2,1)} %pad_maximum_fusion.1), channel_id=1, source_target_pairs={{0,256},{128,384},{256,0},{384,128},{1,257},{129,385},{257,1},{385... | collective-permute-start | bytes 1572872 | tf_op jit(solution)/shard_map/ppermute | solution.py:203
  128.5 25.7 %collective-permute-start.4 = (bf16[128,16,128]{2,1,0:T(8,128)(2,1)}, bf16[128,16,128]{2,1,0:T(8,128)(2,1)}, u32[]{:S(2)}, u32[]{:S(2)}) collective-permute-start(bf16[128,16,128]{2,1,0:T(8,128)(2,1)} %pad_maximum_fusion.1), channel_id=1, source_target_pairs={{0,128},{128,256},{256,384},{384,0},{1,129},{129,257},{257,385},{3... | collective-permute-start | bytes 1572872 | tf_op jit(solution)/shard_map/ppermute | solution.py:203
  131.6 25.9 %copy-start.7 = (bf16[256,256]{1,0:T(8,128)(2,1)S(1)}, bf16[256,256]{1,0:T(8,128)(2,1)}, u32[]{:S(2)}) copy-start(bf16[256,256]{1,0:T(8,128)(2,1)} %constant.82.clone.fast_inv) | copy-start | bytes 393220
  131.6 25.9 %copy-start.8 = (bf16[2,32,160]{2,1,0:T(8,128)(2,1)S(1)}, bf16[2,32,160]{2,1,0:T(8,128)(2,1)}, u32[]{:S(2)}) copy-start(bf16[2,32,160]{2,1,0:T(8,128)(2,1)} %constant.79.clone.slow_out) | copy-start | bytes 61444
  131.6 25.9 %copy-start.9 = (bf16[4,160,64]{2,1,0:T(8,128)(2,1)S(1)}, bf16[4,160,64]{2,1,0:T(8,128)(2,1)}, u32[]{:S(2)}) copy-start(bf16[4,160,64]{2,1,0:T(8,128)(2,1)} %constant.78.clone.taps_table) | copy-start | bytes 245764
  138.9 31.0 %copy-start = (bf16[10240,256]{1,0:T(8,128)(2,1)}, bf16[10240,256]{1,0:T(8,128)(2,1)S(1)}, u32[]{:S(2)}) copy-start(bf16[10240,256]{1,0:T(8,128)(2,1)S(1)} %shard_map.121.h_in) | copy-start | bytes 15728644
  138.9 75.8 %collective-permute-start.7 = (bf16[64,32,128]{2,1,0:T(8,128)(2,1)}, bf16[64,32,128]{2,1,0:T(8,128)(2,1)S(1)}, u32[]{:S(2)}, u32[]{:S(2)}) collective-permute-start(bf16[64,32,128]{2,1,0:T(8,128)(2,1)} %get-tuple-element.23), channel_id=1, source_target_pairs={{0,32},{32,0},{1,33},{33,1},{2,34},{34,2},{3,35},{35,3},{4,36},{36... | collective-permute-start | bytes 1572872 | tf_op jit(solution)/shard_map/ppermute | solution.py:176
  169.9 2.4 copy-start.2
  173.6 64.4 %all-to-all-start.2 = ((bf16[32,128,128]{2,1,0:T(8,128)(2,1)}), bf16[32,128,128]{2,1,0:T(8,128)(2,1)S(1)}, u32[]{:S(2)}, u32[]{:S(2)}) async-start(bf16[32,128,128]{2,1,0:T(8,128)(2,1)} %copy.23), calls=%async_computation.2 | async-start | bytes 2097152 | tf_op jit(solution)/shard_map/all_to_all | solution.py:209
  185.8 10.9 %copy-start.10 = (bf16[64,160]{1,0:T(8,128)(2,1)S(1)}, bf16[64,160]{1,0:T(8,128)(2,1)}, u32[]{:S(2)}) copy-start(bf16[64,160]{1,0:T(8,128)(2,1)} %constant.80.clone.out_full) | copy-start | bytes 61444
  187.8 2.5 copy-start.1
  190.3 6.5 %copy-start.3 = (bf16[10240,256]{1,0:T(8,128)(2,1)S(1)}, bf16[10240,256]{1,0:T(8,128)(2,1)}, u32[]{:S(2)}) copy-start(bf16[10240,256]{1,0:T(8,128)(2,1)} %copy-done.2) | copy-start | bytes 15728644
  206.8 16.7 %collective-permute-start.10 = (bf16[2,64,16,128]{3,2,1,0:T(8,128)(2,1)S(1)}, bf16[2,64,16,128]{3,2,1,0:T(8,128)(2,1)S(1)}, u32[]{:S(2)}, u32[]{:S(2)}) collective-permute-start(bf16[2,64,16,128]{3,2,1,0:T(8,128)(2,1)S(1)} %pad_maximum_fusion.4), channel_id=1, source_target_pairs={{0,384},{128,0},{256,128},{384,256},{1,385},{129,1},{257,129},{385... | collective-permute-start | bytes 1572872 | tf_op jit(solution)/shard_map/ppermute | solution.py:203
  209.5 18.2 %collective-permute-start.9 = (bf16[2,64,16,128]{3,2,1,0:T(8,128)(2,1)S(1)}, bf16[2,64,16,128]{3,2,1,0:T(8,128)(2,1)S(1)}, u32[]{:S(2)}, u32[]{:S(2)}) collective-permute-start(bf16[2,64,16,128]{3,2,1,0:T(8,128)(2,1)S(1)} %pad_maximum_fusion.3), channel_id=1, source_target_pairs={{0,256},{128,384},{256,0},{384,128},{1,257},{129,385},{257,1},{385... | collective-permute-start | bytes 1572872 | tf_op jit(solution)/shard_map/ppermute | solution.py:203
  212.1 25.7 %collective-permute-start.8 = (bf16[2,64,16,128]{3,2,1,0:T(8,128)(2,1)S(1)}, bf16[2,64,16,128]{3,2,1,0:T(8,128)(2,1)S(1)}, u32[]{:S(2)}, u32[]{:S(2)}) collective-permute-start(bf16[2,64,16,128]{3,2,1,0:T(8,128)(2,1)S(1)} %pad_maximum_fusion.2), channel_id=1, source_target_pairs={{0,128},{128,256},{256,384},{384,0},{1,129},{129,257},{257,385},{3... | collective-permute-start | bytes 1572872 | tf_op jit(solution)/shard_map/ppermute | solution.py:203
  240.7 63.5 %all-to-all-start.3 = ((bf16[32,128,128]{2,1,0:T(8,128)(2,1)}), bf16[32,128,128]{2,1,0:T(8,128)(2,1)}, u32[]{:S(2)}, u32[]{:S(2)}) async-start(bf16[32,128,128]{2,1,0:T(8,128)(2,1)} %copy.24), calls=%async_computation.3 | async-start | bytes 2097152 | tf_op jit(solution)/shard_map/all_to_all | solution.py:209
  248.7 43.8 %collective-permute-start.11 = (bf16[2,64,8,128]{3,2,1,0:T(8,128)(2,1)S(1)}, bf16[2,64,8,128]{3,2,1,0:T(8,128)(2,1)S(1)}, u32[]{:S(2)}, u32[]{:S(2)}) collective-permute-start(bf16[2,64,8,128]{3,2,1,0:T(8,128)(2,1)S(1)} %pad_maximum_fusion.7), channel_id=1, source_target_pairs={{0,32},{32,0},{1,33},{33,1},{2,34},{34,2},{3,35},{35,3},{4,36},{36... | collective-permute-start | bytes 786440 | tf_op jit(solution)/shard_map/ppermute | solution.py:176
  292.5 10.8 %collective-permute-start.12 = (bf16[64,8,128]{2,1,0:T(8,128)(2,1)S(1)}, bf16[64,8,128]{2,1,0:T(8,128)(2,1)S(1)}, u32[]{:S(2)}, u32[]{:S(2)}) collective-permute-start(bf16[64,8,128]{2,1,0:T(8,128)(2,1)S(1)} %fusion.3), channel_id=1, source_target_pairs={{0,96},{32,64},{64,32},{96,0},{1,97},{33,65},{65,33},{97,1},{2,98}... | collective-permute-start | bytes 393224 | tf_op jit(solution)/shard_map/ppermute | solution.py:180

commit v6 on v5

--- a/solution.py
+++ b/solution.py
@@ -209,15 +209,14 @@
         return lax.all_to_all(item, span, split_axis=0, concat_axis=0, tiled=True)
 
     taps = filter_taps.reshape(own, HALF // 8, FAST)
-    far_here, far_there = swap(taps, "zb"), diagonal(taps)
+    across = diagonal(taps)
 
     v_parts, g_parts = spread(values), spread(grads)
-    first_raw = move(jnp.where(low, v_parts, g_parts))
-    second_in = jnp.where(low, g_parts, v_parts)
-    first_raw, second_in, far_here, far_there = lax.optimization_barrier(
-        (first_raw, second_in, far_here, far_there)
-    )
-    own_there = swap(far_there, "zb")
+    first_in, second_in = jnp.where(low, v_parts, g_parts), jnp.where(low, g_parts, v_parts)
+    first_in, across = lax.optimization_barrier((first_in, across))
+    first_raw = move(first_in)
+    swapped = swap(jnp.stack([taps, across]), "zb")
+    first_raw, second_in, swapped = lax.optimization_barrier((first_raw, second_in, swapped))
 
     first = first_raw.transpose(1, 0, 2)
     n_own = own // BLOCK
@@ -234,12 +233,10 @@
     quarter = own // 2
     to_own, to_far = pick_half(first, 1 - zb), pick_half(first, zb)
     cross_own = swap(to_own, "zb")
-    cross_own, to_far = lax.optimization_barrier((cross_own, to_far))
-    cross_far = swap(to_far, "zb")
 
     second = move(second_in).transpose(1, 0, 2)
-    near_taps = ordered(left, taps, own_there, axis=1)
-    far_taps = ordered(left, far_here, far_there, axis=1)
+    near_taps = ordered(left, taps, swapped[1], axis=1)
+    far_taps = ordered(left, swapped[0], across, axis=1)
     taps = ordered(low, near_taps, far_taps)
     taps = jnp.concatenate([taps] + [ring(taps, step) for step in range(1, RING)], axis=1)
     (far_terms,) = call(
@@ -252,7 +249,9 @@
         [(h_spec, "s", at_start), (taps, "x", at_start), (consts["slow_taps"], "t", row), out_near,
          fast_fwd, fast_inv, twid], [0, NEAR],
     )
-    local_back = move(local_out.transpose(1, 0, 2))
+    local_in, cross_own, to_far = lax.optimization_barrier((local_out.transpose(1, 0, 2), cross_own, to_far))
+    local_back = move(local_in)
+    cross_far = swap(to_far, "zb")
     own_terms, out_own = call(
         own_kernel, place, own,
         [(second, "x", at_own), (cross_own, "x", at_start), (h_spec, "s", at_own), (k_spec, "s", at_own),

time: 309 us -> 308 us (level)
  the two profiles are of different devices: /device:TPU:66 before, /device:TPU:36 now
where the time goes in v6:
time: 308 us; the launch traced here: 307 us
  starting transfers between devices  137 us (44%)
  waiting for transfers between devices  97.8 us (32%)
  Pallas kernels  42.9 us (14%)
  local copies, waits for them, and re-layouts  18.7 us (6%)
  other arithmetic  9.16 us (3%)
    all_to_all x4, starting transfers between devices, move(): return lax.all_to_all(item, span, split_axis=0, concat_axis=0, tiled=True)  67.5 us
    ppermute x4, waiting for transfers between devices, swap(): return lax.ppermute(item, axis, [(0, 1), (1, 0)])  65.3 us
    pallas_call x5, Pallas kernels, call(): pl.pallas_call(kernel, grid_spec=pltpu.PrefetchScalarGridSpec(num_scalar_...  42.9 us
    ppermute x2, starting transfers between devices, diagonal(): return lax.ppermute(item, ('zh', 'zb'), [(0, 3), (1, 2), (2, 1), (3, 0)])  32.8 us
    ppermute x6, starting transfers between devices, ring(): lax.ppermute(item, 'y', [(i, (i + step) % RING) for i in range(RING)])  23.8 us
    ppermute x6, waiting for transfers between devices, ring(): lax.ppermute(item, 'y', [(i, (i + step) % RING) for i in range(RING)])  21.7 us
    ppermute x4, starting transfers between devices, swap(): return lax.ppermute(item, axis, [(0, 1), (1, 0)])  12.7 us
    ppermute x2, waiting for transfers between devices, diagonal(): return lax.ppermute(item, ('zh', 'zb'), [(0, 3), (1, 2), (2, 1), (3, 0)])  9.37 us
  transfers between devices with their start and end apart: 16, of which 10 were waited for; matrix products, arithmetic and copies ran while one was open for 5% of the time, Pallas kernels for 14%

profile of v6, /device:TPU:36, one launch (start us, length us, event | category | flops | bytes accessed | tf_op | source)
XLA Modules:
  0.0 306.5 jit_solution(17166085617480061793)
XLA Ops:
  0.6 0.9 copy.27
  1.6 11.8 %collective-permute-start = (bf16[64,8,128]{2,1,0:T(8,128)(2,1)S(1)}, bf16[64,8,128]{2,1,0:T(8,128)(2,1)S(1)}, u32[]{:S(2)}, u32[]{:S(2)}) collective-permute-start(bf16[64,8,128]{2,1,0:T(8,128)(2,1)S(1)} %bitcast.80), channel_id=1, source_target_pairs={{0,96},{32,64},{64,32},{96,0},{1,97},{33,65},{65,33},{97,1},{2,98}... | collective-permute-start | bytes 393224 | tf_op jit(solution)/shard_map/ppermute | solution.py:180
  13.4 1.7 broadcast_select_fusion
  15.1 1.0 copy.17
  16.1 5.7 %collective-permute-done = bf16[64,8,128]{2,1,0:T(8,128)(2,1)S(1)} collective-permute-done((bf16[64,8,128]{2,1,0:T(8,128)(2,1)S(1)}, bf16[64,8,128]{2,1,0:T(8,128)(2,1)S(1)}, u32[]{:S(2)}, u32[]{:S(2)}) %collective-permute-start) | collective-permute-done | bytes 131104 | tf_op jit(solution)/shard_map/ppermute | solution.py:180
  21.8 10.3 %all-to-all-start = ((bf16[32,128,128]{2,1,0:T(8,128)(2,1)}), bf16[32,128,128]{2,1,0:T(8,128)(2,1)S(1)}, u32[]{:S(2)}, u32[]{:S(2)}) async-start(bf16[32,128,128]{2,1,0:T(8,128)(2,1)} %bitcast.79), calls=%async_computation | async-start | bytes 2097152 | tf_op jit(solution)/shard_map/all_to_all | solution.py:209
  32.1 4.7 %collective-permute-start.1 = (bf16[2,64,8,128]{3,2,1,0:T(8,128)(2,1)S(1)}, bf16[2,64,8,128]{3,2,1,0:T(8,128)(2,1)S(1)}, u32[]{:S(2)}, u32[]{:S(2)}) collective-permute-start(bf16[2,64,8,128]{3,2,1,0:T(8,128)(2,1)S(1)} %pad_maximum_fusion.5), channel_id=1, source_target_pairs={{0,32},{32,0},{1,33},{33,1},{2,34},{34,2},{3,35},{35,3},{4,36},{36... | collective-permute-start | bytes 786440 | tf_op jit(solution)/shard_map/ppermute | solution.py:176
  36.8 1.1 copy.18
  37.9 28.6 %collective-permute-done.1 = bf16[2,64,8,128]{3,2,1,0:T(8,128)(2,1)S(1)} collective-permute-done((bf16[2,64,8,128]{3,2,1,0:T(8,128)(2,1)S(1)}, bf16[2,64,8,128]{3,2,1,0:T(8,128)(2,1)S(1)}, u32[]{:S(2)}, u32[]{:S(2)}) %collective-permute-start.1) | collective-permute-done | bytes 262176 | tf_op jit(solution)/shard_map/ppermute | solution.py:176
  66.5 1.3 all-to-all-done
  67.8 8.7 %all-to-all-start.1 = ((bf16[32,128,128]{2,1,0:T(8,128)(2,1)}), bf16[32,128,128]{2,1,0:T(8,128)(2,1)}, u32[]{:S(2)}, u32[]{:S(2)}) async-start(bf16[32,128,128]{2,1,0:T(8,128)(2,1)} %bitcast.7), calls=%async_computation.1 | async-start | bytes 2097152 | tf_op jit(solution)/shard_map/all_to_all | solution.py:209
  76.5 0.0 copy-start.4
  76.6 0.0 copy-start.5
  76.6 0.0 copy-start.6
  76.6 0.1 broadcast_select_fusion.7
  76.8 0.8 pad_maximum_fusion.1
  77.6 4.9 %collective-permute-start.4 = (bf16[128,16,128]{2,1,0:T(8,128)(2,1)}, bf16[128,16,128]{2,1,0:T(8,128)(2,1)}, u32[]{:S(2)}, u32[]{:S(2)}) collective-permute-start(bf16[128,16,128]{2,1,0:T(8,128)(2,1)} %pad_maximum_fusion.1), channel_id=1, source_target_pairs={{0,384},{128,0},{256,128},{384,256},{1,385},{129,1},{257,129},{385... | collective-permute-start | bytes 1572872 | tf_op jit(solution)/shard_map/ppermute | solution.py:203
  82.5 2.5 collective-permute-start.3
  85.1 2.9 collective-permute-start.2
  88.0 0.7 copy.36
  88.7 0.9 dynamic-slice_bitcast_fusion
  89.5 4.1 %collective-permute-start.5 = (bf16[64,32,128]{2,1,0:T(8,128)(2,1)S(1)}, bf16[64,32,128]{2,1,0:T(8,128)(2,1)S(1)}, u32[]{:S(2)}, u32[]{:S(2)}) collective-permute-start(bf16[64,32,128]{2,1,0:T(8,128)(2,1)S(1)} %get-tuple-element.46), channel_id=1, source_target_pairs={{0,32},{32,0},{1,33},{33,1},{2,34},{34,2},{3,35},{35,3},{4,36},{36... | collective-permute-start | bytes 1572872 | tf_op jit(solution)/shard_map/ppermute | solution.py:176
  93.8 0.1 pad_add_fusion.place
  93.9 0.0 copy-start.8
  93.9 7.3 %shard_map.121.h_in = bf16[10240,256]{1,0:T(8,128)(2,1)S(1)} custom-call(s32[2]{0:T(128)S(1)} %pad_add_fusion.place, bf16[128,32,128]{2,1,0:T(8,128)(2,1)S(1)} %bitcast.73, bf16[2,160,32]{2,1,0:T(8,128)(2,1)S(1)} %copy-done.5, bf16[256,256]{1,0:T(8,128)(2,1)S(1)} %copy-done.4, f32[2,80,128]{2,1,0:T(8,128)S(1)} %copy-done.6), custom_call_target="tpu_custom_call" | custom-call | flops 1 | bytes 1 | tf_op jit(solution)/shard_map/pallas_call | solution.py:164
  101.2 4.4 %collective-permute-done.4 = bf16[128,16,128]{2,1,0:T(8,128)(2,1)} collective-permute-done((bf16[128,16,128]{2,1,0:T(8,128)(2,1)}, bf16[128,16,128]{2,1,0:T(8,128)(2,1)}, u32[]{:S(2)}, u32[]{:S(2)}) %collective-permute-start.4) | collective-permute-done | bytes 524320 | tf_op jit(solution)/shard_map/ppermute | solution.py:203
  105.6 5.6 %collective-permute-done.2 = bf16[128,16,128]{2,1,0:T(8,128)(2,1)} collective-permute-done((bf16[128,16,128]{2,1,0:T(8,128)(2,1)}, bf16[128,16,128]{2,1,0:T(8,128)(2,1)}, u32[]{:S(2)}, u32[]{:S(2)}) %collective-permute-start.2) | collective-permute-done | bytes 524320 | tf_op jit(solution)/shard_map/ppermute | solution.py:203
  111.2 3.2 %pad_maximum_fusion.taps = bf16[128,64,128]{2,1,0:T(8,128)(2,1)S(1)} fusion(bf16[128,16,128]{2,1,0:T(8,128)(2,1)} %collective-permute-done.4, bf16[128,16,128]{2,1,0:T(8,128)(2,1)} %collective-permute-done.3, bf16[128,16,128]{2,1,0:T(8,128)(2,1)} %collective-permute-done.2, bf16[64,16,128]{2,1,0:T(8,128)(2,1)S(1)} %get-tuple-element.54, ...), kind=kLoop, calls=%fused_computation | loop fusion | flops 10485760 | bytes 4194304 | tf_op jit(solution)/shard_map/concatenate | solution.py:241
  114.5 12.4 %shard_map.122 = (bf16[10240,256]{1,0:T(8,128)(2,1)S(1)}, bf16[128,32,128]{2,1,0:T(8,128)(2,1)S(1)}) custom-call(s32[2]{0:T(128)S(1)} %pad_add_fusion.place, bf16[10240,256]{1,0:T(8,128)(2,1)S(1)} %shard_map.121.h_in, bf16[128,64,128]{2,1,0:T(8,128)(2,1)S(1)} %pad_maximum_fusion.taps, bf16[4,160,64]{2,1,0:T(8,128)(2,1)S(1)} %copy-done.9, ...), custom_call_target="tpu_custom_call" | custom-call | flops 1 | bytes 1 | tf_op jit(solution)/shard_map/pallas_call | solution.py:164
  126.9 0.0 copy-done
  126.9 2.4 copy-done.2
  129.3 4.6 %collective-permute-done.5.crossed = bf16[64,32,128]{2,1,0:T(8,128)(2,1)S(1)} collective-permute-done((bf16[64,32,128]{2,1,0:T(8,128)(2,1)S(1)}, bf16[64,32,128]{2,1,0:T(8,128)(2,1)S(1)}, u32[]{:S(2)}, u32[]{:S(2)}) %collective-permute-start.5) | collective-permute-done | bytes 524320 | tf_op jit(solution)/shard_map/ppermute | solution.py:176
  133.9 1.9 collective-permute-start.6
  135.8 1.4 copy.23
  137.2 40.7 %all-to-all-start.2 = ((bf16[32,128,128]{2,1,0:T(8,128)(2,1)}), bf16[32,128,128]{2,1,0:T(8,128)(2,1)S(1)}, u32[]{:S(2)}, u32[]{:S(2)}) async-start(bf16[32,128,128]{2,1,0:T(8,128)(2,1)} %copy.23), calls=%async_computation.2 | async-start | bytes 2097152 | tf_op jit(solution)/shard_map/all_to_all | solution.py:209
  177.9 1.9 copy.34
  179.8 2.5 copy-done.1
  182.3 6.5 %shard_map.125 = bf16[64,32,128]{2,1,0:T(8,128)(2,1)S(1)} custom-call(s32[2]{0:T(128)S(1)} %pad_add_fusion.place, bf16[128,32,128]{2,1,0:T(8,128)(2,1)S(1)} %bitcast.70, bf16[10240,256]{1,0:T(8,128)(2,1)S(1)} %copy-done.1, bf16[2,160,32]{2,1,0:T(8,128)(2,1)S(1)} %copy-done.5, bf16[2,32,160]{2,1,0:T(8,128)(2,1)S(1)} %copy-done.8, ...), custom_call_target="tpu_custom_call" | custom-call | flops 1 | bytes 1 | tf_op jit(solution)/shard_map/pallas_call | solution.py:164
  188.8 0.0 copy-done.10
  188.8 9.6 %shard_map.123 = (bf16[64,64,128]{2,1,0:T(8,128)(2,1)S(1)}, bf16[64,32,128]{2,1,0:T(8,128)(2,1)S(1)}) custom-call(s32[2]{0:T(128)S(1)} %pad_add_fusion.place, bf16[128,32,128]{2,1,0:T(8,128)(2,1)S(1)} %bitcast.71, bf16[64,32,128]{2,1,0:T(8,128)(2,1)S(1)} %collective-permute-done.5.crossed, bf16[10240,256]{1,0:T(8,128)(2,1)S(1)} %copy-done.1, ...), custom_call_target="tpu_custom_call" | custom-call | flops 1 | bytes 1 | tf_op jit(solution)/shard_map/pallas_call | solution.py:164
  198.4 0.4 dynamic-slice_bitcast_fusion.8
  198.8 0.1 pad_maximum_fusion.4
  198.9 4.1 %collective-permute-start.9 = (bf16[2,64,16,128]{3,2,1,0:T(8,128)(2,1)S(1)}, bf16[2,64,16,128]{3,2,1,0:T(8,128)(2,1)S(1)}, u32[]{:S(2)}, u32[]{:S(2)}) collective-permute-start(bf16[2,64,16,128]{3,2,1,0:T(8,128)(2,1)S(1)} %pad_maximum_fusion.4), channel_id=1, source_target_pairs={{0,384},{128,0},{256,128},{384,256},{1,385},{129,1},{257,129},{385... | collective-permute-start | bytes 1572872 | tf_op jit(solution)/shard_map/ppermute | solution.py:203
  203.0 0.1 pad_maximum_fusion.3
  203.1 6.0 %collective-permute-start.8 = (bf16[2,64,16,128]{3,2,1,0:T(8,128)(2,1)S(1)}, bf16[2,64,16,128]{3,2,1,0:T(8,128)(2,1)S(1)}, u32[]{:S(2)}, u32[]{:S(2)}) collective-permute-start(bf16[2,64,16,128]{3,2,1,0:T(8,128)(2,1)S(1)} %pad_maximum_fusion.3), channel_id=1, source_target_pairs={{0,256},{128,384},{256,0},{384,128},{1,257},{129,385},{257,1},{385... | collective-permute-start | bytes 1572872 | tf_op jit(solution)/shard_map/ppermute | solution.py:203
  209.1 0.1 pad_maximum_fusion.2
  209.2 3.3 %collective-permute-start.7 = (bf16[2,64,16,128]{3,2,1,0:T(8,128)(2,1)S(1)}, bf16[2,64,16,128]{3,2,1,0:T(8,128)(2,1)S(1)}, u32[]{:S(2)}, u32[]{:S(2)}) collective-permute-start(bf16[2,64,16,128]{3,2,1,0:T(8,128)(2,1)S(1)} %pad_maximum_fusion.2), channel_id=1, source_target_pairs={{0,128},{128,256},{256,384},{384,0},{1,129},{129,257},{257,385},{3... | collective-permute-start | bytes 1572872 | tf_op jit(solution)/shard_map/ppermute | solution.py:203
  212.5 7.1 %shard_map.124 = bf16[64,32,128]{2,1,0:T(8,128)(2,1)S(1)} custom-call(s32[2]{0:T(128)S(1)} %pad_add_fusion.place, bf16[128,32,128]{2,1,0:T(8,128)(2,1)S(1)} %bitcast.72, bf16[64,32,128]{2,1,0:T(8,128)(2,1)S(1)} %collective-permute-done.6.crossed, bf16[10240,256]{1,0:T(8,128)(2,1)S(1)} %copy-done.3, bf16[2,160,32]{2,1,0:T(8,128)(2,1)S(1)} %copy-done.5, ...), custom_call_target="tpu_custom_call" | custom-call | flops 44999999488 | bytes 1 | tf_op jit(solution)/shard_map/pallas_call | solution.py:164
  219.7 0.1 broadcast_select_fusion.5
  219.8 1.1 maximum_bitcast_fusion
  220.8 5.0 %collective-permute-done.9 = bf16[2,64,16,128]{3,2,1,0:T(8,128)(2,1)S(1)} collective-permute-done((bf16[2,64,16,128]{3,2,1,0:T(8,128)(2,1)S(1)}, bf16[2,64,16,128]{3,2,1,0:T(8,128)(2,1)S(1)}, u32[]{:S(2)}, u32[]{:S(2)}) %collective-permute-start.9) | collective-permute-done | bytes 524320 | tf_op jit(solution)/shard_map/ppermute | solution.py:203
  225.8 6.8 %collective-permute-done.7 = bf16[2,64,16,128]{3,2,1,0:T(8,128)(2,1)S(1)} collective-permute-done((bf16[2,64,16,128]{3,2,1,0:T(8,128)(2,1)S(1)}, bf16[2,64,16,128]{3,2,1,0:T(8,128)(2,1)S(1)}, u32[]{:S(2)}, u32[]{:S(2)}) %collective-permute-start.7) | collective-permute-done | bytes 524320 | tf_op jit(solution)/shard_map/ppermute | solution.py:203
  232.6 0.2 convert_add_fusion
  232.8 2.6 copy.24
  235.4 7.8 %all-to-all-start.3 = ((bf16[32,128,128]{2,1,0:T(8,128)(2,1)}), bf16[32,128,128]{2,1,0:T(8,128)(2,1)}, u32[]{:S(2)}, u32[]{:S(2)}) async-start(bf16[32,128,128]{2,1,0:T(8,128)(2,1)} %copy.24), calls=%async_computation.3 | async-start | bytes 2097152 | tf_op jit(solution)/shard_map/all_to_all | solution.py:209
  243.2 0.1 slice_select_fusion
  243.4 1.9 collective-permute-start.10
  245.4 32.2 %collective-permute-done.10 = bf16[2,64,8,128]{3,2,1,0:T(8,128)(2,1)S(1)} collective-permute-done((bf16[2,64,8,128]{3,2,1,0:T(8,128)(2,1)S(1)}, bf16[2,64,8,128]{3,2,1,0:T(8,128)(2,1)S(1)}, u32[]{:S(2)}, u32[]{:S(2)}) %collective-permute-start.10) | collective-permute-done | bytes 262176 | tf_op jit(solution)/shard_map/ppermute | solution.py:176
  277.6 20.9 %collective-permute-start.11 = (bf16[64,8,128]{2,1,0:T(8,128)(2,1)S(1)}, bf16[64,8,128]{2,1,0:T(8,128)(2,1)S(1)}, u32[]{:S(2)}, u32[]{:S(2)}) collective-permute-start(bf16[64,8,128]{2,1,0:T(8,128)(2,1)S(1)} %fusion.3), channel_id=1, source_target_pairs={{0,96},{32,64},{64,32},{96,0},{1,97},{33,65},{65,33},{97,1},{2,98}... | collective-permute-start | bytes 393224 | tf_op jit(solution)/shard_map/ppermute | solution.py:180
  298.6 3.7 %collective-permute-done.11 = bf16[64,8,128]{2,1,0:T(8,128)(2,1)S(1)} collective-permute-done((bf16[64,8,128]{2,1,0:T(8,128)(2,1)S(1)}, bf16[64,8,128]{2,1,0:T(8,128)(2,1)S(1)}, u32[]{:S(2)}, u32[]{:S(2)}) %collective-permute-start.11) | collective-permute-done | bytes 131104 | tf_op jit(solution)/shard_map/ppermute | solution.py:180
  302.3 0.8 copy.35
  303.1 1.4 broadcast_select_fusion.2
  304.5 1.0 copy.25
  305.5 1.0 copy.26
  (30 shorter events, 0.3 us)
Async XLA Ops:
  1.6 20.2 %collective-permute-start = (bf16[64,8,128]{2,1,0:T(8,128)(2,1)S(1)}, bf16[64,8,128]{2,1,0:T(8,128)(2,1)S(1)}, u32[]{:S(2)}, u32[]{:S(2)}) collective-permute-start(bf16[64,8,128]{2,1,0:T(8,128)(2,1)S(1)} %bitcast.80), channel_id=1, source_target_pairs={{0,96},{32,64},{64,32},{96,0},{1,97},{33,65},{65,33},{97,1},{2,98}... | collective-permute-start | bytes 393224 | tf_op jit(solution)/shard_map/ppermute | solution.py:180
  21.8 46.0 %all-to-all-start = ((bf16[32,128,128]{2,1,0:T(8,128)(2,1)}), bf16[32,128,128]{2,1,0:T(8,128)(2,1)S(1)}, u32[]{:S(2)}, u32[]{:S(2)}) async-start(bf16[32,128,128]{2,1,0:T(8,128)(2,1)} %bitcast.79), calls=%async_computation | async-start | bytes 2097152 | tf_op jit(solution)/shard_map/all_to_all | solution.py:209
  32.1 34.3 %collective-permute-start.1 = (bf16[2,64,8,128]{3,2,1,0:T(8,128)(2,1)S(1)}, bf16[2,64,8,128]{3,2,1,0:T(8,128)(2,1)S(1)}, u32[]{:S(2)}, u32[]{:S(2)}) collective-permute-start(bf16[2,64,8,128]{3,2,1,0:T(8,128)(2,1)S(1)} %pad_maximum_fusion.5), channel_id=1, source_target_pairs={{0,32},{32,0},{1,33},{33,1},{2,34},{34,2},{3,35},{35,3},{4,36},{36... | collective-permute-start | bytes 786440 | tf_op jit(solution)/shard_map/ppermute | solution.py:176
  67.8 69.4 %all-to-all-start.1 = ((bf16[32,128,128]{2,1,0:T(8,128)(2,1)}), bf16[32,128,128]{2,1,0:T(8,128)(2,1)}, u32[]{:S(2)}, u32[]{:S(2)}) async-start(bf16[32,128,128]{2,1,0:T(8,128)(2,1)} %bitcast.7), calls=%async_computation.1 | async-start | bytes 2097152 | tf_op jit(solution)/shard_map/all_to_all | solution.py:209
  76.5 17.3 %copy-start.4 = (bf16[256,256]{1,0:T(8,128)(2,1)S(1)}, bf16[256,256]{1,0:T(8,128)(2,1)}, u32[]{:S(2)}) copy-start(bf16[256,256]{1,0:T(8,128)(2,1)} %constant.81.clone.fast_fwd) | copy-start | bytes 393220
  76.6 17.3 %copy-start.5 = (bf16[2,160,32]{2,1,0:T(8,128)(2,1)S(1)}, bf16[2,160,32]{2,1,0:T(8,128)(2,1)}, u32[]{:S(2)}) copy-start(bf16[2,160,32]{2,1,0:T(8,128)(2,1)} %constant.77.clone.near.far) | copy-start | bytes 61444
  76.6 17.3 %copy-start.6 = (f32[2,80,128]{2,1,0:T(8,128)S(1)}, f32[2,80,128]{2,1,0:T(8,128)}, u32[]{:S(2)}) copy-start(f32[2,80,128]{2,1,0:T(8,128)} %constant.83.clone.twid) | copy-start | bytes 245764
  77.6 27.9 %collective-permute-start.4 = (bf16[128,16,128]{2,1,0:T(8,128)(2,1)}, bf16[128,16,128]{2,1,0:T(8,128)(2,1)}, u32[]{:S(2)}, u32[]{:S(2)}) collective-permute-start(bf16[128,16,128]{2,1,0:T(8,128)(2,1)} %pad_maximum_fusion.1), channel_id=1, source_target_pairs={{0,384},{128,0},{256,128},{384,256},{1,385},{129,1},{257,129},{385... | collective-permute-start | bytes 1572872 | tf_op jit(solution)/shard_map/ppermute | solution.py:203
  82.5 23.0 %collective-permute-start.3 = (bf16[128,16,128]{2,1,0:T(8,128)(2,1)}, bf16[128,16,128]{2,1,0:T(8,128)(2,1)}, u32[]{:S(2)}, u32[]{:S(2)}) collective-permute-start(bf16[128,16,128]{2,1,0:T(8,128)(2,1)} %pad_maximum_fusion.1), channel_id=1, source_target_pairs={{0,256},{128,384},{256,0},{384,128},{1,257},{129,385},{257,1},{385... | collective-permute-start | bytes 1572872 | tf_op jit(solution)/shard_map/ppermute | solution.py:203
  85.1 26.1 %collective-permute-start.2 = (bf16[128,16,128]{2,1,0:T(8,128)(2,1)}, bf16[128,16,128]{2,1,0:T(8,128)(2,1)}, u32[]{:S(2)}, u32[]{:S(2)}) collective-permute-start(bf16[128,16,128]{2,1,0:T(8,128)(2,1)} %pad_maximum_fusion.1), channel_id=1, source_target_pairs={{0,128},{128,256},{256,384},{384,0},{1,129},{129,257},{257,385},{3... | collective-permute-start | bytes 1572872 | tf_op jit(solution)/shard_map/ppermute | solution.py:203
  89.5 44.3 %collective-permute-start.5 = (bf16[64,32,128]{2,1,0:T(8,128)(2,1)S(1)}, bf16[64,32,128]{2,1,0:T(8,128)(2,1)S(1)}, u32[]{:S(2)}, u32[]{:S(2)}) collective-permute-start(bf16[64,32,128]{2,1,0:T(8,128)(2,1)S(1)} %get-tuple-element.46), channel_id=1, source_target_pairs={{0,32},{32,0},{1,33},{33,1},{2,34},{34,2},{3,35},{35,3},{4,36},{36... | collective-permute-start | bytes 1572872 | tf_op jit(solution)/shard_map/ppermute | solution.py:176
  93.8 20.6 %copy-start.7 = (bf16[256,256]{1,0:T(8,128)(2,1)S(1)}, bf16[256,256]{1,0:T(8,128)(2,1)}, u32[]{:S(2)}) copy-start(bf16[256,256]{1,0:T(8,128)(2,1)} %constant.82.clone.fast_inv) | copy-start | bytes 393220
  93.9 20.6 %copy-start.8 = (bf16[2,32,160]{2,1,0:T(8,128)(2,1)S(1)}, bf16[2,32,160]{2,1,0:T(8,128)(2,1)}, u32[]{:S(2)}) copy-start(bf16[2,32,160]{2,1,0:T(8,128)(2,1)} %constant.79.clone.slow_out) | copy-start | bytes 61444
  93.9 20.6 %copy-start.9 = (bf16[4,160,64]{2,1,0:T(8,128)(2,1)S(1)}, bf16[4,160,64]{2,1,0:T(8,128)(2,1)}, u32[]{:S(2)}) copy-start(bf16[4,160,64]{2,1,0:T(8,128)(2,1)} %constant.78.clone.taps_table) | copy-start | bytes 245764
  101.2 25.7 %copy-start = (bf16[10240,256]{1,0:T(8,128)(2,1)}, bf16[10240,256]{1,0:T(8,128)(2,1)S(1)}, u32[]{:S(2)}) copy-start(bf16[10240,256]{1,0:T(8,128)(2,1)S(1)} %shard_map.121.h_in) | copy-start | bytes 15728644
  114.5 19.4 %copy-start.11 = (bf16[64,32,128]{2,1,0:T(8,128)(2,1)S(1)}, bf16[64,32,128]{2,1,0:T(8,128)(2,1)}, u32[]{:S(2)}) copy-start(bf16[64,32,128]{2,1,0:T(8,128)(2,1)} %get-tuple-element.27) | copy-start | bytes 1572868
  126.9 2.4 copy-start.2
  133.9 78.7 %collective-permute-start.6 = (bf16[64,32,128]{2,1,0:T(8,128)(2,1)S(1)}, bf16[64,32,128]{2,1,0:T(8,128)(2,1)S(1)}, u32[]{:S(2)}, u32[]{:S(2)}) collective-permute-start(bf16[64,32,128]{2,1,0:T(8,128)(2,1)S(1)} %copy-done.11), channel_id=1, source_target_pairs={{0,32},{32,0},{1,33},{33,1},{2,34},{34,2},{3,35},{35,3},{4,36},{36... | collective-permute-start | bytes 1572872 | tf_op jit(solution)/shard_map/ppermute | solution.py:176
  137.2 95.7 %all-to-all-start.2 = ((bf16[32,128,128]{2,1,0:T(8,128)(2,1)}), bf16[32,128,128]{2,1,0:T(8,128)(2,1)S(1)}, u32[]{:S(2)}, u32[]{:S(2)}) async-start(bf16[32,128,128]{2,1,0:T(8,128)(2,1)} %copy.23), calls=%async_computation.2 | async-start | bytes 2097152 | tf_op jit(solution)/shard_map/all_to_all | solution.py:209
  177.9 10.9 %copy-start.10 = (bf16[64,160]{1,0:T(8,128)(2,1)S(1)}, bf16[64,160]{1,0:T(8,128)(2,1)}, u32[]{:S(2)}) copy-start(bf16[64,160]{1,0:T(8,128)(2,1)} %constant.80.clone.out_full) | copy-start | bytes 61444
  179.8 2.5 copy-start.1
  182.3 6.5 %copy-start.3 = (bf16[10240,256]{1,0:T(8,128)(2,1)S(1)}, bf16[10240,256]{1,0:T(8,128)(2,1)}, u32[]{:S(2)}) copy-start(bf16[10240,256]{1,0:T(8,128)(2,1)} %copy-done.2) | copy-start | bytes 15728644
  198.9 26.9 %collective-permute-start.9 = (bf16[2,64,16,128]{3,2,1,0:T(8,128)(2,1)S(1)}, bf16[2,64,16,128]{3,2,1,0:T(8,128)(2,1)S(1)}, u32[]{:S(2)}, u32[]{:S(2)}) collective-permute-start(bf16[2,64,16,128]{3,2,1,0:T(8,128)(2,1)S(1)} %pad_maximum_fusion.4), channel_id=1, source_target_pairs={{0,384},{128,0},{256,128},{384,256},{1,385},{129,1},{257,129},{385... | collective-permute-start | bytes 1572872 | tf_op jit(solution)/shard_map/ppermute | solution.py:203
  203.1 22.7 %collective-permute-start.8 = (bf16[2,64,16,128]{3,2,1,0:T(8,128)(2,1)S(1)}, bf16[2,64,16,128]{3,2,1,0:T(8,128)(2,1)S(1)}, u32[]{:S(2)}, u32[]{:S(2)}) collective-permute-start(bf16[2,64,16,128]{3,2,1,0:T(8,128)(2,1)S(1)} %pad_maximum_fusion.3), channel_id=1, source_target_pairs={{0,256},{128,384},{256,0},{384,128},{1,257},{129,385},{257,1},{385... | collective-permute-start | bytes 1572872 | tf_op jit(solution)/shard_map/ppermute | solution.py:203
  209.2 23.4 %collective-permute-start.7 = (bf16[2,64,16,128]{3,2,1,0:T(8,128)(2,1)S(1)}, bf16[2,64,16,128]{3,2,1,0:T(8,128)(2,1)S(1)}, u32[]{:S(2)}, u32[]{:S(2)}) collective-permute-start(bf16[2,64,16,128]{3,2,1,0:T(8,128)(2,1)S(1)} %pad_maximum_fusion.2), channel_id=1, source_target_pairs={{0,128},{128,256},{256,384},{384,0},{1,129},{129,257},{257,385},{3... | collective-permute-start | bytes 1572872 | tf_op jit(solution)/shard_map/ppermute | solution.py:203
  235.4 67.7 %all-to-all-start.3 = ((bf16[32,128,128]{2,1,0:T(8,128)(2,1)}), bf16[32,128,128]{2,1,0:T(8,128)(2,1)}, u32[]{:S(2)}, u32[]{:S(2)}) async-start(bf16[32,128,128]{2,1,0:T(8,128)(2,1)} %copy.24), calls=%async_computation.3 | async-start | bytes 2097152 | tf_op jit(solution)/shard_map/all_to_all | solution.py:209
  243.4 34.1 %collective-permute-start.10 = (bf16[2,64,8,128]{3,2,1,0:T(8,128)(2,1)S(1)}, bf16[2,64,8,128]{3,2,1,0:T(8,128)(2,1)S(1)}, u32[]{:S(2)}, u32[]{:S(2)}) collective-permute-start(bf16[2,64,8,128]{3,2,1,0:T(8,128)(2,1)S(1)} %pad_maximum_fusion.8), channel_id=1, source_target_pairs={{0,32},{32,0},{1,33},{33,1},{2,34},{34,2},{3,35},{35,3},{4,36},{36... | collective-permute-start | bytes 786440 | tf_op jit(solution)/shard_map/ppermute | solution.py:176
  277.6 24.7 %collective-permute-start.11 = (bf16[64,8,128]{2,1,0:T(8,128)(2,1)S(1)}, bf16[64,8,128]{2,1,0:T(8,128)(2,1)S(1)}, u32[]{:S(2)}, u32[]{:S(2)}) collective-permute-start(bf16[64,8,128]{2,1,0:T(8,128)(2,1)S(1)} %fusion.3), channel_id=1, source_target_pairs={{0,96},{32,64},{64,32},{96,0},{1,97},{33,65},{65,33},{97,1},{2,98}... | collective-permute-start | bytes 393224 | tf_op jit(solution)/shard_map/ppermute | solution.py:180

commit v7 on v6

--- a/solution.py
+++ b/solution.py
@@ -19,7 +19,7 @@
 RING = 4
 QUARTER = HALF // RING
 BLOCK = 8
-LONG = 45 * 10**9
+LONG = 30 * 10**9
 
 
 def tables():
@@ -232,56 +232,58 @@
     (h_spec,) = call(first_kernel, place, chans, [(first, "x", at_start), near, fast_fwd, twid], [0])
     quarter = own // 2
     to_own, to_far = pick_half(first, 1 - zb), pick_half(first, zb)
-    cross_own = swap(to_own, "zb")
+    cross_own, cross_far = swap(to_own, "zb"), swap(to_far, "zb")
 
     second = move(second_in).transpose(1, 0, 2)
     near_taps = ordered(left, taps, swapped[1], axis=1)
     far_taps = ordered(left, swapped[0], across, axis=1)
     taps = ordered(low, near_taps, far_taps)
     taps = jnp.concatenate([taps] + [ring(taps, step) for step in range(1, RING)], axis=1)
-    (far_terms,) = call(
-        other_kernel, place, own,
-        [(second, "x", at_far), (h_spec, "s", at_far), near, out_start, fast_fwd, fast_inv, twid], [NEAR],
-    )
-
     k_spec, local_out = call(
         local_kernel, place, chans,
         [(h_spec, "s", at_start), (taps, "x", at_start), (consts["slow_taps"], "t", row), out_near,
          fast_fwd, fast_inv, twid], [0, NEAR],
     )
-    local_in, cross_own, to_far = lax.optimization_barrier((local_out.transpose(1, 0, 2), cross_own, to_far))
-    local_back = move(local_in)
-    cross_far = swap(to_far, "zb")
+    local_back = move(local_out.transpose(1, 0, 2))
+    (far_terms,) = call(
+        other_kernel, place, own,
+        [(second, "x", at_far), (h_spec, "s", at_far), near, out_start, fast_fwd, fast_inv, twid], [NEAR],
+    )
+
+    def along(terms):
+        total = None
+        for step in range(RING):
+            to = jnp.minimum((y + step) % RING, terms.shape[1] // QUARTER - 1)
+            block = lax.dynamic_slice_in_dim(terms, to * QUARTER, QUARTER, 1)
+            block = (ring(block, step) if step else block).astype(jnp.float32)
+            total = block if total is None else total + block
+        return total
+
+    far_sum = jnp.where(y < RING // 2, along(far_terms), 0.0).astype(jnp.bfloat16)
+    from_both = diagonal(pick_half(far_sum, 1 - zh, 1))
+    cross_own, cross_far, far_sum, from_both = lax.optimization_barrier((cross_own, cross_far, far_sum, from_both))
+    from_half = swap(pick_half(far_sum, zh, 1), "zb")
     own_terms, out_own = call(
         own_kernel, place, own,
         [(second, "x", at_own), (cross_own, "x", at_start), (h_spec, "s", at_own), (k_spec, "s", at_own),
          near, far, out_near, out_full, fast_fwd, fast_inv, twid], [HALF, NEAR],
     )
 
-    sums = None
-    for step in range(RING):
-        to = (y + step) % RING
-        block = jnp.stack([
-            lax.dynamic_slice_in_dim(own_terms, to * QUARTER, QUARTER, 1),
-            lax.dynamic_slice_in_dim(far_terms, jnp.minimum(to, 1) * QUARTER, QUARTER, 1),
-        ])
-        block = (ring(block, step) if step else block).astype(jnp.float32)
-        sums = block if sums is None else sums + block
+    own_sum = along(own_terms)
+    cross_far, own_sum, from_half = lax.optimization_barrier((cross_far, own_sum, from_half))
+    from_z = swap(pick_half(own_sum, 1 - zh, 1).astype(jnp.bfloat16), "zh")
+    filter_grads = pick_half(own_sum, zh, 1)
+    for item in (from_half, from_both, from_z):
+        filter_grads = filter_grads + item.astype(jnp.float32)
+
     (out_far,) = call(
         cross_kernel, place, own,
         [(second, "x", at_far), (cross_far, "x", at_start), (k_spec, "s", at_far), near, far, out_near,
          fast_fwd, fast_inv, twid], [NEAR], flops=LONG,
     )
     cross_in = ordered(low, out_own, out_far).transpose(1, 0, 2)
-    cross_in, local_back, sums = lax.optimization_barrier((cross_in, local_back, sums))
+    cross_in, local_back = lax.optimization_barrier((cross_in, local_back))
     cross_back = move(cross_in)
-
-    own_sum, far_sum = sums[0], jnp.where(y < RING // 2, sums[1], 0.0)
-    far_here, far_there = pick_half(far_sum, zh, 1), pick_half(far_sum, 1 - zh, 1)
-    own_here, own_there = pick_half(own_sum, zh, 1), pick_half(own_sum, 1 - zh, 1)
-    arrived = swap(jnp.stack([far_here, own_there]).astype(jnp.bfloat16), "zb").astype(jnp.float32)
-    passed = diagonal((far_there + arrived[1]).astype(jnp.bfloat16)).astype(jnp.float32)
-    filter_grads = own_here + arrived[0] + passed
 
     def gathered(item):
         return item.reshape(n_span, 2, own, FAST).transpose(1, 0, 2, 3).reshape(values.shape)

time: 308 us -> 347 us (1.13)
  the two profiles are of different devices: /device:TPU:36 before, /device:TPU:1 now
where the time goes in v7:
time: 347 us; the launch traced here: 346 us
  waiting for transfers between devices  161 us (46%)
  starting transfers between devices  96 us (28%)
  Pallas kernels  42.9 us (12%)
  local copies, waits for them, and re-layouts  34.7 us (10%)
  other arithmetic  10.2 us (3%)
    ppermute x5, waiting for transfers between devices, swap(): return lax.ppermute(item, axis, [(0, 1), (1, 0)])  95.3 us
    pallas_call x5, Pallas kernels, call(): pl.pallas_call(kernel, grid_spec=pltpu.PrefetchScalarGridSpec(num_scalar_...  42.9 us
    ppermute x2, waiting for transfers between devices, diagonal(): return lax.ppermute(item, ('zh', 'zb'), [(0, 3), (1, 2), (2, 1), (3, 0)])  31.7 us
    ppermute x9, starting transfers between devices, ring(): lax.ppermute(item, 'y', [(i, (i + step) % RING) for i in range(RING)])  29.3 us
    all_to_all x4, waiting for transfers between devices, move(): return lax.all_to_all(item, span, split_axis=0, concat_axis=0, tiled=True)  25.8 us
    all_to_all x4, starting transfers between devices, move(): return lax.all_to_all(item, span, split_axis=0, concat_axis=0, tiled=True)  25.2 us
    ppermute x5, starting transfers between devices, swap(): return lax.ppermute(item, axis, [(0, 1), (1, 0)])  21 us
    unnamed x50, local copies, waits for them, and re-layouts  21 us
  transfers between devices with their start and end apart: 20, of which 12 were waited for; matrix products, arithmetic and copies ran while one was open for 6% of the time, Pallas kernels for 12%

profile of v7, /device:TPU:1, one launch (start us, length us, event | category | flops | bytes accessed | tf_op | source)
XLA Modules:
  0.0 345.9 jit_solution(4056656468470729015)
XLA Ops:
  0.6 0.9 copy.27
  1.6 13.3 %collective-permute-start = (bf16[64,8,128]{2,1,0:T(8,128)(2,1)S(1)}, bf16[64,8,128]{2,1,0:T(8,128)(2,1)S(1)}, u32[]{:S(2)}, u32[]{:S(2)}) collective-permute-start(bf16[64,8,128]{2,1,0:T(8,128)(2,1)S(1)} %bitcast.60), channel_id=1, source_target_pairs={{0,96},{32,64},{64,32},{96,0},{1,97},{33,65},{65,33},{97,1},{2,98}... | collective-permute-start | bytes 393224 | tf_op jit(solution)/shard_map/ppermute | solution.py:180
  14.9 1.7 broadcast_select_fusion
  16.5 1.0 copy.17
  17.6 8.4 %collective-permute-done = bf16[64,8,128]{2,1,0:T(8,128)(2,1)S(1)} collective-permute-done((bf16[64,8,128]{2,1,0:T(8,128)(2,1)S(1)}, bf16[64,8,128]{2,1,0:T(8,128)(2,1)S(1)}, u32[]{:S(2)}, u32[]{:S(2)}) %collective-permute-start) | collective-permute-done | bytes 131104 | tf_op jit(solution)/shard_map/ppermute | solution.py:180
  26.0 7.5 %all-to-all-start = ((bf16[32,128,128]{2,1,0:T(8,128)(2,1)}), bf16[32,128,128]{2,1,0:T(8,128)(2,1)S(1)}, u32[]{:S(2)}, u32[]{:S(2)}) async-start(bf16[32,128,128]{2,1,0:T(8,128)(2,1)} %bitcast.4), calls=%async_computation | async-start | bytes 2097152 | tf_op jit(solution)/shard_map/all_to_all | solution.py:209
  33.6 4.4 %collective-permute-start.1 = (bf16[2,64,8,128]{3,2,1,0:T(8,128)(2,1)S(1)}, bf16[2,64,8,128]{3,2,1,0:T(8,128)(2,1)S(1)}, u32[]{:S(2)}, u32[]{:S(2)}) collective-permute-start(bf16[2,64,8,128]{3,2,1,0:T(8,128)(2,1)S(1)} %pad_maximum_fusion.2), channel_id=1, source_target_pairs={{0,32},{32,0},{1,33},{33,1},{2,34},{34,2},{3,35},{35,3},{4,36},{36... | collective-permute-start | bytes 786440 | tf_op jit(solution)/shard_map/ppermute | solution.py:176
  38.0 1.1 copy.18
  39.1 17.3 %collective-permute-done.1 = bf16[2,64,8,128]{3,2,1,0:T(8,128)(2,1)S(1)} collective-permute-done((bf16[2,64,8,128]{3,2,1,0:T(8,128)(2,1)S(1)}, bf16[2,64,8,128]{3,2,1,0:T(8,128)(2,1)S(1)}, u32[]{:S(2)}, u32[]{:S(2)}) %collective-permute-start.1) | collective-permute-done | bytes 262176 | tf_op jit(solution)/shard_map/ppermute | solution.py:176
  56.4 15.0 %all-to-all-done = bf16[32,128,128]{2,1,0:T(8,128)(2,1)S(1)} async-done(((bf16[32,128,128]{2,1,0:T(8,128)(2,1)}), bf16[32,128,128]{2,1,0:T(8,128)(2,1)S(1)}, u32[]{:S(2)}, u32[]{:S(2)}) %all-to-all-start) | async-done | bytes 1048608 | tf_op jit(solution)/shard_map/all_to_all | solution.py:209
  71.4 6.6 %all-to-all-start.1 = ((bf16[32,128,128]{2,1,0:T(8,128)(2,1)}), bf16[32,128,128]{2,1,0:T(8,128)(2,1)}, u32[]{:S(2)}, u32[]{:S(2)}) async-start(bf16[32,128,128]{2,1,0:T(8,128)(2,1)} %bitcast.7), calls=%async_computation.1 | async-start | bytes 2097152 | tf_op jit(solution)/shard_map/all_to_all | solution.py:209
  78.2 0.9 pad_maximum_fusion.1
  79.1 4.6 %collective-permute-start.10 = (bf16[128,16,128]{2,1,0:T(8,128)(2,1)}, bf16[128,16,128]{2,1,0:T(8,128)(2,1)}, u32[]{:S(2)}, u32[]{:S(2)}) collective-permute-start(bf16[128,16,128]{2,1,0:T(8,128)(2,1)} %pad_maximum_fusion.1), channel_id=1, source_target_pairs={{0,384},{128,0},{256,128},{384,256},{1,385},{129,1},{257,129},{385... | collective-permute-start | bytes 1572872 | tf_op jit(solution)/shard_map/ppermute | solution.py:203
  83.7 1.9 collective-permute-start.8
  85.6 3.5 %collective-permute-start.9 = (bf16[128,16,128]{2,1,0:T(8,128)(2,1)}, bf16[128,16,128]{2,1,0:T(8,128)(2,1)}, u32[]{:S(2)}, u32[]{:S(2)}) collective-permute-start(bf16[128,16,128]{2,1,0:T(8,128)(2,1)} %pad_maximum_fusion.1), channel_id=1, source_target_pairs={{0,256},{128,384},{256,0},{384,128},{1,257},{129,385},{257,1},{385... | collective-permute-start | bytes 1572872 | tf_op jit(solution)/shard_map/ppermute | solution.py:203
  89.4 1.9 copy.36
  91.3 7.3 %shard_map.121.h_in = bf16[10240,256]{1,0:T(8,128)(2,1)S(1)} custom-call(s32[2]{0:T(128)S(1)} %pad_add_fusion.place, bf16[128,32,128]{2,1,0:T(8,128)(2,1)S(1)} %bitcast.54, bf16[2,160,32]{2,1,0:T(8,128)(2,1)S(1)} %copy-done.7, bf16[256,256]{1,0:T(8,128)(2,1)S(1)} %copy-done.6, f32[2,80,128]{2,1,0:T(8,128)S(1)} %copy-done.8), custom_call_target="tpu_custom_call" | custom-call | flops 1 | bytes 1 | tf_op jit(solution)/shard_map/pallas_call | solution.py:164
  98.7 2.3 copy-done
  101.0 3.6 %all-to-all-done.1 = bf16[32,128,128]{2,1,0:T(8,128)(2,1)} async-done(((bf16[32,128,128]{2,1,0:T(8,128)(2,1)}), bf16[32,128,128]{2,1,0:T(8,128)(2,1)}, u32[]{:S(2)}, u32[]{:S(2)}) %all-to-all-start.1) | async-done | bytes 1048608 | tf_op jit(solution)/shard_map/all_to_all | solution.py:209
  104.6 1.9 copy.34
  106.6 2.5 copy-done.1
  109.0 6.5 %shard_map.122 = bf16[64,32,128]{2,1,0:T(8,128)(2,1)S(1)} custom-call(s32[2]{0:T(128)S(1)} %pad_add_fusion.place, bf16[128,32,128]{2,1,0:T(8,128)(2,1)S(1)} %bitcast.51, bf16[10240,256]{1,0:T(8,128)(2,1)S(1)} %copy-done.1, bf16[2,160,32]{2,1,0:T(8,128)(2,1)S(1)} %copy-done.7, bf16[2,32,160]{2,1,0:T(8,128)(2,1)S(1)} %copy-done.14, ...), custom_call_target="tpu_custom_call" | custom-call | flops 1 | bytes 1 | tf_op jit(solution)/shard_map/pallas_call | solution.py:164
  115.5 1.0 constant_dynamic-slice_fusion.7
  116.5 3.2 collective-permute-start.4
  119.7 4.5 %collective-permute-start.5 = (bf16[64,16,128]{2,1,0:T(8,128)(2,1)}, bf16[64,16,128]{2,1,0:T(8,128)(2,1)}, u32[]{:S(2)}, u32[]{:S(2)}) collective-permute-start(bf16[64,16,128]{2,1,0:T(8,128)(2,1)} %get-tuple-element.56), channel_id=1, source_target_pairs={{0,256},{128,384},{256,0},{384,128},{1,257},{129,385},{257,1},{385... | collective-permute-start | bytes 786440 | tf_op jit(solution)/shard_map/ppermute | solution.py:203
  124.3 3.0 collective-permute-start.6
  127.3 1.1 dynamic-slice_bitcast_fusion
  128.3 3.9 %collective-permute-start.2 = (bf16[64,32,128]{2,1,0:T(8,128)(2,1)}, bf16[64,32,128]{2,1,0:T(8,128)(2,1)S(1)}, u32[]{:S(2)}, u32[]{:S(2)}) collective-permute-start(bf16[64,32,128]{2,1,0:T(8,128)(2,1)} %get-tuple-element.51), channel_id=1, source_target_pairs={{0,32},{32,0},{1,33},{33,1},{2,34},{34,2},{3,35},{35,3},{4,36},{36... | collective-permute-start | bytes 1572872 | tf_op jit(solution)/shard_map/ppermute | solution.py:176
  132.2 5.3 %collective-permute-start.3 = (bf16[64,32,128]{2,1,0:T(8,128)(2,1)}, bf16[64,32,128]{2,1,0:T(8,128)(2,1)S(1)}, u32[]{:S(2)}, u32[]{:S(2)}) collective-permute-start(bf16[64,32,128]{2,1,0:T(8,128)(2,1)} %get-tuple-element.50), channel_id=1, source_target_pairs={{0,32},{32,0},{1,33},{33,1},{2,34},{34,2},{3,35},{35,3},{4,36},{36... | collective-permute-start | bytes 1572872 | tf_op jit(solution)/shard_map/ppermute | solution.py:176
  137.6 3.2 pad_maximum_fusion.taps
  140.8 12.4 %shard_map.123 = (bf16[10240,256]{1,0:T(8,128)(2,1)S(1)}, bf16[128,32,128]{2,1,0:T(8,128)(2,1)S(1)}) custom-call(s32[2]{0:T(128)S(1)} %pad_add_fusion.place, bf16[10240,256]{1,0:T(8,128)(2,1)S(1)} %bitcast.50, bf16[128,64,128]{2,1,0:T(8,128)(2,1)S(1)} %pad_maximum_fusion.taps, bf16[4,160,64]{2,1,0:T(8,128)(2,1)S(1)} %copy-done.15, ...), custom_call_target="tpu_custom_call" | custom-call | flops 1 | bytes 1 | tf_op jit(solution)/shard_map/pallas_call | solution.py:164
  153.3 2.4 copy-done.3
  155.7 1.4 copy.23
  157.0 6.7 %all-to-all-start.2 = ((bf16[32,128,128]{2,1,0:T(8,128)(2,1)}), bf16[32,128,128]{2,1,0:T(8,128)(2,1)}, u32[]{:S(2)}, u32[]{:S(2)}) async-start(bf16[32,128,128]{2,1,0:T(8,128)(2,1)} %copy.23), calls=%async_computation.2 | async-start | bytes 2097152 | tf_op jit(solution)/shard_map/all_to_all | solution.py:209
  163.8 1.3 select_convert_fusion
  165.1 7.1 %collective-permute-start.7 = (bf16[64,8,128]{2,1,0:T(8,128)(2,1)S(1)}, bf16[64,8,128]{2,1,0:T(8,128)(2,1)S(1)}, u32[]{:S(2)}, u32[]{:S(2)}) collective-permute-start(bf16[64,8,128]{2,1,0:T(8,128)(2,1)S(1)} %constant_dynamic-slice_fusion.4), channel_id=1, source_target_pairs={{0,96},{32,64},{64,32},{96,0},{1,97},{33,65},{65,33},{97,1},{2,98}... | collective-permute-start | bytes 393224 | tf_op jit(solution)/shard_map/ppermute | solution.py:180
  172.2 30.2 %collective-permute-done.2.crossed = bf16[64,32,128]{2,1,0:T(8,128)(2,1)S(1)} collective-permute-done((bf16[64,32,128]{2,1,0:T(8,128)(2,1)}, bf16[64,32,128]{2,1,0:T(8,128)(2,1)S(1)}, u32[]{:S(2)}, u32[]{:S(2)}) %collective-permute-start.2) | collective-permute-done | bytes 524320 | tf_op jit(solution)/shard_map/ppermute | solution.py:176
  202.4 0.8 copy-done.10
  203.3 22.6 %collective-permute-done.3.crossed = bf16[64,32,128]{2,1,0:T(8,128)(2,1)S(1)} collective-permute-done((bf16[64,32,128]{2,1,0:T(8,128)(2,1)}, bf16[64,32,128]{2,1,0:T(8,128)(2,1)S(1)}, u32[]{:S(2)}, u32[]{:S(2)}) %collective-permute-start.3) | collective-permute-done | bytes 524320 | tf_op jit(solution)/shard_map/ppermute | solution.py:176
  226.7 23.3 %collective-permute-done.7 = bf16[64,8,128]{2,1,0:T(8,128)(2,1)S(1)} collective-permute-done((bf16[64,8,128]{2,1,0:T(8,128)(2,1)S(1)}, bf16[64,8,128]{2,1,0:T(8,128)(2,1)S(1)}, u32[]{:S(2)}, u32[]{:S(2)}) %collective-permute-start.7) | collective-permute-done | bytes 131104 | tf_op jit(solution)/shard_map/ppermute | solution.py:180
  250.0 2.5 copy-done.2
  252.5 2.5 copy-done.4
  255.0 1.0 copy-done.11
  256.0 9.6 %shard_map.124 = (bf16[64,64,128]{2,1,0:T(8,128)(2,1)S(1)}, bf16[64,32,128]{2,1,0:T(8,128)(2,1)S(1)}) custom-call(s32[2]{0:T(128)S(1)} %pad_add_fusion.place, bf16[128,32,128]{2,1,0:T(8,128)(2,1)S(1)} %bitcast.52, bf16[64,32,128]{2,1,0:T(8,128)(2,1)S(1)} %copy-done.11, bf16[10240,256]{1,0:T(8,128)(2,1)S(1)} %copy-done.2, bf16[10240,256]{1,0:T(8,128)(2,1)S(1)} %copy-done.4, ...), custom_call_target="tpu_custom_call" | custom-call | flops 1 | bytes 1 | tf_op jit(solution)/shard_map/pallas_call | solution.py:164
  266.4 0.9 constant_dynamic-slice_fusion.3
  267.3 2.3 collective-permute-start.11
  269.6 2.7 collective-permute-start.12
  272.3 3.5 %collective-permute-start.13 = (bf16[64,16,128]{2,1,0:T(8,128)(2,1)S(1)}, bf16[64,16,128]{2,1,0:T(8,128)(2,1)}, u32[]{:S(2)}, u32[]{:S(2)}) collective-permute-start(bf16[64,16,128]{2,1,0:T(8,128)(2,1)S(1)} %get-tuple-element.46), channel_id=1, source_target_pairs={{0,384},{128,0},{256,128},{384,256},{1,385},{129,1},{257,129},{385... | collective-permute-start | bytes 786440 | tf_op jit(solution)/shard_map/ppermute | solution.py:203
  275.9 1.9 collective-permute-start.14
  277.8 6.0 %collective-permute-done.11 = bf16[64,16,128]{2,1,0:T(8,128)(2,1)} collective-permute-done((bf16[64,16,128]{2,1,0:T(8,128)(2,1)}, bf16[64,16,128]{2,1,0:T(8,128)(2,1)}, u32[]{:S(2)}, u32[]{:S(2)}) %collective-permute-start.11) | collective-permute-done | bytes 262176 | tf_op jit(solution)/shard_map/ppermute | solution.py:203
  283.8 2.0 collective-permute-done.13
  285.8 1.2 convert_add_fusion
  287.0 0.8 collective-permute-done.14
  287.8 2.5 copy-done.5
  290.3 1.0 copy-done.18
  291.4 7.1 %shard_map.125 = bf16[64,32,128]{2,1,0:T(8,128)(2,1)S(1)} custom-call(s32[2]{0:T(128)S(1)} %pad_add_fusion.place, bf16[128,32,128]{2,1,0:T(8,128)(2,1)S(1)} %bitcast.53, bf16[64,32,128]{2,1,0:T(8,128)(2,1)S(1)} %copy-done.18, bf16[10240,256]{1,0:T(8,128)(2,1)S(1)} %copy-done.5, bf16[2,160,32]{2,1,0:T(8,128)(2,1)S(1)} %copy-done.7, ...), custom_call_target="tpu_custom_call" | custom-call | flops 30000001024 | bytes 1 | tf_op jit(solution)/shard_map/pallas_call | solution.py:164
  298.7 1.4 copy.24
  300.1 4.4 %all-to-all-start.3 = ((bf16[32,128,128]{2,1,0:T(8,128)(2,1)}), bf16[32,128,128]{2,1,0:T(8,128)(2,1)S(1)}, u32[]{:S(2)}, u32[]{:S(2)}) async-start(bf16[32,128,128]{2,1,0:T(8,128)(2,1)} %copy.24), calls=%async_computation.3 | async-start | bytes 2097152 | tf_op jit(solution)/shard_map/all_to_all | solution.py:209
  304.5 5.5 %collective-permute-start.15 = (bf16[64,8,128]{2,1,0:T(8,128)(2,1)S(1)}, bf16[64,8,128]{2,1,0:T(8,128)(2,1)S(1)}, u32[]{:S(2)}, u32[]{:S(2)}) collective-permute-start(bf16[64,8,128]{2,1,0:T(8,128)(2,1)S(1)} %dynamic-slice_convert_fusion), channel_id=1, source_target_pairs={{0,64},{64,0},{1,65},{65,1},{2,66},{66,2},{3,67},{67,3},{4,68},{68... | collective-permute-start | bytes 393224 | tf_op jit(solution)/shard_map/ppermute | solution.py:176
  310.0 24.4 %collective-permute-done.15 = bf16[64,8,128]{2,1,0:T(8,128)(2,1)S(1)} collective-permute-done((bf16[64,8,128]{2,1,0:T(8,128)(2,1)S(1)}, bf16[64,8,128]{2,1,0:T(8,128)(2,1)S(1)}, u32[]{:S(2)}, u32[]{:S(2)}) %collective-permute-start.15) | collective-permute-done | bytes 131104 | tf_op jit(solution)/shard_map/ppermute | solution.py:176
  335.2 7.2 %all-to-all-done.3 = bf16[32,128,128]{2,1,0:T(8,128)(2,1)S(1)} async-done(((bf16[32,128,128]{2,1,0:T(8,128)(2,1)}), bf16[32,128,128]{2,1,0:T(8,128)(2,1)S(1)}, u32[]{:S(2)}, u32[]{:S(2)}) %all-to-all-start.3) | async-done | bytes 1048608 | tf_op jit(solution)/shard_map/all_to_all | solution.py:209
  342.4 1.4 broadcast_select_fusion.2
  343.8 1.0 copy.25
  344.8 1.0 copy.26
  (59 shorter events, 3.1 us)
Async XLA Ops:
  1.6 24.4 %collective-permute-start = (bf16[64,8,128]{2,1,0:T(8,128)(2,1)S(1)}, bf16[64,8,128]{2,1,0:T(8,128)(2,1)S(1)}, u32[]{:S(2)}, u32[]{:S(2)}) collective-permute-start(bf16[64,8,128]{2,1,0:T(8,128)(2,1)S(1)} %bitcast.60), channel_id=1, source_target_pairs={{0,96},{32,64},{64,32},{96,0},{1,97},{33,65},{65,33},{97,1},{2,98}... | collective-permute-start | bytes 393224 | tf_op jit(solution)/shard_map/ppermute | solution.py:180
  26.0 45.4 %all-to-all-start = ((bf16[32,128,128]{2,1,0:T(8,128)(2,1)}), bf16[32,128,128]{2,1,0:T(8,128)(2,1)S(1)}, u32[]{:S(2)}, u32[]{:S(2)}) async-start(bf16[32,128,128]{2,1,0:T(8,128)(2,1)} %bitcast.4), calls=%async_computation | async-start | bytes 2097152 | tf_op jit(solution)/shard_map/all_to_all | solution.py:209
  33.6 22.8 %collective-permute-start.1 = (bf16[2,64,8,128]{3,2,1,0:T(8,128)(2,1)S(1)}, bf16[2,64,8,128]{3,2,1,0:T(8,128)(2,1)S(1)}, u32[]{:S(2)}, u32[]{:S(2)}) collective-permute-start(bf16[2,64,8,128]{3,2,1,0:T(8,128)(2,1)S(1)} %pad_maximum_fusion.2), channel_id=1, source_target_pairs={{0,32},{32,0},{1,33},{33,1},{2,34},{34,2},{3,35},{35,3},{4,36},{36... | collective-permute-start | bytes 786440 | tf_op jit(solution)/shard_map/ppermute | solution.py:176
  39.1 52.2 %copy-start.6 = (bf16[256,256]{1,0:T(8,128)(2,1)S(1)}, bf16[256,256]{1,0:T(8,128)(2,1)}, u32[]{:S(2)}) copy-start(bf16[256,256]{1,0:T(8,128)(2,1)} %constant.85.clone.fast_fwd) | copy-start | bytes 393220
  39.1 52.2 %copy-start.7 = (bf16[2,160,32]{2,1,0:T(8,128)(2,1)S(1)}, bf16[2,160,32]{2,1,0:T(8,128)(2,1)}, u32[]{:S(2)}) copy-start(bf16[2,160,32]{2,1,0:T(8,128)(2,1)} %constant.81.clone.near.far) | copy-start | bytes 61444
  39.1 52.2 %copy-start.8 = (f32[2,80,128]{2,1,0:T(8,128)S(1)}, f32[2,80,128]{2,1,0:T(8,128)}, u32[]{:S(2)}) copy-start(f32[2,80,128]{2,1,0:T(8,128)} %constant.87.clone.twid) | copy-start | bytes 245764
  71.4 17.9 %copy-start.19 = (bf16[32,128,128]{2,1,0:T(8,128)(2,1)}, bf16[32,128,128]{2,1,0:T(8,128)(2,1)S(1)}, u32[]{:S(2)}) copy-start(bf16[32,128,128]{2,1,0:T(8,128)(2,1)S(1)} %all-to-all-done) | copy-start | bytes 3145732
  71.4 33.3 %all-to-all-start.1 = ((bf16[32,128,128]{2,1,0:T(8,128)(2,1)}), bf16[32,128,128]{2,1,0:T(8,128)(2,1)}, u32[]{:S(2)}, u32[]{:S(2)}) async-start(bf16[32,128,128]{2,1,0:T(8,128)(2,1)} %bitcast.7), calls=%async_computation.1 | async-start | bytes 2097152 | tf_op jit(solution)/shard_map/all_to_all | solution.py:209
  78.2 11.1 %copy-start.20 = (bf16[64,16,128]{2,1,0:T(8,128)(2,1)}, bf16[64,16,128]{2,1,0:T(8,128)(2,1)S(1)}, u32[]{:S(2)}) copy-start(bf16[64,16,128]{2,1,0:T(8,128)(2,1)S(1)} %get-tuple-element.53) | copy-start | bytes 786436
  79.1 45.2 %collective-permute-start.10 = (bf16[128,16,128]{2,1,0:T(8,128)(2,1)}, bf16[128,16,128]{2,1,0:T(8,128)(2,1)}, u32[]{:S(2)}, u32[]{:S(2)}) collective-permute-start(bf16[128,16,128]{2,1,0:T(8,128)(2,1)} %pad_maximum_fusion.1), channel_id=1, source_target_pairs={{0,384},{128,0},{256,128},{384,256},{1,385},{129,1},{257,129},{385... | collective-permute-start | bytes 1572872 | tf_op jit(solution)/shard_map/ppermute | solution.py:203
  83.7 44.6 %collective-permute-start.8 = (bf16[128,16,128]{2,1,0:T(8,128)(2,1)}, bf16[128,16,128]{2,1,0:T(8,128)(2,1)}, u32[]{:S(2)}, u32[]{:S(2)}) collective-permute-start(bf16[128,16,128]{2,1,0:T(8,128)(2,1)} %pad_maximum_fusion.1), channel_id=1, source_target_pairs={{0,128},{128,256},{256,384},{384,0},{1,129},{129,257},{257,385},{3... | collective-permute-start | bytes 1572872 | tf_op jit(solution)/shard_map/ppermute | solution.py:203
  85.6 46.6 %collective-permute-start.9 = (bf16[128,16,128]{2,1,0:T(8,128)(2,1)}, bf16[128,16,128]{2,1,0:T(8,128)(2,1)}, u32[]{:S(2)}, u32[]{:S(2)}) collective-permute-start(bf16[128,16,128]{2,1,0:T(8,128)(2,1)} %pad_maximum_fusion.1), channel_id=1, source_target_pairs={{0,256},{128,384},{256,0},{384,128},{1,257},{129,385},{257,1},{385... | collective-permute-start | bytes 1572872 | tf_op jit(solution)/shard_map/ppermute | solution.py:203
  91.3 15.2 %copy-start.9 = (bf16[256,256]{1,0:T(8,128)(2,1)S(1)}, bf16[256,256]{1,0:T(8,128)(2,1)}, u32[]{:S(2)}) copy-start(bf16[256,256]{1,0:T(8,128)(2,1)} %constant.86.clone.fast_inv) | copy-start | bytes 393220
  91.3 15.2 %copy-start.14 = (bf16[2,32,160]{2,1,0:T(8,128)(2,1)S(1)}, bf16[2,32,160]{2,1,0:T(8,128)(2,1)}, u32[]{:S(2)}) copy-start(bf16[2,32,160]{2,1,0:T(8,128)(2,1)} %constant.83.clone.slow_out) | copy-start | bytes 61444
  98.6 2.3 copy-start
  106.5 2.5 copy-start.1
  109.0 28.5 %copy-start.21 = (bf16[64,16,128]{2,1,0:T(8,128)(2,1)S(1)}, bf16[64,16,128]{2,1,0:T(8,128)(2,1)}, u32[]{:S(2)}) copy-start(bf16[64,16,128]{2,1,0:T(8,128)(2,1)} %copy-done.20) | copy-start | bytes 786436
  109.0 31.8 %slice-start = ((s8[5242880]{0:T(1024)(128)(4,1)}), s8[4194304]{0:T(1024)(128)(4,1)S(1)}, s32[]{:S(2)}) async-start(s8[5242880]{0:T(1024)(128)(4,1)} %bitcast.49), calls=%async_computation.4 | async-start | bytes 8388608
  115.5 25.3 %slice-start.1 = ((s8[5242880]{0:T(1024)(128)(4,1)}), s8[1048576]{0:T(1024)(128)(4,1)S(1)}, s32[]{:S(2)}) async-start(s8[5242880]{0:T(1024)(128)(4,1)} %bitcast.49), calls=%async_computation.5 | async-start | bytes 2097152
  115.5 25.3 %copy-start.15 = (bf16[4,160,64]{2,1,0:T(8,128)(2,1)S(1)}, bf16[4,160,64]{2,1,0:T(8,128)(2,1)}, u32[]{:S(2)}) copy-start(bf16[4,160,64]{2,1,0:T(8,128)(2,1)} %constant.82.clone.taps_table) | copy-start | bytes 245764
  116.5 47.2 %collective-permute-start.4 = (bf16[64,16,128]{2,1,0:T(8,128)(2,1)}, bf16[64,16,128]{2,1,0:T(8,128)(2,1)}, u32[]{:S(2)}, u32[]{:S(2)}) collective-permute-start(bf16[64,16,128]{2,1,0:T(8,128)(2,1)} %get-tuple-element.54), channel_id=1, source_target_pairs={{0,128},{128,256},{256,384},{384,0},{1,129},{129,257},{257,385},{3... | collective-permute-start | bytes 786440 | tf_op jit(solution)/shard_map/ppermute | solution.py:203
  119.7 44.0 %collective-permute-start.5 = (bf16[64,16,128]{2,1,0:T(8,128)(2,1)}, bf16[64,16,128]{2,1,0:T(8,128)(2,1)}, u32[]{:S(2)}, u32[]{:S(2)}) collective-permute-start(bf16[64,16,128]{2,1,0:T(8,128)(2,1)} %get-tuple-element.56), channel_id=1, source_target_pairs={{0,256},{128,384},{256,0},{384,128},{1,257},{129,385},{257,1},{385... | collective-permute-start | bytes 786440 | tf_op jit(solution)/shard_map/ppermute | solution.py:203
  124.3 39.5 %collective-permute-start.6 = (bf16[64,16,128]{2,1,0:T(8,128)(2,1)}, bf16[64,16,128]{2,1,0:T(8,128)(2,1)}, u32[]{:S(2)}, u32[]{:S(2)}) collective-permute-start(bf16[64,16,128]{2,1,0:T(8,128)(2,1)} %get-tuple-element.55), channel_id=1, source_target_pairs={{0,384},{128,0},{256,128},{384,256},{1,385},{129,1},{257,129},{385... | collective-permute-start | bytes 786440 | tf_op jit(solution)/shard_map/ppermute | solution.py:203
  128.3 74.1 %collective-permute-start.2 = (bf16[64,32,128]{2,1,0:T(8,128)(2,1)}, bf16[64,32,128]{2,1,0:T(8,128)(2,1)S(1)}, u32[]{:S(2)}, u32[]{:S(2)}) collective-permute-start(bf16[64,32,128]{2,1,0:T(8,128)(2,1)} %get-tuple-element.51), channel_id=1, source_target_pairs={{0,32},{32,0},{1,33},{33,1},{2,34},{34,2},{3,35},{35,3},{4,36},{36... | collective-permute-start | bytes 1572872 | tf_op jit(solution)/shard_map/ppermute | solution.py:176
  132.2 93.7 %collective-permute-start.3 = (bf16[64,32,128]{2,1,0:T(8,128)(2,1)}, bf16[64,32,128]{2,1,0:T(8,128)(2,1)S(1)}, u32[]{:S(2)}, u32[]{:S(2)}) collective-permute-start(bf16[64,32,128]{2,1,0:T(8,128)(2,1)} %get-tuple-element.50), channel_id=1, source_target_pairs={{0,32},{32,0},{1,33},{33,1},{2,34},{34,2},{3,35},{35,3},{4,36},{36... | collective-permute-start | bytes 1572872 | tf_op jit(solution)/shard_map/ppermute | solution.py:176
  153.3 2.4 copy-start.3
  155.7 94.3 %copy-start.16 = (bf16[64,160]{1,0:T(8,128)(2,1)S(1)}, bf16[64,160]{1,0:T(8,128)(2,1)}, u32[]{:S(2)}) copy-start(bf16[64,160]{1,0:T(8,128)(2,1)} %constant.84.clone.out_full) | copy-start | bytes 61444
  157.0 141.7 %all-to-all-start.2 = ((bf16[32,128,128]{2,1,0:T(8,128)(2,1)}), bf16[32,128,128]{2,1,0:T(8,128)(2,1)}, u32[]{:S(2)}, u32[]{:S(2)}) async-start(bf16[32,128,128]{2,1,0:T(8,128)(2,1)} %copy.23), calls=%async_computation.2 | async-start | bytes 2097152 | tf_op jit(solution)/shard_map/all_to_all | solution.py:209
  165.1 84.9 %collective-permute-start.7 = (bf16[64,8,128]{2,1,0:T(8,128)(2,1)S(1)}, bf16[64,8,128]{2,1,0:T(8,128)(2,1)S(1)}, u32[]{:S(2)}, u32[]{:S(2)}) collective-permute-start(bf16[64,8,128]{2,1,0:T(8,128)(2,1)S(1)} %constant_dynamic-slice_fusion.4), channel_id=1, source_target_pairs={{0,96},{32,64},{64,32},{96,0},{1,97},{33,65},{65,33},{97,1},{2,98}... | collective-permute-start | bytes 393224 | tf_op jit(solution)/shard_map/ppermute | solution.py:180
  202.4 0.8 copy-start.10
  225.9 0.8 copy-start.17
  250.0 2.5 copy-start.2
  252.5 2.5 copy-start.4
  255.0 1.0 copy-start.11
  265.6 0.8 copy-start.12
  267.3 16.5 %collective-permute-start.11 = (bf16[64,16,128]{2,1,0:T(8,128)(2,1)}, bf16[64,16,128]{2,1,0:T(8,128)(2,1)}, u32[]{:S(2)}, u32[]{:S(2)}) collective-permute-start(bf16[64,16,128]{2,1,0:T(8,128)(2,1)} %get-tuple-element.45), channel_id=1, source_target_pairs={{0,128},{128,256},{256,384},{384,0},{1,129},{129,257},{257,385},{3... | collective-permute-start | bytes 786440 | tf_op jit(solution)/shard_map/ppermute | solution.py:203
  269.6 14.2 %collective-permute-start.12 = (bf16[64,16,128]{2,1,0:T(8,128)(2,1)S(1)}, bf16[64,16,128]{2,1,0:T(8,128)(2,1)}, u32[]{:S(2)}, u32[]{:S(2)}) collective-permute-start(bf16[64,16,128]{2,1,0:T(8,128)(2,1)S(1)} %get-tuple-element.47), channel_id=1, source_target_pairs={{0,256},{128,384},{256,0},{384,128},{1,257},{129,385},{257,1},{385... | collective-permute-start | bytes 786440 | tf_op jit(solution)/shard_map/ppermute | solution.py:203
  272.3 13.5 %collective-permute-start.13 = (bf16[64,16,128]{2,1,0:T(8,128)(2,1)S(1)}, bf16[64,16,128]{2,1,0:T(8,128)(2,1)}, u32[]{:S(2)}, u32[]{:S(2)}) collective-permute-start(bf16[64,16,128]{2,1,0:T(8,128)(2,1)S(1)} %get-tuple-element.46), channel_id=1, source_target_pairs={{0,384},{128,0},{256,128},{384,256},{1,385},{129,1},{257,129},{385... | collective-permute-start | bytes 786440 | tf_op jit(solution)/shard_map/ppermute | solution.py:203
  275.9 12.0 %collective-permute-start.14 = (bf16[64,8,128]{2,1,0:T(8,128)(2,1)S(1)}, bf16[64,8,128]{2,1,0:T(8,128)(2,1)S(1)}, u32[]{:S(2)}, u32[]{:S(2)}) collective-permute-start(bf16[64,8,128]{2,1,0:T(8,128)(2,1)S(1)} %constant_dynamic-slice_fusion), channel_id=1, source_target_pairs={{0,32},{32,0},{1,33},{33,1},{2,34},{34,2},{3,35},{35,3},{4,36},{36... | collective-permute-start | bytes 393224 | tf_op jit(solution)/shard_map/ppermute | solution.py:176
  287.8 2.5 copy-start.5
  290.3 1.0 copy-start.18
  291.4 7.2 %copy-start.13 = (bf16[64,32,128]{2,1,0:T(8,128)(2,1)S(1)}, bf16[64,32,128]{2,1,0:T(8,128)(2,1)}, u32[]{:S(2)}) copy-start(bf16[64,32,128]{2,1,0:T(8,128)(2,1)} %copy-done.12) | copy-start | bytes 1572868
  300.1 42.3 %all-to-all-start.3 = ((bf16[32,128,128]{2,1,0:T(8,128)(2,1)}), bf16[32,128,128]{2,1,0:T(8,128)(2,1)S(1)}, u32[]{:S(2)}, u32[]{:S(2)}) async-start(bf16[32,128,128]{2,1,0:T(8,128)(2,1)} %copy.24), calls=%async_computation.3 | async-start | bytes 2097152 | tf_op jit(solution)/shard_map/all_to_all | solution.py:209
  304.5 29.9 %collective-permute-start.15 = (bf16[64,8,128]{2,1,0:T(8,128)(2,1)S(1)}, bf16[64,8,128]{2,1,0:T(8,128)(2,1)S(1)}, u32[]{:S(2)}, u32[]{:S(2)}) collective-permute-start(bf16[64,8,128]{2,1,0:T(8,128)(2,1)S(1)} %dynamic-slice_convert_fusion), channel_id=1, source_target_pairs={{0,64},{64,0},{1,65},{65,1},{2,66},{66,2},{3,67},{67,3},{4,68},{68... | collective-permute-start | bytes 393224 | tf_op jit(solution)/shard_map/ppermute | solution.py:176

commit v8 on v1

--- a/solution.py
+++ b/solution.py
@@ -45,6 +45,11 @@
     return tuple(map(np.ascontiguousarray, (slow_fwd, slow_inv, fast_fwd, fast_inv, twid)))
 
 
+def turned(places):
+    blocks = np.split(tables()[0], places, axis=1)
+    return np.stack([np.concatenate([blocks[(y - k) % places] for k in range(places)], axis=1) for y in range(places)])
+
+
 def dot(left, right):
     return jnp.dot(left, right, preferred_element_type=jnp.float32)
 
@@ -82,12 +87,14 @@
     return jnp.concatenate([real, imag], axis=1).astype(jnp.bfloat16)
 
 
-def conv_kernel(values, taps, slow_fwd, slow_inv, fast_fwd, fast_inv, twid, u_out, k_out, conv):
+def spectra_kernel(taps, slow_fwd, slow_inv, fast_fwd, fast_inv, twid, k_out):
+    k_out[...] = forward(taps, slow_fwd, twid, fast_fwd)
+
+
+def conv_kernel(values, k_in, slow_fwd, slow_inv, fast_fwd, fast_inv, twid, u_out, conv):
     u_spec = forward(values, slow_fwd, twid, fast_fwd)
-    k_spec = forward(taps, slow_fwd, twid, fast_fwd)
     u_out[...] = u_spec
-    k_out[...] = k_spec
-    (ur, ui), (kr, ki) = halves(u_spec), halves(k_spec)
+    (ur, ui), (kr, ki) = halves(u_spec), halves(k_in[...])
     inverse(joined(ur * kr - ui * ki, ur * ki + ui * kr), conv, slow_inv, twid, fast_inv)
 
 
@@ -103,11 +110,11 @@
     inverse(joined(kr * zr + ki * zi, kr * zi - ki * zr), back, slow_inv, twid, fast_inv)
 
 
-def call(kernel, signals, outs, consts, flops):
-    chans = max(item.shape[0] for item, kind in signals if kind == "x") if any(
-        kind == "x" for _, kind in signals
-    ) else signals[0][0].shape[0] // ROWS
+def call(kernel, signals, outs, consts, start=0):
+    item, kind = signals[-1]
+    chans = item.shape[0] // ROWS if kind == "s" else item.shape[0]
     specs = {
+        "y": pl.BlockSpec((BLOCK, HALF, FAST), lambda i: (start // BLOCK + i, 0, 0)),
         "x": pl.BlockSpec((BLOCK, HALF, FAST), lambda i: (i, 0, 0)),
         "s": pl.BlockSpec((BLOCK * ROWS, 2 * FAST), lambda i: (i, 0)),
     }
@@ -116,15 +123,14 @@
         "s": jax.ShapeDtypeStruct((chans * ROWS, 2 * FAST), jnp.bfloat16),
     }
     whole = [pl.BlockSpec(item.shape, functools.partial(lambda n, i: (0,) * n, item.ndim)) for item in consts]
-    moved = sum(item.size * 2 for item, _ in signals) + sum(shapes[kind].size * 2 for kind in outs)
     return pl.pallas_call(
         kernel,
         grid=(chans // BLOCK,),
         in_specs=[specs[kind] for _, kind in signals] + whole,
         out_specs=[specs[kind] for kind in outs],
         out_shape=[shapes[kind] for kind in outs],
-        compiler_params=pltpu.CompilerParams(vmem_limit_bytes=40 * 1024 * 1024),
-        cost_estimate=pl.CostEstimate(flops=flops * chans, bytes_accessed=moved, transcendentals=0),
+        compiler_params=pltpu.CompilerParams(vmem_limit_bytes=20 * 1024 * 1024),
+        cost_estimate=pl.CostEstimate(flops=1, bytes_accessed=1, transcendentals=0),
     )(*[item for item, _ in signals], *consts)
 
 
@@ -142,37 +148,41 @@
     n_row = lax.axis_size("y")
     wide = filter_taps.shape[1]
 
-    def inward(item):
-        moved = lax.all_to_all(item.reshape(groups, chans, FAST), ctx, split_axis=0, concat_axis=0, tiled=True)
-        return moved.transpose(1, 0, 2)
+    def move(item):
+        return lax.all_to_all(item, ctx, split_axis=0, concat_axis=0, tiled=True)
 
     def outward(item):
-        moved = lax.all_to_all(item.transpose(1, 0, 2), ctx, split_axis=0, concat_axis=0, tiled=True)
-        return moved.reshape(1, groups * chans, FAST)
+        return move(item.transpose(1, 0, 2)).reshape(1, groups * chans, FAST)
 
-    other = exchange(filter_taps, "zh")
-    pair = jnp.stack([jnp.where(high == 0, filter_taps, other), jnp.where(high == 0, other, filter_taps)])
-    gathered = lax.all_gather(pair, "y", axis=0, tiled=True)
-    taps = gathered.transpose(1, 0, 2).reshape(chans, HALF, FAST)
+    def ring(item, step):
+        return lax.ppermute(item, "y", [(i, (i + step) % n_row) for i in range(n_row)])
 
-    v_mine = inward(values)
-    g_mine = inward(grads)
-    fft = 2 * 2 * ROWS * FAST * (HALF + 2 * FAST)
-    u_spec, k_spec, conv = call(conv_kernel, [(v_mine, "x"), (taps, "x")], "ssx", consts, 3 * fft)
+    blocks = filter_taps.reshape(chans, wide // FAST, FAST)
+    other = exchange(blocks, "zh")
+    pair = jnp.concatenate([jnp.where(high == 0, blocks, other), jnp.where(high == 0, other, blocks)], axis=1)
+    taps = jnp.concatenate([pair] + [ring(pair, step) for step in range(1, n_row)], axis=1)
+    slow_taps = lax.dynamic_index_in_dim(jnp.asarray(turned(n_row)), row, 0, keepdims=False)
+    (k_spec,) = call(spectra_kernel, [(taps, "x")], "s", (slow_taps,) + consts[1:])
+
+    both = jnp.concatenate([values.reshape(groups, chans, FAST), grads.reshape(groups, chans, FAST)], axis=1)
+    mine, k_spec = lax.optimization_barrier((move(both), k_spec))
+    mine = mine.transpose(1, 0, 2)
+    u_spec, conv = call(conv_kernel, [(mine, "x"), (k_spec, "s")], "sx", consts)
     conv_out = outward(conv)
-    z_spec, terms = call(taps_kernel, [(g_mine, "x"), (u_spec, "s")], "sx", consts, 2 * fft)
-    (back,) = call(back_kernel, [(z_spec, "s"), (k_spec, "s")], "x", consts, fft)
+    z_spec, terms = call(taps_kernel, [(mine, "y"), (u_spec, "s")], "sx", consts, chans)
+    (back,) = call(back_kernel, [(z_spec, "s"), (k_spec, "s")], "x", consts)
+
+    depth = HALF // n_row
+    total = None
+    for step in range(n_row):
+        block = lax.dynamic_slice_in_dim(terms, (row + step) % n_row * depth, depth, 1)
+        block = (ring(block, step) if step else block).astype(jnp.float32)
+        total = block if total is None else total + block
+    back, total = lax.optimization_barrier((back, total))
     value_grads = outward(back)
-
-    parts = terms.reshape(chans, n_row, 2, wide).transpose(1, 2, 0, 3)
-    total = lax.dynamic_index_in_dim(parts, row, 0, keepdims=False).astype(jnp.float32)
-    for step in range(1, n_row):
-        block = lax.dynamic_index_in_dim(parts, (row + step) % n_row, 0, keepdims=False)
-        arrived = lax.ppermute(block, "y", [(i, (i + step) % n_row) for i in range(n_row)])
-        total = total + arrived.astype(jnp.float32)
-    mine = jnp.where(high == 0, total[0], total[1])
-    sent = jnp.where(high == 0, total[1], total[0]).astype(jnp.bfloat16)
-    filter_grads = mine + exchange(sent, "zh").astype(jnp.float32)
+    kept = lax.dynamic_slice_in_dim(total, high * (depth // 2), depth // 2, 1)
+    sent = lax.dynamic_slice_in_dim(total, (1 - high) * (depth // 2), depth // 2, 1).astype(jnp.bfloat16)
+    filter_grads = (kept + exchange(sent, "zh").astype(jnp.float32)).reshape(filter_taps.shape)
     return conv_out, value_grads, filter_grads
 
 

time: 336 us -> 298 us (0.89)
  blocking collectives: 68.6 us -> 0 us
  starting transfers between devices: 51.9 us -> 90.5 us
  between operations: 14.4 us -> 1.06 us
  local copies, waits for them, and re-layouts: 18.2 us -> 22.7 us
  waiting for transfers between devices: 163 us -> 159 us
    all_to_all x1 -> x0, blocking collectives: 68.6 us -> none  [inward(): lax.all_to_all(item.reshape(groups, chans, FAST), ctx, split_axis=0, conc...]
    all_gather x1 -> x0, waiting for transfers between devices: 56.4 us -> none  [local(): gathered = lax.all_gather(pair, 'y', axis=0, tiled=True)]
    ppermute x2, waiting for transfers between devices: 33.9 us -> 67.4 us  [exchange(): return lax.ppermute(item, axis, [(0, 1), (1, 0)])]
    all_to_all x3, starting transfers between devices: 30.6 us -> 55.9 us  [move(): return lax.all_to_all(item, ctx, split_axis=0, concat_axis=0, tiled=True)]
    all_to_all x3, waiting for transfers between devices: 60.6 us -> 78.1 us  [move(): return lax.all_to_all(item, ctx, split_axis=0, concat_axis=0, tiled=True)]
    ppermute x3 -> x6, starting transfers between devices: 8.36 us -> 20.5 us  [ring(): lax.ppermute(item, 'y', [(i, (i + step) % n_row) for i in range(n_row)])]
    unnamed x27 -> x34, local copies, waits for them, and re-layouts: 7.88 us -> 14.6 us
    pallas_call x3 -> x4, Pallas kernels: 17.3 us -> 19.2 us  [call(): pl.pallas_call(kernel, grid=(chans // BLOCK,), in_specs=[specs[kind] for...]
  transfers between devices with their start and end apart: 9 -> 11, of which waited for: 8 -> 8; matrix products, arithmetic and copies ran while one was open for 4% -> 2% of each run, Pallas kernels for 5% -> 4%
where the time goes in v8:
time: 298 us; the launch traced here: 297 us
  waiting for transfers between devices  159 us (53%)
  starting transfers between devices  90.5 us (30%)
  local copies, waits for them, and re-layouts  22.7 us (8%)
  Pallas kernels  19.2 us (6%)
  other arithmetic  4.48 us (2%)
    all_to_all x3, waiting for transfers between devices, move(): return lax.all_to_all(item, ctx, split_axis=0, concat_axis=0, tiled=True)  78.1 us
    ppermute x2, waiting for transfers between devices, exchange(): return lax.ppermute(item, axis, [(0, 1), (1, 0)])  67.4 us
    all_to_all x3, starting transfers between devices, move(): return lax.all_to_all(item, ctx, split_axis=0, concat_axis=0, tiled=True)  55.9 us
    ppermute x6, starting transfers between devices, ring(): lax.ppermute(item, 'y', [(i, (i + step) % n_row) for i in range(n_row)])  20.5 us
    pallas_call x4, Pallas kernels, call(): pl.pallas_call(kernel, grid=(chans // BLOCK,), in_specs=[specs[kind] for...  19.2 us
    unnamed x34, local copies, waits for them, and re-layouts  14.6 us
    ppermute x2, starting transfers between devices, exchange(): return lax.ppermute(item, axis, [(0, 1), (1, 0)])  14.1 us
    ppermute x6, waiting for transfers between devices, ring(): lax.ppermute(item, 'y', [(i, (i + step) % n_row) for i in range(n_row)])  13.8 us
  transfers between devices with their start and end apart: 11, of which 8 were waited for; matrix products, arithmetic and copies ran while one was open for 2% of the time, Pallas kernels for 4%

profile of v8, /device:TPU:1, one launch (start us, length us, event | category | flops | bytes accessed | tf_op | source)
XLA Modules:
  0.0 297.2 jit_solution(5018357070497504918)
XLA Ops:
  0.6 3.1 %pad_maximum_fusion = bf16[64,128,128]{2,1,0:T(8,128)(2,1)} fusion(bf16[64,64,128]{2,1,0:T(8,128)(2,1)} %bitcast.25, bf16[64,64,128]{2,1,0:T(8,128)(2,1)} %bitcast.26), kind=kLoop, calls=%fused_computation | loop fusion | flops 4194304 | bytes 4194304 | tf_op jit(solution)/shard_map/concatenate | solution.py:167
  3.7 0.0 copy-start.12
  3.7 17.4 %all-to-all-start = ((bf16[64,128,128]{2,1,0:T(8,128)(2,1)}), bf16[64,128,128]{2,1,0:T(8,128)(2,1)}, u32[]{:S(2)}, u32[]{:S(2)}) async-start(bf16[64,128,128]{2,1,0:T(8,128)(2,1)} %pad_maximum_fusion), calls=%async_computation | async-start | bytes 4194304 | tf_op jit(solution)/shard_map/all_to_all | solution.py:152
  21.1 0.0 copy-start.6
  21.1 0.0 copy-start.7
  21.1 0.0 copy-start.8
  21.1 0.0 copy-start.10
  21.1 0.0 copy-done.12
  21.2 8.1 %collective-permute-start = (bf16[64,8,128]{2,1,0:T(8,128)(2,1)S(1)}, bf16[64,8,128]{2,1,0:T(8,128)(2,1)S(1)}, u32[]{:S(2)}, u32[]{:S(2)}) collective-permute-start(bf16[64,8,128]{2,1,0:T(8,128)(2,1)S(1)} %bitcast.27), channel_id=1, source_target_pairs={{0,64},{64,0},{1,65},{65,1},{2,66},{66,2},{3,67},{67,3},{4,68},{68... | collective-permute-start | bytes 393224 | tf_op jit(solution)/shard_map/ppermute | solution.py:138
  29.2 43.5 %collective-permute-done = bf16[64,8,128]{2,1,0:T(8,128)(2,1)S(1)} collective-permute-done((bf16[64,8,128]{2,1,0:T(8,128)(2,1)S(1)}, bf16[64,8,128]{2,1,0:T(8,128)(2,1)S(1)}, u32[]{:S(2)}, u32[]{:S(2)}) %collective-permute-start) | collective-permute-done | bytes 131104 | tf_op jit(solution)/shard_map/ppermute | solution.py:138
  72.8 3.2 %collective-permute-start.1 = (bf16[64,16,128]{2,1,0:T(8,128)(2,1)S(1)}, bf16[64,16,128]{2,1,0:T(8,128)(2,1)S(1)}, u32[]{:S(2)}, u32[]{:S(2)}) collective-permute-start(bf16[64,16,128]{2,1,0:T(8,128)(2,1)S(1)} %pad_maximum_fusion.1), channel_id=1, source_target_pairs={{0,128},{128,256},{256,384},{384,0},{1,129},{129,257},{257,385},{3... | collective-permute-start | bytes 786440 | tf_op jit(solution)/shard_map/ppermute | solution.py:158
  76.0 0.8 dynamic-slice_bitcast_fusion.slow_fwd
  76.8 4.5 %collective-permute-start.2 = (bf16[64,16,128]{2,1,0:T(8,128)(2,1)S(1)}, bf16[64,16,128]{2,1,0:T(8,128)(2,1)S(1)}, u32[]{:S(2)}, u32[]{:S(2)}) collective-permute-start(bf16[64,16,128]{2,1,0:T(8,128)(2,1)S(1)} %pad_maximum_fusion.1), channel_id=1, source_target_pairs={{0,256},{128,384},{256,0},{384,128},{1,257},{129,385},{257,1},{385... | collective-permute-start | bytes 786440 | tf_op jit(solution)/shard_map/ppermute | solution.py:158
  81.4 3.0 %collective-permute-start.3 = (bf16[64,16,128]{2,1,0:T(8,128)(2,1)S(1)}, bf16[64,16,128]{2,1,0:T(8,128)(2,1)S(1)}, u32[]{:S(2)}, u32[]{:S(2)}) collective-permute-start(bf16[64,16,128]{2,1,0:T(8,128)(2,1)S(1)} %pad_maximum_fusion.1), channel_id=1, source_target_pairs={{0,384},{128,0},{256,128},{384,256},{1,385},{129,1},{257,129},{385... | collective-permute-start | bytes 786440 | tf_op jit(solution)/shard_map/ppermute | solution.py:158
  84.4 0.0 collective-permute-done.1
  84.5 5.4 %collective-permute-done.2 = bf16[64,16,128]{2,1,0:T(8,128)(2,1)S(1)} collective-permute-done((bf16[64,16,128]{2,1,0:T(8,128)(2,1)S(1)}, bf16[64,16,128]{2,1,0:T(8,128)(2,1)S(1)}, u32[]{:S(2)}, u32[]{:S(2)}) %collective-permute-start.2) | collective-permute-done | bytes 262176 | tf_op jit(solution)/shard_map/ppermute | solution.py:158
  89.9 1.8 collective-permute-done.3
  91.8 0.0 copy-done.6
  91.8 0.0 copy-done.7
  91.8 0.0 copy-done.8
  91.8 0.0 copy-done.10
  91.8 3.4 %shard_map.112.k_in = bf16[5120,256]{1,0:T(8,128)(2,1)S(1)} custom-call(bf16[64,64,128]{2,1,0:T(8,128)(2,1)S(1)} %constant_dynamic-update-slice_fusion.taps, bf16[160,64]{1,0:T(8,128)(2,1)S(1)} %dynamic-slice_bitcast_fusion.slow_fwd, bf16[64,160]{1,0:T(8,128)(2,1)S(1)} %copy-done.10, bf16[256,256]{1,0:T(8,128)(2,1)S(1)} %copy-done.6, ...), custom_call_target="tpu_custom_call" | custom-call | flops 1 | bytes 1 | tf_op jit(solution)/shard_map/pallas_call | solution.py:126
  95.2 0.0 copy-start.11
  95.2 32.6 %all-to-all-done = bf16[64,128,128]{2,1,0:T(8,128)(2,1)} async-done(((bf16[64,128,128]{2,1,0:T(8,128)(2,1)}), bf16[64,128,128]{2,1,0:T(8,128)(2,1)}, u32[]{:S(2)}, u32[]{:S(2)}) %all-to-all-start) | async-done | bytes 2097184 | tf_op jit(solution)/shard_map/all_to_all | solution.py:152
  127.8 2.9 copy.23
  130.8 0.0 copy-done.11
  130.8 6.1 %shard_map.113 = (bf16[5120,256]{1,0:T(8,128)(2,1)S(1)}, bf16[64,64,128]{2,1,0:T(8,128)(2,1)S(1)}) custom-call(bf16[128,64,128]{2,1,0:T(8,128)(2,1)S(1)} %bitcast.19, bf16[5120,256]{1,0:T(8,128)(2,1)S(1)} %shard_map.112.k_in, bf16[160,64]{1,0:T(8,128)(2,1)S(1)} %copy-done.11, bf16[64,160]{1,0:T(8,128)(2,1)S(1)} %copy-done.10, ...), custom_call_target="tpu_custom_call" | custom-call | flops 1 | bytes 1 | tf_op jit(solution)/shard_map/pallas_call | solution.py:126
  136.8 0.0 copy-start
  136.8 1.4 copy-done
  138.2 0.0 copy-start.4
  138.2 1.5 copy-done.4
  139.7 1.6 copy.17
  141.4 30.7 %all-to-all-start.1 = ((bf16[64,64,128]{2,1,0:T(8,128)(2,1)}), bf16[64,64,128]{2,1,0:T(8,128)(2,1)}, u32[]{:S(2)}, u32[]{:S(2)}) async-start(bf16[64,64,128]{2,1,0:T(8,128)(2,1)} %copy.17), calls=%async_computation.1 | async-start | bytes 2097152 | tf_op jit(solution)/shard_map/all_to_all | solution.py:152
  172.1 0.0 copy-start.1
  172.1 1.6 copy-done.1
  173.7 0.0 copy-start.5
  173.7 1.7 copy-done.5
  175.4 6.0 %shard_map.114 = (bf16[5120,256]{1,0:T(8,128)(2,1)S(1)}, bf16[64,64,128]{2,1,0:T(8,128)(2,1)S(1)}) custom-call(bf16[128,64,128]{2,1,0:T(8,128)(2,1)S(1)} %bitcast.20, bf16[5120,256]{1,0:T(8,128)(2,1)S(1)} %copy-done.5, bf16[160,64]{1,0:T(8,128)(2,1)S(1)} %copy-done.11, bf16[64,160]{1,0:T(8,128)(2,1)S(1)} %copy-done.10, bf16[256,256]{1,0:T(8,128)(2,1)S(1)} %copy-done.6, ...), custom_call_target="tpu_custom_call" | custom-call | flops 1 | bytes 1 | tf_op jit(solution)/shard_map/pallas_call | solution.py:126
  181.5 0.0 copy-start.2
  181.5 1.5 copy-done.2
  183.0 0.0 copy-start.9
  183.0 1.0 copy-done.9
  184.0 1.0 constant_dynamic-slice_fusion.2
  185.0 4.3 %collective-permute-start.6 = (bf16[64,16,128]{2,1,0:T(8,128)(2,1)}, bf16[64,16,128]{2,1,0:T(8,128)(2,1)}, u32[]{:S(2)}, u32[]{:S(2)}) collective-permute-start(bf16[64,16,128]{2,1,0:T(8,128)(2,1)} %get-tuple-element.20), channel_id=1, source_target_pairs={{0,384},{128,0},{256,128},{384,256},{1,385},{129,1},{257,129},{385... | collective-permute-start | bytes 786440 | tf_op jit(solution)/shard_map/ppermute | solution.py:158
  189.3 3.5 %collective-permute-start.5 = (bf16[64,16,128]{2,1,0:T(8,128)(2,1)}, bf16[64,16,128]{2,1,0:T(8,128)(2,1)}, u32[]{:S(2)}, u32[]{:S(2)}) collective-permute-start(bf16[64,16,128]{2,1,0:T(8,128)(2,1)} %get-tuple-element.21), channel_id=1, source_target_pairs={{0,256},{128,384},{256,0},{384,128},{1,257},{129,385},{257,1},{385... | collective-permute-start | bytes 786440 | tf_op jit(solution)/shard_map/ppermute | solution.py:158
  192.8 1.9 collective-permute-start.4
  194.8 0.0 copy-start.3
  194.8 1.7 copy-done.3
  196.5 3.7 %shard_map.115 = bf16[64,64,128]{2,1,0:T(8,128)(2,1)S(1)} custom-call(bf16[5120,256]{1,0:T(8,128)(2,1)S(1)} %copy-done.3, bf16[5120,256]{1,0:T(8,128)(2,1)S(1)} %shard_map.112.k_in, bf16[160,64]{1,0:T(8,128)(2,1)S(1)} %copy-done.11, bf16[64,160]{1,0:T(8,128)(2,1)S(1)} %copy-done.10, bf16[256,256]{1,0:T(8,128)(2,1)S(1)} %copy-done.6, ...), custom_call_target="tpu_custom_call" | custom-call | flops 1 | bytes 1 | tf_op jit(solution)/shard_map/pallas_call | solution.py:126
  200.2 0.0 collective-permute-done.6
  200.2 0.0 collective-permute-done.5
  200.2 6.6 %collective-permute-done.4 = bf16[64,16,128]{2,1,0:T(8,128)(2,1)} collective-permute-done((bf16[64,16,128]{2,1,0:T(8,128)(2,1)S(1)}, bf16[64,16,128]{2,1,0:T(8,128)(2,1)}, u32[]{:S(2)}, u32[]{:S(2)}) %collective-permute-start.4) | collective-permute-done | bytes 262176 | tf_op jit(solution)/shard_map/ppermute | solution.py:158
  206.8 1.3 convert_add_fusion
  208.1 1.6 copy.18
  209.8 13.7 %all-to-all-done.1 = bf16[64,64,128]{2,1,0:T(8,128)(2,1)} async-done(((bf16[64,64,128]{2,1,0:T(8,128)(2,1)}), bf16[64,64,128]{2,1,0:T(8,128)(2,1)}, u32[]{:S(2)}, u32[]{:S(2)}) %all-to-all-start.1) | async-done | bytes 1048608 | tf_op jit(solution)/shard_map/all_to_all | solution.py:152
  223.4 7.8 %all-to-all-start.2 = ((bf16[64,64,128]{2,1,0:T(8,128)(2,1)}), bf16[64,64,128]{2,1,0:T(8,128)(2,1)S(1)}, u32[]{:S(2)}, u32[]{:S(2)}) async-start(bf16[64,64,128]{2,1,0:T(8,128)(2,1)} %copy.18), calls=%async_computation.2 | async-start | bytes 2097152 | tf_op jit(solution)/shard_map/all_to_all | solution.py:152
  231.3 6.1 %collective-permute-start.7 = (bf16[64,8,128]{2,1,0:T(8,128)(2,1)S(1)}, bf16[64,8,128]{2,1,0:T(8,128)(2,1)S(1)}, u32[]{:S(2)}, u32[]{:S(2)}) collective-permute-start(bf16[64,8,128]{2,1,0:T(8,128)(2,1)S(1)} %dynamic-slice_convert_fusion), channel_id=1, source_target_pairs={{0,64},{64,0},{1,65},{65,1},{2,66},{66,2},{3,67},{67,3},{4,68},{68... | collective-permute-start | bytes 393224 | tf_op jit(solution)/shard_map/ppermute | solution.py:138
  237.4 24.0 %collective-permute-done.7 = bf16[64,8,128]{2,1,0:T(8,128)(2,1)S(1)} collective-permute-done((bf16[64,8,128]{2,1,0:T(8,128)(2,1)S(1)}, bf16[64,8,128]{2,1,0:T(8,128)(2,1)S(1)}, u32[]{:S(2)}, u32[]{:S(2)}) %collective-permute-start.7) | collective-permute-done | bytes 131104 | tf_op jit(solution)/shard_map/ppermute | solution.py:138
  261.4 0.8 copy.24
  262.1 31.8 %all-to-all-done.2 = bf16[64,64,128]{2,1,0:T(8,128)(2,1)S(1)} async-done(((bf16[64,64,128]{2,1,0:T(8,128)(2,1)}), bf16[64,64,128]{2,1,0:T(8,128)(2,1)S(1)}, u32[]{:S(2)}, u32[]{:S(2)}) %all-to-all-start.2) | async-done | bytes 1048608 | tf_op jit(solution)/shard_map/all_to_all | solution.py:152
  294.0 2.3 copy.31
  296.2 1.0 copy.32
  (10 shorter events, 0.3 us)
Async XLA Ops:
  3.7 17.4 %copy-start.12 = (bf16[64,1024]{1,0:T(8,128)(2,1)S(1)}, bf16[64,1024]{1,0:T(8,128)(2,1)}, u32[]{:S(2)}) copy-start(bf16[64,1024]{1,0:T(8,128)(2,1)} %param.11) | copy-start | bytes 393220
  3.7 124.1 %all-to-all-start = ((bf16[64,128,128]{2,1,0:T(8,128)(2,1)}), bf16[64,128,128]{2,1,0:T(8,128)(2,1)}, u32[]{:S(2)}, u32[]{:S(2)}) async-start(bf16[64,128,128]{2,1,0:T(8,128)(2,1)} %pad_maximum_fusion), calls=%async_computation | async-start | bytes 4194304 | tf_op jit(solution)/shard_map/all_to_all | solution.py:152
  21.1 70.7 %copy-start.6 = (bf16[256,256]{1,0:T(8,128)(2,1)S(1)}, bf16[256,256]{1,0:T(8,128)(2,1)}, u32[]{:S(2)}) copy-start(bf16[256,256]{1,0:T(8,128)(2,1)} %constant.67.clone.fast_fwd) | copy-start | bytes 393220
  21.1 70.7 %copy-start.7 = (bf16[256,256]{1,0:T(8,128)(2,1)S(1)}, bf16[256,256]{1,0:T(8,128)(2,1)}, u32[]{:S(2)}) copy-start(bf16[256,256]{1,0:T(8,128)(2,1)} %constant.68.clone.fast_inv) | copy-start | bytes 393220
  21.1 70.7 %copy-start.8 = (f32[2,80,128]{2,1,0:T(8,128)S(1)}, f32[2,80,128]{2,1,0:T(8,128)}, u32[]{:S(2)}) copy-start(f32[2,80,128]{2,1,0:T(8,128)} %constant.69.clone.twid) | copy-start | bytes 245764
  21.1 70.7 %copy-start.10 = (bf16[64,160]{1,0:T(8,128)(2,1)S(1)}, bf16[64,160]{1,0:T(8,128)(2,1)}, u32[]{:S(2)}) copy-start(bf16[64,160]{1,0:T(8,128)(2,1)} %constant.66.clone.slow_inv) | copy-start | bytes 61444
  21.2 51.6 %collective-permute-start = (bf16[64,8,128]{2,1,0:T(8,128)(2,1)S(1)}, bf16[64,8,128]{2,1,0:T(8,128)(2,1)S(1)}, u32[]{:S(2)}, u32[]{:S(2)}) collective-permute-start(bf16[64,8,128]{2,1,0:T(8,128)(2,1)S(1)} %bitcast.27), channel_id=1, source_target_pairs={{0,64},{64,0},{1,65},{65,1},{2,66},{66,2},{3,67},{67,3},{4,68},{68... | collective-permute-start | bytes 393224 | tf_op jit(solution)/shard_map/ppermute | solution.py:138
  72.8 11.6 %collective-permute-start.1 = (bf16[64,16,128]{2,1,0:T(8,128)(2,1)S(1)}, bf16[64,16,128]{2,1,0:T(8,128)(2,1)S(1)}, u32[]{:S(2)}, u32[]{:S(2)}) collective-permute-start(bf16[64,16,128]{2,1,0:T(8,128)(2,1)S(1)} %pad_maximum_fusion.1), channel_id=1, source_target_pairs={{0,128},{128,256},{256,384},{384,0},{1,129},{129,257},{257,385},{3... | collective-permute-start | bytes 786440 | tf_op jit(solution)/shard_map/ppermute | solution.py:158
  76.8 13.0 %collective-permute-start.2 = (bf16[64,16,128]{2,1,0:T(8,128)(2,1)S(1)}, bf16[64,16,128]{2,1,0:T(8,128)(2,1)S(1)}, u32[]{:S(2)}, u32[]{:S(2)}) collective-permute-start(bf16[64,16,128]{2,1,0:T(8,128)(2,1)S(1)} %pad_maximum_fusion.1), channel_id=1, source_target_pairs={{0,256},{128,384},{256,0},{384,128},{1,257},{129,385},{257,1},{385... | collective-permute-start | bytes 786440 | tf_op jit(solution)/shard_map/ppermute | solution.py:158
  81.4 10.3 %collective-permute-start.3 = (bf16[64,16,128]{2,1,0:T(8,128)(2,1)S(1)}, bf16[64,16,128]{2,1,0:T(8,128)(2,1)S(1)}, u32[]{:S(2)}, u32[]{:S(2)}) collective-permute-start(bf16[64,16,128]{2,1,0:T(8,128)(2,1)S(1)} %pad_maximum_fusion.1), channel_id=1, source_target_pairs={{0,384},{128,0},{256,128},{384,256},{1,385},{129,1},{257,129},{385... | collective-permute-start | bytes 786440 | tf_op jit(solution)/shard_map/ppermute | solution.py:158
  95.2 35.5 %copy-start.11 = (bf16[160,64]{1,0:T(8,128)(2,1)S(1)}, bf16[160,64]{1,0:T(8,128)(2,1)}, u32[]{:S(2)}) copy-start(bf16[160,64]{1,0:T(8,128)(2,1)} %constant.65.clone.slow_fwd) | copy-start | bytes 61444
  136.8 1.4 copy-start
  138.2 1.5 copy-start.4
  141.4 82.1 %all-to-all-start.1 = ((bf16[64,64,128]{2,1,0:T(8,128)(2,1)}), bf16[64,64,128]{2,1,0:T(8,128)(2,1)}, u32[]{:S(2)}, u32[]{:S(2)}) async-start(bf16[64,64,128]{2,1,0:T(8,128)(2,1)} %copy.17), calls=%async_computation.1 | async-start | bytes 2097152 | tf_op jit(solution)/shard_map/all_to_all | solution.py:152
  172.1 1.6 copy-start.1
  173.7 1.7 copy-start.5
  181.5 1.5 copy-start.2
  183.0 1.0 copy-start.9
  185.0 15.2 %collective-permute-start.6 = (bf16[64,16,128]{2,1,0:T(8,128)(2,1)}, bf16[64,16,128]{2,1,0:T(8,128)(2,1)}, u32[]{:S(2)}, u32[]{:S(2)}) collective-permute-start(bf16[64,16,128]{2,1,0:T(8,128)(2,1)} %get-tuple-element.20), channel_id=1, source_target_pairs={{0,384},{128,0},{256,128},{384,256},{1,385},{129,1},{257,129},{385... | collective-permute-start | bytes 786440 | tf_op jit(solution)/shard_map/ppermute | solution.py:158
  189.3 10.9 %collective-permute-start.5 = (bf16[64,16,128]{2,1,0:T(8,128)(2,1)}, bf16[64,16,128]{2,1,0:T(8,128)(2,1)}, u32[]{:S(2)}, u32[]{:S(2)}) collective-permute-start(bf16[64,16,128]{2,1,0:T(8,128)(2,1)} %get-tuple-element.21), channel_id=1, source_target_pairs={{0,256},{128,384},{256,0},{384,128},{1,257},{129,385},{257,1},{385... | collective-permute-start | bytes 786440 | tf_op jit(solution)/shard_map/ppermute | solution.py:158
  192.8 14.0 %collective-permute-start.4 = (bf16[64,16,128]{2,1,0:T(8,128)(2,1)S(1)}, bf16[64,16,128]{2,1,0:T(8,128)(2,1)}, u32[]{:S(2)}, u32[]{:S(2)}) collective-permute-start(bf16[64,16,128]{2,1,0:T(8,128)(2,1)S(1)} %get-tuple-element.19), channel_id=1, source_target_pairs={{0,128},{128,256},{256,384},{384,0},{1,129},{129,257},{257,385},{3... | collective-permute-start | bytes 786440 | tf_op jit(solution)/shard_map/ppermute | solution.py:158
  194.8 1.7 copy-start.3
  223.4 70.5 %all-to-all-start.2 = ((bf16[64,64,128]{2,1,0:T(8,128)(2,1)}), bf16[64,64,128]{2,1,0:T(8,128)(2,1)S(1)}, u32[]{:S(2)}, u32[]{:S(2)}) async-start(bf16[64,64,128]{2,1,0:T(8,128)(2,1)} %copy.18), calls=%async_computation.2 | async-start | bytes 2097152 | tf_op jit(solution)/shard_map/all_to_all | solution.py:152
  231.3 30.0 %collective-permute-start.7 = (bf16[64,8,128]{2,1,0:T(8,128)(2,1)S(1)}, bf16[64,8,128]{2,1,0:T(8,128)(2,1)S(1)}, u32[]{:S(2)}, u32[]{:S(2)}) collective-permute-start(bf16[64,8,128]{2,1,0:T(8,128)(2,1)S(1)} %dynamic-slice_convert_fusion), channel_id=1, source_target_pairs={{0,64},{64,0},{1,65},{65,1},{2,66},{66,2},{3,67},{67,3},{4,68},{68... | collective-permute-start | bytes 393224 | tf_op jit(solution)/shard_map/ppermute | solution.py:138

commit v9 on v8

--- a/solution.py
+++ b/solution.py
@@ -91,34 +91,28 @@
     k_out[...] = forward(taps, slow_fwd, twid, fast_fwd)
 
 
-def conv_kernel(values, k_in, slow_fwd, slow_inv, fast_fwd, fast_inv, twid, u_out, conv):
-    u_spec = forward(values, slow_fwd, twid, fast_fwd)
-    u_out[...] = u_spec
-    (ur, ui), (kr, ki) = halves(u_spec), halves(k_in[...])
-    inverse(joined(ur * kr - ui * ki, ur * ki + ui * kr), conv, slow_inv, twid, fast_inv)
-
-
-def taps_kernel(grads, u_in, slow_fwd, slow_inv, fast_fwd, fast_inv, twid, z_out, taps):
-    z_spec = forward(grads, slow_fwd, twid, fast_fwd)
-    z_out[...] = z_spec
-    (ur, ui), (zr, zi) = halves(u_in[...]), halves(z_spec)
+def products_kernel(
+    values, grads, k_in, slow_fwd, slow_inv, fast_fwd, fast_inv, twid, taps, outs
+):
+    ur, ui = halves(forward(values, slow_fwd, twid, fast_fwd))
+    zr, zi = halves(forward(grads, slow_fwd, twid, fast_fwd))
     inverse(joined(ur * zr + ui * zi, ur * zi - ui * zr), taps, slow_inv, twid, fast_inv)
-
-
-def back_kernel(z_in, k_in, slow_fwd, slow_inv, fast_fwd, fast_inv, twid, back):
-    (zr, zi), (kr, ki) = halves(z_in[...]), halves(k_in[...])
-    inverse(joined(kr * zr + ki * zi, kr * zi - ki * zr), back, slow_inv, twid, fast_inv)
+    kr, ki = halves(k_in[...])
+    inverse(joined(ur * kr - ui * ki, ur * ki + ui * kr), outs.at[0], slow_inv, twid, fast_inv)
+    inverse(joined(kr * zr + ki * zi, kr * zi - ki * zr), outs.at[1], slow_inv, twid, fast_inv)
 
 
 def call(kernel, signals, outs, consts, start=0):
     item, kind = signals[-1]
     chans = item.shape[0] // ROWS if kind == "s" else item.shape[0]
     specs = {
+        "w": pl.BlockSpec((2, BLOCK, HALF, FAST), lambda i: (0, i, 0, 0)),
         "y": pl.BlockSpec((BLOCK, HALF, FAST), lambda i: (start // BLOCK + i, 0, 0)),
         "x": pl.BlockSpec((BLOCK, HALF, FAST), lambda i: (i, 0, 0)),
         "s": pl.BlockSpec((BLOCK * ROWS, 2 * FAST), lambda i: (i, 0)),
     }
     shapes = {
+        "w": jax.ShapeDtypeStruct((2, chans, HALF, FAST), jnp.bfloat16),
         "x": jax.ShapeDtypeStruct((chans, HALF, FAST), jnp.bfloat16),
         "s": jax.ShapeDtypeStruct((chans * ROWS, 2 * FAST), jnp.bfloat16),
     }
@@ -151,9 +145,6 @@
     def move(item):
         return lax.all_to_all(item, ctx, split_axis=0, concat_axis=0, tiled=True)
 
-    def outward(item):
-        return move(item.transpose(1, 0, 2)).reshape(1, groups * chans, FAST)
-
     def ring(item, step):
         return lax.ppermute(item, "y", [(i, (i + step) % n_row) for i in range(n_row)])
 
@@ -167,10 +158,10 @@
     both = jnp.concatenate([values.reshape(groups, chans, FAST), grads.reshape(groups, chans, FAST)], axis=1)
     mine, k_spec = lax.optimization_barrier((move(both), k_spec))
     mine = mine.transpose(1, 0, 2)
-    u_spec, conv = call(conv_kernel, [(mine, "x"), (k_spec, "s")], "sx", consts)
-    conv_out = outward(conv)
-    z_spec, terms = call(taps_kernel, [(mine, "y"), (u_spec, "s")], "sx", consts, chans)
-    (back,) = call(back_kernel, [(z_spec, "s"), (k_spec, "s")], "x", consts)
+    terms, outs = call(products_kernel, [(mine, "x"), (mine, "y"), (k_spec, "s")], "xw", consts, chans)
+    arrived = move(outs.reshape(2 * chans, HALF, FAST).transpose(1, 0, 2))
+    conv_out = arrived[:, :chans].reshape(values.shape)
+    value_grads = arrived[:, chans:].reshape(values.shape)
 
     depth = HALF // n_row
     total = None
@@ -178,8 +169,6 @@
         block = lax.dynamic_slice_in_dim(terms, (row + step) % n_row * depth, depth, 1)
         block = (ring(block, step) if step else block).astype(jnp.float32)
         total = block if total is None else total + block
-    back, total = lax.optimization_barrier((back, total))
-    value_grads = outward(back)
     kept = lax.dynamic_slice_in_dim(total, high * (depth // 2), depth // 2, 1)
     sent = lax.dynamic_slice_in_dim(total, (1 - high) * (depth // 2), depth // 2, 1).astype(jnp.bfloat16)
     filter_grads = (kept + exchange(sent, "zh").astype(jnp.float32)).reshape(filter_taps.shape)

time: 298 us -> 286 us (0.960)
  local copies, waits for them, and re-layouts: 22.7 us -> 10.9 us
  waiting for transfers between devices: 159 us -> 168 us
  starting transfers between devices: 90.5 us -> 83.5 us
  Pallas kernels: 19.2 us -> 16 us
    unnamed x34 -> x22, local copies, waits for them, and re-layouts: 14.6 us -> 0.96 us
    all_to_all x3 -> x2, waiting for transfers between devices: 78.1 us -> 87.7 us  [move(): return lax.all_to_all(item, ctx, split_axis=0, concat_axis=0, tiled=True)]
    all_to_all x3 -> x2, starting transfers between devices: 55.9 us -> 48 us  [move(): return lax.all_to_all(item, ctx, split_axis=0, concat_axis=0, tiled=True)]
    transpose x2 -> x0, local copies, waits for them, and re-layouts: 3.3 us -> none  [outward(): return move(item.transpose(1, 0, 2)).reshape(1, groups * chans, FAST)]
    pallas_call x4 -> x2, Pallas kernels: 19.2 us -> 16 us  [call(): pl.pallas_call(kernel, grid=(chans // BLOCK,), in_specs=[specs[kind] for...]
  transfers between devices with their start and end apart: 11 -> 10, of which waited for: 8 -> 9; matrix products, arithmetic and copies ran while one was open for 2% -> 2% of each run, Pallas kernels for 4% -> 1%
where the time goes in v9:
time: 286 us; the launch traced here: 285 us
  waiting for transfers between devices  168 us (59%)
  starting transfers between devices  83.5 us (29%)
  Pallas kernels  16 us (6%)
  local copies, waits for them, and re-layouts  10.9 us (4%)
  other arithmetic  6.13 us (2%)
    all_to_all x2, waiting for transfers between devices, move(): return lax.all_to_all(item, ctx, split_axis=0, concat_axis=0, tiled=True)  87.7 us
    ppermute x2, waiting for transfers between devices, exchange(): return lax.ppermute(item, axis, [(0, 1), (1, 0)])  64.8 us
    all_to_all x2, starting transfers between devices, move(): return lax.all_to_all(item, ctx, split_axis=0, concat_axis=0, tiled=True)  48 us
    ppermute x6, starting transfers between devices, ring(): lax.ppermute(item, 'y', [(i, (i + step) % n_row) for i in range(n_row)])  21.4 us
    pallas_call x2, Pallas kernels, call(): pl.pallas_call(kernel, grid=(chans // BLOCK,), in_specs=[specs[kind] for...  16 us
    ppermute x6, waiting for transfers between devices, ring(): lax.ppermute(item, 'y', [(i, (i + step) % n_row) for i in range(n_row)])  15.1 us
    ppermute x2, starting transfers between devices, exchange(): return lax.ppermute(item, axis, [(0, 1), (1, 0)])  14.1 us
  transfers between devices with their start and end apart: 10, of which 9 were waited for; matrix products, arithmetic and copies ran while one was open for 2% of the time, Pallas kernels for 1%

profile of v9, /device:TPU:1, one launch (start us, length us, event | category | flops | bytes accessed | tf_op | source)
XLA Modules:
  0.0 285.0 jit_solution(12343456467552519199)
XLA Ops:
  0.6 3.1 %pad_maximum_fusion = bf16[64,128,128]{2,1,0:T(8,128)(2,1)} fusion(bf16[64,64,128]{2,1,0:T(8,128)(2,1)} %bitcast.26, bf16[64,64,128]{2,1,0:T(8,128)(2,1)} %bitcast.27), kind=kLoop, calls=%fused_computation | loop fusion | flops 4194304 | bytes 4194304 | tf_op jit(solution)/shard_map/concatenate | solution.py:158
  3.7 0.0 copy-start.7
  3.7 17.4 %all-to-all-start = ((bf16[64,128,128]{2,1,0:T(8,128)(2,1)}), bf16[64,128,128]{2,1,0:T(8,128)(2,1)}, u32[]{:S(2)}, u32[]{:S(2)}) async-start(bf16[64,128,128]{2,1,0:T(8,128)(2,1)} %pad_maximum_fusion), calls=%async_computation | async-start | bytes 4194304 | tf_op jit(solution)/shard_map/all_to_all | solution.py:146
  21.1 0.0 copy-start.2
  21.1 0.0 copy-start.3
  21.1 0.0 copy-start.4
  21.1 0.0 copy-start.5
  21.1 0.0 copy-done.7
  21.2 8.1 %collective-permute-start = (bf16[64,8,128]{2,1,0:T(8,128)(2,1)S(1)}, bf16[64,8,128]{2,1,0:T(8,128)(2,1)S(1)}, u32[]{:S(2)}, u32[]{:S(2)}) collective-permute-start(bf16[64,8,128]{2,1,0:T(8,128)(2,1)S(1)} %bitcast.30), channel_id=1, source_target_pairs={{0,64},{64,0},{1,65},{65,1},{2,66},{66,2},{3,67},{67,3},{4,68},{68... | collective-permute-start | bytes 393224 | tf_op jit(solution)/shard_map/ppermute | solution.py:132
  29.2 43.5 %collective-permute-done = bf16[64,8,128]{2,1,0:T(8,128)(2,1)S(1)} collective-permute-done((bf16[64,8,128]{2,1,0:T(8,128)(2,1)S(1)}, bf16[64,8,128]{2,1,0:T(8,128)(2,1)S(1)}, u32[]{:S(2)}, u32[]{:S(2)}) %collective-permute-start) | collective-permute-done | bytes 131104 | tf_op jit(solution)/shard_map/ppermute | solution.py:132
  72.8 3.2 %collective-permute-start.1 = (bf16[64,16,128]{2,1,0:T(8,128)(2,1)S(1)}, bf16[64,16,128]{2,1,0:T(8,128)(2,1)S(1)}, u32[]{:S(2)}, u32[]{:S(2)}) collective-permute-start(bf16[64,16,128]{2,1,0:T(8,128)(2,1)S(1)} %pad_maximum_fusion.1), channel_id=1, source_target_pairs={{0,128},{128,256},{256,384},{384,0},{1,129},{129,257},{257,385},{3... | collective-permute-start | bytes 786440 | tf_op jit(solution)/shard_map/ppermute | solution.py:149
  76.0 0.8 dynamic-slice_bitcast_fusion.slow_fwd
  76.8 4.5 %collective-permute-start.2 = (bf16[64,16,128]{2,1,0:T(8,128)(2,1)S(1)}, bf16[64,16,128]{2,1,0:T(8,128)(2,1)S(1)}, u32[]{:S(2)}, u32[]{:S(2)}) collective-permute-start(bf16[64,16,128]{2,1,0:T(8,128)(2,1)S(1)} %pad_maximum_fusion.1), channel_id=1, source_target_pairs={{0,256},{128,384},{256,0},{384,128},{1,257},{129,385},{257,1},{385... | collective-permute-start | bytes 786440 | tf_op jit(solution)/shard_map/ppermute | solution.py:149
  81.4 3.0 %collective-permute-start.3 = (bf16[64,16,128]{2,1,0:T(8,128)(2,1)S(1)}, bf16[64,16,128]{2,1,0:T(8,128)(2,1)S(1)}, u32[]{:S(2)}, u32[]{:S(2)}) collective-permute-start(bf16[64,16,128]{2,1,0:T(8,128)(2,1)S(1)} %pad_maximum_fusion.1), channel_id=1, source_target_pairs={{0,384},{128,0},{256,128},{384,256},{1,385},{129,1},{257,129},{385... | collective-permute-start | bytes 786440 | tf_op jit(solution)/shard_map/ppermute | solution.py:149
  84.4 0.0 collective-permute-done.1
  84.5 5.4 %collective-permute-done.2 = bf16[64,16,128]{2,1,0:T(8,128)(2,1)S(1)} collective-permute-done((bf16[64,16,128]{2,1,0:T(8,128)(2,1)S(1)}, bf16[64,16,128]{2,1,0:T(8,128)(2,1)S(1)}, u32[]{:S(2)}, u32[]{:S(2)}) %collective-permute-start.2) | collective-permute-done | bytes 262176 | tf_op jit(solution)/shard_map/ppermute | solution.py:149
  89.9 1.8 collective-permute-done.3
  91.8 0.0 copy-done.2
  91.8 0.0 copy-done.3
  91.8 0.0 copy-done.4
  91.8 0.0 copy-done.5
  91.8 3.4 %shard_map.112.k_in = bf16[5120,256]{1,0:T(8,128)(2,1)S(1)} custom-call(bf16[64,64,128]{2,1,0:T(8,128)(2,1)S(1)} %constant_dynamic-update-slice_fusion.taps, bf16[160,64]{1,0:T(8,128)(2,1)S(1)} %dynamic-slice_bitcast_fusion.slow_fwd, bf16[64,160]{1,0:T(8,128)(2,1)S(1)} %copy-done.5, bf16[256,256]{1,0:T(8,128)(2,1)S(1)} %copy-done.2, ...), custom_call_target="tpu_custom_call" | custom-call | flops 1 | bytes 1 | tf_op jit(solution)/shard_map/pallas_call | solution.py:120
  95.2 0.0 copy-start.6
  95.2 32.6 %all-to-all-done = bf16[64,128,128]{2,1,0:T(8,128)(2,1)} async-done(((bf16[64,128,128]{2,1,0:T(8,128)(2,1)}), bf16[64,128,128]{2,1,0:T(8,128)(2,1)}, u32[]{:S(2)}, u32[]{:S(2)}) %all-to-all-start) | async-done | bytes 2097184 | tf_op jit(solution)/shard_map/all_to_all | solution.py:146
  127.8 2.9 %copy.26 = bf16[64,128,128]{2,0,1:T(8,128)(2,1)S(1)} copy(bf16[64,128,128]{2,1,0:T(8,128)(2,1)} %all-to-all-done) | data formatting | bytes 4194304 | tf_op jit(solution)/shard_map/optimization_barrier | solution.py:159
  130.8 0.0 copy-done.6
  130.8 12.6 %shard_map.113 = (bf16[64,64,128]{2,1,0:T(8,128)(2,1)S(1)}, bf16[2,64,64,128]{3,2,1,0:T(8,128)(2,1)S(1)}) custom-call(bf16[128,64,128]{2,1,0:T(8,128)(2,1)S(1)} %bitcast.21, bf16[128,64,128]{2,1,0:T(8,128)(2,1)S(1)} %bitcast.22, bf16[5120,256]{1,0:T(8,128)(2,1)S(1)} %shard_map.112.k_in, bf16[160,64]{1,0:T(8,128)(2,1)S(1)} %copy-done.6, ...), custom_call_target="tpu_custom_call" | custom-call | flops 1 | bytes 1 | tf_op jit(solution)/shard_map/pallas_call | solution.py:120
  143.3 0.0 copy-start
  143.3 2.7 copy.25
  146.0 0.0 copy-done
  146.0 0.0 copy-start.1
  146.0 30.6 %all-to-all-start.1 = ((bf16[64,128,128]{2,1,0:T(8,128)(2,1)}), bf16[64,128,128]{2,1,0:T(8,128)(2,1)S(1)}, u32[]{:S(2)}, u32[]{:S(2)}) async-start(bf16[64,128,128]{2,1,0:T(8,128)(2,1)} %bitcast.24), calls=%async_computation.1 | async-start | bytes 4194304 | tf_op jit(solution)/shard_map/all_to_all | solution.py:146
  176.7 0.0 copy-done.1
  176.7 1.0 constant_dynamic-slice_fusion.2
  177.7 4.1 %collective-permute-start.4 = (bf16[64,16,128]{2,1,0:T(8,128)(2,1)}, bf16[64,16,128]{2,1,0:T(8,128)(2,1)}, u32[]{:S(2)}, u32[]{:S(2)}) collective-permute-start(bf16[64,16,128]{2,1,0:T(8,128)(2,1)} %get-tuple-element.13), channel_id=1, source_target_pairs={{0,128},{128,256},{256,384},{384,0},{1,129},{129,257},{257,385},{3... | collective-permute-start | bytes 786440 | tf_op jit(solution)/shard_map/ppermute | solution.py:149
  181.8 3.3 %collective-permute-start.5 = (bf16[64,16,128]{2,1,0:T(8,128)(2,1)}, bf16[64,16,128]{2,1,0:T(8,128)(2,1)}, u32[]{:S(2)}, u32[]{:S(2)}) collective-permute-start(bf16[64,16,128]{2,1,0:T(8,128)(2,1)} %get-tuple-element.15), channel_id=1, source_target_pairs={{0,256},{128,384},{256,0},{384,128},{1,257},{129,385},{257,1},{385... | collective-permute-start | bytes 786440 | tf_op jit(solution)/shard_map/ppermute | solution.py:149
  185.1 3.3 %collective-permute-start.6 = (bf16[64,16,128]{2,1,0:T(8,128)(2,1)S(1)}, bf16[64,16,128]{2,1,0:T(8,128)(2,1)}, u32[]{:S(2)}, u32[]{:S(2)}) collective-permute-start(bf16[64,16,128]{2,1,0:T(8,128)(2,1)S(1)} %get-tuple-element.14), channel_id=1, source_target_pairs={{0,384},{128,0},{256,128},{384,256},{1,385},{129,1},{257,129},{385... | collective-permute-start | bytes 786440 | tf_op jit(solution)/shard_map/ppermute | solution.py:149
  188.4 0.1 collective-permute-done.4
  188.5 6.5 %collective-permute-done.5 = bf16[64,16,128]{2,1,0:T(8,128)(2,1)} collective-permute-done((bf16[64,16,128]{2,1,0:T(8,128)(2,1)}, bf16[64,16,128]{2,1,0:T(8,128)(2,1)}, u32[]{:S(2)}, u32[]{:S(2)}) %collective-permute-start.5) | collective-permute-done | bytes 262176 | tf_op jit(solution)/shard_map/ppermute | solution.py:149
  195.1 1.3 collective-permute-done.6
  196.3 2.0 convert_add_fusion
  198.3 1.0 dynamic-slice_convert_fusion
  199.3 6.1 %collective-permute-start.7 = (bf16[64,8,128]{2,1,0:T(8,128)(2,1)S(1)}, bf16[64,8,128]{2,1,0:T(8,128)(2,1)S(1)}, u32[]{:S(2)}, u32[]{:S(2)}) collective-permute-start(bf16[64,8,128]{2,1,0:T(8,128)(2,1)S(1)} %dynamic-slice_convert_fusion), channel_id=1, source_target_pairs={{0,64},{64,0},{1,65},{65,1},{2,66},{66,2},{3,67},{67,3},{4,68},{68... | collective-permute-start | bytes 393224 | tf_op jit(solution)/shard_map/ppermute | solution.py:132
  205.4 21.3 %collective-permute-done.7 = bf16[64,8,128]{2,1,0:T(8,128)(2,1)S(1)} collective-permute-done((bf16[64,8,128]{2,1,0:T(8,128)(2,1)S(1)}, bf16[64,8,128]{2,1,0:T(8,128)(2,1)S(1)}, u32[]{:S(2)}, u32[]{:S(2)}) %collective-permute-start.7) | collective-permute-done | bytes 131104 | tf_op jit(solution)/shard_map/ppermute | solution.py:132
  226.7 1.0 convert_add_fusion.1
  227.6 0.8 copy.27
  228.4 55.1 %all-to-all-done.1 = bf16[64,128,128]{2,1,0:T(8,128)(2,1)S(1)} async-done(((bf16[64,128,128]{2,1,0:T(8,128)(2,1)}), bf16[64,128,128]{2,1,0:T(8,128)(2,1)S(1)}, u32[]{:S(2)}, u32[]{:S(2)}) %all-to-all-start.1) | async-done | bytes 2097184 | tf_op jit(solution)/shard_map/all_to_all | solution.py:146
  283.5 1.5 fusion
  (8 shorter events, 0.3 us)
Async XLA Ops:
  3.7 17.4 %copy-start.7 = (bf16[64,1024]{1,0:T(8,128)(2,1)S(1)}, bf16[64,1024]{1,0:T(8,128)(2,1)}, u32[]{:S(2)}) copy-start(bf16[64,1024]{1,0:T(8,128)(2,1)} %param.11) | copy-start | bytes 393220
  3.7 124.1 %all-to-all-start = ((bf16[64,128,128]{2,1,0:T(8,128)(2,1)}), bf16[64,128,128]{2,1,0:T(8,128)(2,1)}, u32[]{:S(2)}, u32[]{:S(2)}) async-start(bf16[64,128,128]{2,1,0:T(8,128)(2,1)} %pad_maximum_fusion), calls=%async_computation | async-start | bytes 4194304 | tf_op jit(solution)/shard_map/all_to_all | solution.py:146
  21.1 70.7 %copy-start.2 = (bf16[256,256]{1,0:T(8,128)(2,1)S(1)}, bf16[256,256]{1,0:T(8,128)(2,1)}, u32[]{:S(2)}) copy-start(bf16[256,256]{1,0:T(8,128)(2,1)} %constant.67.clone.fast_fwd) | copy-start | bytes 393220
  21.1 70.7 %copy-start.3 = (bf16[256,256]{1,0:T(8,128)(2,1)S(1)}, bf16[256,256]{1,0:T(8,128)(2,1)}, u32[]{:S(2)}) copy-start(bf16[256,256]{1,0:T(8,128)(2,1)} %constant.68.clone.fast_inv) | copy-start | bytes 393220
  21.1 70.7 %copy-start.4 = (f32[2,80,128]{2,1,0:T(8,128)S(1)}, f32[2,80,128]{2,1,0:T(8,128)}, u32[]{:S(2)}) copy-start(f32[2,80,128]{2,1,0:T(8,128)} %constant.69.clone.twid) | copy-start | bytes 245764
  21.1 70.7 %copy-start.5 = (bf16[64,160]{1,0:T(8,128)(2,1)S(1)}, bf16[64,160]{1,0:T(8,128)(2,1)}, u32[]{:S(2)}) copy-start(bf16[64,160]{1,0:T(8,128)(2,1)} %constant.66.clone.slow_inv) | copy-start | bytes 61444
  21.2 51.6 %collective-permute-start = (bf16[64,8,128]{2,1,0:T(8,128)(2,1)S(1)}, bf16[64,8,128]{2,1,0:T(8,128)(2,1)S(1)}, u32[]{:S(2)}, u32[]{:S(2)}) collective-permute-start(bf16[64,8,128]{2,1,0:T(8,128)(2,1)S(1)} %bitcast.30), channel_id=1, source_target_pairs={{0,64},{64,0},{1,65},{65,1},{2,66},{66,2},{3,67},{67,3},{4,68},{68... | collective-permute-start | bytes 393224 | tf_op jit(solution)/shard_map/ppermute | solution.py:132
  72.8 11.6 %collective-permute-start.1 = (bf16[64,16,128]{2,1,0:T(8,128)(2,1)S(1)}, bf16[64,16,128]{2,1,0:T(8,128)(2,1)S(1)}, u32[]{:S(2)}, u32[]{:S(2)}) collective-permute-start(bf16[64,16,128]{2,1,0:T(8,128)(2,1)S(1)} %pad_maximum_fusion.1), channel_id=1, source_target_pairs={{0,128},{128,256},{256,384},{384,0},{1,129},{129,257},{257,385},{3... | collective-permute-start | bytes 786440 | tf_op jit(solution)/shard_map/ppermute | solution.py:149
  76.8 13.0 %collective-permute-start.2 = (bf16[64,16,128]{2,1,0:T(8,128)(2,1)S(1)}, bf16[64,16,128]{2,1,0:T(8,128)(2,1)S(1)}, u32[]{:S(2)}, u32[]{:S(2)}) collective-permute-start(bf16[64,16,128]{2,1,0:T(8,128)(2,1)S(1)} %pad_maximum_fusion.1), channel_id=1, source_target_pairs={{0,256},{128,384},{256,0},{384,128},{1,257},{129,385},{257,1},{385... | collective-permute-start | bytes 786440 | tf_op jit(solution)/shard_map/ppermute | solution.py:149
  81.4 10.3 %collective-permute-start.3 = (bf16[64,16,128]{2,1,0:T(8,128)(2,1)S(1)}, bf16[64,16,128]{2,1,0:T(8,128)(2,1)S(1)}, u32[]{:S(2)}, u32[]{:S(2)}) collective-permute-start(bf16[64,16,128]{2,1,0:T(8,128)(2,1)S(1)} %pad_maximum_fusion.1), channel_id=1, source_target_pairs={{0,384},{128,0},{256,128},{384,256},{1,385},{129,1},{257,129},{385... | collective-permute-start | bytes 786440 | tf_op jit(solution)/shard_map/ppermute | solution.py:149
  95.2 35.5 %copy-start.6 = (bf16[160,64]{1,0:T(8,128)(2,1)S(1)}, bf16[160,64]{1,0:T(8,128)(2,1)}, u32[]{:S(2)}) copy-start(bf16[160,64]{1,0:T(8,128)(2,1)} %constant.65.clone.slow_fwd) | copy-start | bytes 61444
  143.3 2.7 copy-start
  146.0 30.7 %copy-start.1 = (bf16[64,64,128]{2,1,0:T(8,128)(2,1)S(1)}, bf16[64,64,128]{2,1,0:T(8,128)(2,1)}, u32[]{:S(2)}) copy-start(bf16[64,64,128]{2,1,0:T(8,128)(2,1)} %copy-done) | copy-start | bytes 3145732
  146.0 137.5 %all-to-all-start.1 = ((bf16[64,128,128]{2,1,0:T(8,128)(2,1)}), bf16[64,128,128]{2,1,0:T(8,128)(2,1)S(1)}, u32[]{:S(2)}, u32[]{:S(2)}) async-start(bf16[64,128,128]{2,1,0:T(8,128)(2,1)} %bitcast.24), calls=%async_computation.1 | async-start | bytes 4194304 | tf_op jit(solution)/shard_map/all_to_all | solution.py:146
  177.7 10.8 %collective-permute-start.4 = (bf16[64,16,128]{2,1,0:T(8,128)(2,1)}, bf16[64,16,128]{2,1,0:T(8,128)(2,1)}, u32[]{:S(2)}, u32[]{:S(2)}) collective-permute-start(bf16[64,16,128]{2,1,0:T(8,128)(2,1)} %get-tuple-element.13), channel_id=1, source_target_pairs={{0,128},{128,256},{256,384},{384,0},{1,129},{129,257},{257,385},{3... | collective-permute-start | bytes 786440 | tf_op jit(solution)/shard_map/ppermute | solution.py:149
  181.8 13.2 %collective-permute-start.5 = (bf16[64,16,128]{2,1,0:T(8,128)(2,1)}, bf16[64,16,128]{2,1,0:T(8,128)(2,1)}, u32[]{:S(2)}, u32[]{:S(2)}) collective-permute-start(bf16[64,16,128]{2,1,0:T(8,128)(2,1)} %get-tuple-element.15), channel_id=1, source_target_pairs={{0,256},{128,384},{256,0},{384,128},{1,257},{129,385},{257,1},{385... | collective-permute-start | bytes 786440 | tf_op jit(solution)/shard_map/ppermute | solution.py:149
  185.1 11.2 %collective-permute-start.6 = (bf16[64,16,128]{2,1,0:T(8,128)(2,1)S(1)}, bf16[64,16,128]{2,1,0:T(8,128)(2,1)}, u32[]{:S(2)}, u32[]{:S(2)}) collective-permute-start(bf16[64,16,128]{2,1,0:T(8,128)(2,1)S(1)} %get-tuple-element.14), channel_id=1, source_target_pairs={{0,384},{128,0},{256,128},{384,256},{1,385},{129,1},{257,129},{385... | collective-permute-start | bytes 786440 | tf_op jit(solution)/shard_map/ppermute | solution.py:149
  199.3 27.4 %collective-permute-start.7 = (bf16[64,8,128]{2,1,0:T(8,128)(2,1)S(1)}, bf16[64,8,128]{2,1,0:T(8,128)(2,1)S(1)}, u32[]{:S(2)}, u32[]{:S(2)}) collective-permute-start(bf16[64,8,128]{2,1,0:T(8,128)(2,1)S(1)} %dynamic-slice_convert_fusion), channel_id=1, source_target_pairs={{0,64},{64,0},{1,65},{65,1},{2,66},{66,2},{3,67},{67,3},{4,68},{68... | collective-permute-start | bytes 393224 | tf_op jit(solution)/shard_map/ppermute | solution.py:132

commit v10 on v9

--- a/solution.py
+++ b/solution.py
@@ -16,6 +16,7 @@
 ROWS = 80
 FACTOR = 1.0 / (TOTAL * math.sqrt(TOTAL // 2))
 BLOCK = 8
+BESIDE = 80 * 10**9
 
 
 def tables():
@@ -102,7 +103,7 @@
     inverse(joined(kr * zr + ki * zi, kr * zi - ki * zr), outs.at[1], slow_inv, twid, fast_inv)
 
 
-def call(kernel, signals, outs, consts, start=0):
+def call(kernel, signals, outs, consts, start=0, flops=1):
     item, kind = signals[-1]
     chans = item.shape[0] // ROWS if kind == "s" else item.shape[0]
     specs = {
@@ -124,7 +125,7 @@
         out_specs=[specs[kind] for kind in outs],
         out_shape=[shapes[kind] for kind in outs],
         compiler_params=pltpu.CompilerParams(vmem_limit_bytes=20 * 1024 * 1024),
-        cost_estimate=pl.CostEstimate(flops=1, bytes_accessed=1, transcendentals=0),
+        cost_estimate=pl.CostEstimate(flops=flops, bytes_accessed=1, transcendentals=0),
     )(*[item for item, _ in signals], *consts)
 
 
@@ -153,7 +154,7 @@
     pair = jnp.concatenate([jnp.where(high == 0, blocks, other), jnp.where(high == 0, other, blocks)], axis=1)
     taps = jnp.concatenate([pair] + [ring(pair, step) for step in range(1, n_row)], axis=1)
     slow_taps = lax.dynamic_index_in_dim(jnp.asarray(turned(n_row)), row, 0, keepdims=False)
-    (k_spec,) = call(spectra_kernel, [(taps, "x")], "s", (slow_taps,) + consts[1:])
+    (k_spec,) = call(spectra_kernel, [(taps, "x")], "s", (slow_taps,) + consts[1:], flops=BESIDE)
 
     both = jnp.concatenate([values.reshape(groups, chans, FAST), grads.reshape(groups, chans, FAST)], axis=1)
     mine, k_spec = lax.optimization_barrier((move(both), k_spec))

time: 286 us -> 262 us (0.916)
  starting transfers between devices: 83.5 us -> 62.8 us
  waiting for transfers between devices: 168 us -> 163 us
    ppermute x2, waiting for transfers between devices: 64.8 us -> 21.1 us  [exchange(): return lax.ppermute(item, axis, [(0, 1), (1, 0)])]
    all_to_all x2, waiting for transfers between devices: 87.7 us -> 127 us  [move(): return lax.all_to_all(item, ctx, split_axis=0, concat_axis=0, tiled=True)]
    all_to_all x2, starting transfers between devices: 48 us -> 17.9 us  [move(): return lax.all_to_all(item, ctx, split_axis=0, concat_axis=0, tiled=True)]
    ppermute x2, starting transfers between devices: 14.1 us -> 23.3 us  [exchange(): return lax.ppermute(item, axis, [(0, 1), (1, 0)])]
  transfers between devices with their start and end apart: 10 -> 10, of which waited for: 9 -> 8; matrix products, arithmetic and copies ran while one was open for 2% -> 4% of each run, Pallas kernels for 1% -> 1%
where the time goes in v10:
time: 262 us; the launch traced here: 261 us
  waiting for transfers between devices  163 us (62%)
  starting transfers between devices  62.8 us (24%)
  Pallas kernels  16 us (6%)
  local copies, waits for them, and re-layouts  11.8 us (5%)
  other arithmetic  6.14 us (2%)
    all_to_all x2, waiting for transfers between devices, move(): return lax.all_to_all(item, ctx, split_axis=0, concat_axis=0, tiled=True)  127 us
    ppermute x2, starting transfers between devices, exchange(): return lax.ppermute(item, axis, [(0, 1), (1, 0)])  23.3 us
    ppermute x6, starting transfers between devices, ring(): lax.ppermute(item, 'y', [(i, (i + step) % n_row) for i in range(n_row)])  21.5 us
    ppermute x2, waiting for transfers between devices, exchange(): return lax.ppermute(item, axis, [(0, 1), (1, 0)])  21.1 us
    all_to_all x2, starting transfers between devices, move(): return lax.all_to_all(item, ctx, split_axis=0, concat_axis=0, tiled=True)  17.9 us
    pallas_call x2, Pallas kernels, call(): pl.pallas_call(kernel, grid=(chans // BLOCK,), in_specs=[specs[kind] for...  16 us
    ppermute x6, waiting for transfers between devices, ring(): lax.ppermute(item, 'y', [(i, (i + step) % n_row) for i in range(n_row)])  15.6 us
  transfers between devices with their start and end apart: 10, of which 8 were waited for; matrix products, arithmetic and copies ran while one was open for 4% of the time, Pallas kernels for 1%

profile of v10, /device:TPU:1, one launch (start us, length us, event | category | flops | bytes accessed | tf_op | source)
XLA Modules:
  0.0 261.0 jit_solution(18422640808347359200)
XLA Ops:
  0.6 0.9 copy.20
  1.6 16.3 %collective-permute-start = (bf16[64,8,128]{2,1,0:T(8,128)(2,1)S(1)}, bf16[64,8,128]{2,1,0:T(8,128)(2,1)S(1)}, u32[]{:S(2)}, u32[]{:S(2)}) collective-permute-start(bf16[64,8,128]{2,1,0:T(8,128)(2,1)S(1)} %bitcast.30), channel_id=1, source_target_pairs={{0,64},{64,0},{1,65},{65,1},{2,66},{66,2},{3,67},{67,3},{4,68},{68... | collective-permute-start | bytes 393224 | tf_op jit(solution)/shard_map/ppermute | solution.py:133
  17.8 3.1 %pad_maximum_fusion = bf16[64,128,128]{2,1,0:T(8,128)(2,1)} fusion(bf16[64,64,128]{2,1,0:T(8,128)(2,1)} %bitcast.26, bf16[64,64,128]{2,1,0:T(8,128)(2,1)} %bitcast.27), kind=kLoop, calls=%fused_computation | loop fusion | flops 4194304 | bytes 4194304 | tf_op jit(solution)/shard_map/concatenate | solution.py:159
  20.9 9.2 %all-to-all-start = ((bf16[64,128,128]{2,1,0:T(8,128)(2,1)}), bf16[64,128,128]{2,1,0:T(8,128)(2,1)}, u32[]{:S(2)}, u32[]{:S(2)}) async-start(bf16[64,128,128]{2,1,0:T(8,128)(2,1)} %pad_maximum_fusion), calls=%async_computation | async-start | bytes 4194304 | tf_op jit(solution)/shard_map/all_to_all | solution.py:147
  30.1 0.0 copy-start.2
  30.1 0.0 copy-start.3
  30.1 0.0 copy-start.4
  30.1 0.0 copy-start.6
  30.2 0.0 collective-permute-done
  30.3 3.3 %collective-permute-start.1 = (bf16[64,16,128]{2,1,0:T(8,128)(2,1)S(1)}, bf16[64,16,128]{2,1,0:T(8,128)(2,1)S(1)}, u32[]{:S(2)}, u32[]{:S(2)}) collective-permute-start(bf16[64,16,128]{2,1,0:T(8,128)(2,1)S(1)} %pad_maximum_fusion.1), channel_id=1, source_target_pairs={{0,128},{128,256},{256,384},{384,0},{1,129},{129,257},{257,385},{3... | collective-permute-start | bytes 786440 | tf_op jit(solution)/shard_map/ppermute | solution.py:150
  33.6 0.8 dynamic-slice_bitcast_fusion.slow_fwd
  34.4 4.5 %collective-permute-start.2 = (bf16[64,16,128]{2,1,0:T(8,128)(2,1)S(1)}, bf16[64,16,128]{2,1,0:T(8,128)(2,1)S(1)}, u32[]{:S(2)}, u32[]{:S(2)}) collective-permute-start(bf16[64,16,128]{2,1,0:T(8,128)(2,1)S(1)} %pad_maximum_fusion.1), channel_id=1, source_target_pairs={{0,256},{128,384},{256,0},{384,128},{1,257},{129,385},{257,1},{385... | collective-permute-start | bytes 786440 | tf_op jit(solution)/shard_map/ppermute | solution.py:150
  39.0 3.0 %collective-permute-start.3 = (bf16[64,16,128]{2,1,0:T(8,128)(2,1)S(1)}, bf16[64,16,128]{2,1,0:T(8,128)(2,1)S(1)}, u32[]{:S(2)}, u32[]{:S(2)}) collective-permute-start(bf16[64,16,128]{2,1,0:T(8,128)(2,1)S(1)} %pad_maximum_fusion.1), channel_id=1, source_target_pairs={{0,384},{128,0},{256,128},{384,256},{1,385},{129,1},{257,129},{385... | collective-permute-start | bytes 786440 | tf_op jit(solution)/shard_map/ppermute | solution.py:150
  42.0 0.0 collective-permute-done.1
  42.0 5.8 %collective-permute-done.2 = bf16[64,16,128]{2,1,0:T(8,128)(2,1)S(1)} collective-permute-done((bf16[64,16,128]{2,1,0:T(8,128)(2,1)S(1)}, bf16[64,16,128]{2,1,0:T(8,128)(2,1)S(1)}, u32[]{:S(2)}, u32[]{:S(2)}) %collective-permute-start.2) | collective-permute-done | bytes 262176 | tf_op jit(solution)/shard_map/ppermute | solution.py:150
  47.8 1.8 collective-permute-done.3
  49.7 0.0 copy-done.2
  49.7 0.0 copy-done.3
  49.7 0.0 copy-done.4
  49.7 0.0 copy-done.6
  49.7 3.4 %shard_map.112.k_in = bf16[5120,256]{1,0:T(8,128)(2,1)S(1)} custom-call(bf16[64,64,128]{2,1,0:T(8,128)(2,1)S(1)} %constant_dynamic-update-slice_fusion.taps, bf16[160,64]{1,0:T(8,128)(2,1)S(1)} %dynamic-slice_bitcast_fusion.slow_fwd, bf16[64,160]{1,0:T(8,128)(2,1)S(1)} %copy-done.6, bf16[256,256]{1,0:T(8,128)(2,1)S(1)} %copy-done.2, ...), custom_call_target="tpu_custom_call" | custom-call | flops 80000000000 | bytes 1 | tf_op jit(solution)/shard_map/pallas_call | solution.py:121
  53.2 0.0 copy-start.5
  53.2 72.4 %all-to-all-done = bf16[64,128,128]{2,1,0:T(8,128)(2,1)} async-done(((bf16[64,128,128]{2,1,0:T(8,128)(2,1)}), bf16[64,128,128]{2,1,0:T(8,128)(2,1)}, u32[]{:S(2)}, u32[]{:S(2)}) %all-to-all-start) | async-done | bytes 2097184 | tf_op jit(solution)/shard_map/all_to_all | solution.py:147
  125.6 2.9 %copy.26 = bf16[64,128,128]{2,0,1:T(8,128)(2,1)S(1)} copy(bf16[64,128,128]{2,1,0:T(8,128)(2,1)} %all-to-all-done) | data formatting | bytes 4194304 | tf_op jit(solution)/shard_map/optimization_barrier | solution.py:160
  128.5 0.0 copy-done.5
  128.6 12.6 %shard_map.113 = (bf16[64,64,128]{2,1,0:T(8,128)(2,1)S(1)}, bf16[2,64,64,128]{3,2,1,0:T(8,128)(2,1)S(1)}) custom-call(bf16[128,64,128]{2,1,0:T(8,128)(2,1)S(1)} %bitcast.21, bf16[128,64,128]{2,1,0:T(8,128)(2,1)S(1)} %bitcast.22, bf16[5120,256]{1,0:T(8,128)(2,1)S(1)} %shard_map.112.k_in, bf16[160,64]{1,0:T(8,128)(2,1)S(1)} %copy-done.5, ...), custom_call_target="tpu_custom_call" | custom-call | flops 1 | bytes 1 | tf_op jit(solution)/shard_map/pallas_call | solution.py:121
  141.2 0.0 copy-start
  141.2 2.7 %copy.25 = bf16[128,64,128]{2,0,1:T(8,128)(2,1)} copy(bf16[128,64,128]{2,1,0:T(8,128)(2,1)S(1)} %bitcast.23) | data formatting | bytes 4194304 | tf_op jit(solution)/shard_map/reshape | solution.py:163
  143.9 0.0 copy-done
  143.9 0.0 copy-start.1
  143.9 8.8 %all-to-all-start.1 = ((bf16[64,128,128]{2,1,0:T(8,128)(2,1)}), bf16[64,128,128]{2,1,0:T(8,128)(2,1)S(1)}, u32[]{:S(2)}, u32[]{:S(2)}) async-start(bf16[64,128,128]{2,1,0:T(8,128)(2,1)} %bitcast.24), calls=%async_computation.1 | async-start | bytes 4194304 | tf_op jit(solution)/shard_map/all_to_all | solution.py:147
  152.7 0.0 copy-done.1
  152.7 1.0 constant_dynamic-slice_fusion.2
  153.7 3.2 %collective-permute-start.4 = (bf16[64,16,128]{2,1,0:T(8,128)(2,1)}, bf16[64,16,128]{2,1,0:T(8,128)(2,1)}, u32[]{:S(2)}, u32[]{:S(2)}) collective-permute-start(bf16[64,16,128]{2,1,0:T(8,128)(2,1)} %get-tuple-element.13), channel_id=1, source_target_pairs={{0,128},{128,256},{256,384},{384,0},{1,129},{129,257},{257,385},{3... | collective-permute-start | bytes 786440 | tf_op jit(solution)/shard_map/ppermute | solution.py:150
  156.9 4.5 %collective-permute-start.5 = (bf16[64,16,128]{2,1,0:T(8,128)(2,1)}, bf16[64,16,128]{2,1,0:T(8,128)(2,1)}, u32[]{:S(2)}, u32[]{:S(2)}) collective-permute-start(bf16[64,16,128]{2,1,0:T(8,128)(2,1)} %get-tuple-element.15), channel_id=1, source_target_pairs={{0,256},{128,384},{256,0},{384,128},{1,257},{129,385},{257,1},{385... | collective-permute-start | bytes 786440 | tf_op jit(solution)/shard_map/ppermute | solution.py:150
  161.4 3.0 %collective-permute-start.6 = (bf16[64,16,128]{2,1,0:T(8,128)(2,1)S(1)}, bf16[64,16,128]{2,1,0:T(8,128)(2,1)}, u32[]{:S(2)}, u32[]{:S(2)}) collective-permute-start(bf16[64,16,128]{2,1,0:T(8,128)(2,1)S(1)} %get-tuple-element.14), channel_id=1, source_target_pairs={{0,384},{128,0},{256,128},{384,256},{1,385},{129,1},{257,129},{385... | collective-permute-start | bytes 786440 | tf_op jit(solution)/shard_map/ppermute | solution.py:150
  164.4 0.2 collective-permute-done.4
  164.7 6.7 %collective-permute-done.5 = bf16[64,16,128]{2,1,0:T(8,128)(2,1)} collective-permute-done((bf16[64,16,128]{2,1,0:T(8,128)(2,1)}, bf16[64,16,128]{2,1,0:T(8,128)(2,1)}, u32[]{:S(2)}, u32[]{:S(2)}) %collective-permute-start.5) | collective-permute-done | bytes 262176 | tf_op jit(solution)/shard_map/ppermute | solution.py:150
  171.4 1.1 collective-permute-done.6
  172.5 2.0 convert_add_fusion
  174.5 1.0 dynamic-slice_convert_fusion
  175.4 7.0 %collective-permute-start.7 = (bf16[64,8,128]{2,1,0:T(8,128)(2,1)S(1)}, bf16[64,8,128]{2,1,0:T(8,128)(2,1)S(1)}, u32[]{:S(2)}, u32[]{:S(2)}) collective-permute-start(bf16[64,8,128]{2,1,0:T(8,128)(2,1)S(1)} %dynamic-slice_convert_fusion), channel_id=1, source_target_pairs={{0,64},{64,0},{1,65},{65,1},{2,66},{66,2},{3,67},{67,3},{4,68},{68... | collective-permute-start | bytes 393224 | tf_op jit(solution)/shard_map/ppermute | solution.py:133
  182.5 21.1 %collective-permute-done.7 = bf16[64,8,128]{2,1,0:T(8,128)(2,1)S(1)} collective-permute-done((bf16[64,8,128]{2,1,0:T(8,128)(2,1)S(1)}, bf16[64,8,128]{2,1,0:T(8,128)(2,1)S(1)}, u32[]{:S(2)}, u32[]{:S(2)}) %collective-permute-start.7) | collective-permute-done | bytes 131104 | tf_op jit(solution)/shard_map/ppermute | solution.py:133
  203.6 1.0 convert_add_fusion.1
  204.6 0.8 copy.27
  205.3 54.1 %all-to-all-done.1 = bf16[64,128,128]{2,1,0:T(8,128)(2,1)S(1)} async-done(((bf16[64,128,128]{2,1,0:T(8,128)(2,1)}), bf16[64,128,128]{2,1,0:T(8,128)(2,1)S(1)}, u32[]{:S(2)}, u32[]{:S(2)}) %all-to-all-start.1) | async-done | bytes 2097184 | tf_op jit(solution)/shard_map/all_to_all | solution.py:147
  259.5 1.5 fusion
  (7 shorter events, 0.3 us)
Async XLA Ops:
  1.6 28.6 %collective-permute-start = (bf16[64,8,128]{2,1,0:T(8,128)(2,1)S(1)}, bf16[64,8,128]{2,1,0:T(8,128)(2,1)S(1)}, u32[]{:S(2)}, u32[]{:S(2)}) collective-permute-start(bf16[64,8,128]{2,1,0:T(8,128)(2,1)S(1)} %bitcast.30), channel_id=1, source_target_pairs={{0,64},{64,0},{1,65},{65,1},{2,66},{66,2},{3,67},{67,3},{4,68},{68... | collective-permute-start | bytes 393224 | tf_op jit(solution)/shard_map/ppermute | solution.py:133
  20.9 104.7 %all-to-all-start = ((bf16[64,128,128]{2,1,0:T(8,128)(2,1)}), bf16[64,128,128]{2,1,0:T(8,128)(2,1)}, u32[]{:S(2)}, u32[]{:S(2)}) async-start(bf16[64,128,128]{2,1,0:T(8,128)(2,1)} %pad_maximum_fusion), calls=%async_computation | async-start | bytes 4194304 | tf_op jit(solution)/shard_map/all_to_all | solution.py:147
  30.1 19.6 %copy-start.2 = (bf16[256,256]{1,0:T(8,128)(2,1)S(1)}, bf16[256,256]{1,0:T(8,128)(2,1)}, u32[]{:S(2)}) copy-start(bf16[256,256]{1,0:T(8,128)(2,1)} %constant.67.clone.fast_fwd) | copy-start | bytes 393220
  30.1 19.6 %copy-start.3 = (bf16[256,256]{1,0:T(8,128)(2,1)S(1)}, bf16[256,256]{1,0:T(8,128)(2,1)}, u32[]{:S(2)}) copy-start(bf16[256,256]{1,0:T(8,128)(2,1)} %constant.68.clone.fast_inv) | copy-start | bytes 393220
  30.1 19.6 %copy-start.4 = (f32[2,80,128]{2,1,0:T(8,128)S(1)}, f32[2,80,128]{2,1,0:T(8,128)}, u32[]{:S(2)}) copy-start(f32[2,80,128]{2,1,0:T(8,128)} %constant.69.clone.twid) | copy-start | bytes 245764
  30.1 19.6 %copy-start.6 = (bf16[64,160]{1,0:T(8,128)(2,1)S(1)}, bf16[64,160]{1,0:T(8,128)(2,1)}, u32[]{:S(2)}) copy-start(bf16[64,160]{1,0:T(8,128)(2,1)} %constant.66.clone.slow_inv) | copy-start | bytes 61444
  30.3 11.7 %collective-permute-start.1 = (bf16[64,16,128]{2,1,0:T(8,128)(2,1)S(1)}, bf16[64,16,128]{2,1,0:T(8,128)(2,1)S(1)}, u32[]{:S(2)}, u32[]{:S(2)}) collective-permute-start(bf16[64,16,128]{2,1,0:T(8,128)(2,1)S(1)} %pad_maximum_fusion.1), channel_id=1, source_target_pairs={{0,128},{128,256},{256,384},{384,0},{1,129},{129,257},{257,385},{3... | collective-permute-start | bytes 786440 | tf_op jit(solution)/shard_map/ppermute | solution.py:150
  34.4 13.4 %collective-permute-start.2 = (bf16[64,16,128]{2,1,0:T(8,128)(2,1)S(1)}, bf16[64,16,128]{2,1,0:T(8,128)(2,1)S(1)}, u32[]{:S(2)}, u32[]{:S(2)}) collective-permute-start(bf16[64,16,128]{2,1,0:T(8,128)(2,1)S(1)} %pad_maximum_fusion.1), channel_id=1, source_target_pairs={{0,256},{128,384},{256,0},{384,128},{1,257},{129,385},{257,1},{385... | collective-permute-start | bytes 786440 | tf_op jit(solution)/shard_map/ppermute | solution.py:150
  39.0 10.7 %collective-permute-start.3 = (bf16[64,16,128]{2,1,0:T(8,128)(2,1)S(1)}, bf16[64,16,128]{2,1,0:T(8,128)(2,1)S(1)}, u32[]{:S(2)}, u32[]{:S(2)}) collective-permute-start(bf16[64,16,128]{2,1,0:T(8,128)(2,1)S(1)} %pad_maximum_fusion.1), channel_id=1, source_target_pairs={{0,384},{128,0},{256,128},{384,256},{1,385},{129,1},{257,129},{385... | collective-permute-start | bytes 786440 | tf_op jit(solution)/shard_map/ppermute | solution.py:150
  53.2 75.4 %copy-start.5 = (bf16[160,64]{1,0:T(8,128)(2,1)S(1)}, bf16[160,64]{1,0:T(8,128)(2,1)}, u32[]{:S(2)}) copy-start(bf16[160,64]{1,0:T(8,128)(2,1)} %constant.65.clone.slow_fwd) | copy-start | bytes 61444
  141.2 2.7 %copy-start = (bf16[64,64,128]{2,1,0:T(8,128)(2,1)}, bf16[64,64,128]{2,1,0:T(8,128)(2,1)S(1)}, u32[]{:S(2)}) copy-start(bf16[64,64,128]{2,1,0:T(8,128)(2,1)S(1)} %get-tuple-element.10) | copy-start | bytes 3145732
  143.9 8.8 %copy-start.1 = (bf16[64,64,128]{2,1,0:T(8,128)(2,1)S(1)}, bf16[64,64,128]{2,1,0:T(8,128)(2,1)}, u32[]{:S(2)}) copy-start(bf16[64,64,128]{2,1,0:T(8,128)(2,1)} %copy-done) | copy-start | bytes 3145732
  143.9 115.6 %all-to-all-start.1 = ((bf16[64,128,128]{2,1,0:T(8,128)(2,1)}), bf16[64,128,128]{2,1,0:T(8,128)(2,1)S(1)}, u32[]{:S(2)}, u32[]{:S(2)}) async-start(bf16[64,128,128]{2,1,0:T(8,128)(2,1)} %bitcast.24), calls=%async_computation.1 | async-start | bytes 4194304 | tf_op jit(solution)/shard_map/all_to_all | solution.py:147
  153.7 11.0 %collective-permute-start.4 = (bf16[64,16,128]{2,1,0:T(8,128)(2,1)}, bf16[64,16,128]{2,1,0:T(8,128)(2,1)}, u32[]{:S(2)}, u32[]{:S(2)}) collective-permute-start(bf16[64,16,128]{2,1,0:T(8,128)(2,1)} %get-tuple-element.13), channel_id=1, source_target_pairs={{0,128},{128,256},{256,384},{384,0},{1,129},{129,257},{257,385},{3... | collective-permute-start | bytes 786440 | tf_op jit(solution)/shard_map/ppermute | solution.py:150
  156.9 14.5 %collective-permute-start.5 = (bf16[64,16,128]{2,1,0:T(8,128)(2,1)}, bf16[64,16,128]{2,1,0:T(8,128)(2,1)}, u32[]{:S(2)}, u32[]{:S(2)}) collective-permute-start(bf16[64,16,128]{2,1,0:T(8,128)(2,1)} %get-tuple-element.15), channel_id=1, source_target_pairs={{0,256},{128,384},{256,0},{384,128},{1,257},{129,385},{257,1},{385... | collective-permute-start | bytes 786440 | tf_op jit(solution)/shard_map/ppermute | solution.py:150
  161.4 11.0 %collective-permute-start.6 = (bf16[64,16,128]{2,1,0:T(8,128)(2,1)S(1)}, bf16[64,16,128]{2,1,0:T(8,128)(2,1)}, u32[]{:S(2)}, u32[]{:S(2)}) collective-permute-start(bf16[64,16,128]{2,1,0:T(8,128)(2,1)S(1)} %get-tuple-element.14), channel_id=1, source_target_pairs={{0,384},{128,0},{256,128},{384,256},{1,385},{129,1},{257,129},{385... | collective-permute-start | bytes 786440 | tf_op jit(solution)/shard_map/ppermute | solution.py:150
  175.4 28.2 %collective-permute-start.7 = (bf16[64,8,128]{2,1,0:T(8,128)(2,1)S(1)}, bf16[64,8,128]{2,1,0:T(8,128)(2,1)S(1)}, u32[]{:S(2)}, u32[]{:S(2)}) collective-permute-start(bf16[64,8,128]{2,1,0:T(8,128)(2,1)S(1)} %dynamic-slice_convert_fusion), channel_id=1, source_target_pairs={{0,64},{64,0},{1,65},{65,1},{2,66},{66,2},{3,67},{67,3},{4,68},{68... | collective-permute-start | bytes 393224 | tf_op jit(solution)/shard_map/ppermute | solution.py:133

commit v11 on v10

--- a/solution.py
+++ b/solution.py
@@ -15,7 +15,7 @@
 HALF = SLOW // 2
 ROWS = 80
 FACTOR = 1.0 / (TOTAL * math.sqrt(TOTAL // 2))
-BLOCK = 8
+BLOCK = 16
 BESIDE = 80 * 10**9
 
 
@@ -67,7 +67,7 @@
     return dot(jnp.concatenate(parts, axis=0), fast_fwd[...]).astype(jnp.bfloat16)
 
 
-def inverse(spectrum, out, slow_inv, twid, fast_inv):
+def inverse(spectrum, slow_inv, twid, fast_inv):
     section = dot(spectrum, fast_inv[...])
     wr, wi = twid[0], twid[1]
     parts = []
@@ -76,8 +76,7 @@
         bi = section[j * ROWS : (j + 1) * ROWS, FAST:]
         parts.append(jnp.concatenate([br * wr - bi * wi, bi * wr + br * wi], axis=0).astype(jnp.bfloat16))
     result = dot(slow_inv[...], jnp.concatenate(parts, axis=1)) * FACTOR
-    for j in range(BLOCK):
-        out[j] = result[:, j * FAST : (j + 1) * FAST].astype(out.dtype)
+    return jnp.stack([result[:, j * FAST : (j + 1) * FAST].astype(jnp.bfloat16) for j in range(BLOCK)])
 
 
 def halves(spectrum):
@@ -92,41 +91,28 @@
     k_out[...] = forward(taps, slow_fwd, twid, fast_fwd)
 
 
-def products_kernel(
-    values, grads, k_in, slow_fwd, slow_inv, fast_fwd, fast_inv, twid, taps, outs
-):
-    ur, ui = halves(forward(values, slow_fwd, twid, fast_fwd))
-    zr, zi = halves(forward(grads, slow_fwd, twid, fast_fwd))
-    inverse(joined(ur * zr + ui * zi, ur * zi - ui * zr), taps, slow_inv, twid, fast_inv)
+def products_kernel(values, grads, k_in, slow_fwd, slow_inv, fast_fwd, fast_inv, twid, terms, outs):
+    ur, ui = halves(forward(jnp.swapaxes(values[...], 0, 1), slow_fwd, twid, fast_fwd))
+    zr, zi = halves(forward(jnp.swapaxes(grads[...], 0, 1), slow_fwd, twid, fast_fwd))
+    terms[...] = inverse(joined(ur * zr + ui * zi, ur * zi - ui * zr), slow_inv, twid, fast_inv)
     kr, ki = halves(k_in[...])
-    inverse(joined(ur * kr - ui * ki, ur * ki + ui * kr), outs.at[0], slow_inv, twid, fast_inv)
-    inverse(joined(kr * zr + ki * zi, kr * zi - ki * zr), outs.at[1], slow_inv, twid, fast_inv)
+    conv = inverse(joined(ur * kr - ui * ki, ur * ki + ui * kr), slow_inv, twid, fast_inv)
+    outs[:, 0] = jnp.swapaxes(conv, 0, 1)
+    back = inverse(joined(kr * zr + ki * zi, kr * zi - ki * zr), slow_inv, twid, fast_inv)
+    outs[:, 1] = jnp.swapaxes(back, 0, 1)
 
 
-def call(kernel, signals, outs, consts, start=0, flops=1):
-    item, kind = signals[-1]
-    chans = item.shape[0] // ROWS if kind == "s" else item.shape[0]
-    specs = {
-        "w": pl.BlockSpec((2, BLOCK, HALF, FAST), lambda i: (0, i, 0, 0)),
-        "y": pl.BlockSpec((BLOCK, HALF, FAST), lambda i: (start // BLOCK + i, 0, 0)),
-        "x": pl.BlockSpec((BLOCK, HALF, FAST), lambda i: (i, 0, 0)),
-        "s": pl.BlockSpec((BLOCK * ROWS, 2 * FAST), lambda i: (i, 0)),
-    }
-    shapes = {
-        "w": jax.ShapeDtypeStruct((2, chans, HALF, FAST), jnp.bfloat16),
-        "x": jax.ShapeDtypeStruct((chans, HALF, FAST), jnp.bfloat16),
-        "s": jax.ShapeDtypeStruct((chans * ROWS, 2 * FAST), jnp.bfloat16),
-    }
+def call(kernel, chans, items, outs, consts, flops=1):
     whole = [pl.BlockSpec(item.shape, functools.partial(lambda n, i: (0,) * n, item.ndim)) for item in consts]
     return pl.pallas_call(
         kernel,
         grid=(chans // BLOCK,),
-        in_specs=[specs[kind] for _, kind in signals] + whole,
-        out_specs=[specs[kind] for kind in outs],
-        out_shape=[shapes[kind] for kind in outs],
-        compiler_params=pltpu.CompilerParams(vmem_limit_bytes=20 * 1024 * 1024),
+        in_specs=[pl.BlockSpec(block, index) for _, block, index in items] + whole,
+        out_specs=[pl.BlockSpec(block, index) for _, block, index in outs],
+        out_shape=[jax.ShapeDtypeStruct(shape, jnp.bfloat16) for shape, _, _ in outs],
+        compiler_params=pltpu.CompilerParams(vmem_limit_bytes=30 * 1024 * 1024),
         cost_estimate=pl.CostEstimate(flops=flops, bytes_accessed=1, transcendentals=0),
-    )(*[item for item, _ in signals], *consts)
+    )(*[item for item, _, _ in items], *consts)
 
 
 def exchange(item, axis):
@@ -149,18 +135,29 @@
     def ring(item, step):
         return lax.ppermute(item, "y", [(i, (i + step) % n_row) for i in range(n_row)])
 
+    both = jnp.concatenate([values.reshape(groups, chans, FAST), grads.reshape(groups, chans, FAST)], axis=1)
+    both, filter_taps = lax.optimization_barrier((both, filter_taps))
+
     blocks = filter_taps.reshape(chans, wide // FAST, FAST)
     other = exchange(blocks, "zh")
     pair = jnp.concatenate([jnp.where(high == 0, blocks, other), jnp.where(high == 0, other, blocks)], axis=1)
     taps = jnp.concatenate([pair] + [ring(pair, step) for step in range(1, n_row)], axis=1)
     slow_taps = lax.dynamic_index_in_dim(jnp.asarray(turned(n_row)), row, 0, keepdims=False)
-    (k_spec,) = call(spectra_kernel, [(taps, "x")], "s", (slow_taps,) + consts[1:], flops=BESIDE)
+    rows = ((chans * ROWS, 2 * FAST), (BLOCK * ROWS, 2 * FAST), lambda i: (i, 0))
+    lines = ((chans, HALF, FAST), (BLOCK, HALF, FAST), lambda i: (i, 0, 0))
+    (k_spec,) = call(
+        spectra_kernel, chans, [(taps,) + lines[1:]], [rows], (slow_taps,) + consts[1:], flops=BESIDE
+    )
 
-    both = jnp.concatenate([values.reshape(groups, chans, FAST), grads.reshape(groups, chans, FAST)], axis=1)
     mine, k_spec = lax.optimization_barrier((move(both), k_spec))
-    mine = mine.transpose(1, 0, 2)
-    terms, outs = call(products_kernel, [(mine, "x"), (mine, "y"), (k_spec, "s")], "xw", consts, chans)
-    arrived = move(outs.reshape(2 * chans, HALF, FAST).transpose(1, 0, 2))
+    across = (HALF, BLOCK, FAST)
+    terms, outs = call(
+        products_kernel, chans,
+        [(mine, across, lambda i: (0, i, 0)), (mine, across, lambda i: (0, chans // BLOCK + i, 0)),
+         (k_spec,) + rows[1:]],
+        [lines, ((HALF, 2, chans, FAST), (HALF, 2, BLOCK, FAST), lambda i: (0, 0, i, 0))], consts,
+    )
+    arrived = move(outs.reshape(groups, 2 * chans, FAST))
     conv_out = arrived[:, :chans].reshape(values.shape)
     value_grads = arrived[:, chans:].reshape(values.shape)
 

time: 262 us -> 258 us (0.985)
  Pallas kernels: 16 us -> 13 us
    unnamed x20 -> x28, local copies, waits for them, and re-layouts: 1.86 us -> 7.05 us
    pallas_call x2, Pallas kernels: 16 us -> 13 us  [call(): pl.pallas_call(kernel, grid=(chans // BLOCK,), in_specs=[pl.BlockSpec(blo...]
    optimization_barrier x1 -> x0, local copies, waits for them, and re-layouts: 2.94 us -> none  [local(): mine, k_spec = lax.optimization_barrier((move(both), k_spec))]
    reshape x1 -> x0, local copies, waits for them, and re-layouts: 2.68 us -> none  [local(): arrived = move(outs.reshape(2 * chans, HALF, FAST).transpose(1, 0, 2))]
  transfers between devices with their start and end apart: 10 -> 10, of which waited for: 8 -> 8; matrix products, arithmetic and copies ran while one was open for 4% -> 2% of each run, Pallas kernels for 1% -> 1%
where the time goes in v11:
time: 258 us; the launch traced here: 257 us
  waiting for transfers between devices  163 us (63%)
  starting transfers between devices  63.9 us (25%)
  Pallas kernels  13 us (5%)
  local copies, waits for them, and re-layouts  10.4 us (4%)
  other arithmetic  5.44 us (2%)
    all_to_all x2, waiting for transfers between devices, move(): return lax.all_to_all(item, ctx, split_axis=0, concat_axis=0, tiled=True)  125 us
    ppermute x2, starting transfers between devices, exchange(): return lax.ppermute(item, axis, [(0, 1), (1, 0)])  24.2 us
    ppermute x2, waiting for transfers between devices, exchange(): return lax.ppermute(item, axis, [(0, 1), (1, 0)])  22.1 us
    ppermute x6, starting transfers between devices, ring(): lax.ppermute(item, 'y', [(i, (i + step) % n_row) for i in range(n_row)])  21.5 us
    all_to_all x2, starting transfers between devices, move(): return lax.all_to_all(item, ctx, split_axis=0, concat_axis=0, tiled=True)  18.2 us
    ppermute x6, waiting for transfers between devices, ring(): lax.ppermute(item, 'y', [(i, (i + step) % n_row) for i in range(n_row)])  15.6 us
    pallas_call x2, Pallas kernels, call(): pl.pallas_call(kernel, grid=(chans // BLOCK,), in_specs=[pl.BlockSpec(blo...  13 us
    unnamed x28, local copies, waits for them, and re-layouts  7.05 us
  transfers between devices with their start and end apart: 10, of which 8 were waited for; matrix products, arithmetic and copies ran while one was open for 2% of the time, Pallas kernels for 1%

profile of v11, /device:TPU:1, one launch (start us, length us, event | category | flops | bytes accessed | tf_op | source)
XLA Modules:
  0.0 256.7 jit_solution(9054142944578194685)
XLA Ops:
  0.6 0.0 copy-start.10
  0.6 3.2 %pad_maximum_fusion = bf16[64,128,128]{2,1,0:T(8,128)(2,1)} fusion(bf16[64,64,128]{2,1,0:T(8,128)(2,1)} %bitcast.17, bf16[64,64,128]{2,1,0:T(8,128)(2,1)} %bitcast.18), kind=kLoop, calls=%fused_computation | loop fusion | flops 4194304 | bytes 4194304 | tf_op jit(solution)/shard_map/concatenate | solution.py:138
  3.8 0.0 copy-done.10
  3.8 16.3 %collective-permute-start = (bf16[64,8,128]{2,1,0:T(8,128)(2,1)S(1)}, bf16[64,8,128]{2,1,0:T(8,128)(2,1)S(1)}, u32[]{:S(2)}, u32[]{:S(2)}) collective-permute-start(bf16[64,8,128]{2,1,0:T(8,128)(2,1)S(1)} %bitcast.21), channel_id=1, source_target_pairs={{0,64},{64,0},{1,65},{65,1},{2,66},{66,2},{3,67},{67,3},{4,68},{68... | collective-permute-start | bytes 393224 | tf_op jit(solution)/shard_map/ppermute | solution.py:119
  20.1 9.0 %all-to-all-start = ((bf16[64,128,128]{2,1,0:T(8,128)(2,1)}), bf16[64,128,128]{2,1,0:T(8,128)(2,1)S(1)}, u32[]{:S(2)}, u32[]{:S(2)}) async-start(bf16[64,128,128]{2,1,0:T(8,128)(2,1)} %pad_maximum_fusion), calls=%async_computation | async-start | bytes 4194304 | tf_op jit(solution)/shard_map/all_to_all | solution.py:133
  29.1 0.0 copy-start.3
  29.1 0.0 copy-start.4
  29.1 0.0 copy-start.5
  29.2 0.0 copy-start.7
  29.2 0.0 collective-permute-done
  29.3 3.3 %collective-permute-start.1 = (bf16[64,16,128]{2,1,0:T(8,128)(2,1)S(1)}, bf16[64,16,128]{2,1,0:T(8,128)(2,1)S(1)}, u32[]{:S(2)}, u32[]{:S(2)}) collective-permute-start(bf16[64,16,128]{2,1,0:T(8,128)(2,1)S(1)} %pad_maximum_fusion.1), channel_id=1, source_target_pairs={{0,128},{128,256},{256,384},{384,0},{1,129},{129,257},{257,385},{3... | collective-permute-start | bytes 786440 | tf_op jit(solution)/shard_map/ppermute | solution.py:136
  32.6 0.8 dynamic-slice_bitcast_fusion.slow_fwd
  33.4 4.5 %collective-permute-start.2 = (bf16[64,16,128]{2,1,0:T(8,128)(2,1)S(1)}, bf16[64,16,128]{2,1,0:T(8,128)(2,1)S(1)}, u32[]{:S(2)}, u32[]{:S(2)}) collective-permute-start(bf16[64,16,128]{2,1,0:T(8,128)(2,1)S(1)} %pad_maximum_fusion.1), channel_id=1, source_target_pairs={{0,256},{128,384},{256,0},{384,128},{1,257},{129,385},{257,1},{385... | collective-permute-start | bytes 786440 | tf_op jit(solution)/shard_map/ppermute | solution.py:136
  38.0 3.0 %collective-permute-start.3 = (bf16[64,16,128]{2,1,0:T(8,128)(2,1)S(1)}, bf16[64,16,128]{2,1,0:T(8,128)(2,1)S(1)}, u32[]{:S(2)}, u32[]{:S(2)}) collective-permute-start(bf16[64,16,128]{2,1,0:T(8,128)(2,1)S(1)} %pad_maximum_fusion.1), channel_id=1, source_target_pairs={{0,384},{128,0},{256,128},{384,256},{1,385},{129,1},{257,129},{385... | collective-permute-start | bytes 786440 | tf_op jit(solution)/shard_map/ppermute | solution.py:136
  41.0 0.0 collective-permute-done.1
  41.1 5.7 %collective-permute-done.2 = bf16[64,16,128]{2,1,0:T(8,128)(2,1)S(1)} collective-permute-done((bf16[64,16,128]{2,1,0:T(8,128)(2,1)S(1)}, bf16[64,16,128]{2,1,0:T(8,128)(2,1)S(1)}, u32[]{:S(2)}, u32[]{:S(2)}) %collective-permute-start.2) | collective-permute-done | bytes 262176 | tf_op jit(solution)/shard_map/ppermute | solution.py:136
  46.8 1.8 collective-permute-done.3
  48.7 0.0 copy-done.3
  48.7 0.0 copy-done.4
  48.7 0.0 copy-done.5
  48.7 0.0 copy-done.7
  48.7 0.0 copy-start.6
  48.8 2.3 shard_map.112.k_in
  51.1 0.0 copy-start
  51.1 1.5 copy-done
  52.6 72.1 %all-to-all-done.values.grads = bf16[64,128,128]{2,1,0:T(8,128)(2,1)S(1)} async-done(((bf16[64,128,128]{2,1,0:T(8,128)(2,1)}), bf16[64,128,128]{2,1,0:T(8,128)(2,1)S(1)}, u32[]{:S(2)}, u32[]{:S(2)}) %all-to-all-start) | async-done | bytes 2097184 | tf_op jit(solution)/shard_map/all_to_all | solution.py:133
  124.7 0.0 copy-done.6
  124.7 0.0 copy-start.1
  124.7 1.7 copy-done.1
  126.5 0.0 copy-start.8
  126.5 0.8 copy-done.8
  127.2 10.7 %shard_map.113 = (bf16[64,64,128]{2,1,0:T(8,128)(2,1)S(1)}, bf16[64,2,64,128]{3,2,1,0:T(8,128)(2,1)S(1)}) custom-call(bf16[64,128,128]{2,1,0:T(8,128)(2,1)S(1)} %all-to-all-done.values.grads, bf16[64,128,128]{2,1,0:T(8,128)(2,1)S(1)} %all-to-all-done.values.grads, bf16[5120,256]{1,0:T(8,128)(2,1)S(1)} %copy-done.1, bf16[160,64]{1,0:T(8,128)(2,1)S(1)} %copy-done.6, ...), custom_call_target="tpu_custom_call" | custom-call | flops 1 | bytes 1 | tf_op jit(solution)/shard_map/pallas_call | solution.py:107
  137.9 0.0 copy-start.2
  137.9 1.3 copy-done.2
  139.2 9.2 %all-to-all-start.1 = ((bf16[64,128,128]{2,1,0:T(8,128)(2,1)}), bf16[64,128,128]{2,1,0:T(8,128)(2,1)S(1)}, u32[]{:S(2)}, u32[]{:S(2)}) async-start(bf16[64,128,128]{2,1,0:T(8,128)(2,1)} %bitcast.15), calls=%async_computation.1 | async-start | bytes 4194304 | tf_op jit(solution)/shard_map/all_to_all | solution.py:133
  148.4 1.0 constant_dynamic-slice_fusion.2
  149.4 3.2 %collective-permute-start.4 = (bf16[64,16,128]{2,1,0:T(8,128)(2,1)}, bf16[64,16,128]{2,1,0:T(8,128)(2,1)}, u32[]{:S(2)}, u32[]{:S(2)}) collective-permute-start(bf16[64,16,128]{2,1,0:T(8,128)(2,1)} %get-tuple-element.17), channel_id=1, source_target_pairs={{0,128},{128,256},{256,384},{384,0},{1,129},{129,257},{257,385},{3... | collective-permute-start | bytes 786440 | tf_op jit(solution)/shard_map/ppermute | solution.py:136
  152.6 4.5 %collective-permute-start.5 = (bf16[64,16,128]{2,1,0:T(8,128)(2,1)}, bf16[64,16,128]{2,1,0:T(8,128)(2,1)}, u32[]{:S(2)}, u32[]{:S(2)}) collective-permute-start(bf16[64,16,128]{2,1,0:T(8,128)(2,1)} %get-tuple-element.19), channel_id=1, source_target_pairs={{0,256},{128,384},{256,0},{384,128},{1,257},{129,385},{257,1},{385... | collective-permute-start | bytes 786440 | tf_op jit(solution)/shard_map/ppermute | solution.py:136
  157.2 3.0 %collective-permute-start.6 = (bf16[64,16,128]{2,1,0:T(8,128)(2,1)S(1)}, bf16[64,16,128]{2,1,0:T(8,128)(2,1)}, u32[]{:S(2)}, u32[]{:S(2)}) collective-permute-start(bf16[64,16,128]{2,1,0:T(8,128)(2,1)S(1)} %get-tuple-element.18), channel_id=1, source_target_pairs={{0,384},{128,0},{256,128},{384,256},{1,385},{129,1},{257,129},{385... | collective-permute-start | bytes 786440 | tf_op jit(solution)/shard_map/ppermute | solution.py:136
  160.2 0.2 collective-permute-done.4
  160.4 6.7 %collective-permute-done.5 = bf16[64,16,128]{2,1,0:T(8,128)(2,1)} collective-permute-done((bf16[64,16,128]{2,1,0:T(8,128)(2,1)}, bf16[64,16,128]{2,1,0:T(8,128)(2,1)}, u32[]{:S(2)}, u32[]{:S(2)}) %collective-permute-start.5) | collective-permute-done | bytes 262176 | tf_op jit(solution)/shard_map/ppermute | solution.py:136
  167.1 1.1 collective-permute-done.6
  168.2 1.2 convert_add_fusion
  169.4 0.0 copy-start.9
  169.5 0.8 copy-done.9
  170.3 7.9 %collective-permute-start.7 = (bf16[64,8,128]{2,1,0:T(8,128)(2,1)S(1)}, bf16[64,8,128]{2,1,0:T(8,128)(2,1)S(1)}, u32[]{:S(2)}, u32[]{:S(2)}) collective-permute-start(bf16[64,8,128]{2,1,0:T(8,128)(2,1)S(1)} %dynamic-slice_convert_fusion), channel_id=1, source_target_pairs={{0,64},{64,0},{1,65},{65,1},{2,66},{66,2},{3,67},{67,3},{4,68},{68... | collective-permute-start | bytes 393224 | tf_op jit(solution)/shard_map/ppermute | solution.py:119
  178.2 22.1 %collective-permute-done.7 = bf16[64,8,128]{2,1,0:T(8,128)(2,1)S(1)} collective-permute-done((bf16[64,8,128]{2,1,0:T(8,128)(2,1)S(1)}, bf16[64,8,128]{2,1,0:T(8,128)(2,1)S(1)}, u32[]{:S(2)}, u32[]{:S(2)}) %collective-permute-start.7) | collective-permute-done | bytes 131104 | tf_op jit(solution)/shard_map/ppermute | solution.py:119
  200.3 1.0 convert_add_fusion.1
  201.2 0.8 copy.15
  202.0 53.2 %all-to-all-done.1 = bf16[64,128,128]{2,1,0:T(8,128)(2,1)S(1)} async-done(((bf16[64,128,128]{2,1,0:T(8,128)(2,1)}), bf16[64,128,128]{2,1,0:T(8,128)(2,1)S(1)}, u32[]{:S(2)}, u32[]{:S(2)}) %all-to-all-start.1) | async-done | bytes 2097184 | tf_op jit(solution)/shard_map/all_to_all | solution.py:133
  255.2 1.5 fusion
  (9 shorter events, 0.3 us)
Async XLA Ops:
  0.6 3.2 %copy-start.10 = (bf16[64,1024]{1,0:T(8,128)(2,1)S(1)}, bf16[64,1024]{1,0:T(8,128)(2,1)}, u32[]{:S(2)}) copy-start(bf16[64,1024]{1,0:T(8,128)(2,1)} %param.11) | copy-start | bytes 393220
  3.8 25.4 %collective-permute-start = (bf16[64,8,128]{2,1,0:T(8,128)(2,1)S(1)}, bf16[64,8,128]{2,1,0:T(8,128)(2,1)S(1)}, u32[]{:S(2)}, u32[]{:S(2)}) collective-permute-start(bf16[64,8,128]{2,1,0:T(8,128)(2,1)S(1)} %bitcast.21), channel_id=1, source_target_pairs={{0,64},{64,0},{1,65},{65,1},{2,66},{66,2},{3,67},{67,3},{4,68},{68... | collective-permute-start | bytes 393224 | tf_op jit(solution)/shard_map/ppermute | solution.py:119
  20.1 104.6 %all-to-all-start = ((bf16[64,128,128]{2,1,0:T(8,128)(2,1)}), bf16[64,128,128]{2,1,0:T(8,128)(2,1)S(1)}, u32[]{:S(2)}, u32[]{:S(2)}) async-start(bf16[64,128,128]{2,1,0:T(8,128)(2,1)} %pad_maximum_fusion), calls=%async_computation | async-start | bytes 4194304 | tf_op jit(solution)/shard_map/all_to_all | solution.py:133
  29.1 19.6 %copy-start.3 = (bf16[256,256]{1,0:T(8,128)(2,1)S(1)}, bf16[256,256]{1,0:T(8,128)(2,1)}, u32[]{:S(2)}) copy-start(bf16[256,256]{1,0:T(8,128)(2,1)} %constant.67.clone.fast_fwd) | copy-start | bytes 393220
  29.1 19.6 %copy-start.4 = (bf16[256,256]{1,0:T(8,128)(2,1)S(1)}, bf16[256,256]{1,0:T(8,128)(2,1)}, u32[]{:S(2)}) copy-start(bf16[256,256]{1,0:T(8,128)(2,1)} %constant.68.clone.fast_inv) | copy-start | bytes 393220
  29.1 19.6 %copy-start.5 = (f32[2,80,128]{2,1,0:T(8,128)S(1)}, f32[2,80,128]{2,1,0:T(8,128)}, u32[]{:S(2)}) copy-start(f32[2,80,128]{2,1,0:T(8,128)} %constant.69.clone.twid) | copy-start | bytes 245764
  29.2 19.6 %copy-start.7 = (bf16[64,160]{1,0:T(8,128)(2,1)S(1)}, bf16[64,160]{1,0:T(8,128)(2,1)}, u32[]{:S(2)}) copy-start(bf16[64,160]{1,0:T(8,128)(2,1)} %constant.66.clone.slow_inv) | copy-start | bytes 61444
  29.3 11.7 %collective-permute-start.1 = (bf16[64,16,128]{2,1,0:T(8,128)(2,1)S(1)}, bf16[64,16,128]{2,1,0:T(8,128)(2,1)S(1)}, u32[]{:S(2)}, u32[]{:S(2)}) collective-permute-start(bf16[64,16,128]{2,1,0:T(8,128)(2,1)S(1)} %pad_maximum_fusion.1), channel_id=1, source_target_pairs={{0,128},{128,256},{256,384},{384,0},{1,129},{129,257},{257,385},{3... | collective-permute-start | bytes 786440 | tf_op jit(solution)/shard_map/ppermute | solution.py:136
  33.4 13.4 %collective-permute-start.2 = (bf16[64,16,128]{2,1,0:T(8,128)(2,1)S(1)}, bf16[64,16,128]{2,1,0:T(8,128)(2,1)S(1)}, u32[]{:S(2)}, u32[]{:S(2)}) collective-permute-start(bf16[64,16,128]{2,1,0:T(8,128)(2,1)S(1)} %pad_maximum_fusion.1), channel_id=1, source_target_pairs={{0,256},{128,384},{256,0},{384,128},{1,257},{129,385},{257,1},{385... | collective-permute-start | bytes 786440 | tf_op jit(solution)/shard_map/ppermute | solution.py:136
  38.0 10.7 %collective-permute-start.3 = (bf16[64,16,128]{2,1,0:T(8,128)(2,1)S(1)}, bf16[64,16,128]{2,1,0:T(8,128)(2,1)S(1)}, u32[]{:S(2)}, u32[]{:S(2)}) collective-permute-start(bf16[64,16,128]{2,1,0:T(8,128)(2,1)S(1)} %pad_maximum_fusion.1), channel_id=1, source_target_pairs={{0,384},{128,0},{256,128},{384,256},{1,385},{129,1},{257,129},{385... | collective-permute-start | bytes 786440 | tf_op jit(solution)/shard_map/ppermute | solution.py:136
  48.7 76.0 %copy-start.6 = (bf16[160,64]{1,0:T(8,128)(2,1)S(1)}, bf16[160,64]{1,0:T(8,128)(2,1)}, u32[]{:S(2)}) copy-start(bf16[160,64]{1,0:T(8,128)(2,1)} %constant.65.clone.slow_fwd) | copy-start | bytes 61444
  51.1 1.5 copy-start
  124.7 1.7 copy-start.1
  126.5 0.8 copy-start.8
  137.9 1.3 copy-start.2
  139.2 116.0 %all-to-all-start.1 = ((bf16[64,128,128]{2,1,0:T(8,128)(2,1)}), bf16[64,128,128]{2,1,0:T(8,128)(2,1)S(1)}, u32[]{:S(2)}, u32[]{:S(2)}) async-start(bf16[64,128,128]{2,1,0:T(8,128)(2,1)} %bitcast.15), calls=%async_computation.1 | async-start | bytes 4194304 | tf_op jit(solution)/shard_map/all_to_all | solution.py:133
  149.4 11.0 %collective-permute-start.4 = (bf16[64,16,128]{2,1,0:T(8,128)(2,1)}, bf16[64,16,128]{2,1,0:T(8,128)(2,1)}, u32[]{:S(2)}, u32[]{:S(2)}) collective-permute-start(bf16[64,16,128]{2,1,0:T(8,128)(2,1)} %get-tuple-element.17), channel_id=1, source_target_pairs={{0,128},{128,256},{256,384},{384,0},{1,129},{129,257},{257,385},{3... | collective-permute-start | bytes 786440 | tf_op jit(solution)/shard_map/ppermute | solution.py:136
  152.6 14.5 %collective-permute-start.5 = (bf16[64,16,128]{2,1,0:T(8,128)(2,1)}, bf16[64,16,128]{2,1,0:T(8,128)(2,1)}, u32[]{:S(2)}, u32[]{:S(2)}) collective-permute-start(bf16[64,16,128]{2,1,0:T(8,128)(2,1)} %get-tuple-element.19), channel_id=1, source_target_pairs={{0,256},{128,384},{256,0},{384,128},{1,257},{129,385},{257,1},{385... | collective-permute-start | bytes 786440 | tf_op jit(solution)/shard_map/ppermute | solution.py:136
  157.2 11.0 %collective-permute-start.6 = (bf16[64,16,128]{2,1,0:T(8,128)(2,1)S(1)}, bf16[64,16,128]{2,1,0:T(8,128)(2,1)}, u32[]{:S(2)}, u32[]{:S(2)}) collective-permute-start(bf16[64,16,128]{2,1,0:T(8,128)(2,1)S(1)} %get-tuple-element.18), channel_id=1, source_target_pairs={{0,384},{128,0},{256,128},{384,256},{1,385},{129,1},{257,129},{385... | collective-permute-start | bytes 786440 | tf_op jit(solution)/shard_map/ppermute | solution.py:136
  169.4 0.8 copy-start.9
  170.3 30.0 %collective-permute-start.7 = (bf16[64,8,128]{2,1,0:T(8,128)(2,1)S(1)}, bf16[64,8,128]{2,1,0:T(8,128)(2,1)S(1)}, u32[]{:S(2)}, u32[]{:S(2)}) collective-permute-start(bf16[64,8,128]{2,1,0:T(8,128)(2,1)S(1)} %dynamic-slice_convert_fusion), channel_id=1, source_target_pairs={{0,64},{64,0},{1,65},{65,1},{2,66},{66,2},{3,67},{67,3},{4,68},{68... | collective-permute-start | bytes 393224 | tf_op jit(solution)/shard_map/ppermute | solution.py:119

commit v12 on v11

--- a/solution.py
+++ b/solution.py
@@ -13,7 +13,7 @@
 FAST = 128
 TOTAL = SLOW * FAST
 HALF = SLOW // 2
-ROWS = 80
+ROWS = 72
 FACTOR = 1.0 / (TOTAL * math.sqrt(TOTAL // 2))
 BLOCK = 16
 BESIDE = 80 * 10**9
@@ -63,8 +63,8 @@
     for j in range(BLOCK):
         sr = section[:ROWS, j * FAST : (j + 1) * FAST]
         si = section[ROWS:, j * FAST : (j + 1) * FAST]
-        parts.append(jnp.concatenate([sr * wr + si * wi, si * wr - sr * wi], axis=1).astype(jnp.bfloat16))
-    return dot(jnp.concatenate(parts, axis=0), fast_fwd[...]).astype(jnp.bfloat16)
+        parts.append(jnp.concatenate([sr * wr + si * wi, si * wr - sr * wi], axis=1))
+    return dot(jnp.concatenate(parts, axis=0).astype(jnp.bfloat16), fast_fwd[...]).astype(jnp.bfloat16)
 
 
 def inverse(spectrum, slow_inv, twid, fast_inv):
@@ -91,15 +91,20 @@
     k_out[...] = forward(taps, slow_fwd, twid, fast_fwd)
 
 
-def products_kernel(values, grads, k_in, slow_fwd, slow_inv, fast_fwd, fast_inv, twid, terms, outs):
+def outs_kernel(values, grads, k_in, slow_fwd, slow_inv, fast_fwd, fast_inv, twid, outs):
+    ur, ui = halves(forward(jnp.swapaxes(values[...], 0, 1), slow_fwd, twid, fast_fwd))
+    kr, ki = halves(k_in[...])
+    conv = inverse(joined(ur * kr - ui * ki, ur * ki + ui * kr), slow_inv, twid, fast_inv)
+    outs[:, 0] = jnp.swapaxes(conv, 0, 1)
+    zr, zi = halves(forward(jnp.swapaxes(grads[...], 0, 1), slow_fwd, twid, fast_fwd))
+    back = inverse(joined(kr * zr + ki * zi, kr * zi - ki * zr), slow_inv, twid, fast_inv)
+    outs[:, 1] = jnp.swapaxes(back, 0, 1)
+
+
+def terms_kernel(values, grads, slow_fwd, slow_inv, fast_fwd, fast_inv, twid, terms):
     ur, ui = halves(forward(jnp.swapaxes(values[...], 0, 1), slow_fwd, twid, fast_fwd))
     zr, zi = halves(forward(jnp.swapaxes(grads[...], 0, 1), slow_fwd, twid, fast_fwd))
     terms[...] = inverse(joined(ur * zr + ui * zi, ur * zi - ui * zr), slow_inv, twid, fast_inv)
-    kr, ki = halves(k_in[...])
-    conv = inverse(joined(ur * kr - ui * ki, ur * ki + ui * kr), slow_inv, twid, fast_inv)
-    outs[:, 0] = jnp.swapaxes(conv, 0, 1)
-    back = inverse(joined(kr * zr + ki * zi, kr * zi - ki * zr), slow_inv, twid, fast_inv)
-    outs[:, 1] = jnp.swapaxes(back, 0, 1)
 
 
 def call(kernel, chans, items, outs, consts, flops=1):
@@ -151,12 +156,12 @@
 
     mine, k_spec = lax.optimization_barrier((move(both), k_spec))
     across = (HALF, BLOCK, FAST)
-    terms, outs = call(
-        products_kernel, chans,
-        [(mine, across, lambda i: (0, i, 0)), (mine, across, lambda i: (0, chans // BLOCK + i, 0)),
-         (k_spec,) + rows[1:]],
-        [lines, ((HALF, 2, chans, FAST), (HALF, 2, BLOCK, FAST), lambda i: (0, 0, i, 0))], consts,
+    signals = [(mine, across, lambda i: (0, i, 0)), (mine, across, lambda i: (0, chans // BLOCK + i, 0))]
+    (outs,) = call(
+        outs_kernel, chans, signals + [(k_spec,) + rows[1:]],
+        [((HALF, 2, chans, FAST), (HALF, 2, BLOCK, FAST), lambda i: (0, 0, i, 0))], consts,
     )
+    (terms,) = call(terms_kernel, chans, signals, [lines], consts)
     arrived = move(outs.reshape(groups, 2 * chans, FAST))
     conv_out = arrived[:, :chans].reshape(values.shape)
     value_grads = arrived[:, chans:].reshape(values.shape)

time: 258 us -> 255 us (0.988)
  Pallas kernels: 13 us -> 15.7 us
    ppermute x2, waiting for transfers between devices: 22.1 us -> 14.4 us  [exchange(): return lax.ppermute(item, axis, [(0, 1), (1, 0)])]
    ppermute x6, waiting for transfers between devices: 15.6 us -> 20 us  [ring(): lax.ppermute(item, 'y', [(i, (i + step) % n_row) for i in range(n_row)])]
    pallas_call x2 -> x3, Pallas kernels: 13 us -> 15.7 us  [call(): pl.pallas_call(kernel, grid=(chans // BLOCK,), in_specs=[pl.BlockSpec(blo...]
    all_to_all x2, waiting for transfers between devices: 125 us -> 128 us  [move(): return lax.all_to_all(item, ctx, split_axis=0, concat_axis=0, tiled=True)]
    unnamed x28 -> x24, local copies, waits for them, and re-layouts: 7.05 us -> 5.34 us
  transfers between devices with their start and end apart: 10 -> 10, of which waited for: 8 -> 7; matrix products, arithmetic and copies ran while one was open for 2% -> 1% of each run, Pallas kernels for 1% -> 3%
where the time goes in v12:
time: 255 us
  waiting for transfers between devices  162 us (64%)
  starting transfers between devices  62.9 us (25%)
  Pallas kernels  15.7 us (6%)
  local copies, waits for them, and re-layouts  9.42 us (4%)
  other arithmetic  3.39 us (1%)
    all_to_all x2, waiting for transfers between devices, move(): return lax.all_to_all(item, ctx, split_axis=0, concat_axis=0, tiled=True)  128 us
    ppermute x2, starting transfers between devices, exchange(): return lax.ppermute(item, axis, [(0, 1), (1, 0)])  24.2 us
    ppermute x6, starting transfers between devices, ring(): lax.ppermute(item, 'y', [(i, (i + step) % n_row) for i in range(n_row)])  20.3 us
    ppermute x6, waiting for transfers between devices, ring(): lax.ppermute(item, 'y', [(i, (i + step) % n_row) for i in range(n_row)])  20 us
    all_to_all x2, starting transfers between devices, move(): return lax.all_to_all(item, ctx, split_axis=0, concat_axis=0, tiled=True)  18.4 us
    pallas_call x3, Pallas kernels, call(): pl.pallas_call(kernel, grid=(chans // BLOCK,), in_specs=[pl.BlockSpec(blo...  15.7 us
    ppermute x2, waiting for transfers between devices, exchange(): return lax.ppermute(item, axis, [(0, 1), (1, 0)])  14.4 us
    unnamed x24, local copies, waits for them, and re-layouts  5.34 us
  transfers between devices with their start and end apart: 10, of which 7 were waited for; matrix products, arithmetic and copies ran while one was open for 1% of the time, Pallas kernels for 3%

profile of v12, /device:TPU:1, one launch (start us, length us, event | category | flops | bytes accessed | tf_op | source)
XLA Modules:
  0.0 254.7 jit_solution(10940347598032678056)
XLA Ops:
  0.6 0.0 copy-start.8
  0.6 3.1 %pad_maximum_fusion = bf16[64,128,128]{2,1,0:T(8,128)(2,1)} fusion(bf16[64,64,128]{2,1,0:T(8,128)(2,1)} %bitcast.17, bf16[64,64,128]{2,1,0:T(8,128)(2,1)} %bitcast.18), kind=kLoop, calls=%fused_computation | loop fusion | flops 4194304 | bytes 4194304 | tf_op jit(solution)/shard_map/concatenate | solution.py:143
  3.8 0.0 copy-done.8
  3.8 16.3 %collective-permute-start = (bf16[64,8,128]{2,1,0:T(8,128)(2,1)S(1)}, bf16[64,8,128]{2,1,0:T(8,128)(2,1)S(1)}, u32[]{:S(2)}, u32[]{:S(2)}) collective-permute-start(bf16[64,8,128]{2,1,0:T(8,128)(2,1)S(1)} %bitcast.21), channel_id=1, source_target_pairs={{0,64},{64,0},{1,65},{65,1},{2,66},{66,2},{3,67},{67,3},{4,68},{68... | collective-permute-start | bytes 393224 | tf_op jit(solution)/shard_map/ppermute | solution.py:124
  20.1 9.0 %all-to-all-start = ((bf16[64,128,128]{2,1,0:T(8,128)(2,1)}), bf16[64,128,128]{2,1,0:T(8,128)(2,1)S(1)}, u32[]{:S(2)}, u32[]{:S(2)}) async-start(bf16[64,128,128]{2,1,0:T(8,128)(2,1)} %pad_maximum_fusion), calls=%async_computation | async-start | bytes 4194304 | tf_op jit(solution)/shard_map/all_to_all | solution.py:138
  29.1 0.0 copy-start.3
  29.1 0.0 copy-start.4
  29.1 0.0 copy-start.5
  29.1 0.0 copy-start.7
  29.1 0.0 collective-permute-done
  29.3 3.3 %collective-permute-start.1 = (bf16[64,16,128]{2,1,0:T(8,128)(2,1)S(1)}, bf16[64,16,128]{2,1,0:T(8,128)(2,1)S(1)}, u32[]{:S(2)}, u32[]{:S(2)}) collective-permute-start(bf16[64,16,128]{2,1,0:T(8,128)(2,1)S(1)} %pad_maximum_fusion.1), channel_id=1, source_target_pairs={{0,128},{128,256},{256,384},{384,0},{1,129},{129,257},{257,385},{3... | collective-permute-start | bytes 786440 | tf_op jit(solution)/shard_map/ppermute | solution.py:141
  32.6 0.8 dynamic-slice_bitcast_fusion.slow_fwd
  33.4 4.5 %collective-permute-start.2 = (bf16[64,16,128]{2,1,0:T(8,128)(2,1)S(1)}, bf16[64,16,128]{2,1,0:T(8,128)(2,1)S(1)}, u32[]{:S(2)}, u32[]{:S(2)}) collective-permute-start(bf16[64,16,128]{2,1,0:T(8,128)(2,1)S(1)} %pad_maximum_fusion.1), channel_id=1, source_target_pairs={{0,256},{128,384},{256,0},{384,128},{1,257},{129,385},{257,1},{385... | collective-permute-start | bytes 786440 | tf_op jit(solution)/shard_map/ppermute | solution.py:141
  37.9 3.0 %collective-permute-start.3 = (bf16[64,16,128]{2,1,0:T(8,128)(2,1)S(1)}, bf16[64,16,128]{2,1,0:T(8,128)(2,1)S(1)}, u32[]{:S(2)}, u32[]{:S(2)}) collective-permute-start(bf16[64,16,128]{2,1,0:T(8,128)(2,1)S(1)} %pad_maximum_fusion.1), channel_id=1, source_target_pairs={{0,384},{128,0},{256,128},{384,256},{1,385},{129,1},{257,129},{385... | collective-permute-start | bytes 786440 | tf_op jit(solution)/shard_map/ppermute | solution.py:141
  41.0 0.0 collective-permute-done.1
  41.0 5.7 %collective-permute-done.2 = bf16[64,16,128]{2,1,0:T(8,128)(2,1)S(1)} collective-permute-done((bf16[64,16,128]{2,1,0:T(8,128)(2,1)S(1)}, bf16[64,16,128]{2,1,0:T(8,128)(2,1)S(1)}, u32[]{:S(2)}, u32[]{:S(2)}) %collective-permute-start.2) | collective-permute-done | bytes 262176 | tf_op jit(solution)/shard_map/ppermute | solution.py:141
  46.8 1.8 collective-permute-done.3
  48.7 0.0 copy-done.3
  48.7 0.0 copy-done.4
  48.7 0.0 copy-done.5
  48.7 0.0 copy-done.7
  48.7 0.0 copy-start.6
  48.7 2.2 shard_map.112.k_in
  50.9 0.0 copy-start.1
  50.9 1.4 copy-done.1
  52.4 72.3 %all-to-all-done.values.grads = bf16[64,128,128]{2,1,0:T(8,128)(2,1)S(1)} async-done(((bf16[64,128,128]{2,1,0:T(8,128)(2,1)}), bf16[64,128,128]{2,1,0:T(8,128)(2,1)S(1)}, u32[]{:S(2)}, u32[]{:S(2)}) %all-to-all-start) | async-done | bytes 2097184 | tf_op jit(solution)/shard_map/all_to_all | solution.py:138
  124.7 0.0 copy-done.6
  124.7 0.0 copy-start.2
  124.7 1.7 copy-done.2
  126.3 7.9 %shard_map.113 = bf16[64,2,64,128]{3,2,1,0:T(8,128)(2,1)S(1)} custom-call(bf16[64,128,128]{2,1,0:T(8,128)(2,1)S(1)} %all-to-all-done.values.grads, bf16[64,128,128]{2,1,0:T(8,128)(2,1)S(1)} %all-to-all-done.values.grads, bf16[4608,256]{1,0:T(8,128)(2,1)S(1)} %copy-done.2, bf16[144,64]{1,0:T(8,128)(2,1)S(1)} %copy-done.6, bf16[64,144]{1,0:T(8,128)(2,1)S(1)} %copy-done.7, ...), custom_call_target="tpu_custom_call" | custom-call | flops 1 | bytes 1 | tf_op jit(solution)/shard_map/pallas_call | solution.py:112
  134.2 0.0 copy-start
  134.2 1.3 copy-done
  135.5 9.3 %all-to-all-start.1 = ((bf16[64,128,128]{2,1,0:T(8,128)(2,1)}), bf16[64,128,128]{2,1,0:T(8,128)(2,1)}, u32[]{:S(2)}, u32[]{:S(2)}) async-start(bf16[64,128,128]{2,1,0:T(8,128)(2,1)} %bitcast.15), calls=%async_computation.1 | async-start | bytes 4194304 | tf_op jit(solution)/shard_map/all_to_all | solution.py:138
  144.9 5.6 %shard_map.114 = bf16[64,64,128]{2,1,0:T(8,128)(2,1)S(1)} custom-call(bf16[64,128,128]{2,1,0:T(8,128)(2,1)S(1)} %all-to-all-done.values.grads, bf16[64,128,128]{2,1,0:T(8,128)(2,1)S(1)} %all-to-all-done.values.grads, bf16[144,64]{1,0:T(8,128)(2,1)S(1)} %copy-done.6, bf16[64,144]{1,0:T(8,128)(2,1)S(1)} %copy-done.7, bf16[256,256]{1,0:T(8,128)(2,1)S(1)} %copy-done.3, ...), custom_call_target="tpu_custom_call" | custom-call | flops 1 | bytes 1 | tf_op jit(solution)/shard_map/pallas_call | solution.py:112
  150.5 0.2 constant_dynamic-slice_fusion.2
  150.7 4.6 %collective-permute-start.6 = (bf16[64,16,128]{2,1,0:T(8,128)(2,1)S(1)}, bf16[64,16,128]{2,1,0:T(8,128)(2,1)S(1)}, u32[]{:S(2)}, u32[]{:S(2)}) collective-permute-start(bf16[64,16,128]{2,1,0:T(8,128)(2,1)S(1)} %get-tuple-element.14), channel_id=1, source_target_pairs={{0,384},{128,0},{256,128},{384,256},{1,385},{129,1},{257,129},{385... | collective-permute-start | bytes 786440 | tf_op jit(solution)/shard_map/ppermute | solution.py:141
  155.4 2.3 collective-permute-start.5
  157.6 2.6 %collective-permute-start.4 = (bf16[64,16,128]{2,1,0:T(8,128)(2,1)S(1)}, bf16[64,16,128]{2,1,0:T(8,128)(2,1)S(1)}, u32[]{:S(2)}, u32[]{:S(2)}) collective-permute-start(bf16[64,16,128]{2,1,0:T(8,128)(2,1)S(1)} %get-tuple-element.13), channel_id=1, source_target_pairs={{0,128},{128,256},{256,384},{384,0},{1,129},{129,257},{257,385},{3... | collective-permute-start | bytes 786440 | tf_op jit(solution)/shard_map/ppermute | solution.py:141
  160.3 5.7 %collective-permute-done.6 = bf16[64,16,128]{2,1,0:T(8,128)(2,1)S(1)} collective-permute-done((bf16[64,16,128]{2,1,0:T(8,128)(2,1)S(1)}, bf16[64,16,128]{2,1,0:T(8,128)(2,1)S(1)}, u32[]{:S(2)}, u32[]{:S(2)}) %collective-permute-start.6) | collective-permute-done | bytes 262176 | tf_op jit(solution)/shard_map/ppermute | solution.py:141
  165.9 0.0 collective-permute-done.5
  166.0 6.8 %collective-permute-done.4 = bf16[64,16,128]{2,1,0:T(8,128)(2,1)S(1)} collective-permute-done((bf16[64,16,128]{2,1,0:T(8,128)(2,1)S(1)}, bf16[64,16,128]{2,1,0:T(8,128)(2,1)S(1)}, u32[]{:S(2)}, u32[]{:S(2)}) %collective-permute-start.4) | collective-permute-done | bytes 262176 | tf_op jit(solution)/shard_map/ppermute | solution.py:141
  172.7 0.1 convert_add_fusion
  172.9 7.9 %collective-permute-start.7 = (bf16[64,8,128]{2,1,0:T(8,128)(2,1)S(1)}, bf16[64,8,128]{2,1,0:T(8,128)(2,1)S(1)}, u32[]{:S(2)}, u32[]{:S(2)}) collective-permute-start(bf16[64,8,128]{2,1,0:T(8,128)(2,1)S(1)} %dynamic-slice_convert_fusion), channel_id=1, source_target_pairs={{0,64},{64,0},{1,65},{65,1},{2,66},{66,2},{3,67},{67,3},{4,68},{68... | collective-permute-start | bytes 393224 | tf_op jit(solution)/shard_map/ppermute | solution.py:124
  180.8 14.4 %collective-permute-done.7 = bf16[64,8,128]{2,1,0:T(8,128)(2,1)S(1)} collective-permute-done((bf16[64,8,128]{2,1,0:T(8,128)(2,1)S(1)}, bf16[64,8,128]{2,1,0:T(8,128)(2,1)S(1)}, u32[]{:S(2)}, u32[]{:S(2)}) %collective-permute-start.7) | collective-permute-done | bytes 131104 | tf_op jit(solution)/shard_map/ppermute | solution.py:124
  195.2 0.8 copy.15
  196.0 55.7 %all-to-all-done.1 = bf16[64,128,128]{2,1,0:T(8,128)(2,1)} async-done(((bf16[64,128,128]{2,1,0:T(8,128)(2,1)}), bf16[64,128,128]{2,1,0:T(8,128)(2,1)}, u32[]{:S(2)}, u32[]{:S(2)}) %all-to-all-start.1) | async-done | bytes 2097184 | tf_op jit(solution)/shard_map/all_to_all | solution.py:138
  251.6 3.0 %fusion = (bf16[64,64,128]{2,1,0:T(8,128)(2,1)}, bf16[64,64,128]{2,1,0:T(8,128)(2,1)}) fusion(bf16[64,128,128]{2,1,0:T(8,128)(2,1)} %all-to-all-done.1), kind=kLoop, calls=%fused_computation.17 | loop fusion | bytes 4194304 | tf_op jit(solution)/shard_map/slice | solution.py:167
  (10 shorter events, 0.3 us)
Async XLA Ops:
  0.6 3.1 %copy-start.8 = (bf16[64,1024]{1,0:T(8,128)(2,1)S(1)}, bf16[64,1024]{1,0:T(8,128)(2,1)}, u32[]{:S(2)}) copy-start(bf16[64,1024]{1,0:T(8,128)(2,1)} %param.11) | copy-start | bytes 393220
  3.8 25.4 %collective-permute-start = (bf16[64,8,128]{2,1,0:T(8,128)(2,1)S(1)}, bf16[64,8,128]{2,1,0:T(8,128)(2,1)S(1)}, u32[]{:S(2)}, u32[]{:S(2)}) collective-permute-start(bf16[64,8,128]{2,1,0:T(8,128)(2,1)S(1)} %bitcast.21), channel_id=1, source_target_pairs={{0,64},{64,0},{1,65},{65,1},{2,66},{66,2},{3,67},{67,3},{4,68},{68... | collective-permute-start | bytes 393224 | tf_op jit(solution)/shard_map/ppermute | solution.py:124
  20.1 104.6 %all-to-all-start = ((bf16[64,128,128]{2,1,0:T(8,128)(2,1)}), bf16[64,128,128]{2,1,0:T(8,128)(2,1)S(1)}, u32[]{:S(2)}, u32[]{:S(2)}) async-start(bf16[64,128,128]{2,1,0:T(8,128)(2,1)} %pad_maximum_fusion), calls=%async_computation | async-start | bytes 4194304 | tf_op jit(solution)/shard_map/all_to_all | solution.py:138
  29.1 19.6 %copy-start.3 = (bf16[256,256]{1,0:T(8,128)(2,1)S(1)}, bf16[256,256]{1,0:T(8,128)(2,1)}, u32[]{:S(2)}) copy-start(bf16[256,256]{1,0:T(8,128)(2,1)} %constant.67.clone.fast_fwd) | copy-start | bytes 393220
  29.1 19.6 %copy-start.4 = (bf16[256,256]{1,0:T(8,128)(2,1)S(1)}, bf16[256,256]{1,0:T(8,128)(2,1)}, u32[]{:S(2)}) copy-start(bf16[256,256]{1,0:T(8,128)(2,1)} %constant.68.clone.fast_inv) | copy-start | bytes 393220
  29.1 19.6 %copy-start.5 = (f32[2,72,128]{2,1,0:T(8,128)S(1)}, f32[2,72,128]{2,1,0:T(8,128)}, u32[]{:S(2)}) copy-start(f32[2,72,128]{2,1,0:T(8,128)} %constant.69.clone.twid) | copy-start | bytes 221188
  29.1 19.6 %copy-start.7 = (bf16[64,144]{1,0:T(8,128)(2,1)S(1)}, bf16[64,144]{1,0:T(8,128)(2,1)}, u32[]{:S(2)}) copy-start(bf16[64,144]{1,0:T(8,128)(2,1)} %constant.66.clone.slow_inv) | copy-start | bytes 55300
  29.3 11.7 %collective-permute-start.1 = (bf16[64,16,128]{2,1,0:T(8,128)(2,1)S(1)}, bf16[64,16,128]{2,1,0:T(8,128)(2,1)S(1)}, u32[]{:S(2)}, u32[]{:S(2)}) collective-permute-start(bf16[64,16,128]{2,1,0:T(8,128)(2,1)S(1)} %pad_maximum_fusion.1), channel_id=1, source_target_pairs={{0,128},{128,256},{256,384},{384,0},{1,129},{129,257},{257,385},{3... | collective-permute-start | bytes 786440 | tf_op jit(solution)/shard_map/ppermute | solution.py:141
  33.4 13.4 %collective-permute-start.2 = (bf16[64,16,128]{2,1,0:T(8,128)(2,1)S(1)}, bf16[64,16,128]{2,1,0:T(8,128)(2,1)S(1)}, u32[]{:S(2)}, u32[]{:S(2)}) collective-permute-start(bf16[64,16,128]{2,1,0:T(8,128)(2,1)S(1)} %pad_maximum_fusion.1), channel_id=1, source_target_pairs={{0,256},{128,384},{256,0},{384,128},{1,257},{129,385},{257,1},{385... | collective-permute-start | bytes 786440 | tf_op jit(solution)/shard_map/ppermute | solution.py:141
  37.9 10.7 %collective-permute-start.3 = (bf16[64,16,128]{2,1,0:T(8,128)(2,1)S(1)}, bf16[64,16,128]{2,1,0:T(8,128)(2,1)S(1)}, u32[]{:S(2)}, u32[]{:S(2)}) collective-permute-start(bf16[64,16,128]{2,1,0:T(8,128)(2,1)S(1)} %pad_maximum_fusion.1), channel_id=1, source_target_pairs={{0,384},{128,0},{256,128},{384,256},{1,385},{129,1},{257,129},{385... | collective-permute-start | bytes 786440 | tf_op jit(solution)/shard_map/ppermute | solution.py:141
  48.7 76.0 %copy-start.6 = (bf16[144,64]{1,0:T(8,128)(2,1)S(1)}, bf16[144,64]{1,0:T(8,128)(2,1)}, u32[]{:S(2)}) copy-start(bf16[144,64]{1,0:T(8,128)(2,1)} %constant.65.clone.slow_fwd) | copy-start | bytes 55300
  50.9 1.4 copy-start.1
  124.7 1.7 copy-start.2
  134.2 1.3 copy-start
  135.5 116.1 %all-to-all-start.1 = ((bf16[64,128,128]{2,1,0:T(8,128)(2,1)}), bf16[64,128,128]{2,1,0:T(8,128)(2,1)}, u32[]{:S(2)}, u32[]{:S(2)}) async-start(bf16[64,128,128]{2,1,0:T(8,128)(2,1)} %bitcast.15), calls=%async_computation.1 | async-start | bytes 4194304 | tf_op jit(solution)/shard_map/all_to_all | solution.py:138
  150.7 15.2 %collective-permute-start.6 = (bf16[64,16,128]{2,1,0:T(8,128)(2,1)S(1)}, bf16[64,16,128]{2,1,0:T(8,128)(2,1)S(1)}, u32[]{:S(2)}, u32[]{:S(2)}) collective-permute-start(bf16[64,16,128]{2,1,0:T(8,128)(2,1)S(1)} %get-tuple-element.14), channel_id=1, source_target_pairs={{0,384},{128,0},{256,128},{384,256},{1,385},{129,1},{257,129},{385... | collective-permute-start | bytes 786440 | tf_op jit(solution)/shard_map/ppermute | solution.py:141
  155.4 10.6 %collective-permute-start.5 = (bf16[64,16,128]{2,1,0:T(8,128)(2,1)S(1)}, bf16[64,16,128]{2,1,0:T(8,128)(2,1)S(1)}, u32[]{:S(2)}, u32[]{:S(2)}) collective-permute-start(bf16[64,16,128]{2,1,0:T(8,128)(2,1)S(1)} %get-tuple-element.15), channel_id=1, source_target_pairs={{0,256},{128,384},{256,0},{384,128},{1,257},{129,385},{257,1},{385... | collective-permute-start | bytes 786440 | tf_op jit(solution)/shard_map/ppermute | solution.py:141
  157.6 15.1 %collective-permute-start.4 = (bf16[64,16,128]{2,1,0:T(8,128)(2,1)S(1)}, bf16[64,16,128]{2,1,0:T(8,128)(2,1)S(1)}, u32[]{:S(2)}, u32[]{:S(2)}) collective-permute-start(bf16[64,16,128]{2,1,0:T(8,128)(2,1)S(1)} %get-tuple-element.13), channel_id=1, source_target_pairs={{0,128},{128,256},{256,384},{384,0},{1,129},{129,257},{257,385},{3... | collective-permute-start | bytes 786440 | tf_op jit(solution)/shard_map/ppermute | solution.py:141
  172.9 22.3 %collective-permute-start.7 = (bf16[64,8,128]{2,1,0:T(8,128)(2,1)S(1)}, bf16[64,8,128]{2,1,0:T(8,128)(2,1)S(1)}, u32[]{:S(2)}, u32[]{:S(2)}) collective-permute-start(bf16[64,8,128]{2,1,0:T(8,128)(2,1)S(1)} %dynamic-slice_convert_fusion), channel_id=1, source_target_pairs={{0,64},{64,0},{1,65},{65,1},{2,66},{66,2},{3,67},{67,3},{4,68},{68... | collective-permute-start | bytes 393224 | tf_op jit(solution)/shard_map/ppermute | solution.py:124

commit v13 on v12

--- a/solution.py
+++ b/solution.py
@@ -15,7 +15,7 @@
 HALF = SLOW // 2
 ROWS = 72
 FACTOR = 1.0 / (TOTAL * math.sqrt(TOTAL // 2))
-BLOCK = 16
+BLOCK = 32
 BESIDE = 80 * 10**9
 
 

time: 255 us -> 254 us (level)
  no operation moved by 1% of the time
where the time goes in v13:
time: 254 us
  waiting for transfers between devices  164 us (65%)
  starting transfers between devices  62.9 us (25%)
  Pallas kernels  13.4 us (5%)
  local copies, waits for them, and re-layouts  9.42 us (4%)
  other arithmetic  3.39 us (1%)
    all_to_all x2, waiting for transfers between devices, move(): return lax.all_to_all(item, ctx, split_axis=0, concat_axis=0, tiled=True)  128 us
    ppermute x2, starting transfers between devices, exchange(): return lax.ppermute(item, axis, [(0, 1), (1, 0)])  24.2 us
    ppermute x6, starting transfers between devices, ring(): lax.ppermute(item, 'y', [(i, (i + step) % n_row) for i in range(n_row)])  20.3 us
    ppermute x6, waiting for transfers between devices, ring(): lax.ppermute(item, 'y', [(i, (i + step) % n_row) for i in range(n_row)])  20 us
    all_to_all x2, starting transfers between devices, move(): return lax.all_to_all(item, ctx, split_axis=0, concat_axis=0, tiled=True)  18.4 us
    ppermute x2, waiting for transfers between devices, exchange(): return lax.ppermute(item, axis, [(0, 1), (1, 0)])  15.2 us
    pallas_call x3, Pallas kernels, call(): pl.pallas_call(kernel, grid=(chans // BLOCK,), in_specs=[pl.BlockSpec(blo...  13.4 us
    unnamed x24, local copies, waits for them, and re-layouts  5.34 us
  transfers between devices with their start and end apart: 10, of which 7 were waited for; matrix products, arithmetic and copies ran while one was open for 1% of the time, Pallas kernels for 3%

profile of v13, /device:TPU:1, one launch (start us, length us, event | category | flops | bytes accessed | tf_op | source)
XLA Modules:
  0.0 253.7 jit_solution(641752215589445977)
XLA Ops:
  0.6 0.0 copy-start.8
  0.6 3.1 %pad_maximum_fusion = bf16[64,128,128]{2,1,0:T(8,128)(2,1)} fusion(bf16[64,64,128]{2,1,0:T(8,128)(2,1)} %bitcast.17, bf16[64,64,128]{2,1,0:T(8,128)(2,1)} %bitcast.18), kind=kLoop, calls=%fused_computation | loop fusion | flops 4194304 | bytes 4194304 | tf_op jit(solution)/shard_map/concatenate | solution.py:143
  3.8 0.0 copy-done.8
  3.8 16.3 %collective-permute-start = (bf16[64,8,128]{2,1,0:T(8,128)(2,1)S(1)}, bf16[64,8,128]{2,1,0:T(8,128)(2,1)S(1)}, u32[]{:S(2)}, u32[]{:S(2)}) collective-permute-start(bf16[64,8,128]{2,1,0:T(8,128)(2,1)S(1)} %bitcast.21), channel_id=1, source_target_pairs={{0,64},{64,0},{1,65},{65,1},{2,66},{66,2},{3,67},{67,3},{4,68},{68... | collective-permute-start | bytes 393224 | tf_op jit(solution)/shard_map/ppermute | solution.py:124
  20.1 9.0 %all-to-all-start = ((bf16[64,128,128]{2,1,0:T(8,128)(2,1)}), bf16[64,128,128]{2,1,0:T(8,128)(2,1)S(1)}, u32[]{:S(2)}, u32[]{:S(2)}) async-start(bf16[64,128,128]{2,1,0:T(8,128)(2,1)} %pad_maximum_fusion), calls=%async_computation | async-start | bytes 4194304 | tf_op jit(solution)/shard_map/all_to_all | solution.py:138
  29.1 0.0 copy-start.3
  29.1 0.0 copy-start.4
  29.1 0.0 copy-start.5
  29.1 0.0 copy-start.7
  29.1 0.0 collective-permute-done
  29.3 3.3 %collective-permute-start.1 = (bf16[64,16,128]{2,1,0:T(8,128)(2,1)S(1)}, bf16[64,16,128]{2,1,0:T(8,128)(2,1)S(1)}, u32[]{:S(2)}, u32[]{:S(2)}) collective-permute-start(bf16[64,16,128]{2,1,0:T(8,128)(2,1)S(1)} %pad_maximum_fusion.1), channel_id=1, source_target_pairs={{0,128},{128,256},{256,384},{384,0},{1,129},{129,257},{257,385},{3... | collective-permute-start | bytes 786440 | tf_op jit(solution)/shard_map/ppermute | solution.py:141
  32.6 0.8 dynamic-slice_bitcast_fusion.slow_fwd
  33.4 4.5 %collective-permute-start.2 = (bf16[64,16,128]{2,1,0:T(8,128)(2,1)S(1)}, bf16[64,16,128]{2,1,0:T(8,128)(2,1)S(1)}, u32[]{:S(2)}, u32[]{:S(2)}) collective-permute-start(bf16[64,16,128]{2,1,0:T(8,128)(2,1)S(1)} %pad_maximum_fusion.1), channel_id=1, source_target_pairs={{0,256},{128,384},{256,0},{384,128},{1,257},{129,385},{257,1},{385... | collective-permute-start | bytes 786440 | tf_op jit(solution)/shard_map/ppermute | solution.py:141
  37.9 3.0 %collective-permute-start.3 = (bf16[64,16,128]{2,1,0:T(8,128)(2,1)S(1)}, bf16[64,16,128]{2,1,0:T(8,128)(2,1)S(1)}, u32[]{:S(2)}, u32[]{:S(2)}) collective-permute-start(bf16[64,16,128]{2,1,0:T(8,128)(2,1)S(1)} %pad_maximum_fusion.1), channel_id=1, source_target_pairs={{0,384},{128,0},{256,128},{384,256},{1,385},{129,1},{257,129},{385... | collective-permute-start | bytes 786440 | tf_op jit(solution)/shard_map/ppermute | solution.py:141
  41.0 0.0 collective-permute-done.1
  41.0 5.7 %collective-permute-done.2 = bf16[64,16,128]{2,1,0:T(8,128)(2,1)S(1)} collective-permute-done((bf16[64,16,128]{2,1,0:T(8,128)(2,1)S(1)}, bf16[64,16,128]{2,1,0:T(8,128)(2,1)S(1)}, u32[]{:S(2)}, u32[]{:S(2)}) %collective-permute-start.2) | collective-permute-done | bytes 262176 | tf_op jit(solution)/shard_map/ppermute | solution.py:141
  46.8 1.8 collective-permute-done.3
  48.7 0.0 copy-done.3
  48.7 0.0 copy-done.4
  48.7 0.0 copy-done.5
  48.7 0.0 copy-done.7
  48.7 0.0 copy-start.6
  48.7 1.6 shard_map.112.k_in
  50.3 0.0 copy-start.1
  50.3 1.4 copy-done.1
  51.8 72.9 %all-to-all-done.values.grads = bf16[64,128,128]{2,1,0:T(8,128)(2,1)S(1)} async-done(((bf16[64,128,128]{2,1,0:T(8,128)(2,1)}), bf16[64,128,128]{2,1,0:T(8,128)(2,1)S(1)}, u32[]{:S(2)}, u32[]{:S(2)}) %all-to-all-start) | async-done | bytes 2097184 | tf_op jit(solution)/shard_map/all_to_all | solution.py:138
  124.7 0.0 copy-done.6
  124.7 0.0 copy-start.2
  124.7 1.7 copy-done.2
  126.3 6.9 %shard_map.113 = bf16[64,2,64,128]{3,2,1,0:T(8,128)(2,1)S(1)} custom-call(bf16[64,128,128]{2,1,0:T(8,128)(2,1)S(1)} %all-to-all-done.values.grads, bf16[64,128,128]{2,1,0:T(8,128)(2,1)S(1)} %all-to-all-done.values.grads, bf16[4608,256]{1,0:T(8,128)(2,1)S(1)} %copy-done.2, bf16[144,64]{1,0:T(8,128)(2,1)S(1)} %copy-done.6, bf16[64,144]{1,0:T(8,128)(2,1)S(1)} %copy-done.7, ...), custom_call_target="tpu_custom_call" | custom-call | flops 1 | bytes 1 | tf_op jit(solution)/shard_map/pallas_call | solution.py:112
  133.2 0.0 copy-start
  133.2 1.3 copy-done
  134.5 9.4 %all-to-all-start.1 = ((bf16[64,128,128]{2,1,0:T(8,128)(2,1)}), bf16[64,128,128]{2,1,0:T(8,128)(2,1)}, u32[]{:S(2)}, u32[]{:S(2)}) async-start(bf16[64,128,128]{2,1,0:T(8,128)(2,1)} %bitcast.15), calls=%async_computation.1 | async-start | bytes 4194304 | tf_op jit(solution)/shard_map/all_to_all | solution.py:138
  143.9 4.9 %shard_map.114 = bf16[64,64,128]{2,1,0:T(8,128)(2,1)S(1)} custom-call(bf16[64,128,128]{2,1,0:T(8,128)(2,1)S(1)} %all-to-all-done.values.grads, bf16[64,128,128]{2,1,0:T(8,128)(2,1)S(1)} %all-to-all-done.values.grads, bf16[144,64]{1,0:T(8,128)(2,1)S(1)} %copy-done.6, bf16[64,144]{1,0:T(8,128)(2,1)S(1)} %copy-done.7, bf16[256,256]{1,0:T(8,128)(2,1)S(1)} %copy-done.3, ...), custom_call_target="tpu_custom_call" | custom-call | flops 1 | bytes 1 | tf_op jit(solution)/shard_map/pallas_call | solution.py:112
  148.9 0.2 constant_dynamic-slice_fusion.2
  149.1 4.6 %collective-permute-start.6 = (bf16[64,16,128]{2,1,0:T(8,128)(2,1)S(1)}, bf16[64,16,128]{2,1,0:T(8,128)(2,1)S(1)}, u32[]{:S(2)}, u32[]{:S(2)}) collective-permute-start(bf16[64,16,128]{2,1,0:T(8,128)(2,1)S(1)} %get-tuple-element.14), channel_id=1, source_target_pairs={{0,384},{128,0},{256,128},{384,256},{1,385},{129,1},{257,129},{385... | collective-permute-start | bytes 786440 | tf_op jit(solution)/shard_map/ppermute | solution.py:141
  153.7 2.3 collective-permute-start.5
  156.0 2.6 %collective-permute-start.4 = (bf16[64,16,128]{2,1,0:T(8,128)(2,1)S(1)}, bf16[64,16,128]{2,1,0:T(8,128)(2,1)S(1)}, u32[]{:S(2)}, u32[]{:S(2)}) collective-permute-start(bf16[64,16,128]{2,1,0:T(8,128)(2,1)S(1)} %get-tuple-element.13), channel_id=1, source_target_pairs={{0,128},{128,256},{256,384},{384,0},{1,129},{129,257},{257,385},{3... | collective-permute-start | bytes 786440 | tf_op jit(solution)/shard_map/ppermute | solution.py:141
  158.6 5.7 %collective-permute-done.6 = bf16[64,16,128]{2,1,0:T(8,128)(2,1)S(1)} collective-permute-done((bf16[64,16,128]{2,1,0:T(8,128)(2,1)S(1)}, bf16[64,16,128]{2,1,0:T(8,128)(2,1)S(1)}, u32[]{:S(2)}, u32[]{:S(2)}) %collective-permute-start.6) | collective-permute-done | bytes 262176 | tf_op jit(solution)/shard_map/ppermute | solution.py:141
  164.3 0.0 collective-permute-done.5
  164.3 6.7 %collective-permute-done.4 = bf16[64,16,128]{2,1,0:T(8,128)(2,1)S(1)} collective-permute-done((bf16[64,16,128]{2,1,0:T(8,128)(2,1)S(1)}, bf16[64,16,128]{2,1,0:T(8,128)(2,1)S(1)}, u32[]{:S(2)}, u32[]{:S(2)}) %collective-permute-start.4) | collective-permute-done | bytes 262176 | tf_op jit(solution)/shard_map/ppermute | solution.py:141
  171.1 0.1 convert_add_fusion
  171.3 7.9 %collective-permute-start.7 = (bf16[64,8,128]{2,1,0:T(8,128)(2,1)S(1)}, bf16[64,8,128]{2,1,0:T(8,128)(2,1)S(1)}, u32[]{:S(2)}, u32[]{:S(2)}) collective-permute-start(bf16[64,8,128]{2,1,0:T(8,128)(2,1)S(1)} %dynamic-slice_convert_fusion), channel_id=1, source_target_pairs={{0,64},{64,0},{1,65},{65,1},{2,66},{66,2},{3,67},{67,3},{4,68},{68... | collective-permute-start | bytes 393224 | tf_op jit(solution)/shard_map/ppermute | solution.py:124
  179.2 15.2 %collective-permute-done.7 = bf16[64,8,128]{2,1,0:T(8,128)(2,1)S(1)} collective-permute-done((bf16[64,8,128]{2,1,0:T(8,128)(2,1)S(1)}, bf16[64,8,128]{2,1,0:T(8,128)(2,1)S(1)}, u32[]{:S(2)}, u32[]{:S(2)}) %collective-permute-start.7) | collective-permute-done | bytes 131104 | tf_op jit(solution)/shard_map/ppermute | solution.py:124
  194.4 0.8 copy.15
  195.1 55.5 %all-to-all-done.1 = bf16[64,128,128]{2,1,0:T(8,128)(2,1)} async-done(((bf16[64,128,128]{2,1,0:T(8,128)(2,1)}), bf16[64,128,128]{2,1,0:T(8,128)(2,1)}, u32[]{:S(2)}, u32[]{:S(2)}) %all-to-all-start.1) | async-done | bytes 2097184 | tf_op jit(solution)/shard_map/all_to_all | solution.py:138
  250.6 3.0 %fusion = (bf16[64,64,128]{2,1,0:T(8,128)(2,1)}, bf16[64,64,128]{2,1,0:T(8,128)(2,1)}) fusion(bf16[64,128,128]{2,1,0:T(8,128)(2,1)} %all-to-all-done.1), kind=kLoop, calls=%fused_computation.17 | loop fusion | bytes 4194304 | tf_op jit(solution)/shard_map/slice | solution.py:167
  (10 shorter events, 0.3 us)
Async XLA Ops:
  0.6 3.1 %copy-start.8 = (bf16[64,1024]{1,0:T(8,128)(2,1)S(1)}, bf16[64,1024]{1,0:T(8,128)(2,1)}, u32[]{:S(2)}) copy-start(bf16[64,1024]{1,0:T(8,128)(2,1)} %param.11) | copy-start | bytes 393220
  3.8 25.4 %collective-permute-start = (bf16[64,8,128]{2,1,0:T(8,128)(2,1)S(1)}, bf16[64,8,128]{2,1,0:T(8,128)(2,1)S(1)}, u32[]{:S(2)}, u32[]{:S(2)}) collective-permute-start(bf16[64,8,128]{2,1,0:T(8,128)(2,1)S(1)} %bitcast.21), channel_id=1, source_target_pairs={{0,64},{64,0},{1,65},{65,1},{2,66},{66,2},{3,67},{67,3},{4,68},{68... | collective-permute-start | bytes 393224 | tf_op jit(solution)/shard_map/ppermute | solution.py:124
  20.1 104.6 %all-to-all-start = ((bf16[64,128,128]{2,1,0:T(8,128)(2,1)}), bf16[64,128,128]{2,1,0:T(8,128)(2,1)S(1)}, u32[]{:S(2)}, u32[]{:S(2)}) async-start(bf16[64,128,128]{2,1,0:T(8,128)(2,1)} %pad_maximum_fusion), calls=%async_computation | async-start | bytes 4194304 | tf_op jit(solution)/shard_map/all_to_all | solution.py:138
  29.1 19.6 %copy-start.3 = (bf16[256,256]{1,0:T(8,128)(2,1)S(1)}, bf16[256,256]{1,0:T(8,128)(2,1)}, u32[]{:S(2)}) copy-start(bf16[256,256]{1,0:T(8,128)(2,1)} %constant.67.clone.fast_fwd) | copy-start | bytes 393220
  29.1 19.6 %copy-start.4 = (bf16[256,256]{1,0:T(8,128)(2,1)S(1)}, bf16[256,256]{1,0:T(8,128)(2,1)}, u32[]{:S(2)}) copy-start(bf16[256,256]{1,0:T(8,128)(2,1)} %constant.68.clone.fast_inv) | copy-start | bytes 393220
  29.1 19.6 %copy-start.5 = (f32[2,72,128]{2,1,0:T(8,128)S(1)}, f32[2,72,128]{2,1,0:T(8,128)}, u32[]{:S(2)}) copy-start(f32[2,72,128]{2,1,0:T(8,128)} %constant.69.clone.twid) | copy-start | bytes 221188
  29.1 19.6 %copy-start.7 = (bf16[64,144]{1,0:T(8,128)(2,1)S(1)}, bf16[64,144]{1,0:T(8,128)(2,1)}, u32[]{:S(2)}) copy-start(bf16[64,144]{1,0:T(8,128)(2,1)} %constant.66.clone.slow_inv) | copy-start | bytes 55300
  29.3 11.7 %collective-permute-start.1 = (bf16[64,16,128]{2,1,0:T(8,128)(2,1)S(1)}, bf16[64,16,128]{2,1,0:T(8,128)(2,1)S(1)}, u32[]{:S(2)}, u32[]{:S(2)}) collective-permute-start(bf16[64,16,128]{2,1,0:T(8,128)(2,1)S(1)} %pad_maximum_fusion.1), channel_id=1, source_target_pairs={{0,128},{128,256},{256,384},{384,0},{1,129},{129,257},{257,385},{3... | collective-permute-start | bytes 786440 | tf_op jit(solution)/shard_map/ppermute | solution.py:141
  33.4 13.4 %collective-permute-start.2 = (bf16[64,16,128]{2,1,0:T(8,128)(2,1)S(1)}, bf16[64,16,128]{2,1,0:T(8,128)(2,1)S(1)}, u32[]{:S(2)}, u32[]{:S(2)}) collective-permute-start(bf16[64,16,128]{2,1,0:T(8,128)(2,1)S(1)} %pad_maximum_fusion.1), channel_id=1, source_target_pairs={{0,256},{128,384},{256,0},{384,128},{1,257},{129,385},{257,1},{385... | collective-permute-start | bytes 786440 | tf_op jit(solution)/shard_map/ppermute | solution.py:141
  37.9 10.7 %collective-permute-start.3 = (bf16[64,16,128]{2,1,0:T(8,128)(2,1)S(1)}, bf16[64,16,128]{2,1,0:T(8,128)(2,1)S(1)}, u32[]{:S(2)}, u32[]{:S(2)}) collective-permute-start(bf16[64,16,128]{2,1,0:T(8,128)(2,1)S(1)} %pad_maximum_fusion.1), channel_id=1, source_target_pairs={{0,384},{128,0},{256,128},{384,256},{1,385},{129,1},{257,129},{385... | collective-permute-start | bytes 786440 | tf_op jit(solution)/shard_map/ppermute | solution.py:141
  48.7 76.0 %copy-start.6 = (bf16[144,64]{1,0:T(8,128)(2,1)S(1)}, bf16[144,64]{1,0:T(8,128)(2,1)}, u32[]{:S(2)}) copy-start(bf16[144,64]{1,0:T(8,128)(2,1)} %constant.65.clone.slow_fwd) | copy-start | bytes 55300
  50.3 1.4 copy-start.1
  124.7 1.7 copy-start.2
  133.2 1.3 copy-start
  134.5 116.1 %all-to-all-start.1 = ((bf16[64,128,128]{2,1,0:T(8,128)(2,1)}), bf16[64,128,128]{2,1,0:T(8,128)(2,1)}, u32[]{:S(2)}, u32[]{:S(2)}) async-start(bf16[64,128,128]{2,1,0:T(8,128)(2,1)} %bitcast.15), calls=%async_computation.1 | async-start | bytes 4194304 | tf_op jit(solution)/shard_map/all_to_all | solution.py:138
  149.1 15.2 %collective-permute-start.6 = (bf16[64,16,128]{2,1,0:T(8,128)(2,1)S(1)}, bf16[64,16,128]{2,1,0:T(8,128)(2,1)S(1)}, u32[]{:S(2)}, u32[]{:S(2)}) collective-permute-start(bf16[64,16,128]{2,1,0:T(8,128)(2,1)S(1)} %get-tuple-element.14), channel_id=1, source_target_pairs={{0,384},{128,0},{256,128},{384,256},{1,385},{129,1},{257,129},{385... | collective-permute-start | bytes 786440 | tf_op jit(solution)/shard_map/ppermute | solution.py:141
  153.7 10.6 %collective-permute-start.5 = (bf16[64,16,128]{2,1,0:T(8,128)(2,1)S(1)}, bf16[64,16,128]{2,1,0:T(8,128)(2,1)S(1)}, u32[]{:S(2)}, u32[]{:S(2)}) collective-permute-start(bf16[64,16,128]{2,1,0:T(8,128)(2,1)S(1)} %get-tuple-element.15), channel_id=1, source_target_pairs={{0,256},{128,384},{256,0},{384,128},{1,257},{129,385},{257,1},{385... | collective-permute-start | bytes 786440 | tf_op jit(solution)/shard_map/ppermute | solution.py:141
  156.0 15.1 %collective-permute-start.4 = (bf16[64,16,128]{2,1,0:T(8,128)(2,1)S(1)}, bf16[64,16,128]{2,1,0:T(8,128)(2,1)S(1)}, u32[]{:S(2)}, u32[]{:S(2)}) collective-permute-start(bf16[64,16,128]{2,1,0:T(8,128)(2,1)S(1)} %get-tuple-element.13), channel_id=1, source_target_pairs={{0,128},{128,256},{256,384},{384,0},{1,129},{129,257},{257,385},{3... | collective-permute-start | bytes 786440 | tf_op jit(solution)/shard_map/ppermute | solution.py:141
  171.3 23.1 %collective-permute-start.7 = (bf16[64,8,128]{2,1,0:T(8,128)(2,1)S(1)}, bf16[64,8,128]{2,1,0:T(8,128)(2,1)S(1)}, u32[]{:S(2)}, u32[]{:S(2)}) collective-permute-start(bf16[64,8,128]{2,1,0:T(8,128)(2,1)S(1)} %dynamic-slice_convert_fusion), channel_id=1, source_target_pairs={{0,64},{64,0},{1,65},{65,1},{2,66},{66,2},{3,67},{67,3},{4,68},{68... | collective-permute-start | bytes 393224 | tf_op jit(solution)/shard_map/ppermute | solution.py:124
